TPU v7x, 256 devices: a whole 4x4x8 slice. The times are simulated.
256 devices in a mesh: atoms: 128 (over z, y, x), chan: 2 (over core).
Axes of the slice: x: 4, y: 4, z: 8, core: 2. Of those that a mesh axis runs over, the one named last changes fastest.
Arguments:
- features: bfloat16 [4096, 6400], P('atoms', 'chan'), may hold values from -6 to 6
- send_rows: int32 [512, 32], P('atoms'), may hold values from 0 to 31
- edge_source: int32 [65536], P(('atoms', 'chan')), may hold values from 0 to 159
- edge_dest: int32 [65536], P(('atoms', 'chan')), may hold values from 0 to 32, as said below
- edge_rot: int32 [65536], P(('atoms', 'chan')), may hold values from 0 to 511
- edge_weight: float32 [65536], P(('atoms', 'chan')), may hold values from 0.25 to 1
- rot_table: float32 [512, 165], replicated, may hold values from -2.5 to 2.5
- mix_zero: bfloat16 [640, 640], replicated, may hold values from -0.25 to 0.25
- mix_one: bfloat16 [2, 512, 512], replicated, may hold values from -0.1875 to 0.1875
- mix_two: bfloat16 [2, 384, 384], replicated, may hold values from -0.21875 to 0.21875
- atom_species: int32 [4096], P('atoms'), may hold values from 0 to 3
- species_orbitals: int32 [4], replicated, may hold values from 2 to 16, as said below
- head_weight: bfloat16 [6400, 512], P(None, 'chan'), may hold values from -0.078125 to 0.078125
- target_blocks: float32 [4096, 512], P('atoms', 'chan'), may hold values from -6 to 6
Outputs:
- atom_loss: float32 [4096], P('atoms')
- grad_head: bfloat16 [6400, 512], P(None, 'chan')
- grad_features: float32 [4096, 6400], P('atoms', 'chan')
Inputs may be any that keep to these rules, and one draw needn't show every extreme that they name: edge_dest == 32 marks an empty edge slot; live slots come first on each device, and some device has all 256 slots live. `species_orbitals`: each value is even; some species has 16, another 16 - 2.
All inputs are finite; a program needn't handle non-finite values.
Results may differ from a plain program's by a relative error of at most 0.0057.
Values may be sent and summed in bfloat16 or wider, within the bound.
No kernel may reach another device: no remote copies, remote signals or barrier semaphores. Data moves between devices by JAX's collectives and lax.ppermute only.
A program may use at most 128 MiB of HBM per device.

v0:
```python
import jax
import jax.numpy as jnp
import numpy as np
from jax import lax
from jax.sharding import PartitionSpec as P

ORB = 16


lmax_value = 4
mmax_value = 2
branch_scale = 0.125
shift_offsets = (1, -1, 2, -2)
highest = lax.Precision.HIGHEST


def from_behind(x, axis, by):
    count = lax.axis_size(axis)
    return lax.ppermute(x, axis, [(i, (i + by) % count) for i in range(count)])


def coefficient_tables():
    retained = []
    for degree in range(lmax_value + 1):
        m_top = min(degree, mmax_value)
        for m_order in range(-m_top, m_top + 1):
            retained.append((degree, m_order))
    starts = [0]
    for degree in range(lmax_value + 1):
        starts.append(starts[-1] + (2 * degree + 1) ** 2)
    lookup = np.full((len(retained), (lmax_value + 1) ** 2), starts[-1], dtype=np.int32)
    for row_pos, pair in enumerate(retained):
        degree, m_order = pair
        size_l = 2 * degree + 1
        for column in range(size_l):
            lookup[row_pos, degree * degree + column] = (
                starts[degree] + (degree + m_order) * size_l + column
            )
    groups = []
    for m_order in range(mmax_value + 1):
        plus_side = [row_pos for row_pos, pair in enumerate(retained) if pair[1] == m_order]
        minus_side = [row_pos for row_pos, pair in enumerate(retained) if pair[1] == -m_order]
        groups.append((plus_side, minus_side))
    return (lookup, groups)


def edge_frames(rot_table, rot_ids):
    lookup = coefficient_tables()[0]
    packed = jnp.take(rot_table, rot_ids, axis=0)
    padded = jnp.concatenate([packed, jnp.zeros((packed.shape[0], 1), jnp.float32)], axis=1)
    return jnp.take(padded, jnp.asarray(lookup), axis=1)


def rotate_in(source, frames):
    return jnp.einsum(
        "eik,ecpk->ecpi", frames, source.astype(jnp.float32), precision=highest
    ).astype(jnp.bfloat16)


def mixing_step(rotated, mix_zero, mix_one, mix_two):
    edge_count = rotated.shape[0]
    channels = rotated.shape[1]
    groups = coefficient_tables()[1]

    def flatten(positions):
        selected = rotated[:, :, :, np.array(positions)]
        return jnp.transpose(selected, (0, 2, 1, 3)).reshape(
            edge_count * 2, channels * len(positions)
        )

    def unflatten(values, width_count):
        return values.reshape(edge_count, 2, channels, width_count)

    zero_side = groups[0][0]
    pieces = [
        unflatten(
            jnp.dot(flatten(zero_side), mix_zero, preferred_element_type=jnp.float32),
            len(zero_side),
        )
    ]
    placed = list(zero_side)
    for m_order, mix_pair in ((1, mix_one), (2, mix_two)):
        plus_side, minus_side = groups[m_order]
        plus_in = flatten(plus_side)
        minus_in = flatten(minus_side)
        plus_out = jnp.dot(plus_in, mix_pair[0], preferred_element_type=jnp.float32) - jnp.dot(
            minus_in, mix_pair[1], preferred_element_type=jnp.float32
        )
        minus_out = jnp.dot(minus_in, mix_pair[0], preferred_element_type=jnp.float32) + jnp.dot(
            plus_in, mix_pair[1], preferred_element_type=jnp.float32
        )
        pieces.append(unflatten(plus_out, len(plus_side)))
        pieces.append(unflatten(minus_out, len(minus_side)))
        placed = placed + list(plus_side) + list(minus_side)
    joined = jnp.concatenate(pieces, axis=3)
    inverse = np.argsort(np.array(placed))
    return jnp.transpose(joined[:, :, :, inverse], (0, 2, 1, 3))


def rotate_out(mixture, frames, weights):
    scaled = mixture * weights[:, None, None, None]
    back = jnp.einsum("eik,ecpi->ecpk", frames, scaled, precision=highest)
    return back.reshape(back.shape[0], -1)


def body(
    features,
    send_rows,
    edge_source,
    edge_dest,
    edge_rot,
    edge_weight,
    rot_table,
    mix_zero,
    mix_one,
    mix_two,
    atom_species,
    species_orbitals,
    head_weight,
    target_blocks,
):
    atoms_here = features.shape[0]
    local_width = features.shape[1]
    local_channels = local_width // 50
    arrivals = [features]
    for position, offset in enumerate(shift_offsets):
        leaving = jnp.take(features, send_rows[position], axis=0)
        arrivals.append(from_behind(leaving, "atoms", offset))
    buffer_rows = jnp.concatenate(arrivals, axis=0)
    own_frames = edge_frames(rot_table, edge_rot)
    shard_source, shard_rot = (
        lax.all_gather(edge_source, "chan", axis=0, tiled=True),
        lax.all_gather(edge_rot, "chan", axis=0, tiled=True),
    )
    picked = jnp.take(buffer_rows, shard_source, axis=0).reshape(
        shard_source.shape[0], local_channels, 2, 25
    )
    partial_rotated = rotate_in(picked, edge_frames(rot_table, shard_rot))
    rotated = lax.all_to_all(partial_rotated, "chan", split_axis=0, concat_axis=1, tiled=True)
    mixture = mixing_step(rotated, mix_zero, mix_one, mix_two)
    messages = rotate_out(mixture, own_frames, edge_weight)
    onehot = (edge_dest[None, :] == jnp.arange(atoms_here, dtype=jnp.int32)[:, None]).astype(
        jnp.float32
    )
    partial_sums = jnp.dot(onehot, messages, precision=highest, preferred_element_type=jnp.float32)
    aggregate = lax.psum_scatter(partial_sums, "chan", scatter_dimension=1, tiled=True)
    updated = (features.astype(jnp.float32) + branch_scale * aggregate).astype(jnp.bfloat16)
    full_rows = lax.all_gather(updated, "chan", axis=1, tiled=True)
    blocks = jnp.dot(full_rows, head_weight, preferred_element_type=jnp.float32)
    block_cols = head_weight.shape[1]
    columns = lax.axis_index("chan") * block_cols + jnp.arange(block_cols, dtype=jnp.int32)
    species_ids = jnp.arange(species_orbitals.shape[0], dtype=jnp.int32)
    norbitals = jnp.sum(
        jnp.where(atom_species[:, None] == species_ids[None, :], species_orbitals[None, :], 0),
        axis=1,
    )
    valid_entry = ((columns // (2 * ORB))[None, :] < norbitals[:, None]) & (
        (columns // 2 % ORB)[None, :] < norbitals[:, None]
    )
    block_error = jnp.where(valid_entry, blocks - target_blocks, 0.0)
    divisor = norbitals.astype(jnp.float32)
    atom_loss = lax.psum(jnp.sum(block_error * block_error, axis=1) / divisor, "chan")
    dblocks = (2.0 * block_error / divisor[:, None]).astype(jnp.bfloat16)
    grad_part = lax.dot_general(
        full_rows, dblocks, (((0,), (0,)), ((), ())), preferred_element_type=jnp.float32
    )
    grad_head = lax.psum(grad_part, "atoms").astype(jnp.bfloat16)
    feature_part = lax.dot_general(
        dblocks, head_weight, (((1,), (1,)), ((), ())), preferred_element_type=jnp.float32
    )
    grad_features = lax.psum_scatter(feature_part, "chan", scatter_dimension=1, tiled=True)
    return (atom_loss, grad_head, grad_features)


def solution(mesh):
    return jax.shard_map(
        body,
        mesh=mesh,
        in_specs=(
            P("atoms", "chan"),
            P("atoms", None),
            P(("atoms", "chan")),
            P(("atoms", "chan")),
            P(("atoms", "chan")),
            P(("atoms", "chan")),
            P(),
            P(),
            P(),
            P(),
            P("atoms"),
            P(),
            P(None, "chan"),
            P("atoms", "chan"),
        ),
        out_specs=(P("atoms"), P(None, "chan"), P("atoms", "chan")),
        check_vma=False,
    )
```

profile of v0, /device:TPU:1, one launch (start us, length us, event | category | flops | bytes accessed | tf_op | source)
XLA Modules:
  0.0 1532.3 jit_solution(18148704495616798800)
XLA Ops:
  8.2 2.7 gather_fusion.11
  14.6 2.5 gather_fusion.12
  18.8 9.0 collective-permute-start.1
  34.0 7.2 collective-permute-start.3
  41.9 3.0 all-gather.1
  49.5 3.3 gather_fusion.1
  58.4 3.7 gather_fusion.2
  62.1 2.4 reshape.187
  64.5 5.4 copy.155
  84.6 3.1 copy.157
  94.9 8.6 gather_fusion
  103.5 5.6 copy.124
  109.2 5.7 gather.44
  114.9 4.5 broadcast_select_fusion
  119.4 15.7 %copy.127 = bf16[512,64,2,25]{1,3,2,0:T(8,128)(2,1)} copy(bf16[512,64,2,25]{0,3,2,1:T(8,128)(2,1)} %broadcast_select_fusion) | data formatting | bytes 6553600 | tf_op jit(solution)/shard_map/jit(_take)/select_n | solution.py:135
  135.1 10.9 convolution_convert_fusion
  146.0 10.1 copy.176
  156.1 6.6 reshape.279
  162.8 9.3 all_to_all.18
  172.1 6.5 reshape.280
  178.6 11.1 copy.162
  189.7 3.1 gather_fusion.4
  192.8 27.6 %copy.138 = bf16[256,2,128,4]{3,2,1,0:T(8,128)(2,1)} copy(bf16[256,2,128,4]{0,2,1,3:T(8,128)(2,1)} %bitcast.105) | data formatting | bytes 1048576 | tf_op jit(solution)/shard_map/transpose | solution.py:67
  220.3 33.2 %reshape.125 = bf16[512,512]{1,0:T(8,128)(2,1)} reshape(bf16[256,2,128,4]{3,2,1,0:T(8,128)(2,1)} %copy.138) | data formatting | bytes 1048576 | tf_op jit(solution)/shard_map/reshape | solution.py:67
  253.5 3.1 gather_fusion.5
  256.6 27.6 %copy.140 = bf16[256,2,128,4]{3,2,1,0:T(8,128)(2,1)} copy(bf16[256,2,128,4]{0,2,1,3:T(8,128)(2,1)} %bitcast.106) | data formatting | bytes 1048576 | tf_op jit(solution)/shard_map/transpose | solution.py:67
  284.2 33.2 %reshape.126 = bf16[512,512]{1,0:T(8,128)(2,1)} reshape(bf16[256,2,128,4]{3,2,1,0:T(8,128)(2,1)} %copy.140) | data formatting | bytes 1048576 | tf_op jit(solution)/shard_map/reshape | solution.py:67
  319.0 2.6 fusion.5
  321.7 2.6 convolution_subtract_fusion
  324.3 36.8 %reshape.127 = f32[256,2,128,4]{3,2,1,0:T(8,128)} reshape(f32[512,512]{1,0:T(8,128)} %convolution_subtract_fusion) | data formatting | bytes 2097152 | tf_op jit(solution)/shard_map/reshape | solution.py:72
  361.1 19.5 %copy.145 = f32[256,2,128,4]{2,0,1,3:T(8,128)} copy(f32[256,2,128,4]{3,2,1,0:T(8,128)} %reshape.127) | data formatting | bytes 2097152 | tf_op jit(solution)/shard_map/reshape | solution.py:72
  380.6 3.2 gather_fusion.3
  383.7 2.6 copy.133
  386.3 2.9 copy.135
  389.2 3.0 convolution_add_fusion
  392.2 37.0 %reshape.128 = f32[256,2,128,4]{3,2,1,0:T(8,128)} reshape(f32[512,512]{1,0:T(8,128)} %convolution_add_fusion) | data formatting | bytes 2097152 | tf_op jit(solution)/shard_map/reshape | solution.py:72
  429.2 19.5 %copy.146 = f32[256,2,128,4]{2,0,1,3:T(8,128)} copy(f32[256,2,128,4]{3,2,1,0:T(8,128)} %reshape.128) | data formatting | bytes 2097152 | tf_op jit(solution)/shard_map/reshape | solution.py:72
  448.7 3.0 gather_fusion.6
  451.7 25.2 %copy.142 = bf16[256,2,128,3]{3,2,1,0:T(8,128)(2,1)} copy(bf16[256,2,128,3]{0,2,1,3:T(8,128)(2,1)} %bitcast.104) | data formatting | bytes 786432 | tf_op jit(solution)/shard_map/transpose | solution.py:67
  476.9 20.8 %reshape.129 = bf16[512,384]{1,0:T(8,128)(2,1)} reshape(bf16[256,2,128,3]{3,2,1,0:T(8,128)(2,1)} %copy.142) | data formatting | bytes 786432 | tf_op jit(solution)/shard_map/reshape | solution.py:67
  497.7 3.0 gather_fusion.7
  500.7 25.2 %copy.144 = bf16[256,2,128,3]{3,2,1,0:T(8,128)(2,1)} copy(bf16[256,2,128,3]{0,2,1,3:T(8,128)(2,1)} %bitcast.103) | data formatting | bytes 786432 | tf_op jit(solution)/shard_map/transpose | solution.py:67
  526.0 20.8 %reshape.130 = bf16[512,384]{1,0:T(8,128)(2,1)} reshape(bf16[256,2,128,3]{3,2,1,0:T(8,128)(2,1)} %copy.144) | data formatting | bytes 786432 | tf_op jit(solution)/shard_map/reshape | solution.py:67
  548.2 2.3 fusion.15
  550.6 2.4 convolution_subtract_fusion.1
  552.9 33.9 %reshape.131 = f32[256,2,128,3]{3,2,1,0:T(8,128)} reshape(f32[512,384]{1,0:T(8,128)} %convolution_subtract_fusion.1) | data formatting | bytes 1572864 | tf_op jit(solution)/shard_map/reshape | solution.py:72
  586.8 19.4 %copy.147 = f32[256,2,128,3]{2,0,1,3:T(8,128)} copy(f32[256,2,128,3]{3,2,1,0:T(8,128)} %reshape.131) | data formatting | bytes 1572864 | tf_op jit(solution)/shard_map/reshape | solution.py:72
  606.2 2.6 convolution_add_fusion.1
  608.8 33.9 %reshape.132 = f32[256,2,128,3]{3,2,1,0:T(8,128)} reshape(f32[512,384]{1,0:T(8,128)} %convolution_add_fusion.1) | data formatting | bytes 1572864 | tf_op jit(solution)/shard_map/reshape | solution.py:72
  642.7 19.8 %copy.148 = f32[256,2,128,3]{2,0,1,3:T(8,128)} copy(f32[256,2,128,3]{3,2,1,0:T(8,128)} %reshape.132) | data formatting | bytes 1572864 | tf_op jit(solution)/shard_map/reshape | solution.py:72
  662.6 3.5 convolution_dynamic-update-slice_fusion
  666.1 2.3 constant_dynamic-update-slice_fusion.8
  671.3 5.8 copy.149
  677.2 5.6 gather_fusion.8
  682.8 5.3 multiply_bitcast_fusion
  688.1 6.4 copy.152
  694.5 15.0 fusion.29
  709.5 10.5 copy.154
  720.0 8.6 reshape.133
  728.6 7.1 fusion.23
  736.0 8.8 reduce-scatter.3.cloned.1.call-done
  748.8 3.8 fusion.28
  754.6 660.9 %all-reduce.3 = bf16[6400,256]{1,0:T(8,128)(2,1)} all-reduce(f32[6400,256]{1,0:T(8,128)} %fusion.28), channel_id=1, replica_groups=mesh['atoms'=128,'chan'=2] {'atoms'}, use_global_device_ids=true, to_apply=%region_4.6 | all-reduce | flops 1638400 | bytes 9830400 | tf_op jit(solution)/shard_map/psum | solution.py:167
  1415.5 109.8 %psum.14 = f32[32]{0:T(128)} all-reduce(f32[32]{0:T(128)S(1)} %convert_divide_fusion), channel_id=1, replica_groups=mesh['atoms'=128,'chan'=2] {'chan'}, use_global_device_ids=true, to_apply=%region_3.5 | all-reduce | flops 32 | bytes 256 | tf_op jit(solution)/shard_map/psum | solution.py:162
  (105 shorter events, 57.6 us)
Async XLA Ops:
  7.2 740.8 %copy-start = (bf16[6400,256]{1,0:T(8,128)(2,1)S(1)}, bf16[6400,256]{1,0:T(8,128)(2,1)}, u32[]{:S(2)}) copy-start(bf16[6400,256]{1,0:T(8,128)(2,1)} %param.42) | copy-start | bytes 9830404
  7.2 20.7 %copy-start.1 = (bf16[32,3200]{1,0:T(8,128)(2,1)S(1)}, bf16[32,3200]{1,0:T(8,128)(2,1)}, u32[]{:S(2)}) copy-start(bf16[32,3200]{1,0:T(8,128)(2,1)} %param.30) | copy-start | bytes 614404
  7.2 34.7 %copy-start.7 = (s32[256]{0:T(256)S(1)}, s32[256]{0:T(256)}, u32[]{:S(2)}) copy-start(s32[256]{0:T(256)} %param.34) | copy-start | bytes 3076
  7.2 38.2 %copy-start.10 = (s32[256]{0:T(256)S(1)}, s32[256]{0:T(256)}, u32[]{:S(2)}) copy-start(s32[256]{0:T(256)} %param.32) | copy-start | bytes 3076
  7.2 737.6 %reduce-scatter.3.cloned.1.call-start = ((), (), s32[]{:S(2)}) async-start(), calls=%async_computation.3 | async-start | bytes 1228800 | tf_op jit(solution)/shard_map/reduce_scatter | solution.py:146
  8.2 41.3 %copy-start.8 = (s32[475]{0:T(512)S(1)}, s32[475]{0:T(512)}, u32[]{:S(2)}) copy-start(s32[475]{0:T(512)} %constant.189) | copy-start | bytes 5704
  12.6 75.8 %collective-permute-start = (bf16[32,3200]{1,0:T(8,128)(2,1)}, bf16[32,3200]{1,0:T(8,128)(2,1)}, u32[]{:S(2)}, u32[]{:S(2)}) collective-permute-start(bf16[32,3200]{1,0:T(8,128)(2,1)} %broadcast_select_fusion.5), channel_id=1, source_target_pairs={{0,2},{2,4},{4,6},{6,8},{8,10},{10,12},{12,14},{14,16},{16,18},{18... | collective-permute-start | bytes 614408 | tf_op jit(solution)/shard_map/ppermute | solution.py:19
  18.8 71.2 %collective-permute-start.1 = (bf16[32,3200]{1,0:T(8,128)(2,1)}, bf16[32,3200]{1,0:T(8,128)(2,1)}, u32[]{:S(2)}, u32[]{:S(2)}) collective-permute-start(bf16[32,3200]{1,0:T(8,128)(2,1)} %broadcast_select_fusion.4), channel_id=1, source_target_pairs={{0,254},{2,0},{4,2},{6,4},{8,6},{10,8},{12,10},{14,12},{16,14},{18... | collective-permute-start | bytes 614408 | tf_op jit(solution)/shard_map/ppermute | solution.py:19
  30.9 60.7 %collective-permute-start.2 = (bf16[32,3200]{1,0:T(8,128)(2,1)}, bf16[32,3200]{1,0:T(8,128)(2,1)}, u32[]{:S(2)}, u32[]{:S(2)}) collective-permute-start(bf16[32,3200]{1,0:T(8,128)(2,1)} %broadcast_select_fusion.3), channel_id=1, source_target_pairs={{0,4},{2,6},{4,8},{6,10},{8,12},{10,14},{12,16},{14,18},{16,20},{1... | collective-permute-start | bytes 614408 | tf_op jit(solution)/shard_map/ppermute | solution.py:19
  34.0 59.3 %collective-permute-start.3 = (bf16[32,3200]{1,0:T(8,128)(2,1)}, bf16[32,3200]{1,0:T(8,128)(2,1)}, u32[]{:S(2)}, u32[]{:S(2)}) collective-permute-start(bf16[32,3200]{1,0:T(8,128)(2,1)} %broadcast_select_fusion.2), channel_id=1, source_target_pairs={{0,252},{2,254},{4,0},{6,2},{8,4},{10,6},{12,8},{14,10},{16,12},{1... | collective-permute-start | bytes 614408 | tf_op jit(solution)/shard_map/ppermute | solution.py:19
  80.4 7.3 copy-start.16
  80.4 7.3 copy-start.17
  80.4 7.3 copy-start.14
  80.5 7.3 copy-start.15
  80.5 7.3 copy-start.12
  80.5 7.3 copy-start.13
  662.5 5.8 copy-start.3
  662.5 6.9 copy-start.4
  662.5 7.8 copy-start.5
  677.2 5.6 copy-start.9
  720.0 8.6 copy-start.11
  728.6 7.3 copy-start.18
  728.6 7.3 copy-start.19
  728.6 16.2 %copy-start.2 = (bf16[32,3200]{1,0:T(8,128)(2,1)S(1)}, bf16[32,3200]{1,0:T(8,128)(2,1)}, u32[]{:S(2)}) copy-start(bf16[32,3200]{1,0:T(8,128)(2,1)} %param.30) | copy-start | bytes 614404
  728.6 19.4 %copy-start.6 = (f32[32,256]{1,0:T(8,128)S(1)}, f32[32,256]{1,0:T(8,128)}, u32[]{:S(2)}) copy-start(f32[32,256]{1,0:T(8,128)} %param.43) | copy-start | bytes 98308
  735.8 789.5 %reduce-scatter.5.cloned.1.call-start = ((), (), s32[]{:S(2)}) async-start(), calls=%async_computation.4 | async-start | bytes 1228800 | tf_op jit(solution)/shard_map/reduce_scatter | solution.py:171
Sparse Core Ops, SparseCore 0:
  735.9 8.8 reduce-scatter.2
  754.7 14.9 reduce-scatter.4
where the time goes:
time: 1540 us; the launch traced here: 1530 us
  blocking collectives  787 us (51%)
  local copies, waits for them, and re-layouts  618 us (40%)
  matrix products  61.9 us (4%)
  other arithmetic  23.3 us (2%)
  starting transfers between devices  18.3 us (1%)
    psum x1, blocking collectives, body(): grad_head = lax.psum(grad_part, 'atoms').astype(jnp.bfloat16)  661 us
    reshape x8, local copies, waits for them, and re-layouts, unflatten(): return values.reshape(edge_count, 2, channels, width_count)  220 us
    psum x1, blocking collectives, body(): lax.psum(jnp.sum(block_error * block_error, axis=1) / divisor, 'chan')  110 us
    transpose x5, local copies, waits for them, and re-layouts, flatten(): jnp.transpose(selected, (0, 2, 1, 3))  108 us
    reshape x4, local copies, waits for them, and re-layouts, flatten(): jnp.transpose(selected, (0, 2, 1, 3))  108 us
  transfers between devices with their start and end apart: 6, of which 1 were waited for; matrix products, arithmetic and copies ran while one was open for 4% of the time, Pallas kernels for 0%

commit v1 on v0

v1 whole, which is shorter than its diff:
```python
import functools
import jax
import jax.numpy as jnp
import numpy as np
from jax import lax
from jax.experimental import pallas as pl
from jax.experimental.pallas import tpu as pltpu
from jax.sharding import Mesh, PartitionSpec as P

ORB = 16
LMAX = 4
MMAX = 2
OFFSETS = (1, -1, 2, -2)
BRANCH = 0.125
GROUP = ("zl", "y", "x")
ATOMS = ("zh", "zl", "y", "x")
F32 = jnp.float32
BF16 = jnp.bfloat16


def frame_entries():
    slots = {}
    start = 0
    for l in range(LMAX + 1):
        width = 2 * l + 1
        for m in range(-min(l, MMAX), min(l, MMAX) + 1):
            for n in range(width):
                slots[(l, m, n)] = (len(slots), start + (l + m) * width + n)
        start += width * width
    return slots


SLOTS = frame_entries()


def dot(a, b, ca, cb):
    return lax.dot_general(a, b, (((ca,), (cb,)), ((), ())), preferred_element_type=F32)


def message_kernel(
    core_ref, esrc_ref, edst_ref, erot_ref, ew_ref, rot_ref,
    mix0_ref, mix1_ref, mix2_ref,
    fo_ref, ho0_ref, ho1_ref, ho2_ref, ho3_ref,
    fx_ref, hx0_ref, hx1_ref, hx2_ref, hx3_ref,
    out_ref,
    rows, nat, frames, wframes, packed, z0, z1, z2, xb0, xb1, xb2,
):
    core = core_ref[0]
    other = 1 - core
    edges = esrc_ref.shape[1]
    atoms, half = fo_ref.shape

    for q, (own, oth) in enumerate(
        zip((fo_ref, ho0_ref, ho1_ref, ho2_ref, ho3_ref), (fx_ref, hx0_ref, hx1_ref, hx2_ref, hx3_ref))
    ):
        rows[core, q * atoms : (q + 1) * atoms, :] = own[...]
        rows[other, q * atoms : (q + 1) * atoms, :] = oth[...]

    source_rows = lax.broadcasted_iota(jnp.int32, (5 * atoms, edges), 0)
    onehot = (esrc_ref[...] == source_rows).astype(BF16)

    rot_count = rot_ref.shape[1]
    picks = (erot_ref[...] == lax.broadcasted_iota(jnp.int32, (rot_count, edges), 0)).astype(BF16)
    rot = rot_ref[...]
    rot_hi = rot.astype(BF16)
    rot_lo = (rot - rot_hi.astype(F32)).astype(BF16)
    packed[...] = dot(rot_hi, picks, 1, 0) + dot(rot_lo, picks, 1, 0)
    for blk in range(edges // 128):
        lanes = slice(blk * 128, (blk + 1) * 128)
        weight = jnp.broadcast_to(ew_ref[:, lanes], (8, 128))
        for slot, entry in SLOTS.values():
            value = jnp.broadcast_to(packed[entry : entry + 1, lanes], (8, 128))
            frames[blk, slot] = value
            wframes[blk, slot] = value * weight

    step = 640

    def gather(i, _):
        h = i // (half // step)
        n = i % (half // step)
        got = dot(rows[h, :, pl.ds(pl.multiple_of(n * step, 128), step)], onehot, 0, 0)
        at = pl.multiple_of(i * step, 8)
        for blk in range(edges // 128):
            nat[blk, pl.ds(at, step), :] = got[:, blk * 128 : (blk + 1) * 128]
        return 0

    lax.fori_loop(0, 2 * half // step, gather, 0)

    groups = 2 * half // 400

    def rotate_in(i, _):
        blk = i // groups
        g = i % groups
        for p in range(2):
            nb = blk * 2 + p
            for l in range(LMAX + 1):
                xs = [nat[blk, pl.ds(g * 400 + p * 25 + l * l + n, 8, stride=50), :] for n in range(2 * l + 1)]
                for m in range(-min(l, MMAX), min(l, MMAX) + 1):
                    acc = frames[blk, SLOTS[(l, m, 0)][0]] * xs[0]
                    for n in range(1, 2 * l + 1):
                        acc = acc + frames[blk, SLOTS[(l, m, n)][0]] * xs[n]
                    if m == 0:
                        z0[nb, pl.ds(g * 40 + l, 8, stride=5), :] = acc
                    else:
                        side = nb if m > 0 else nb + 4
                        if abs(m) == 1:
                            z1[side, pl.ds(g * 32 + l - 1, 8, stride=4), :] = acc
                        else:
                            z2[side, pl.ds(g * 24 + l - 2, 8, stride=3), :] = acc
        return 0

    lax.fori_loop(0, groups * (edges // 128), rotate_in, 0)

    for nb in range(4):
        xb0[:, nb * 128 : (nb + 1) * 128] = z0[nb].astype(BF16)
    for nb in range(8):
        xb1[:, nb * 128 : (nb + 1) * 128] = z1[nb].astype(BF16)
        xb2[:, nb * 128 : (nb + 1) * 128] = z2[nb].astype(BF16)

    def mix_zero(t, _):
        at = pl.multiple_of(t * 128, 128)
        y = dot(mix0_ref[:, pl.ds(at, 128)], xb0[...], 0, 0)
        for nb in range(4):
            z0[nb, pl.ds(at, 128), :] = y[:, nb * 128 : (nb + 1) * 128]
        return 0

    lax.fori_loop(0, mix0_ref.shape[1] // 128, mix_zero, 0)

    def mix_pair(mix_ref, xb, z):
        def tile(t, _):
            at = pl.multiple_of(t * 128, 128)
            a = dot(mix_ref[0, :, pl.ds(at, 128)], xb[...], 0, 0)
            b = dot(mix_ref[1, :, pl.ds(at, 128)], xb[...], 0, 0)
            for nb in range(4):
                lo = slice(nb * 128, (nb + 1) * 128)
                hi = slice(512 + nb * 128, 512 + (nb + 1) * 128)
                z[nb, pl.ds(at, 128), :] = a[:, lo] - b[:, hi]
                z[nb + 4, pl.ds(at, 128), :] = a[:, hi] + b[:, lo]
            return 0

        lax.fori_loop(0, mix_ref.shape[2] // 128, tile, 0)

    mix_pair(mix1_ref, xb1, z1)
    mix_pair(mix2_ref, xb2, z2)

    def rotate_out(i, _):
        blk = i // groups
        g = i % groups
        for p in range(2):
            nb = blk * 2 + p
            for l in range(LMAX + 1):
                ms = range(-min(l, MMAX), min(l, MMAX) + 1)
                ys = {}
                for m in ms:
                    side = nb if m >= 0 else nb + 4
                    if m == 0:
                        ys[m] = z0[nb, pl.ds(g * 40 + l, 8, stride=5), :]
                    elif abs(m) == 1:
                        ys[m] = z1[side, pl.ds(g * 32 + l - 1, 8, stride=4), :]
                    else:
                        ys[m] = z2[side, pl.ds(g * 24 + l - 2, 8, stride=3), :]
                for n in range(2 * l + 1):
                    acc = None
                    for m in ms:
                        term = wframes[blk, SLOTS[(l, m, n)][0]] * ys[m]
                        acc = term if acc is None else acc + term
                    nat[blk, pl.ds(g * 400 + p * 25 + l * l + n, 8, stride=50), :] = acc
        return 0

    lax.fori_loop(0, groups * (edges // 128), rotate_out, 0)

    scatter = (edst_ref[...] == lax.broadcasted_iota(jnp.int32, (atoms, edges), 0)).astype(BF16)

    def aggregate(i, _):
        at = pl.multiple_of(i * step, 128)
        msgs = jnp.concatenate(
            [nat[blk, pl.ds(at, step), :].astype(BF16) for blk in range(edges // 128)], axis=1
        )
        out_ref[:, pl.ds(at, step)] = dot(scatter, msgs, 1, 1).astype(BF16)
        return 0

    lax.fori_loop(0, 2 * half // step, aggregate, 0)


def messages(core, esrc, edst, erot, ew, rot_table, mixes, own, oth):
    edges = esrc.shape[-1]
    atoms, half = own[0].shape
    row = lambda a: a.reshape(1, -1)
    vmem = pl.BlockSpec(memory_space=pltpu.VMEM)
    return pl.pallas_call(
        message_kernel,
        out_shape=jax.ShapeDtypeStruct((atoms, 2 * half), BF16),
        in_specs=[pl.BlockSpec(memory_space=pltpu.SMEM)] + [vmem] * 18,
        out_specs=vmem,
        scratch_shapes=[
            pltpu.VMEM((2, 5 * atoms, half), BF16),
            pltpu.VMEM((edges // 128, 2 * half, 128), F32),
            pltpu.VMEM((edges // 128, len(SLOTS), 8, 128), F32),
            pltpu.VMEM((edges // 128, len(SLOTS), 8, 128), F32),
            pltpu.VMEM((rot_table.shape[0], edges), F32),
            pltpu.VMEM((4, 640, 128), F32),
            pltpu.VMEM((8, 512, 128), F32),
            pltpu.VMEM((8, 384, 128), F32),
            pltpu.VMEM((640, 512), BF16),
            pltpu.VMEM((512, 1024), BF16),
            pltpu.VMEM((384, 1024), BF16),
        ],
        compiler_params=pltpu.CompilerParams(vmem_limit_bytes=36 * 1024 * 1024),
        cost_estimate=pl.CostEstimate(flops=5_000_000_000, bytes_accessed=6_000_000, transcendentals=0),
        name="messages",
    )(core, row(esrc), row(edst), row(erot), row(ew), rot_table, *mixes, *own, *oth)


def head_kernel(
    core_ref, orbitals_ref, species_ref, fo_ref, fx_ref, mine_ref, recv_ref, weight_ref, target_ref,
    load_ref, loss_ref, keep_ref, send_ref,
    feats, upd,
):
    core = core_ref[0]
    atoms, half = fo_ref.shape
    feats[core] = fo_ref[...]
    feats[1 - core] = fx_ref[...]
    for h in range(2):
        cols = slice(h * half, (h + 1) * half)
        total = mine_ref[:, cols].astype(F32) + recv_ref[:, cols].astype(F32)
        upd[:, cols] = (feats[h].astype(F32) + BRANCH * total).astype(BF16)
    blocks = dot(upd[...], weight_ref[...], 1, 0)
    width = blocks.shape[1]
    species = species_ref[...]
    norb = jnp.zeros_like(species)
    for s in range(orbitals_ref.shape[0]):
        norb = jnp.where(species == s, orbitals_ref[s], norb)
    cols = core * width + lax.broadcasted_iota(jnp.int32, (atoms, width), 1)
    valid = ((cols // (2 * ORB)) < norb) & (((cols // 2) % ORB) < norb)
    error = jnp.where(valid, blocks - target_ref[...], 0.0)
    divisor = norb.astype(F32)
    loss_ref[...] = jnp.sum(error * error, axis=1, keepdims=True) / divisor
    dblk = (2.0 * error / divisor).astype(BF16)
    parts = load_ref.shape[0]
    share = 2 * half // parts
    for g in range(parts):
        where = (g % 2) * (parts // 2) + g // 2
        load_ref[where, :, :width] = dblk
        load_ref[where, :, width : width + share] = upd[:, g * share : (g + 1) * share]
        load_ref[where, :, width + share :] = jnp.zeros((atoms, width - share), BF16)
    keep_ref[...] = dot(dblk, weight_ref[pl.ds(pl.multiple_of(core * half, 128), half), :], 1, 1)
    send_ref[...] = dot(dblk, weight_ref[pl.ds(pl.multiple_of((1 - core) * half, 128), half), :], 1, 1).astype(BF16)


def head(core, orbitals, species, f_own, f_oth, mine, recv, weight, target, parts):
    atoms, half = f_own.shape
    smem = pl.BlockSpec(memory_space=pltpu.SMEM)
    vmem = pl.BlockSpec(memory_space=pltpu.VMEM)
    return pl.pallas_call(
        head_kernel,
        out_shape=(
            jax.ShapeDtypeStruct((parts, atoms, 2 * target.shape[1]), BF16),
            jax.ShapeDtypeStruct((atoms, 1), F32),
            jax.ShapeDtypeStruct((atoms, half), F32),
            jax.ShapeDtypeStruct((atoms, half), BF16),
        ),
        in_specs=[smem, smem] + [vmem] * 7,
        out_specs=(vmem,) * 4,
        scratch_shapes=[pltpu.VMEM((2, atoms, half), BF16), pltpu.VMEM((atoms, 2 * half), BF16)],
        compiler_params=pltpu.CompilerParams(vmem_limit_bytes=32 * 1024 * 1024),
        cost_estimate=pl.CostEstimate(flops=300_000_000, bytes_accessed=6_000_000, transcendentals=0),
        name="head",
    )(core, orbitals, species.reshape(-1, 1), f_own, f_oth, mine, recv, weight, target)


def leaving_kernel(sends_ref, feats_ref, *outs):
    atoms = feats_ref.shape[0]
    places = lax.broadcasted_iota(jnp.int32, (atoms, atoms), 0)
    picks = jnp.concatenate(
        [(sends_ref[q : q + 1, :] == places).astype(F32) for q in range(len(outs))], axis=1
    ).astype(BF16)
    rows = dot(picks, feats_ref[...], 0, 0).astype(BF16)
    for q, out in enumerate(outs):
        out[...] = rows[q * atoms : (q + 1) * atoms, :]


def leaving_rows(send_rows, features):
    vmem = pl.BlockSpec(memory_space=pltpu.VMEM)
    return pl.pallas_call(
        leaving_kernel,
        out_shape=(jax.ShapeDtypeStruct(features.shape, BF16),) * len(OFFSETS),
        in_specs=[vmem, vmem],
        out_specs=(vmem,) * len(OFFSETS),
        compiler_params=pltpu.CompilerParams(vmem_limit_bytes=24 * 1024 * 1024),
        name="leaving",
    )(send_rows, features)


def partial_kernel(got_ref, out_ref):
    width = got_ref.shape[1] // 2
    full = dot(got_ref[:, width:], got_ref[:, :width], 0, 0)
    out_ref[...] = full[: out_ref.shape[0]].astype(BF16)


def partial_grad(got, share):
    vmem = pl.BlockSpec(memory_space=pltpu.VMEM)
    return pl.pallas_call(
        partial_kernel,
        out_shape=jax.ShapeDtypeStruct((share, got.shape[1] // 2), BF16),
        in_specs=[vmem],
        out_specs=vmem,
        compiler_params=pltpu.CompilerParams(vmem_limit_bytes=24 * 1024 * 1024),
        name="partial_grad",
    )(got)


def shift(x, axis, by):
    count = lax.axis_size(axis)
    return lax.ppermute(x, axis, [(i, (i + by) % count) for i in range(count)])


def ring_blocks(x, axis):
    half = x.shape[0] // 2
    behind = shift(x, axis, 1)
    ahead = shift(x, axis, -1)
    return [x, behind, shift(behind[:half], axis, 1), shift(ahead[half:], axis, -1), ahead]


def assemble_kernel(place_ref, *refs):
    blocks, out_ref, sems = refs[:-2], refs[-2], refs[-1]
    y, x = place_ref[0], place_ref[1]
    rows = out_ref.shape[0] // 16
    copies = []
    for path in range(2):
        own, behind, far_lo, far_hi, ahead = blocks[5 * path : 5 * path + 5]
        for late in range(4):
            for early in range(4):
                if late == 2:
                    ref, at = (far_lo, early) if early < 2 else (far_hi, early - 2)
                else:
                    ref, at = {0: own, 1: behind, 3: ahead}[late], early
                dy, dx = (late, early) if path == 0 else (early, late)
                spot = lax.rem(y + 4 - dy, 4) * 4 + lax.rem(x + 4 - dx, 4)
                copies.append(
                    pltpu.make_async_copy(
                        ref.at[pl.ds(at * rows, rows), :],
                        out_ref.at[pl.ds(pl.multiple_of(spot * rows, 16), rows), pl.ds(path * 128, 128)],
                        sems.at[len(copies)],
                    )
                )
    for copy in copies:
        copy.start()
    for copy in copies:
        copy.wait()


def assemble(place, blocks):
    rows = 4 * blocks[0].shape[0]
    hbm = pl.BlockSpec(memory_space=pl.ANY)
    return pl.pallas_call(
        assemble_kernel,
        out_shape=jax.ShapeDtypeStruct((rows, 256), BF16),
        in_specs=[pl.BlockSpec(memory_space=pltpu.SMEM)]
        + [pl.BlockSpec(memory_space=pltpu.VMEM)] * len(blocks),
        out_specs=hbm,
        scratch_shapes=[pltpu.SemaphoreType.DMA((32,))],
        compiler_params=pltpu.CompilerParams(vmem_limit_bytes=16 * 1024 * 1024),
        name="assemble",
    )(place, *blocks)


def body(
    features, send_rows, edge_source, edge_dest, edge_rot, edge_weight, rot_table,
    mix_zero, mix_one, mix_two, atom_species, species_orbitals, head_weight, target_blocks,
):
    core = lax.axis_index("chan").astype(jnp.int32).reshape(1)
    f_oth = shift(features, "chan", 1)
    halo = [shift(rows, ATOMS, off) for rows, off in zip(leaving_rows(send_rows, features), OFFSETS)]
    halo_oth = [shift(h, "chan", 1) for h in halo]
    mine = messages(
        core, edge_source, edge_dest, edge_rot, edge_weight, rot_table.T,
        (mix_zero, mix_one, mix_two), [features] + halo, [f_oth] + halo_oth,
    )
    recv = shift(mine, "chan", 1)
    parts = lax.axis_size(GROUP)
    load, loss, keep, send = head(
        core, species_orbitals, atom_species, features, f_oth, mine, recv, head_weight, target_blocks, parts
    )
    got = lax.all_to_all(load, GROUP, split_axis=0, concat_axis=0, tiled=True)
    atom_loss = loss[:, 0] + shift(loss[:, 0], "chan", 1)
    grad_features = keep + shift(send, "chan", 1).astype(F32)
    share = 2 * features.shape[1] // parts
    part = partial_grad(got.reshape(-1, got.shape[2]), share)
    near = shift(part, "zh", 1).astype(F32) + shift(part, "zh", -1).astype(F32)
    total = (part.astype(F32) + shift(part, "zh", 2).astype(F32) + near).astype(BF16)
    twin = shift(total, "zl", 1)
    low = lax.axis_index("zl") == 0
    pair = jnp.concatenate([jnp.where(low, total, twin), jnp.where(low, twin, total)], axis=0)

    def gather_first(x, axis):
        own, behind, far_lo, far_hi, ahead = ring_blocks(x, axis)
        return jnp.concatenate([own, behind, far_lo, far_hi, ahead], axis=0)

    left = gather_first(pair[:, :128], "x")
    right = gather_first(pair[:, 128:], "y")
    place = jnp.stack([lax.axis_index("y"), lax.axis_index("x")]).astype(jnp.int32)
    grad_head = assemble(place, ring_blocks(left, "y") + ring_blocks(right, "x"))
    return (atom_loss, grad_head, grad_features)


def solution(mesh):
    fine = Mesh(mesh.devices.reshape(4, 2, 4, 4, 2), ("zh", "zl", "y", "x", "chan"))
    both = ATOMS + ("chan",)
    return jax.shard_map(
        body,
        mesh=fine,
        in_specs=(
            P(ATOMS, "chan"), P(ATOMS, None), P(both), P(both), P(both), P(both),
            P(), P(), P(), P(), P(ATOMS), P(), P(None, "chan"), P(ATOMS, "chan"),
        ),
        out_specs=(P(ATOMS), P(None, "chan"), P(ATOMS, "chan")),
        check_vma=False,
    )
```

time: 1540 us -> 153 us (0.10)
  the two profiles are of different devices: /device:TPU:1 before, /device:TPU:32 now
where the time goes in v1:
time: 153 us
  starting transfers between devices  49 us (32%)
  blocking collectives  27.2 us (18%)
  waiting for transfers between devices  27.1 us (18%)
  Pallas kernels  25.8 us (17%)
  local copies, waits for them, and re-layouts  21 us (14%)
  other arithmetic  1.62 us (1%)
    ppermute x32, starting transfers between devices, shift(): return lax.ppermute(x, axis, [(i, (i + by) % count) for i in range(count)])  49 us
    all_to_all x1, blocking collectives, body(): got = lax.all_to_all(load, GROUP, split_axis=0, concat_axis=0, tiled=True)  27.2 us
    ppermute x32, waiting for transfers between devices, shift(): return lax.ppermute(x, axis, [(i, (i + by) % count) for i in range(count)])  27.1 us
    unnamed x70, local copies, waits for them, and re-layouts  20.8 us
    pallas_call x1, Pallas kernels, messages(): pl.pallas_call(message_kernel, out_shape=jax.ShapeDtypeStruct((atoms, 2 *...  18 us
    pallas_call x1, Pallas kernels, head(): pl.pallas_call(head_kernel, out_shape=(jax.ShapeDtypeStruct((parts, atoms...  3.57 us
  transfers between devices with their start and end apart: 32, of which 11 were waited for; matrix products, arithmetic and copies ran while one was open for 1% of the time, Pallas kernels for 0%

profile of v1, /device:TPU:32, one launch (start us, length us, event | category | flops | bytes accessed | tf_op | source)
XLA Modules:
  0.0 152.9 jit_solution(5286288346236627720)
XLA Ops:
  0.6 0.7 copy-done.4
  1.3 1.4 leaving.1
  2.7 1.6 %collective-permute-start.1 = (bf16[32,3200]{1,0:T(8,128)(2,1)S(1)}, bf16[32,3200]{1,0:T(8,128)(2,1)S(1)}, u32[]{:S(2)}, u32[]{:S(2)}) collective-permute-start(bf16[32,3200]{1,0:T(8,128)(2,1)S(1)} %get-tuple-element.11), channel_id=1, source_target_pairs={{0,2},{2,4},{4,6},{6,8},{8,10},{10,12},{12,14},{14,16},{16,18},{18... | collective-permute-start | bytes 614408 | tf_op jit(solution)/shard_map/ppermute | solution.py:314
  4.3 4.8 %collective-permute-start.2 = (bf16[32,3200]{1,0:T(8,128)(2,1)S(1)}, bf16[32,3200]{1,0:T(8,128)(2,1)S(1)}, u32[]{:S(2)}, u32[]{:S(2)}) collective-permute-start(bf16[32,3200]{1,0:T(8,128)(2,1)S(1)} %get-tuple-element.12), channel_id=1, source_target_pairs={{0,254},{2,0},{4,2},{6,4},{8,6},{10,8},{12,10},{14,12},{16,14},{18... | collective-permute-start | bytes 614408 | tf_op jit(solution)/shard_map/ppermute | solution.py:314
  9.0 6.5 %collective-permute-start.4 = (bf16[32,3200]{1,0:T(8,128)(2,1)S(1)}, bf16[32,3200]{1,0:T(8,128)(2,1)S(1)}, u32[]{:S(2)}, u32[]{:S(2)}) collective-permute-start(bf16[32,3200]{1,0:T(8,128)(2,1)S(1)} %get-tuple-element.14), channel_id=1, source_target_pairs={{0,252},{2,254},{4,0},{6,2},{8,4},{10,6},{12,8},{14,10},{16,12},{1... | collective-permute-start | bytes 614408 | tf_op jit(solution)/shard_map/ppermute | solution.py:314
  15.6 0.5 collective-permute-start.5
  16.1 0.7 copy-done.11
  16.8 0.7 copy-done.13
  17.5 2.4 %collective-permute-done.3.ho2_ref = bf16[32,3200]{1,0:T(8,128)(2,1)S(1)} collective-permute-done((bf16[32,3200]{1,0:T(8,128)(2,1)S(1)}, bf16[32,3200]{1,0:T(8,128)(2,1)S(1)}, u32[]{:S(2)}, u32[]{:S(2)}) %collective-permute-start.3) | collective-permute-done | bytes 204832 | tf_op jit(solution)/shard_map/ppermute | solution.py:314
  19.9 0.7 copy-done.15
  20.6 0.5 collective-permute-start.8
  21.1 0.7 copy-done.17
  21.8 0.7 copy-done.19
  22.5 0.7 copy-done.21
  23.2 0.7 copy-done.23
  23.9 0.7 copy-done.25
  24.6 1.2 copy-done.6
  25.8 1.1 copy-done.7
  26.9 1.1 copy-done.8
  28.0 1.0 copy-done.9
  29.0 0.9 copy-done.12
  29.9 0.9 copy-done.14
  30.8 0.9 copy-done.16
  31.8 0.9 copy-done.18
  32.7 0.9 copy-done.20
  33.6 0.9 copy-done.22
  34.5 0.9 copy-done.24
  35.5 0.9 copy-done.26
  36.4 0.7 copy-done.27
  37.1 0.7 copy-done.28
  37.8 0.7 copy-done.29
  38.4 0.7 copy-done.30
  39.1 18.0 %messages.1.mine_ref = bf16[32,6400]{1,0:T(8,128)(2,1)} custom-call(s32[1]{0:T(128)} %bitcast.core_ref, s32[1,256]{1,0:T(1,128)S(1)} %bitcast.12, s32[1,256]{1,0:T(1,128)S(1)} %bitcast.13, s32[1,256]{1,0:T(1,128)S(1)} %bitcast.14, f32[1,256]{1,0:T(1,128)S(1)} %bitcast.15, f32[165,512]{1,0:T(8,128)S(1)} %bitcast.11, bf16[640,640]{1,0:T(8,128)(2,1)S(1)} %copy-done.7, ...), custom_call_target="tpu_custom_call" | custom-call | flops 5000000000 | bytes 6000000 | tf_op jit(solution)/shard_map/messages/pallas_call | solution.py:190
  57.2 2.0 %collective-permute-done.9.recv_ref = bf16[32,6400]{1,0:T(8,128)(2,1)} collective-permute-done((bf16[32,6400]{1,0:T(8,128)(2,1)}, bf16[32,6400]{1,0:T(8,128)(2,1)}, u32[]{:S(2)}, u32[]{:S(2)}) %collective-permute-start.9) | collective-permute-done | bytes 409632 | tf_op jit(solution)/shard_map/ppermute | solution.py:314
  59.2 3.6 %head.1 = (bf16[32,32,512]{2,1,0:T(8,128)(2,1)S(1)}, f32[32,1]{1,0:T(8,128)S(1)}, f32[32,3200]{1,0:T(8,128)S(1)}, bf16[32,3200]{1,0:T(8,128)(2,1)S(1)}) custom-call(s32[1]{0:T(128)} %bitcast.core_ref, s32[4]{0:T(128)S(1)} %copy-done.5, s32[32,1]{1,0:T(8,128)S(1)} %copy.18.species_ref, bf16[32,3200]{1,0:T(8,128)(2,1)} %fo_ref.3, ...), custom_call_target="tpu_custom_call" | custom-call | flops 300000000 | bytes 6000000 | tf_op jit(solution)/shard_map/head/pallas_call | solution.py:254
  62.8 27.2 %all_to_all.5 = bf16[32,32,512]{2,1,0:T(8,128)(2,1)S(1)} all-to-all(bf16[32,32,512]{2,1,0:T(8,128)(2,1)S(1)} %get-tuple-element.16), channel_id=1, replica_groups=mesh['zh'=4,'zl'=2,'y'=4,'x'=4,'chan'=2] {'zl','y','x'}, dimensions={0} | all-to-all | bytes 2097152 | tf_op jit(solution)/shard_map/all_to_all | solution.py:384
  90.0 0.3 partial_grad.1
  90.4 5.5 %collective-permute-start.13 = (bf16[200,256]{1,0:T(8,128)(2,1)S(1)}, bf16[200,256]{1,0:T(8,128)(2,1)S(1)}, u32[]{:S(2)}, u32[]{:S(2)}) collective-permute-start(bf16[200,256]{1,0:T(8,128)(2,1)S(1)} %partial_grad.1), channel_id=1, source_target_pairs={{0,192},{64,0},{128,64},{192,128},{1,193},{65,1},{129,65},{193,129... | collective-permute-start | bytes 307208 | tf_op jit(solution)/shard_map/ppermute | solution.py:314
  95.9 3.8 %collective-permute-start.11 = (bf16[200,256]{1,0:T(8,128)(2,1)S(1)}, bf16[200,256]{1,0:T(8,128)(2,1)S(1)}, u32[]{:S(2)}, u32[]{:S(2)}) collective-permute-start(bf16[200,256]{1,0:T(8,128)(2,1)S(1)} %partial_grad.1), channel_id=1, source_target_pairs={{0,128},{64,192},{128,0},{192,64},{1,129},{65,193},{129,1},{193,65... | collective-permute-start | bytes 307208 | tf_op jit(solution)/shard_map/ppermute | solution.py:314
  99.7 7.7 %collective-permute-done.12 = bf16[200,256]{1,0:T(8,128)(2,1)S(1)} collective-permute-done((bf16[200,256]{1,0:T(8,128)(2,1)S(1)}, bf16[200,256]{1,0:T(8,128)(2,1)S(1)}, u32[]{:S(2)}, u32[]{:S(2)}) %collective-permute-start.12) | collective-permute-done | bytes 102432 | tf_op jit(solution)/shard_map/ppermute | solution.py:314
  107.6 4.6 %collective-permute-done.14 = bf16[200,256]{1,0:T(8,128)(2,1)S(1)} collective-permute-done((bf16[200,256]{1,0:T(8,128)(2,1)S(1)}, bf16[200,256]{1,0:T(8,128)(2,1)S(1)}, u32[]{:S(2)}, u32[]{:S(2)}) %collective-permute-start.14) | collective-permute-done | bytes 102432 | tf_op jit(solution)/shard_map/ppermute | solution.py:314
  112.3 0.6 collective-permute-start.23
  112.9 2.7 %collective-permute-start.25 = (bf16[400,128]{1,0:T(8,128)(2,1)S(1)}, bf16[400,128]{1,0:T(8,128)(2,1)S(1)}, u32[]{:S(2)}, u32[]{:S(2)}) collective-permute-start(bf16[400,128]{1,0:T(8,128)(2,1)S(1)} %get-tuple-element.20), channel_id=1, source_target_pairs={{0,24},{8,0},{16,8},{24,16},{1,25},{9,1},{17,9},{25,17},{2,26},{10... | collective-permute-start | bytes 307208 | tf_op jit(solution)/shard_map/ppermute | solution.py:314
  115.6 1.1 collective-permute-start.15
  116.7 2.1 %collective-permute-start.17 = (bf16[400,128]{1,0:T(8,128)(2,1)S(1)}, bf16[400,128]{1,0:T(8,128)(2,1)S(1)}, u32[]{:S(2)}, u32[]{:S(2)}) collective-permute-start(bf16[400,128]{1,0:T(8,128)(2,1)S(1)} %get-tuple-element.24), channel_id=1, source_target_pairs={{0,6},{2,0},{4,2},{6,4},{1,7},{3,1},{5,3},{7,5},{8,14},{10,8},{12,... | collective-permute-start | bytes 307208 | tf_op jit(solution)/shard_map/ppermute | solution.py:314
  119.0 3.3 %collective-permute-start.26 = (bf16[200,128]{1,0:T(8,128)(2,1)S(1)}, bf16[200,128]{1,0:T(8,128)(2,1)S(1)}, u32[]{:S(2)}, u32[]{:S(2)}) collective-permute-start(bf16[200,128]{1,0:T(8,128)(2,1)S(1)} %slice.47), channel_id=1, source_target_pairs={{0,24},{8,0},{16,8},{24,16},{1,25},{9,1},{17,9},{25,17},{2,26},{10... | collective-permute-start | bytes 153608 | tf_op jit(solution)/shard_map/ppermute | solution.py:314
  122.3 0.8 collective-permute-start.16
  123.1 2.6 %collective-permute-start.18 = (bf16[200,128]{1,0:T(8,128)(2,1)S(1)}, bf16[200,128]{1,0:T(8,128)(2,1)S(1)}, u32[]{:S(2)}, u32[]{:S(2)}) collective-permute-start(bf16[200,128]{1,0:T(8,128)(2,1)S(1)} %slice.43), channel_id=1, source_target_pairs={{0,6},{2,0},{4,2},{6,4},{1,7},{3,1},{5,3},{7,5},{8,14},{10,8},{12,... | collective-permute-start | bytes 153608 | tf_op jit(solution)/shard_map/ppermute | solution.py:314
  125.7 2.0 %collective-permute-done.16 = bf16[200,128]{1,0:T(8,128)(2,1)S(1)} collective-permute-done((bf16[200,128]{1,0:T(8,128)(2,1)S(1)}, bf16[200,128]{1,0:T(8,128)(2,1)S(1)}, u32[]{:S(2)}, u32[]{:S(2)}) %collective-permute-start.16) | collective-permute-done | bytes 51232 | tf_op jit(solution)/shard_map/ppermute | solution.py:314
  127.7 0.2 collective-permute-done.18
  128.0 2.0 %collective-permute-start.19 = (bf16[1600,128]{1,0:T(8,128)(2,1)S(1)}, bf16[1600,128]{1,0:T(8,128)(2,1)S(1)}, u32[]{:S(2)}, u32[]{:S(2)}) collective-permute-start(bf16[1600,128]{1,0:T(8,128)(2,1)S(1)} %constant_dynamic-update-slice_fusion.refs_0_), channel_id=1, source_target_pairs={{0,8},{8,16},{16,24},{24,0},{1,9},{9,17},{17,25},{25,1},{2,10},{10... | collective-permute-start | bytes 1228808 | tf_op jit(solution)/shard_map/ppermute | solution.py:314
  130.1 3.8 %collective-permute-start.29 = (bf16[1600,128]{1,0:T(8,128)(2,1)S(1)}, bf16[1600,128]{1,0:T(8,128)(2,1)S(1)}, u32[]{:S(2)}, u32[]{:S(2)}) collective-permute-start(bf16[1600,128]{1,0:T(8,128)(2,1)S(1)} %constant_dynamic-update-slice_fusion.5.refs_5_), channel_id=1, source_target_pairs={{0,6},{2,0},{4,2},{6,4},{1,7},{3,1},{5,3},{7,5},{8,14},{10,8},{12,... | collective-permute-start | bytes 1228808 | tf_op jit(solution)/shard_map/ppermute | solution.py:314
  134.0 1.1 collective-permute-done.10
  135.1 0.2 collective-permute-start.31
  135.4 0.5 add.15
  136.0 1.6 %collective-permute-start.22 = (bf16[800,128]{1,0:T(8,128)(2,1)S(1)}, bf16[800,128]{1,0:T(8,128)(2,1)S(1)}, u32[]{:S(2)}, u32[]{:S(2)}) collective-permute-start(bf16[800,128]{1,0:T(8,128)(2,1)S(1)} %slice.45), channel_id=1, source_target_pairs={{0,24},{8,0},{16,8},{24,16},{1,25},{9,1},{17,9},{25,17},{2,26},{10... | collective-permute-start | bytes 614408 | tf_op jit(solution)/shard_map/ppermute | solution.py:314
  137.6 0.8 collective-permute-start.20
  138.4 0.9 collective-permute-done.29.refs_9_
  139.3 3.8 %collective-permute-start.30 = (bf16[800,128]{1,0:T(8,128)(2,1)S(1)}, bf16[800,128]{1,0:T(8,128)(2,1)S(1)}, u32[]{:S(2)}, u32[]{:S(2)}) collective-permute-start(bf16[800,128]{1,0:T(8,128)(2,1)S(1)} %slice.49), channel_id=1, source_target_pairs={{0,6},{2,0},{4,2},{6,4},{1,7},{3,1},{5,3},{7,5},{8,14},{10,8},{12,... | collective-permute-start | bytes 614408 | tf_op jit(solution)/shard_map/ppermute | solution.py:314
  143.2 0.8 convert_add_fusion
  144.0 1.9 %collective-permute-done.20.refs_2_ = bf16[800,128]{1,0:T(8,128)(2,1)S(1)} collective-permute-done((bf16[800,128]{1,0:T(8,128)(2,1)S(1)}, bf16[800,128]{1,0:T(8,128)(2,1)S(1)}, u32[]{:S(2)}, u32[]{:S(2)}) %collective-permute-start.20) | collective-permute-done | bytes 204832 | tf_op jit(solution)/shard_map/ppermute | solution.py:314
  145.9 0.5 collective-permute-done.30.refs_8_
  146.4 3.8 %collective-permute-done.28.refs_7_ = bf16[800,128]{1,0:T(8,128)(2,1)S(1)} collective-permute-done((bf16[800,128]{1,0:T(8,128)(2,1)S(1)}, bf16[800,128]{1,0:T(8,128)(2,1)S(1)}, u32[]{:S(2)}, u32[]{:S(2)}) %collective-permute-start.28) | collective-permute-done | bytes 204832 | tf_op jit(solution)/shard_map/ppermute | solution.py:314
  150.2 2.5 %assemble.1 = bf16[6400,256]{1,0:T(8,128)(2,1)} custom-call(s32[2]{0:T(128)S(1)} %pad_add_fusion.place_ref, bf16[1600,128]{1,0:T(8,128)(2,1)S(1)} %constant_dynamic-update-slice_fusion.refs_0_, bf16[1600,128]{1,0:T(8,128)(2,1)S(1)} %collective-permute-done.19.refs_1_, bf16[800,128]{1,0:T(8,128)(2,1)S(1)} %collective-permute-done.20.refs_2_, ...), custom_call_target="tpu_custom_call" | custom-call | tf_op jit(solution)/shard_map/assemble/pallas_call | solution.py:355
  (94 shorter events, 1.2 us)
Async XLA Ops:
  0.6 0.7 copy-start.4
  2.7 12.9 %collective-permute-start.1 = (bf16[32,3200]{1,0:T(8,128)(2,1)S(1)}, bf16[32,3200]{1,0:T(8,128)(2,1)S(1)}, u32[]{:S(2)}, u32[]{:S(2)}) collective-permute-start(bf16[32,3200]{1,0:T(8,128)(2,1)S(1)} %get-tuple-element.11), channel_id=1, source_target_pairs={{0,2},{2,4},{4,6},{6,8},{8,10},{10,12},{12,14},{14,16},{16,18},{18... | collective-permute-start | bytes 614408 | tf_op jit(solution)/shard_map/ppermute | solution.py:314
  4.3 12.5 %collective-permute-start.2 = (bf16[32,3200]{1,0:T(8,128)(2,1)S(1)}, bf16[32,3200]{1,0:T(8,128)(2,1)S(1)}, u32[]{:S(2)}, u32[]{:S(2)}) collective-permute-start(bf16[32,3200]{1,0:T(8,128)(2,1)S(1)} %get-tuple-element.12), channel_id=1, source_target_pairs={{0,254},{2,0},{4,2},{6,4},{8,6},{10,8},{12,10},{14,12},{16,14},{18... | collective-permute-start | bytes 614408 | tf_op jit(solution)/shard_map/ppermute | solution.py:314
  9.0 10.9 %collective-permute-start.3 = (bf16[32,3200]{1,0:T(8,128)(2,1)S(1)}, bf16[32,3200]{1,0:T(8,128)(2,1)S(1)}, u32[]{:S(2)}, u32[]{:S(2)}) collective-permute-start(bf16[32,3200]{1,0:T(8,128)(2,1)S(1)} %get-tuple-element.13), channel_id=1, source_target_pairs={{0,4},{2,6},{4,8},{6,10},{8,12},{10,14},{12,16},{14,18},{16,20},{1... | collective-permute-start | bytes 614408 | tf_op jit(solution)/shard_map/ppermute | solution.py:314
  9.0 11.6 %collective-permute-start.4 = (bf16[32,3200]{1,0:T(8,128)(2,1)S(1)}, bf16[32,3200]{1,0:T(8,128)(2,1)S(1)}, u32[]{:S(2)}, u32[]{:S(2)}) collective-permute-start(bf16[32,3200]{1,0:T(8,128)(2,1)S(1)} %get-tuple-element.14), channel_id=1, source_target_pairs={{0,252},{2,254},{4,0},{6,2},{8,4},{10,6},{12,8},{14,10},{16,12},{1... | collective-permute-start | bytes 614408 | tf_op jit(solution)/shard_map/ppermute | solution.py:314
  15.6 6.2 %collective-permute-start = (bf16[32,3200]{1,0:T(8,128)(2,1)}, bf16[32,3200]{1,0:T(8,128)(2,1)S(1)}, u32[]{:S(2)}, u32[]{:S(2)}) collective-permute-start(bf16[32,3200]{1,0:T(8,128)(2,1)} %fo_ref.3), channel_id=1, source_target_pairs={{0,1},{1,0},{2,3},{3,2},{4,5},{5,4},{6,7},{7,6},{8,9},{9,8},{10,11... | collective-permute-start | bytes 614408 | tf_op jit(solution)/shard_map/ppermute | solution.py:314
  15.6 6.2 %collective-permute-start.5 = (bf16[32,3200]{1,0:T(8,128)(2,1)S(1)}, bf16[32,3200]{1,0:T(8,128)(2,1)S(1)}, u32[]{:S(2)}, u32[]{:S(2)}) collective-permute-start(bf16[32,3200]{1,0:T(8,128)(2,1)S(1)} %collective-permute-done.1.ho0_ref), channel_id=1, source_target_pairs={{0,1},{1,0},{2,3},{3,2},{4,5},{5,4},{6,7},{7,6},{8,9},{9,8},{10,11... | collective-permute-start | bytes 614408 | tf_op jit(solution)/shard_map/ppermute | solution.py:314
  16.1 0.7 copy-start.11
  16.8 5.7 %collective-permute-start.6 = (bf16[32,3200]{1,0:T(8,128)(2,1)S(1)}, bf16[32,3200]{1,0:T(8,128)(2,1)S(1)}, u32[]{:S(2)}, u32[]{:S(2)}) collective-permute-start(bf16[32,3200]{1,0:T(8,128)(2,1)S(1)} %collective-permute-done.2.ho1_ref), channel_id=1, source_target_pairs={{0,1},{1,0},{2,3},{3,2},{4,5},{5,4},{6,7},{7,6},{8,9},{9,8},{10,11... | collective-permute-start | bytes 614408 | tf_op jit(solution)/shard_map/ppermute | solution.py:314
  16.8 0.7 copy-start.13
  19.9 3.3 %collective-permute-start.7 = (bf16[32,3200]{1,0:T(8,128)(2,1)S(1)}, bf16[32,3200]{1,0:T(8,128)(2,1)S(1)}, u32[]{:S(2)}, u32[]{:S(2)}) collective-permute-start(bf16[32,3200]{1,0:T(8,128)(2,1)S(1)} %collective-permute-done.3.ho2_ref), channel_id=1, source_target_pairs={{0,1},{1,0},{2,3},{3,2},{4,5},{5,4},{6,7},{7,6},{8,9},{9,8},{10,11... | collective-permute-start | bytes 614408 | tf_op jit(solution)/shard_map/ppermute | solution.py:314
  19.9 0.7 copy-start.15
  20.6 3.2 %collective-permute-start.8 = (bf16[32,3200]{1,0:T(8,128)(2,1)S(1)}, bf16[32,3200]{1,0:T(8,128)(2,1)S(1)}, u32[]{:S(2)}, u32[]{:S(2)}) collective-permute-start(bf16[32,3200]{1,0:T(8,128)(2,1)S(1)} %collective-permute-done.4.ho3_ref), channel_id=1, source_target_pairs={{0,1},{1,0},{2,3},{3,2},{4,5},{5,4},{6,7},{7,6},{8,9},{9,8},{10,11... | collective-permute-start | bytes 614408 | tf_op jit(solution)/shard_map/ppermute | solution.py:314
  21.1 0.7 copy-start.17
  21.8 0.7 copy-start.19
  22.5 0.7 copy-start.21
  23.2 0.7 copy-start.23
  23.9 0.7 copy-start.25
  24.5 1.2 copy-start.6
  25.8 1.1 copy-start.7
  26.9 1.1 copy-start.8
  28.0 1.0 copy-start.9
  29.0 0.9 copy-start.12
  29.9 0.9 copy-start.14
  30.8 0.9 copy-start.16
  31.8 0.9 copy-start.18
  32.7 0.9 copy-start.20
  33.6 0.9 copy-start.22
  34.5 0.9 copy-start.24
  35.5 0.9 copy-start.26
  36.4 0.7 copy-start.27
  37.1 0.7 copy-start.28
  37.8 0.7 copy-start.29
  38.4 0.7 copy-start.30
  39.1 18.0 %copy-start.31 = (s32[32]{0:T(128)S(1)}, s32[32]{0:T(128)}, u32[]{:S(2)}) copy-start(s32[32]{0:T(128)} %param.24) | copy-start | bytes 388
  39.1 20.1 %copy-start = (bf16[6400,256]{1,0:T(8,128)(2,1)S(1)}, bf16[6400,256]{1,0:T(8,128)(2,1)}, u32[]{:S(2)}) copy-start(bf16[6400,256]{1,0:T(8,128)(2,1)} %weight_ref.1) | copy-start | bytes 9830404
  39.1 20.1 %copy-start.3 = (f32[32,256]{1,0:T(8,128)S(1)}, f32[32,256]{1,0:T(8,128)}, u32[]{:S(2)}) copy-start(f32[32,256]{1,0:T(8,128)} %target_ref.1) | copy-start | bytes 98308
  39.1 20.1 %copy-start.5 = (s32[4]{0:T(128)S(1)}, s32[4]{0:T(128)}, u32[]{:S(2)}) copy-start(s32[4]{0:T(128)} %orbitals_ref.1) | copy-start | bytes 52
  57.1 2.1 %collective-permute-start.9 = (bf16[32,6400]{1,0:T(8,128)(2,1)}, bf16[32,6400]{1,0:T(8,128)(2,1)}, u32[]{:S(2)}, u32[]{:S(2)}) collective-permute-start(bf16[32,6400]{1,0:T(8,128)(2,1)} %messages.1.mine_ref), channel_id=1, source_target_pairs={{0,1},{1,0},{2,3},{3,2},{4,5},{5,4},{6,7},{7,6},{8,9},{9,8},{10,11... | collective-permute-start | bytes 1228808 | tf_op jit(solution)/shard_map/ppermute | solution.py:314
  62.8 44.6 %copy-start.1 = (f32[32,3200]{1,0:T(8,128)}, f32[32,3200]{1,0:T(8,128)S(1)}, u32[]{:S(2)}) copy-start(f32[32,3200]{1,0:T(8,128)S(1)} %get-tuple-element.17) | copy-start | bytes 1228804
  62.8 44.6 %copy-start.10 = (bf16[32,3200]{1,0:T(8,128)(2,1)}, bf16[32,3200]{1,0:T(8,128)(2,1)S(1)}, u32[]{:S(2)}) copy-start(bf16[32,3200]{1,0:T(8,128)(2,1)S(1)} %get-tuple-element.18) | copy-start | bytes 614404
  90.4 9.3 %collective-permute-start.13 = (bf16[200,256]{1,0:T(8,128)(2,1)S(1)}, bf16[200,256]{1,0:T(8,128)(2,1)S(1)}, u32[]{:S(2)}, u32[]{:S(2)}) collective-permute-start(bf16[200,256]{1,0:T(8,128)(2,1)S(1)} %partial_grad.1), channel_id=1, source_target_pairs={{0,192},{64,0},{128,64},{192,128},{1,193},{65,1},{129,65},{193,129... | collective-permute-start | bytes 307208 | tf_op jit(solution)/shard_map/ppermute | solution.py:314
  95.9 11.5 %collective-permute-start.12 = (bf16[200,256]{1,0:T(8,128)(2,1)S(1)}, bf16[200,256]{1,0:T(8,128)(2,1)S(1)}, u32[]{:S(2)}, u32[]{:S(2)}) collective-permute-start(bf16[200,256]{1,0:T(8,128)(2,1)S(1)} %partial_grad.1), channel_id=1, source_target_pairs={{0,64},{64,128},{128,192},{192,0},{1,65},{65,129},{129,193},{193,1... | collective-permute-start | bytes 307208 | tf_op jit(solution)/shard_map/ppermute | solution.py:314
  95.9 11.5 %collective-permute-start.11 = (bf16[200,256]{1,0:T(8,128)(2,1)S(1)}, bf16[200,256]{1,0:T(8,128)(2,1)S(1)}, u32[]{:S(2)}, u32[]{:S(2)}) collective-permute-start(bf16[200,256]{1,0:T(8,128)(2,1)S(1)} %partial_grad.1), channel_id=1, source_target_pairs={{0,128},{64,192},{128,0},{192,64},{1,129},{65,193},{129,1},{193,65... | collective-permute-start | bytes 307208 | tf_op jit(solution)/shard_map/ppermute | solution.py:314
  107.5 4.7 %collective-permute-start.14 = (bf16[200,256]{1,0:T(8,128)(2,1)S(1)}, bf16[200,256]{1,0:T(8,128)(2,1)S(1)}, u32[]{:S(2)}, u32[]{:S(2)}) collective-permute-start(bf16[200,256]{1,0:T(8,128)(2,1)S(1)} %add_convert_fusion), channel_id=1, source_target_pairs={{0,32},{32,0},{1,33},{33,1},{2,34},{34,2},{3,35},{35,3},{4,36},{36... | collective-permute-start | bytes 307208 | tf_op jit(solution)/shard_map/ppermute | solution.py:314
  107.6 35.7 %copy-start.2 = (f32[32,3200]{1,0:T(8,128)S(1)}, f32[32,3200]{1,0:T(8,128)}, u32[]{:S(2)}) copy-start(f32[32,3200]{1,0:T(8,128)} %copy-done.1) | copy-start | bytes 1228804
  112.3 6.6 %collective-permute-start.23 = (bf16[400,128]{1,0:T(8,128)(2,1)S(1)}, bf16[400,128]{1,0:T(8,128)(2,1)S(1)}, u32[]{:S(2)}, u32[]{:S(2)}) collective-permute-start(bf16[400,128]{1,0:T(8,128)(2,1)S(1)} %get-tuple-element.20), channel_id=1, source_target_pairs={{0,8},{8,16},{16,24},{24,0},{1,9},{9,17},{17,25},{25,1},{2,10},{10... | collective-permute-start | bytes 307208 | tf_op jit(solution)/shard_map/ppermute | solution.py:314
  112.9 6.0 %collective-permute-start.25 = (bf16[400,128]{1,0:T(8,128)(2,1)S(1)}, bf16[400,128]{1,0:T(8,128)(2,1)S(1)}, u32[]{:S(2)}, u32[]{:S(2)}) collective-permute-start(bf16[400,128]{1,0:T(8,128)(2,1)S(1)} %get-tuple-element.20), channel_id=1, source_target_pairs={{0,24},{8,0},{16,8},{24,16},{1,25},{9,1},{17,9},{25,17},{2,26},{10... | collective-permute-start | bytes 307208 | tf_op jit(solution)/shard_map/ppermute | solution.py:314
  115.6 6.7 %collective-permute-start.15 = (bf16[400,128]{1,0:T(8,128)(2,1)S(1)}, bf16[400,128]{1,0:T(8,128)(2,1)S(1)}, u32[]{:S(2)}, u32[]{:S(2)}) collective-permute-start(bf16[400,128]{1,0:T(8,128)(2,1)S(1)} %get-tuple-element.24), channel_id=1, source_target_pairs={{0,2},{2,4},{4,6},{6,0},{1,3},{3,5},{5,7},{7,1},{8,10},{10,12},{12... | collective-permute-start | bytes 307208 | tf_op jit(solution)/shard_map/ppermute | solution.py:314
  116.7 6.4 %collective-permute-start.17 = (bf16[400,128]{1,0:T(8,128)(2,1)S(1)}, bf16[400,128]{1,0:T(8,128)(2,1)S(1)}, u32[]{:S(2)}, u32[]{:S(2)}) collective-permute-start(bf16[400,128]{1,0:T(8,128)(2,1)S(1)} %get-tuple-element.24), channel_id=1, source_target_pairs={{0,6},{2,0},{4,2},{6,4},{1,7},{3,1},{5,3},{7,5},{8,14},{10,8},{12,... | collective-permute-start | bytes 307208 | tf_op jit(solution)/shard_map/ppermute | solution.py:314
  118.9 11.1 %collective-permute-start.24 = (bf16[200,128]{1,0:T(8,128)(2,1)S(1)}, bf16[200,128]{1,0:T(8,128)(2,1)S(1)}, u32[]{:S(2)}, u32[]{:S(2)}) collective-permute-start(bf16[200,128]{1,0:T(8,128)(2,1)S(1)} %slice.46), channel_id=1, source_target_pairs={{0,8},{8,16},{16,24},{24,0},{1,9},{9,17},{17,25},{25,1},{2,10},{10... | collective-permute-start | bytes 153608 | tf_op jit(solution)/shard_map/ppermute | solution.py:314
  119.0 11.0 %collective-permute-start.26 = (bf16[200,128]{1,0:T(8,128)(2,1)S(1)}, bf16[200,128]{1,0:T(8,128)(2,1)S(1)}, u32[]{:S(2)}, u32[]{:S(2)}) collective-permute-start(bf16[200,128]{1,0:T(8,128)(2,1)S(1)} %slice.47), channel_id=1, source_target_pairs={{0,24},{8,0},{16,8},{24,16},{1,25},{9,1},{17,9},{25,17},{2,26},{10... | collective-permute-start | bytes 153608 | tf_op jit(solution)/shard_map/ppermute | solution.py:314
  122.3 5.4 %collective-permute-start.16 = (bf16[200,128]{1,0:T(8,128)(2,1)S(1)}, bf16[200,128]{1,0:T(8,128)(2,1)S(1)}, u32[]{:S(2)}, u32[]{:S(2)}) collective-permute-start(bf16[200,128]{1,0:T(8,128)(2,1)S(1)} %slice.42), channel_id=1, source_target_pairs={{0,2},{2,4},{4,6},{6,0},{1,3},{3,5},{5,7},{7,1},{8,10},{10,12},{12... | collective-permute-start | bytes 153608 | tf_op jit(solution)/shard_map/ppermute | solution.py:314
  123.1 4.7 %collective-permute-start.18 = (bf16[200,128]{1,0:T(8,128)(2,1)S(1)}, bf16[200,128]{1,0:T(8,128)(2,1)S(1)}, u32[]{:S(2)}, u32[]{:S(2)}) collective-permute-start(bf16[200,128]{1,0:T(8,128)(2,1)S(1)} %slice.43), channel_id=1, source_target_pairs={{0,6},{2,0},{4,2},{6,4},{1,7},{3,1},{5,3},{7,5},{8,14},{10,8},{12,... | collective-permute-start | bytes 153608 | tf_op jit(solution)/shard_map/ppermute | solution.py:314
  127.9 8.1 %collective-permute-start.21 = (bf16[1600,128]{1,0:T(8,128)(2,1)S(1)}, bf16[1600,128]{1,0:T(8,128)(2,1)S(1)}, u32[]{:S(2)}, u32[]{:S(2)}) collective-permute-start(bf16[1600,128]{1,0:T(8,128)(2,1)S(1)} %constant_dynamic-update-slice_fusion.refs_0_), channel_id=1, source_target_pairs={{0,24},{8,0},{16,8},{24,16},{1,25},{9,1},{17,9},{25,17},{2,26},{10... | collective-permute-start | bytes 1228808 | tf_op jit(solution)/shard_map/ppermute | solution.py:314
  128.0 9.6 %collective-permute-start.19 = (bf16[1600,128]{1,0:T(8,128)(2,1)S(1)}, bf16[1600,128]{1,0:T(8,128)(2,1)S(1)}, u32[]{:S(2)}, u32[]{:S(2)}) collective-permute-start(bf16[1600,128]{1,0:T(8,128)(2,1)S(1)} %constant_dynamic-update-slice_fusion.refs_0_), channel_id=1, source_target_pairs={{0,8},{8,16},{16,24},{24,0},{1,9},{9,17},{17,25},{25,1},{2,10},{10... | collective-permute-start | bytes 1228808 | tf_op jit(solution)/shard_map/ppermute | solution.py:314
  130.1 9.2 %collective-permute-start.29 = (bf16[1600,128]{1,0:T(8,128)(2,1)S(1)}, bf16[1600,128]{1,0:T(8,128)(2,1)S(1)}, u32[]{:S(2)}, u32[]{:S(2)}) collective-permute-start(bf16[1600,128]{1,0:T(8,128)(2,1)S(1)} %constant_dynamic-update-slice_fusion.5.refs_5_), channel_id=1, source_target_pairs={{0,6},{2,0},{4,2},{6,4},{1,7},{3,1},{5,3},{7,5},{8,14},{10,8},{12,... | collective-permute-start | bytes 1228808 | tf_op jit(solution)/shard_map/ppermute | solution.py:314
  133.8 9.3 %collective-permute-start.27 = (bf16[1600,128]{1,0:T(8,128)(2,1)S(1)}, bf16[1600,128]{1,0:T(8,128)(2,1)S(1)}, u32[]{:S(2)}, u32[]{:S(2)}) collective-permute-start(bf16[1600,128]{1,0:T(8,128)(2,1)S(1)} %constant_dynamic-update-slice_fusion.5.refs_5_), channel_id=1, source_target_pairs={{0,2},{2,4},{4,6},{6,0},{1,3},{3,5},{5,7},{7,1},{8,10},{10,12},{12... | collective-permute-start | bytes 1228808 | tf_op jit(solution)/shard_map/ppermute | solution.py:314
  133.9 1.2 collective-permute-start.10
  135.1 8.1 %collective-permute-start.31 = (bf16[32,3200]{1,0:T(8,128)(2,1)}, bf16[32,3200]{1,0:T(8,128)(2,1)S(1)}, u32[]{:S(2)}, u32[]{:S(2)}) collective-permute-start(bf16[32,3200]{1,0:T(8,128)(2,1)} %copy-done.10), channel_id=1, source_target_pairs={{0,1},{1,0},{2,3},{3,2},{4,5},{5,4},{6,7},{7,6},{8,9},{9,8},{10,11... | collective-permute-start | bytes 614408 | tf_op jit(solution)/shard_map/ppermute | solution.py:314
  136.0 8.0 %collective-permute-start.22 = (bf16[800,128]{1,0:T(8,128)(2,1)S(1)}, bf16[800,128]{1,0:T(8,128)(2,1)S(1)}, u32[]{:S(2)}, u32[]{:S(2)}) collective-permute-start(bf16[800,128]{1,0:T(8,128)(2,1)S(1)} %slice.45), channel_id=1, source_target_pairs={{0,24},{8,0},{16,8},{24,16},{1,25},{9,1},{17,9},{25,17},{2,26},{10... | collective-permute-start | bytes 614408 | tf_op jit(solution)/shard_map/ppermute | solution.py:314
  137.6 8.3 %collective-permute-start.20 = (bf16[800,128]{1,0:T(8,128)(2,1)S(1)}, bf16[800,128]{1,0:T(8,128)(2,1)S(1)}, u32[]{:S(2)}, u32[]{:S(2)}) collective-permute-start(bf16[800,128]{1,0:T(8,128)(2,1)S(1)} %slice.44), channel_id=1, source_target_pairs={{0,8},{8,16},{16,24},{24,0},{1,9},{9,17},{17,25},{25,1},{2,10},{10... | collective-permute-start | bytes 614408 | tf_op jit(solution)/shard_map/ppermute | solution.py:314
  139.3 7.0 %collective-permute-start.30 = (bf16[800,128]{1,0:T(8,128)(2,1)S(1)}, bf16[800,128]{1,0:T(8,128)(2,1)S(1)}, u32[]{:S(2)}, u32[]{:S(2)}) collective-permute-start(bf16[800,128]{1,0:T(8,128)(2,1)S(1)} %slice.49), channel_id=1, source_target_pairs={{0,6},{2,0},{4,2},{6,4},{1,7},{3,1},{5,3},{7,5},{8,14},{10,8},{12,... | collective-permute-start | bytes 614408 | tf_op jit(solution)/shard_map/ppermute | solution.py:314
  143.1 7.0 %collective-permute-start.28 = (bf16[800,128]{1,0:T(8,128)(2,1)S(1)}, bf16[800,128]{1,0:T(8,128)(2,1)S(1)}, u32[]{:S(2)}, u32[]{:S(2)}) collective-permute-start(bf16[800,128]{1,0:T(8,128)(2,1)S(1)} %slice.48), channel_id=1, source_target_pairs={{0,2},{2,4},{4,6},{6,0},{1,3},{3,5},{5,7},{7,1},{8,10},{10,12},{12... | collective-permute-start | bytes 614408 | tf_op jit(solution)/shard_map/ppermute | solution.py:314

commit v2 on v1

--- a/solution.py
+++ b/solution.py
@@ -38,23 +38,39 @@
 
 
 def message_kernel(
-    core_ref, esrc_ref, edst_ref, erot_ref, ew_ref, rot_ref,
-    mix0_ref, mix1_ref, mix2_ref,
+    core_ref, esrc_hbm, edst_hbm, erot_hbm, ew_hbm, rot_hbm,
+    mix0_hbm, mix1_hbm, mix2_hbm,
     fo_ref, ho0_ref, ho1_ref, ho2_ref, ho3_ref,
     fx_ref, hx0_ref, hx1_ref, hx2_ref, hx3_ref,
     out_ref,
     rows, nat, frames, wframes, packed, z0, z1, z2, xb0, xb1, xb2,
+    esrc_ref, edst_ref, erot_ref, ew_ref, rot_ref, mix0_ref, mix1_ref, mix2_ref, sems,
 ):
     core = core_ref[0]
     other = 1 - core
     edges = esrc_ref.shape[1]
     atoms, half = fo_ref.shape
 
+    copies = [
+        pltpu.make_async_copy(src, dst, sems.at[i])
+        for i, (src, dst) in enumerate(
+            (
+                (erot_hbm, erot_ref), (ew_hbm, ew_ref), (rot_hbm, rot_ref), (esrc_hbm, esrc_ref),
+                (edst_hbm, edst_ref), (mix0_hbm, mix0_ref), (mix1_hbm, mix1_ref), (mix2_hbm, mix2_ref),
+            )
+        )
+    ]
+    moves = []
     for q, (own, oth) in enumerate(
         zip((fo_ref, ho0_ref, ho1_ref, ho2_ref, ho3_ref), (fx_ref, hx0_ref, hx1_ref, hx2_ref, hx3_ref))
     ):
-        rows[core, q * atoms : (q + 1) * atoms, :] = own[...]
-        rows[other, q * atoms : (q + 1) * atoms, :] = oth[...]
+        at = pl.ds(q * atoms, atoms)
+        moves.append(pltpu.make_async_copy(own, rows.at[core, at, :], sems.at[8 + 2 * q]))
+        moves.append(pltpu.make_async_copy(oth, rows.at[other, at, :], sems.at[9 + 2 * q]))
+    for copy in copies[:5] + moves + copies[5:]:
+        copy.start()
+    for copy in copies[:5]:
+        copy.wait()
 
     source_rows = lax.broadcasted_iota(jnp.int32, (5 * atoms, edges), 0)
     onehot = (esrc_ref[...] == source_rows).astype(BF16)
@@ -84,6 +100,8 @@
             nat[blk, pl.ds(at, step), :] = got[:, blk * 128 : (blk + 1) * 128]
         return 0
 
+    for move in moves:
+        move.wait()
     lax.fori_loop(0, 2 * half // step, gather, 0)
 
     groups = 2 * half // 400
@@ -124,6 +142,8 @@
             z0[nb, pl.ds(at, 128), :] = y[:, nb * 128 : (nb + 1) * 128]
         return 0
 
+    for copy in copies[5:]:
+        copy.wait()
     lax.fori_loop(0, mix0_ref.shape[1] // 128, mix_zero, 0)
 
     def mix_pair(mix_ref, xb, z):
@@ -190,7 +210,7 @@
     return pl.pallas_call(
         message_kernel,
         out_shape=jax.ShapeDtypeStruct((atoms, 2 * half), BF16),
-        in_specs=[pl.BlockSpec(memory_space=pltpu.SMEM)] + [vmem] * 18,
+        in_specs=[pl.BlockSpec(memory_space=pltpu.SMEM)] + [pl.BlockSpec(memory_space=pltpu.HBM)] * 18,
         out_specs=vmem,
         scratch_shapes=[
             pltpu.VMEM((2, 5 * atoms, half), BF16),
@@ -204,8 +224,12 @@
             pltpu.VMEM((640, 512), BF16),
             pltpu.VMEM((512, 1024), BF16),
             pltpu.VMEM((384, 1024), BF16),
-        ],
-        compiler_params=pltpu.CompilerParams(vmem_limit_bytes=36 * 1024 * 1024),
+        ]
+        + [pltpu.VMEM((1, edges), jnp.int32)] * 3
+        + [pltpu.VMEM((1, edges), F32), pltpu.VMEM(rot_table.shape, F32)]
+        + [pltpu.VMEM(mix.shape, BF16) for mix in mixes]
+        + [pltpu.SemaphoreType.DMA((18,))],
+        compiler_params=pltpu.CompilerParams(vmem_limit_bytes=54 * 1024 * 1024),
         cost_estimate=pl.CostEstimate(flops=5_000_000_000, bytes_accessed=6_000_000, transcendentals=0),
         name="messages",
     )(core, row(esrc), row(edst), row(erot), row(ew), rot_table, *mixes, *own, *oth)
@@ -314,35 +338,37 @@
     return lax.ppermute(x, axis, [(i, (i + by) % count) for i in range(count)])
 
 
-def ring_blocks(x, axis):
-    half = x.shape[0] // 2
-    behind = shift(x, axis, 1)
-    ahead = shift(x, axis, -1)
-    return [x, behind, shift(behind[:half], axis, 1), shift(ahead[half:], axis, -1), ahead]
-
-
-def assemble_kernel(place_ref, *refs):
-    blocks, out_ref, sems = refs[:-2], refs[-2], refs[-1]
-    y, x = place_ref[0], place_ref[1]
+def plane_shift(x, early, by):
+    pairs = []
+    for y in range(4):
+        for x_at in range(4):
+            for c in range(2):
+                along_x = (c == 0) == early
+                to = (y, (x_at + by) % 4) if along_x else ((y + by) % 4, x_at)
+                pairs.append(((y * 4 + x_at) * 2 + c, (to[0] * 4 + to[1]) * 2 + c))
+    return lax.ppermute(x, ("y", "x", "chan"), pairs)
+
+
+def assemble_kernel(place_ref, own, behind, far_lo, far_hi, ahead, out_ref, sems):
+    y, x, core = place_ref[0], place_ref[1], place_ref[2]
     rows = out_ref.shape[0] // 16
     copies = []
-    for path in range(2):
-        own, behind, far_lo, far_hi, ahead = blocks[5 * path : 5 * path + 5]
-        for late in range(4):
-            for early in range(4):
-                if late == 2:
-                    ref, at = (far_lo, early) if early < 2 else (far_hi, early - 2)
-                else:
-                    ref, at = {0: own, 1: behind, 3: ahead}[late], early
-                dy, dx = (late, early) if path == 0 else (early, late)
-                spot = lax.rem(y + 4 - dy, 4) * 4 + lax.rem(x + 4 - dx, 4)
-                copies.append(
-                    pltpu.make_async_copy(
-                        ref.at[pl.ds(at * rows, rows), :],
-                        out_ref.at[pl.ds(pl.multiple_of(spot * rows, 16), rows), pl.ds(path * 128, 128)],
-                        sems.at[len(copies)],
-                    )
+    for late in range(4):
+        for early in range(4):
+            if late == 2:
+                ref, at = (far_lo, early) if early < 2 else (far_hi, early - 2)
+            else:
+                ref, at = {0: own, 1: behind, 3: ahead}[late], early
+            dy = late + core * (early - late)
+            dx = early + core * (late - early)
+            spot = lax.rem(y + 4 - dy, 4) * 4 + lax.rem(x + 4 - dx, 4)
+            copies.append(
+                pltpu.make_async_copy(
+                    ref.at[pl.ds(at * rows, rows), :],
+                    out_ref.at[pl.ds(pl.multiple_of(spot * rows, 16), rows), :],
+                    sems.at[len(copies)],
                 )
+            )
     for copy in copies:
         copy.start()
     for copy in copies:
@@ -350,15 +376,14 @@
 
 
 def assemble(place, blocks):
-    rows = 4 * blocks[0].shape[0]
-    hbm = pl.BlockSpec(memory_space=pl.ANY)
+    rows, width = blocks[0].shape
     return pl.pallas_call(
         assemble_kernel,
-        out_shape=jax.ShapeDtypeStruct((rows, 256), BF16),
+        out_shape=jax.ShapeDtypeStruct((4 * rows, width), BF16),
         in_specs=[pl.BlockSpec(memory_space=pltpu.SMEM)]
         + [pl.BlockSpec(memory_space=pltpu.VMEM)] * len(blocks),
-        out_specs=hbm,
-        scratch_shapes=[pltpu.SemaphoreType.DMA((32,))],
+        out_specs=pl.BlockSpec(memory_space=pl.ANY),
+        scratch_shapes=[pltpu.SemaphoreType.DMA((16,))],
         compiler_params=pltpu.CompilerParams(vmem_limit_bytes=16 * 1024 * 1024),
         name="assemble",
     )(place, *blocks)
@@ -392,14 +417,15 @@
     low = lax.axis_index("zl") == 0
     pair = jnp.concatenate([jnp.where(low, total, twin), jnp.where(low, twin, total)], axis=0)
 
-    def gather_first(x, axis):
-        own, behind, far_lo, far_hi, ahead = ring_blocks(x, axis)
-        return jnp.concatenate([own, behind, far_lo, far_hi, ahead], axis=0)
-
-    left = gather_first(pair[:, :128], "x")
-    right = gather_first(pair[:, 128:], "y")
-    place = jnp.stack([lax.axis_index("y"), lax.axis_index("x")]).astype(jnp.int32)
-    grad_head = assemble(place, ring_blocks(left, "y") + ring_blocks(right, "x"))
+    row = jnp.concatenate(
+        [pair, plane_shift(pair, True, 1), plane_shift(pair, True, 2), plane_shift(pair, True, -1)], axis=0
+    )
+    half = row.shape[0] // 2
+    behind = plane_shift(row, False, 1)
+    ahead = plane_shift(row, False, -1)
+    far = [plane_shift(behind[:half], False, 1), plane_shift(ahead[half:], False, -1)]
+    place = jnp.stack([lax.axis_index(name) for name in ("y", "x", "chan")]).astype(jnp.int32)
+    grad_head = assemble(place, [row, behind] + far + [ahead])
     return (atom_loss, grad_head, grad_features)
 
 

time: 153 us -> 138 us (0.902)
  waiting for transfers between devices: 27.1 us -> 45.4 us
  local copies, waits for them, and re-layouts: 21 us -> 3.47 us
  starting transfers between devices: 49 us -> 33.8 us
    ppermute x32 -> x16, starting transfers between devices: 49 us -> 23.8 us  [shift(): return lax.ppermute(x, axis, [(i, (i + by) % count) for i in range(count)])]
    ppermute x0 -> x7, waiting for transfers between devices: none -> 24.4 us  [plane_shift(): return lax.ppermute(x, ('y', 'x', 'chan'), pairs)]
    unnamed x70 -> x40, local copies, waits for them, and re-layouts: 20.8 us -> 3.32 us
    ppermute x0 -> x7, starting transfers between devices: none -> 9.99 us  [plane_shift(): return lax.ppermute(x, ('y', 'x', 'chan'), pairs)]
    ppermute x32 -> x16, waiting for transfers between devices: 27.1 us -> 21 us  [shift(): return lax.ppermute(x, axis, [(i, (i + by) % count) for i in range(count)])]
  transfers between devices with their start and end apart: 32 -> 23, of which waited for: 11 -> 14; matrix products, arithmetic and copies ran while one was open for 1% -> 1% of each run, Pallas kernels for 0% -> 0%
where the time goes in v2:
time: 138 us
  waiting for transfers between devices  45.4 us (33%)
  starting transfers between devices  33.8 us (24%)
  blocking collectives  26.3 us (19%)
  Pallas kernels  26 us (19%)
  local copies, waits for them, and re-layouts  3.47 us (3%)
  other arithmetic  1.62 us (1%)
    all_to_all x1, blocking collectives, body(): got = lax.all_to_all(load, GROUP, split_axis=0, concat_axis=0, tiled=True)  26.3 us
    ppermute x7, waiting for transfers between devices, plane_shift(): return lax.ppermute(x, ('y', 'x', 'chan'), pairs)  24.4 us
    ppermute x16, starting transfers between devices, shift(): return lax.ppermute(x, axis, [(i, (i + by) % count) for i in range(count)])  23.8 us
    ppermute x16, waiting for transfers between devices, shift(): return lax.ppermute(x, axis, [(i, (i + by) % count) for i in range(count)])  21 us
    pallas_call x1, Pallas kernels, messages(): pl.pallas_call(message_kernel, out_shape=jax.ShapeDtypeStruct((atoms, 2 *...  18.4 us
    ppermute x7, starting transfers between devices, plane_shift(): return lax.ppermute(x, ('y', 'x', 'chan'), pairs)  9.99 us
    pallas_call x1, Pallas kernels, head(): pl.pallas_call(head_kernel, out_shape=(jax.ShapeDtypeStruct((parts, atoms...  3.45 us
    unnamed x40, local copies, waits for them, and re-layouts  3.32 us
  transfers between devices with their start and end apart: 23, of which 14 were waited for; matrix products, arithmetic and copies ran while one was open for 1% of the time, Pallas kernels for 0%

profile of v2, /device:TPU:32, one launch (start us, length us, event | category | flops | bytes accessed | tf_op | source)
XLA Modules:
  0.0 137.6 jit_solution(15773383087570612161)
XLA Ops:
  0.6 0.7 copy-done.7
  1.3 1.4 %leaving.1 = (bf16[32,3200]{1,0:T(8,128)(2,1)S(1)}, bf16[32,3200]{1,0:T(8,128)(2,1)S(1)}, bf16[32,3200]{1,0:T(8,128)(2,1)S(1)}, bf16[32,3200]{1,0:T(8,128)(2,1)S(1)}) custom-call(s32[4,32]{1,0:T(4,128)S(1)} %copy-done.7, bf16[32,3200]{1,0:T(8,128)(2,1)} %fo_ref.3), custom_call_target="tpu_custom_call" | custom-call | tf_op jit(solution)/shard_map/leaving/pallas_call | solution.py:308
  2.7 1.6 %collective-permute-start.1 = (bf16[32,3200]{1,0:T(8,128)(2,1)S(1)}, bf16[32,3200]{1,0:T(8,128)(2,1)S(1)}, u32[]{:S(2)}, u32[]{:S(2)}) collective-permute-start(bf16[32,3200]{1,0:T(8,128)(2,1)S(1)} %get-tuple-element.11), channel_id=1, source_target_pairs={{0,2},{2,4},{4,6},{6,8},{8,10},{10,12},{12,14},{14,16},{16,18},{18... | collective-permute-start | bytes 614408 | tf_op jit(solution)/shard_map/ppermute | solution.py:338
  4.3 4.8 %collective-permute-start.2 = (bf16[32,3200]{1,0:T(8,128)(2,1)S(1)}, bf16[32,3200]{1,0:T(8,128)(2,1)S(1)}, u32[]{:S(2)}, u32[]{:S(2)}) collective-permute-start(bf16[32,3200]{1,0:T(8,128)(2,1)S(1)} %get-tuple-element.12), channel_id=1, source_target_pairs={{0,254},{2,0},{4,2},{6,4},{8,6},{10,8},{12,10},{14,12},{16,14},{18... | collective-permute-start | bytes 614408 | tf_op jit(solution)/shard_map/ppermute | solution.py:338
  9.0 0.0 collective-permute-start.3
  9.0 6.5 %collective-permute-start.4 = (bf16[32,3200]{1,0:T(8,128)(2,1)S(1)}, bf16[32,3200]{1,0:T(8,128)(2,1)S(1)}, u32[]{:S(2)}, u32[]{:S(2)}) collective-permute-start(bf16[32,3200]{1,0:T(8,128)(2,1)S(1)} %get-tuple-element.14), channel_id=1, source_target_pairs={{0,252},{2,254},{4,0},{6,2},{8,4},{10,6},{12,8},{14,10},{16,12},{1... | collective-permute-start | bytes 614408 | tf_op jit(solution)/shard_map/ppermute | solution.py:338
  15.6 0.0 collective-permute-start
  15.6 0.0 collective-permute-done.1.ho0_ref
  15.6 0.5 collective-permute-start.5
  16.1 0.3 collective-permute-done.2.ho1_ref
  16.4 0.0 collective-permute-start.6
  16.4 3.5 %collective-permute-done.3.ho2_ref = bf16[32,3200]{1,0:T(8,128)(2,1)S(1)} collective-permute-done((bf16[32,3200]{1,0:T(8,128)(2,1)S(1)}, bf16[32,3200]{1,0:T(8,128)(2,1)S(1)}, u32[]{:S(2)}, u32[]{:S(2)}) %collective-permute-start.3) | collective-permute-done | bytes 204832 | tf_op jit(solution)/shard_map/ppermute | solution.py:338
  19.9 0.0 collective-permute-start.7
  19.9 0.7 collective-permute-done.4.ho3_ref
  20.6 0.0 collective-permute-start.8
  20.6 0.0 collective-permute-done.fx_ref
  20.6 0.0 copy-start.4
  20.6 0.0 collective-permute-done.5.hx0_ref
  20.7 0.7 collective-permute-done.7.hx2_ref
  21.4 0.7 collective-permute-done.8.hx3_ref
  22.1 0.6 copy-done.18
  22.7 0.0 copy-start.8
  22.8 18.4 %messages.1.mine_ref = bf16[32,6400]{1,0:T(8,128)(2,1)} custom-call(s32[1]{0:T(128)} %bitcast.core_ref, s32[1,256]{1,0:T(1,128)} %bitcast.13, s32[1,256]{1,0:T(1,128)} %bitcast.14, s32[1,256]{1,0:T(1,128)} %bitcast.15, f32[1,256]{1,0:T(1,128)} %bitcast.16, f32[165,512]{1,0:T(8,128)} %bitcast.12, bf16[640,640]{1,0:T(8,128)(2,1)} %mix0_hbm.1, ...), custom_call_target="tpu_custom_call" | custom-call | flops 5000000000 | bytes 6000000 | tf_op jit(solution)/shard_map/messages/pallas_call | solution.py:210
  41.2 0.2 collective-permute-start.9
  41.4 0.1 copy.18.species_ref
  41.5 1.9 %collective-permute-done.9.recv_ref = bf16[32,6400]{1,0:T(8,128)(2,1)} collective-permute-done((bf16[32,6400]{1,0:T(8,128)(2,1)}, bf16[32,6400]{1,0:T(8,128)(2,1)}, u32[]{:S(2)}, u32[]{:S(2)}) %collective-permute-start.9) | collective-permute-done | bytes 409632 | tf_op jit(solution)/shard_map/ppermute | solution.py:338
  43.4 0.0 copy-start.1
  43.4 1.0 copy-done.1
  44.4 0.9 copy-done.5
  45.3 3.5 %head.1 = (bf16[32,32,512]{2,1,0:T(8,128)(2,1)S(1)}, f32[32,1]{1,0:T(8,128)S(1)}, f32[32,3200]{1,0:T(8,128)S(1)}, bf16[32,3200]{1,0:T(8,128)(2,1)S(1)}) custom-call(s32[1]{0:T(128)} %bitcast.core_ref, s32[4]{0:T(128)S(1)} %copy-done.8, s32[32,1]{1,0:T(8,128)S(1)} %copy.18.species_ref, bf16[32,3200]{1,0:T(8,128)(2,1)} %fo_ref.3, ...), custom_call_target="tpu_custom_call" | custom-call | flops 300000000 | bytes 6000000 | tf_op jit(solution)/shard_map/head/pallas_call | solution.py:278
  48.8 0.0 copy-start.2
  48.8 0.0 copy-start.9
  48.8 26.3 %all_to_all.5 = bf16[32,32,512]{2,1,0:T(8,128)(2,1)S(1)} all-to-all(bf16[32,32,512]{2,1,0:T(8,128)(2,1)S(1)} %get-tuple-element.16), channel_id=1, replica_groups=mesh['zh'=4,'zl'=2,'y'=4,'x'=4,'chan'=2] {'zl','y','x'}, dimensions={0} | all-to-all | bytes 2097152 | tf_op jit(solution)/shard_map/all_to_all | solution.py:409
  75.0 0.3 partial_grad.1
  75.4 5.7 %collective-permute-start.13 = (bf16[200,256]{1,0:T(8,128)(2,1)S(1)}, bf16[200,256]{1,0:T(8,128)(2,1)S(1)}, u32[]{:S(2)}, u32[]{:S(2)}) collective-permute-start(bf16[200,256]{1,0:T(8,128)(2,1)S(1)} %partial_grad.1), channel_id=1, source_target_pairs={{0,192},{64,0},{128,64},{192,128},{1,193},{65,1},{129,65},{193,129... | collective-permute-start | bytes 307208 | tf_op jit(solution)/shard_map/ppermute | solution.py:338
  81.1 0.5 collective-permute-start.12
  81.6 3.3 %collective-permute-start.11 = (bf16[200,256]{1,0:T(8,128)(2,1)S(1)}, bf16[200,256]{1,0:T(8,128)(2,1)S(1)}, u32[]{:S(2)}, u32[]{:S(2)}) collective-permute-start(bf16[200,256]{1,0:T(8,128)(2,1)S(1)} %partial_grad.1), channel_id=1, source_target_pairs={{0,128},{64,192},{128,0},{192,64},{1,129},{65,193},{129,1},{193,65... | collective-permute-start | bytes 307208 | tf_op jit(solution)/shard_map/ppermute | solution.py:338
  84.9 0.0 collective-permute-done.13
  84.9 7.9 %collective-permute-done.12 = bf16[200,256]{1,0:T(8,128)(2,1)S(1)} collective-permute-done((bf16[200,256]{1,0:T(8,128)(2,1)S(1)}, bf16[200,256]{1,0:T(8,128)(2,1)S(1)}, u32[]{:S(2)}, u32[]{:S(2)}) %collective-permute-start.12) | collective-permute-done | bytes 102432 | tf_op jit(solution)/shard_map/ppermute | solution.py:338
  92.8 0.1 add_convert_fusion
  92.9 0.1 collective-permute-start.14
  93.0 0.0 copy-start.3
  93.0 4.6 %collective-permute-done.14 = bf16[200,256]{1,0:T(8,128)(2,1)S(1)} collective-permute-done((bf16[200,256]{1,0:T(8,128)(2,1)S(1)}, bf16[200,256]{1,0:T(8,128)(2,1)S(1)}, u32[]{:S(2)}, u32[]{:S(2)}) %collective-permute-start.14) | collective-permute-done | bytes 102432 | tf_op jit(solution)/shard_map/ppermute | solution.py:338
  97.7 1.2 collective-permute-start.15
  98.9 1.5 %collective-permute-start.16 = (bf16[400,256]{1,0:T(8,128)(2,1)S(1)}, bf16[400,256]{1,0:T(8,128)(2,1)S(1)}, u32[]{:S(2)}, u32[]{:S(2)}) collective-permute-start(bf16[400,256]{1,0:T(8,128)(2,1)S(1)} %pad_maximum_fusion), channel_id=1, source_target_pairs={{0,4},{1,17},{2,6},{3,19},{4,0},{5,21},{6,2},{7,23},{8,12},{9,25},... | collective-permute-start | bytes 614408 | tf_op jit(solution)/shard_map/ppermute | solution.py:349
  100.4 2.5 %collective-permute-start.17 = (bf16[400,256]{1,0:T(8,128)(2,1)S(1)}, bf16[400,256]{1,0:T(8,128)(2,1)S(1)}, u32[]{:S(2)}, u32[]{:S(2)}) collective-permute-start(bf16[400,256]{1,0:T(8,128)(2,1)S(1)} %pad_maximum_fusion), channel_id=1, source_target_pairs={{0,6},{1,25},{2,0},{3,27},{4,2},{5,29},{6,4},{7,31},{8,14},{9,1},{... | collective-permute-start | bytes 614408 | tf_op jit(solution)/shard_map/ppermute | solution.py:349
  103.0 4.0 %collective-permute-done.15 = bf16[400,256]{1,0:T(8,128)(2,1)S(1)} collective-permute-done((bf16[400,256]{1,0:T(8,128)(2,1)S(1)}, bf16[400,256]{1,0:T(8,128)(2,1)S(1)}, u32[]{:S(2)}, u32[]{:S(2)}) %collective-permute-start.15) | collective-permute-done | bytes 204832 | tf_op jit(solution)/shard_map/ppermute | solution.py:349
  107.0 3.8 %collective-permute-done.17 = bf16[400,256]{1,0:T(8,128)(2,1)S(1)} collective-permute-done((bf16[400,256]{1,0:T(8,128)(2,1)S(1)}, bf16[400,256]{1,0:T(8,128)(2,1)S(1)}, u32[]{:S(2)}, u32[]{:S(2)}) %collective-permute-start.17) | collective-permute-done | bytes 204832 | tf_op jit(solution)/shard_map/ppermute | solution.py:349
  110.8 1.3 collective-permute-start.20
  112.1 0.8 collective-permute-start.18
  112.9 0.0 collective-permute-start.22
  112.9 0.1 reduce
  113.0 0.6 collective-permute-start.10
  113.6 0.1 pad_add_fusion.place_ref
  113.7 0.7 collective-permute-done.10
  114.4 0.5 add.15
  114.9 8.3 %collective-permute-done.20.ahead = bf16[1600,256]{1,0:T(8,128)(2,1)S(1)} collective-permute-done((bf16[1600,256]{1,0:T(8,128)(2,1)S(1)}, bf16[1600,256]{1,0:T(8,128)(2,1)S(1)}, u32[]{:S(2)}, u32[]{:S(2)}) %collective-permute-start.20) | collective-permute-done | bytes 819232 | tf_op jit(solution)/shard_map/ppermute | solution.py:349
  123.2 2.6 %collective-permute-start.21 = (bf16[800,256]{1,0:T(8,128)(2,1)S(1)}, bf16[800,256]{1,0:T(8,128)(2,1)S(1)}, u32[]{:S(2)}, u32[]{:S(2)}) collective-permute-start(bf16[800,256]{1,0:T(8,128)(2,1)S(1)} %slice.9), channel_id=1, source_target_pairs={{0,24},{1,7},{2,26},{3,1},{4,28},{5,3},{6,30},{7,5},{8,0},{9,15},{... | collective-permute-start | bytes 1228808 | tf_op jit(solution)/shard_map/ppermute | solution.py:349
  125.8 0.0 collective-permute-done.18.behind
  125.8 0.1 collective-permute-start.19
  125.9 0.8 convert_add_fusion
  126.7 4.5 %collective-permute-done.21.far_hi = bf16[800,256]{1,0:T(8,128)(2,1)S(1)} collective-permute-done((bf16[800,256]{1,0:T(8,128)(2,1)S(1)}, bf16[800,256]{1,0:T(8,128)(2,1)S(1)}, u32[]{:S(2)}, u32[]{:S(2)}) %collective-permute-start.21) | collective-permute-done | bytes 409632 | tf_op jit(solution)/shard_map/ppermute | solution.py:349
  131.3 3.8 %collective-permute-done.19.far_lo = bf16[800,256]{1,0:T(8,128)(2,1)S(1)} collective-permute-done((bf16[800,256]{1,0:T(8,128)(2,1)S(1)}, bf16[800,256]{1,0:T(8,128)(2,1)S(1)}, u32[]{:S(2)}, u32[]{:S(2)}) %collective-permute-start.19) | collective-permute-done | bytes 409632 | tf_op jit(solution)/shard_map/ppermute | solution.py:349
  135.1 2.4 %assemble.1 = bf16[6400,256]{1,0:T(8,128)(2,1)} custom-call(s32[3]{0:T(128)S(1)} %pad_add_fusion.place_ref, bf16[1600,256]{1,0:T(8,128)(2,1)S(1)} %constant_dynamic-update-slice_fusion.own, bf16[1600,256]{1,0:T(8,128)(2,1)S(1)} %collective-permute-done.18.behind, bf16[800,256]{1,0:T(8,128)(2,1)S(1)} %collective-permute-done.19.far_lo, ...), custom_call_target="tpu_custom_call" | custom-call | tf_op jit(solution)/shard_map/assemble/pallas_call | solution.py:380
  (40 shorter events, 0.2 us)
Async XLA Ops:
  0.6 0.7 copy-start.7
  2.7 12.9 %collective-permute-start.1 = (bf16[32,3200]{1,0:T(8,128)(2,1)S(1)}, bf16[32,3200]{1,0:T(8,128)(2,1)S(1)}, u32[]{:S(2)}, u32[]{:S(2)}) collective-permute-start(bf16[32,3200]{1,0:T(8,128)(2,1)S(1)} %get-tuple-element.11), channel_id=1, source_target_pairs={{0,2},{2,4},{4,6},{6,8},{8,10},{10,12},{12,14},{14,16},{16,18},{18... | collective-permute-start | bytes 614408 | tf_op jit(solution)/shard_map/ppermute | solution.py:338
  4.3 12.1 %collective-permute-start.2 = (bf16[32,3200]{1,0:T(8,128)(2,1)S(1)}, bf16[32,3200]{1,0:T(8,128)(2,1)S(1)}, u32[]{:S(2)}, u32[]{:S(2)}) collective-permute-start(bf16[32,3200]{1,0:T(8,128)(2,1)S(1)} %get-tuple-element.12), channel_id=1, source_target_pairs={{0,254},{2,0},{4,2},{6,4},{8,6},{10,8},{12,10},{14,12},{16,14},{18... | collective-permute-start | bytes 614408 | tf_op jit(solution)/shard_map/ppermute | solution.py:338
  9.0 10.9 %collective-permute-start.3 = (bf16[32,3200]{1,0:T(8,128)(2,1)S(1)}, bf16[32,3200]{1,0:T(8,128)(2,1)S(1)}, u32[]{:S(2)}, u32[]{:S(2)}) collective-permute-start(bf16[32,3200]{1,0:T(8,128)(2,1)S(1)} %get-tuple-element.13), channel_id=1, source_target_pairs={{0,4},{2,6},{4,8},{6,10},{8,12},{10,14},{12,16},{14,18},{16,20},{1... | collective-permute-start | bytes 614408 | tf_op jit(solution)/shard_map/ppermute | solution.py:338
  9.0 11.6 %collective-permute-start.4 = (bf16[32,3200]{1,0:T(8,128)(2,1)S(1)}, bf16[32,3200]{1,0:T(8,128)(2,1)S(1)}, u32[]{:S(2)}, u32[]{:S(2)}) collective-permute-start(bf16[32,3200]{1,0:T(8,128)(2,1)S(1)} %get-tuple-element.14), channel_id=1, source_target_pairs={{0,252},{2,254},{4,0},{6,2},{8,4},{10,6},{12,8},{14,10},{16,12},{1... | collective-permute-start | bytes 614408 | tf_op jit(solution)/shard_map/ppermute | solution.py:338
  15.6 5.0 %collective-permute-start = (bf16[32,3200]{1,0:T(8,128)(2,1)}, bf16[32,3200]{1,0:T(8,128)(2,1)S(1)}, u32[]{:S(2)}, u32[]{:S(2)}) collective-permute-start(bf16[32,3200]{1,0:T(8,128)(2,1)} %fo_ref.3), channel_id=1, source_target_pairs={{0,1},{1,0},{2,3},{3,2},{4,5},{5,4},{6,7},{7,6},{8,9},{9,8},{10,11... | collective-permute-start | bytes 614408 | tf_op jit(solution)/shard_map/ppermute | solution.py:338
  15.6 6.5 %copy-start.11 = (bf16[32,3200]{1,0:T(8,128)(2,1)}, bf16[32,3200]{1,0:T(8,128)(2,1)S(1)}, u32[]{:S(2)}) copy-start(bf16[32,3200]{1,0:T(8,128)(2,1)S(1)} %collective-permute-done.1.ho0_ref) | copy-start | bytes 614404
  15.6 5.0 %collective-permute-start.5 = (bf16[32,3200]{1,0:T(8,128)(2,1)S(1)}, bf16[32,3200]{1,0:T(8,128)(2,1)S(1)}, u32[]{:S(2)}, u32[]{:S(2)}) collective-permute-start(bf16[32,3200]{1,0:T(8,128)(2,1)S(1)} %collective-permute-done.1.ho0_ref), channel_id=1, source_target_pairs={{0,1},{1,0},{2,3},{3,2},{4,5},{5,4},{6,7},{7,6},{8,9},{9,8},{10,11... | collective-permute-start | bytes 614408 | tf_op jit(solution)/shard_map/ppermute | solution.py:338
  16.4 5.7 %copy-start.12 = (bf16[32,3200]{1,0:T(8,128)(2,1)}, bf16[32,3200]{1,0:T(8,128)(2,1)S(1)}, u32[]{:S(2)}) copy-start(bf16[32,3200]{1,0:T(8,128)(2,1)S(1)} %collective-permute-done.2.ho1_ref) | copy-start | bytes 614404
  16.4 4.3 %collective-permute-start.6 = (bf16[32,3200]{1,0:T(8,128)(2,1)S(1)}, bf16[32,3200]{1,0:T(8,128)(2,1)S(1)}, u32[]{:S(2)}, u32[]{:S(2)}) collective-permute-start(bf16[32,3200]{1,0:T(8,128)(2,1)S(1)} %collective-permute-done.2.ho1_ref), channel_id=1, source_target_pairs={{0,1},{1,0},{2,3},{3,2},{4,5},{5,4},{6,7},{7,6},{8,9},{9,8},{10,11... | collective-permute-start | bytes 614408 | tf_op jit(solution)/shard_map/ppermute | solution.py:338
  19.9 2.2 %copy-start.13 = (bf16[32,3200]{1,0:T(8,128)(2,1)}, bf16[32,3200]{1,0:T(8,128)(2,1)S(1)}, u32[]{:S(2)}) copy-start(bf16[32,3200]{1,0:T(8,128)(2,1)S(1)} %collective-permute-done.3.ho2_ref) | copy-start | bytes 614404
  19.9 1.5 %collective-permute-start.7 = (bf16[32,3200]{1,0:T(8,128)(2,1)S(1)}, bf16[32,3200]{1,0:T(8,128)(2,1)S(1)}, u32[]{:S(2)}, u32[]{:S(2)}) collective-permute-start(bf16[32,3200]{1,0:T(8,128)(2,1)S(1)} %collective-permute-done.3.ho2_ref), channel_id=1, source_target_pairs={{0,1},{1,0},{2,3},{3,2},{4,5},{5,4},{6,7},{7,6},{8,9},{9,8},{10,11... | collective-permute-start | bytes 614408 | tf_op jit(solution)/shard_map/ppermute | solution.py:338
  20.6 1.5 %copy-start.14 = (bf16[32,3200]{1,0:T(8,128)(2,1)}, bf16[32,3200]{1,0:T(8,128)(2,1)S(1)}, u32[]{:S(2)}) copy-start(bf16[32,3200]{1,0:T(8,128)(2,1)S(1)} %collective-permute-done.4.ho3_ref) | copy-start | bytes 614404
  20.6 1.5 %collective-permute-start.8 = (bf16[32,3200]{1,0:T(8,128)(2,1)S(1)}, bf16[32,3200]{1,0:T(8,128)(2,1)S(1)}, u32[]{:S(2)}, u32[]{:S(2)}) collective-permute-start(bf16[32,3200]{1,0:T(8,128)(2,1)S(1)} %collective-permute-done.4.ho3_ref), channel_id=1, source_target_pairs={{0,1},{1,0},{2,3},{3,2},{4,5},{5,4},{6,7},{7,6},{8,9},{9,8},{10,11... | collective-permute-start | bytes 614408 | tf_op jit(solution)/shard_map/ppermute | solution.py:338
  20.6 2.1 %copy-start.4 = (bf16[32,3200]{1,0:T(8,128)(2,1)}, bf16[32,3200]{1,0:T(8,128)(2,1)S(1)}, u32[]{:S(2)}) copy-start(bf16[32,3200]{1,0:T(8,128)(2,1)S(1)} %collective-permute-done.fx_ref) | copy-start | bytes 614404
  20.6 1.4 %copy-start.15 = (bf16[32,3200]{1,0:T(8,128)(2,1)}, bf16[32,3200]{1,0:T(8,128)(2,1)S(1)}, u32[]{:S(2)}) copy-start(bf16[32,3200]{1,0:T(8,128)(2,1)S(1)} %collective-permute-done.5.hx0_ref) | copy-start | bytes 614404
  20.7 1.4 %copy-start.16 = (bf16[32,3200]{1,0:T(8,128)(2,1)}, bf16[32,3200]{1,0:T(8,128)(2,1)S(1)}, u32[]{:S(2)}) copy-start(bf16[32,3200]{1,0:T(8,128)(2,1)S(1)} %collective-permute-done.6.hx1_ref) | copy-start | bytes 614404
  21.4 0.7 copy-start.17
  22.1 0.7 copy-start.18
  22.7 18.7 %copy-start.10 = (s32[32]{0:T(128)S(1)}, s32[32]{0:T(128)}, u32[]{:S(2)}) copy-start(s32[32]{0:T(128)} %param.24) | copy-start | bytes 388
  22.7 20.6 %copy-start = (bf16[6400,256]{1,0:T(8,128)(2,1)S(1)}, bf16[6400,256]{1,0:T(8,128)(2,1)}, u32[]{:S(2)}) copy-start(bf16[6400,256]{1,0:T(8,128)(2,1)} %weight_ref.1) | copy-start | bytes 9830404
  22.7 20.6 %copy-start.6 = (f32[32,256]{1,0:T(8,128)S(1)}, f32[32,256]{1,0:T(8,128)}, u32[]{:S(2)}) copy-start(f32[32,256]{1,0:T(8,128)} %target_ref.1) | copy-start | bytes 98308
  22.7 20.6 %copy-start.8 = (s32[4]{0:T(128)S(1)}, s32[4]{0:T(128)}, u32[]{:S(2)}) copy-start(s32[4]{0:T(128)} %orbitals_ref.1) | copy-start | bytes 52
  41.2 2.2 %collective-permute-start.9 = (bf16[32,6400]{1,0:T(8,128)(2,1)}, bf16[32,6400]{1,0:T(8,128)(2,1)}, u32[]{:S(2)}, u32[]{:S(2)}) collective-permute-start(bf16[32,6400]{1,0:T(8,128)(2,1)} %messages.1.mine_ref), channel_id=1, source_target_pairs={{0,1},{1,0},{2,3},{3,2},{4,5},{5,4},{6,7},{7,6},{8,9},{9,8},{10,11... | collective-permute-start | bytes 1228808 | tf_op jit(solution)/shard_map/ppermute | solution.py:338
  43.4 1.0 copy-start.1
  44.4 0.9 copy-start.5
  48.8 44.1 %copy-start.2 = (f32[32,3200]{1,0:T(8,128)}, f32[32,3200]{1,0:T(8,128)S(1)}, u32[]{:S(2)}) copy-start(f32[32,3200]{1,0:T(8,128)S(1)} %get-tuple-element.17) | copy-start | bytes 1228804
  48.8 44.1 %copy-start.9 = (bf16[32,3200]{1,0:T(8,128)(2,1)}, bf16[32,3200]{1,0:T(8,128)(2,1)S(1)}, u32[]{:S(2)}) copy-start(bf16[32,3200]{1,0:T(8,128)(2,1)S(1)} %get-tuple-element.18) | copy-start | bytes 614404
  75.4 9.5 %collective-permute-start.13 = (bf16[200,256]{1,0:T(8,128)(2,1)S(1)}, bf16[200,256]{1,0:T(8,128)(2,1)S(1)}, u32[]{:S(2)}, u32[]{:S(2)}) collective-permute-start(bf16[200,256]{1,0:T(8,128)(2,1)S(1)} %partial_grad.1), channel_id=1, source_target_pairs={{0,192},{64,0},{128,64},{192,128},{1,193},{65,1},{129,65},{193,129... | collective-permute-start | bytes 307208 | tf_op jit(solution)/shard_map/ppermute | solution.py:338
  81.1 11.7 %collective-permute-start.12 = (bf16[200,256]{1,0:T(8,128)(2,1)S(1)}, bf16[200,256]{1,0:T(8,128)(2,1)S(1)}, u32[]{:S(2)}, u32[]{:S(2)}) collective-permute-start(bf16[200,256]{1,0:T(8,128)(2,1)S(1)} %partial_grad.1), channel_id=1, source_target_pairs={{0,64},{64,128},{128,192},{192,0},{1,65},{65,129},{129,193},{193,1... | collective-permute-start | bytes 307208 | tf_op jit(solution)/shard_map/ppermute | solution.py:338
  81.6 11.2 %collective-permute-start.11 = (bf16[200,256]{1,0:T(8,128)(2,1)S(1)}, bf16[200,256]{1,0:T(8,128)(2,1)S(1)}, u32[]{:S(2)}, u32[]{:S(2)}) collective-permute-start(bf16[200,256]{1,0:T(8,128)(2,1)S(1)} %partial_grad.1), channel_id=1, source_target_pairs={{0,128},{64,192},{128,0},{192,64},{1,129},{65,193},{129,1},{193,65... | collective-permute-start | bytes 307208 | tf_op jit(solution)/shard_map/ppermute | solution.py:338
  92.9 4.7 %collective-permute-start.14 = (bf16[200,256]{1,0:T(8,128)(2,1)S(1)}, bf16[200,256]{1,0:T(8,128)(2,1)S(1)}, u32[]{:S(2)}, u32[]{:S(2)}) collective-permute-start(bf16[200,256]{1,0:T(8,128)(2,1)S(1)} %add_convert_fusion), channel_id=1, source_target_pairs={{0,32},{32,0},{1,33},{33,1},{2,34},{34,2},{3,35},{35,3},{4,36},{36... | collective-permute-start | bytes 307208 | tf_op jit(solution)/shard_map/ppermute | solution.py:338
  93.0 33.0 %copy-start.3 = (f32[32,3200]{1,0:T(8,128)S(1)}, f32[32,3200]{1,0:T(8,128)}, u32[]{:S(2)}) copy-start(f32[32,3200]{1,0:T(8,128)} %copy-done.2) | copy-start | bytes 1228804
  97.7 9.2 %collective-permute-start.15 = (bf16[400,256]{1,0:T(8,128)(2,1)S(1)}, bf16[400,256]{1,0:T(8,128)(2,1)S(1)}, u32[]{:S(2)}, u32[]{:S(2)}) collective-permute-start(bf16[400,256]{1,0:T(8,128)(2,1)S(1)} %pad_maximum_fusion), channel_id=1, source_target_pairs={{0,2},{1,9},{2,4},{3,11},{4,6},{5,13},{6,0},{7,15},{8,10},{9,17},{... | collective-permute-start | bytes 614408 | tf_op jit(solution)/shard_map/ppermute | solution.py:349
  98.9 8.0 %collective-permute-start.16 = (bf16[400,256]{1,0:T(8,128)(2,1)S(1)}, bf16[400,256]{1,0:T(8,128)(2,1)S(1)}, u32[]{:S(2)}, u32[]{:S(2)}) collective-permute-start(bf16[400,256]{1,0:T(8,128)(2,1)S(1)} %pad_maximum_fusion), channel_id=1, source_target_pairs={{0,4},{1,17},{2,6},{3,19},{4,0},{5,21},{6,2},{7,23},{8,12},{9,25},... | collective-permute-start | bytes 614408 | tf_op jit(solution)/shard_map/ppermute | solution.py:349
  100.4 10.3 %collective-permute-start.17 = (bf16[400,256]{1,0:T(8,128)(2,1)S(1)}, bf16[400,256]{1,0:T(8,128)(2,1)S(1)}, u32[]{:S(2)}, u32[]{:S(2)}) collective-permute-start(bf16[400,256]{1,0:T(8,128)(2,1)S(1)} %pad_maximum_fusion), channel_id=1, source_target_pairs={{0,6},{1,25},{2,0},{3,27},{4,2},{5,29},{6,4},{7,31},{8,14},{9,1},{... | collective-permute-start | bytes 614408 | tf_op jit(solution)/shard_map/ppermute | solution.py:349
  110.8 12.4 %collective-permute-start.20 = (bf16[1600,256]{1,0:T(8,128)(2,1)S(1)}, bf16[1600,256]{1,0:T(8,128)(2,1)S(1)}, u32[]{:S(2)}, u32[]{:S(2)}) collective-permute-start(bf16[1600,256]{1,0:T(8,128)(2,1)S(1)} %constant_dynamic-update-slice_fusion.own), channel_id=1, source_target_pairs={{0,24},{1,7},{2,26},{3,1},{4,28},{5,3},{6,30},{7,5},{8,0},{9,15},{... | collective-permute-start | bytes 2457608 | tf_op jit(solution)/shard_map/ppermute | solution.py:349
  112.1 13.7 %collective-permute-start.18 = (bf16[1600,256]{1,0:T(8,128)(2,1)S(1)}, bf16[1600,256]{1,0:T(8,128)(2,1)S(1)}, u32[]{:S(2)}, u32[]{:S(2)}) collective-permute-start(bf16[1600,256]{1,0:T(8,128)(2,1)S(1)} %constant_dynamic-update-slice_fusion.own), channel_id=1, source_target_pairs={{0,8},{1,3},{2,10},{3,5},{4,12},{5,7},{6,14},{7,1},{8,16},{9,11},{... | collective-permute-start | bytes 2457608 | tf_op jit(solution)/shard_map/ppermute | solution.py:349
  112.9 13.0 %collective-permute-start.22 = (bf16[32,3200]{1,0:T(8,128)(2,1)}, bf16[32,3200]{1,0:T(8,128)(2,1)S(1)}, u32[]{:S(2)}, u32[]{:S(2)}) collective-permute-start(bf16[32,3200]{1,0:T(8,128)(2,1)} %copy-done.9), channel_id=1, source_target_pairs={{0,1},{1,0},{2,3},{3,2},{4,5},{5,4},{6,7},{7,6},{8,9},{9,8},{10,11... | collective-permute-start | bytes 614408 | tf_op jit(solution)/shard_map/ppermute | solution.py:338
  113.0 1.4 %collective-permute-start.10 = (f32[32]{0:T(128)S(1)}, f32[32]{0:T(128)S(1)}, u32[]{:S(2)}, u32[]{:S(2)}) collective-permute-start(f32[32]{0:T(128)S(1)} %reduce), channel_id=1, source_target_pairs={{0,1},{1,0},{2,3},{3,2},{4,5},{5,4},{6,7},{7,6},{8,9},{9,8},{10,11... | collective-permute-start | bytes 392 | tf_op jit(solution)/shard_map/ppermute | solution.py:338
  123.2 8.0 %collective-permute-start.21 = (bf16[800,256]{1,0:T(8,128)(2,1)S(1)}, bf16[800,256]{1,0:T(8,128)(2,1)S(1)}, u32[]{:S(2)}, u32[]{:S(2)}) collective-permute-start(bf16[800,256]{1,0:T(8,128)(2,1)S(1)} %slice.9), channel_id=1, source_target_pairs={{0,24},{1,7},{2,26},{3,1},{4,28},{5,3},{6,30},{7,5},{8,0},{9,15},{... | collective-permute-start | bytes 1228808 | tf_op jit(solution)/shard_map/ppermute | solution.py:349
  125.8 9.2 %collective-permute-start.19 = (bf16[800,256]{1,0:T(8,128)(2,1)S(1)}, bf16[800,256]{1,0:T(8,128)(2,1)S(1)}, u32[]{:S(2)}, u32[]{:S(2)}) collective-permute-start(bf16[800,256]{1,0:T(8,128)(2,1)S(1)} %slice.8), channel_id=1, source_target_pairs={{0,8},{1,3},{2,10},{3,5},{4,12},{5,7},{6,14},{7,1},{8,16},{9,11},{... | collective-permute-start | bytes 1228808 | tf_op jit(solution)/shard_map/ppermute | solution.py:349

commit v3 on v2

--- a/solution.py
+++ b/solution.py
@@ -11,6 +11,7 @@
 LMAX = 4
 MMAX = 2
 OFFSETS = (1, -1, 2, -2)
+HALO_ORDER = (1, 2, -1, -2)
 BRANCH = 0.125
 GROUP = ("zl", "y", "x")
 ATOMS = ("zh", "zl", "y", "x")
@@ -44,7 +45,7 @@
     fx_ref, hx0_ref, hx1_ref, hx2_ref, hx3_ref,
     out_ref,
     rows, nat, frames, wframes, packed, z0, z1, z2, xb0, xb1, xb2,
-    esrc_ref, edst_ref, erot_ref, ew_ref, rot_ref, mix0_ref, mix1_ref, mix2_ref, sems,
+    esrc_ref, edst_ref, erot_ref, ew_ref, rot_ref, mix0_in, mix1_in, mix2_in, mix0_ref, mix1_ref, mix2_ref, sems,
 ):
     core = core_ref[0]
     other = 1 - core
@@ -56,7 +57,7 @@
         for i, (src, dst) in enumerate(
             (
                 (erot_hbm, erot_ref), (ew_hbm, ew_ref), (rot_hbm, rot_ref), (esrc_hbm, esrc_ref),
-                (edst_hbm, edst_ref), (mix0_hbm, mix0_ref), (mix1_hbm, mix1_ref), (mix2_hbm, mix2_ref),
+                (edst_hbm, edst_ref), (mix0_hbm, mix0_in), (mix1_hbm, mix1_in), (mix2_hbm, mix2_in),
             )
         )
     ]
@@ -64,7 +65,7 @@
     for q, (own, oth) in enumerate(
         zip((fo_ref, ho0_ref, ho1_ref, ho2_ref, ho3_ref), (fx_ref, hx0_ref, hx1_ref, hx2_ref, hx3_ref))
     ):
-        at = pl.ds(q * atoms, atoms)
+        at = pl.ds(0 if q == 0 else (1 + OFFSETS.index(HALO_ORDER[q - 1])) * atoms, atoms)
         moves.append(pltpu.make_async_copy(own, rows.at[core, at, :], sems.at[8 + 2 * q]))
         moves.append(pltpu.make_async_copy(oth, rows.at[other, at, :], sems.at[9 + 2 * q]))
     for copy in copies[:5] + moves + copies[5:]:
@@ -100,6 +101,12 @@
             nat[blk, pl.ds(at, step), :] = got[:, blk * 128 : (blk + 1) * 128]
         return 0
 
+    for copy in copies[5:]:
+        copy.wait()
+    mix0_ref[...] = mix0_in[...].T
+    for i in range(2):
+        mix1_ref[i] = mix1_in[i].T
+        mix2_ref[i] = mix2_in[i].T
     for move in moves:
         move.wait()
     lax.fori_loop(0, 2 * half // step, gather, 0)
@@ -135,30 +142,27 @@
         xb1[:, nb * 128 : (nb + 1) * 128] = z1[nb].astype(BF16)
         xb2[:, nb * 128 : (nb + 1) * 128] = z2[nb].astype(BF16)
 
-    def mix_zero(t, _):
-        at = pl.multiple_of(t * 128, 128)
-        y = dot(mix0_ref[:, pl.ds(at, 128)], xb0[...], 0, 0)
-        for nb in range(4):
-            z0[nb, pl.ds(at, 128), :] = y[:, nb * 128 : (nb + 1) * 128]
+    def mix_zero(n, _):
+        y = dot(mix0_ref[...], xb0[:, pl.ds(pl.multiple_of(n * 256, 256), 256)], 1, 0)
+        z0[2 * n] = y[:, :128]
+        z0[2 * n + 1] = y[:, 128:]
         return 0
 
-    for copy in copies[5:]:
-        copy.wait()
-    lax.fori_loop(0, mix0_ref.shape[1] // 128, mix_zero, 0)
+    lax.fori_loop(0, 2, mix_zero, 0)
 
     def mix_pair(mix_ref, xb, z):
-        def tile(t, _):
-            at = pl.multiple_of(t * 128, 128)
-            a = dot(mix_ref[0, :, pl.ds(at, 128)], xb[...], 0, 0)
-            b = dot(mix_ref[1, :, pl.ds(at, 128)], xb[...], 0, 0)
-            for nb in range(4):
-                lo = slice(nb * 128, (nb + 1) * 128)
-                hi = slice(512 + nb * 128, 512 + (nb + 1) * 128)
-                z[nb, pl.ds(at, 128), :] = a[:, lo] - b[:, hi]
-                z[nb + 4, pl.ds(at, 128), :] = a[:, hi] + b[:, lo]
+        def part(n, _):
+            plus = xb[:, pl.ds(pl.multiple_of(n * 256, 256), 256)]
+            minus = xb[:, pl.ds(pl.multiple_of(n * 256 + 512, 256), 256)]
+            y = dot(mix_ref[0], plus, 1, 0) - dot(mix_ref[1], minus, 1, 0)
+            z[2 * n] = y[:, :128]
+            z[2 * n + 1] = y[:, 128:]
+            y = dot(mix_ref[0], minus, 1, 0) + dot(mix_ref[1], plus, 1, 0)
+            z[2 * n + 4] = y[:, :128]
+            z[2 * n + 5] = y[:, 128:]
             return 0
 
-        lax.fori_loop(0, mix_ref.shape[2] // 128, tile, 0)
+        lax.fori_loop(0, 2, part, 0)
 
     mix_pair(mix1_ref, xb1, z1)
     mix_pair(mix2_ref, xb2, z2)
@@ -227,7 +231,7 @@
         ]
         + [pltpu.VMEM((1, edges), jnp.int32)] * 3
         + [pltpu.VMEM((1, edges), F32), pltpu.VMEM(rot_table.shape, F32)]
-        + [pltpu.VMEM(mix.shape, BF16) for mix in mixes]
+        + [pltpu.VMEM(mix.shape, BF16) for mix in mixes + mixes]
         + [pltpu.SemaphoreType.DMA((18,))],
         compiler_params=pltpu.CompilerParams(vmem_limit_bytes=54 * 1024 * 1024),
         cost_estimate=pl.CostEstimate(flops=5_000_000_000, bytes_accessed=6_000_000, transcendentals=0),
@@ -251,9 +255,11 @@
     blocks = dot(upd[...], weight_ref[...], 1, 0)
     width = blocks.shape[1]
     species = species_ref[...]
-    norb = jnp.zeros_like(species)
+    lanes = jnp.zeros_like(species)
     for s in range(orbitals_ref.shape[0]):
-        norb = jnp.where(species == s, orbitals_ref[s], norb)
+        lanes = jnp.where(species == s, orbitals_ref[s], lanes)
+    square = [lax.broadcasted_iota(jnp.int32, (atoms, atoms), d) for d in (0, 1)]
+    norb = jnp.sum(jnp.where(square[0] == square[1], lanes, 0), axis=1, keepdims=True)
     cols = core * width + lax.broadcasted_iota(jnp.int32, (atoms, width), 1)
     valid = ((cols // (2 * ORB)) < norb) & (((cols // 2) % ORB) < norb)
     error = jnp.where(valid, blocks - target_ref[...], 0.0)
@@ -285,11 +291,14 @@
         ),
         in_specs=[smem, smem] + [vmem] * 7,
         out_specs=(vmem,) * 4,
-        scratch_shapes=[pltpu.VMEM((2, atoms, half), BF16), pltpu.VMEM((atoms, 2 * half), BF16)],
+        scratch_shapes=[
+            pltpu.VMEM((2, atoms, half), BF16),
+            pltpu.VMEM((atoms, 2 * half), BF16),
+        ],
         compiler_params=pltpu.CompilerParams(vmem_limit_bytes=32 * 1024 * 1024),
         cost_estimate=pl.CostEstimate(flops=300_000_000, bytes_accessed=6_000_000, transcendentals=0),
         name="head",
-    )(core, orbitals, species.reshape(-1, 1), f_own, f_oth, mine, recv, weight, target)
+    )(core, orbitals, species.reshape(1, -1), f_own, f_oth, mine, recv, weight, target)
 
 
 def leaving_kernel(sends_ref, feats_ref, *outs):
@@ -349,16 +358,14 @@
     return lax.ppermute(x, ("y", "x", "chan"), pairs)
 
 
-def assemble_kernel(place_ref, own, behind, far_lo, far_hi, ahead, out_ref, sems):
+def assemble_kernel(place_ref, *refs):
+    halves, out_ref, sems = refs[:8], refs[8], refs[9]
     y, x, core = place_ref[0], place_ref[1], place_ref[2]
     rows = out_ref.shape[0] // 16
     copies = []
     for late in range(4):
         for early in range(4):
-            if late == 2:
-                ref, at = (far_lo, early) if early < 2 else (far_hi, early - 2)
-            else:
-                ref, at = {0: own, 1: behind, 3: ahead}[late], early
+            ref, at = halves[2 * late + early // 2], early % 2
             dy = late + core * (early - late)
             dx = early + core * (late - early)
             spot = lax.rem(y + 4 - dy, 4) * 4 + lax.rem(x + 4 - dx, 4)
@@ -376,7 +383,7 @@
 
 
 def assemble(place, blocks):
-    rows, width = blocks[0].shape
+    rows, width = 2 * blocks[0].shape[0], blocks[0].shape[1]
     return pl.pallas_call(
         assemble_kernel,
         out_shape=jax.ShapeDtypeStruct((4 * rows, width), BF16),
@@ -395,7 +402,8 @@
 ):
     core = lax.axis_index("chan").astype(jnp.int32).reshape(1)
     f_oth = shift(features, "chan", 1)
-    halo = [shift(rows, ATOMS, off) for rows, off in zip(leaving_rows(send_rows, features), OFFSETS)]
+    leaving = leaving_rows(send_rows, features)
+    halo = [shift(leaving[OFFSETS.index(off)], ATOMS, off) for off in HALO_ORDER]
     halo_oth = [shift(h, "chan", 1) for h in halo]
     mine = messages(
         core, edge_source, edge_dest, edge_rot, edge_weight, rot_table.T,
@@ -407,25 +415,33 @@
         core, species_orbitals, atom_species, features, f_oth, mine, recv, head_weight, target_blocks, parts
     )
     got = lax.all_to_all(load, GROUP, split_axis=0, concat_axis=0, tiled=True)
-    atom_loss = loss[:, 0] + shift(loss[:, 0], "chan", 1)
-    grad_features = keep + shift(send, "chan", 1).astype(F32)
     share = 2 * features.shape[1] // parts
     part = partial_grad(got.reshape(-1, got.shape[2]), share)
-    near = shift(part, "zh", 1).astype(F32) + shift(part, "zh", -1).astype(F32)
-    total = (part.astype(F32) + shift(part, "zh", 2).astype(F32) + near).astype(BF16)
+    part, loss, send = lax.optimization_barrier((part, loss, send))
+    sums = [shift(part, "zh", by) for by in (1, -1, 2)]
+    loss_oth, feat_oth = shift(loss[:, 0], "chan", 1), shift(send, "chan", 1)
+    sums, loss_oth, feat_oth = lax.optimization_barrier((sums, loss_oth, feat_oth))
+    near = sums[0].astype(F32) + sums[1].astype(F32)
+    total = (part.astype(F32) + sums[2].astype(F32) + near).astype(BF16)
+    atom_loss = loss[:, 0] + loss_oth
+    grad_features = keep + feat_oth.astype(F32)
     twin = shift(total, "zl", 1)
-    low = lax.axis_index("zl") == 0
-    pair = jnp.concatenate([jnp.where(low, total, twin), jnp.where(low, twin, total)], axis=0)
-
-    row = jnp.concatenate(
-        [pair, plane_shift(pair, True, 1), plane_shift(pair, True, 2), plane_shift(pair, True, -1)], axis=0
+    first = lax.axis_index("zl") == 0
+    pair = jnp.concatenate([jnp.where(first, total, twin), jnp.where(first, twin, total)], axis=0)
+
+    early = {by: plane_shift(pair, True, by) for by in (1, -1, 2)}
+    low = jnp.concatenate([pair, early[1]], axis=0)
+    low_behind = plane_shift(low, False, 1)
+    low_ahead = plane_shift(low, False, -1)
+    high = jnp.concatenate([early[2], early[-1]], axis=0)
+    high_ahead = plane_shift(high, False, -1)
+    high_behind = plane_shift(high, False, 1)
+    low_far = plane_shift(low_behind, False, 1)
+    high_far = plane_shift(high_ahead, False, -1)
+    place = jnp.stack([lax.axis_index(name) for name in ("y", "x", "chan")]).astype(jnp.int32)
+    grad_head = assemble(
+        place, [low, high, low_behind, high_behind, low_far, high_far, low_ahead, high_ahead]
     )
-    half = row.shape[0] // 2
-    behind = plane_shift(row, False, 1)
-    ahead = plane_shift(row, False, -1)
-    far = [plane_shift(behind[:half], False, 1), plane_shift(ahead[half:], False, -1)]
-    place = jnp.stack([lax.axis_index(name) for name in ("y", "x", "chan")]).astype(jnp.int32)
-    grad_head = assemble(place, [row, behind] + far + [ahead])
     return (atom_loss, grad_head, grad_features)
 
 

time: 138 us -> 130 us (0.942)
  waiting for transfers between devices: 45.4 us -> 36.6 us
  starting transfers between devices: 33.8 us -> 36.5 us
  blocking collectives: 26.3 us -> 24.3 us
    ppermute x7 -> x9, waiting for transfers between devices: 24.4 us -> 10.9 us  [plane_shift(): return lax.ppermute(x, ('y', 'x', 'chan'), pairs)]
    ppermute x7 -> x9, starting transfers between devices: 9.99 us -> 16.2 us  [plane_shift(): return lax.ppermute(x, ('y', 'x', 'chan'), pairs)]
    ppermute x16, waiting for transfers between devices: 21 us -> 25.7 us  [shift(): return lax.ppermute(x, axis, [(i, (i + by) % count) for i in range(count)])]
    ppermute x16, starting transfers between devices: 23.8 us -> 20.4 us  [shift(): return lax.ppermute(x, axis, [(i, (i + by) % count) for i in range(count)])]
    all_to_all x1, blocking collectives: 26.3 us -> 24.3 us  [body(): got = lax.all_to_all(load, GROUP, split_axis=0, concat_axis=0, tiled=True)]
    unnamed x40 -> x33, local copies, waits for them, and re-layouts: 3.32 us -> 3.29 us
  transfers between devices with their start and end apart: 23 -> 25, of which waited for: 14 -> 15; matrix products, arithmetic and copies ran while one was open for 1% -> 1% of each run, Pallas kernels for 0% -> 0%
where the time goes in v3:
time: 130 us; the launch traced here: 129 us
  waiting for transfers between devices  36.6 us (28%)
  starting transfers between devices  36.5 us (28%)
  Pallas kernels  25.9 us (20%)
  blocking collectives  24.3 us (19%)
  local copies, waits for them, and re-layouts  3.31 us (3%)
  other arithmetic  1.6 us (1%)
    ppermute x16, waiting for transfers between devices, shift(): return lax.ppermute(x, axis, [(i, (i + by) % count) for i in range(count)])  25.7 us
    all_to_all x1, blocking collectives, body(): got = lax.all_to_all(load, GROUP, split_axis=0, concat_axis=0, tiled=True)  24.3 us
    ppermute x16, starting transfers between devices, shift(): return lax.ppermute(x, axis, [(i, (i + by) % count) for i in range(count)])  20.4 us
    pallas_call x1, Pallas kernels, messages(): pl.pallas_call(message_kernel, out_shape=jax.ShapeDtypeStruct((atoms, 2 *...  18.5 us
    ppermute x9, starting transfers between devices, plane_shift(): return lax.ppermute(x, ('y', 'x', 'chan'), pairs)  16.2 us
    ppermute x9, waiting for transfers between devices, plane_shift(): return lax.ppermute(x, ('y', 'x', 'chan'), pairs)  10.9 us
    pallas_call x1, Pallas kernels, head(): pl.pallas_call(head_kernel, out_shape=(jax.ShapeDtypeStruct((parts, atoms...  3.3 us
    unnamed x33, local copies, waits for them, and re-layouts  3.29 us
  transfers between devices with their start and end apart: 25, of which 15 were waited for; matrix products, arithmetic and copies ran while one was open for 1% of the time, Pallas kernels for 0%

profile of v3, /device:TPU:32, one launch (start us, length us, event | category | flops | bytes accessed | tf_op | source)
XLA Modules:
  0.0 129.2 jit_solution(1707401296260229529)
XLA Ops:
  0.6 0.7 copy-done.5
  1.3 1.4 %leaving.1 = (bf16[32,3200]{1,0:T(8,128)(2,1)S(1)}, bf16[32,3200]{1,0:T(8,128)(2,1)S(1)}, bf16[32,3200]{1,0:T(8,128)(2,1)S(1)}, bf16[32,3200]{1,0:T(8,128)(2,1)S(1)}) custom-call(s32[4,32]{1,0:T(4,128)S(1)} %copy-done.5, bf16[32,3200]{1,0:T(8,128)(2,1)} %fo_ref.3), custom_call_target="tpu_custom_call" | custom-call | tf_op jit(solution)/shard_map/leaving/pallas_call | solution.py:317
  2.7 1.6 %collective-permute-start.1 = (bf16[32,3200]{1,0:T(8,128)(2,1)S(1)}, bf16[32,3200]{1,0:T(8,128)(2,1)S(1)}, u32[]{:S(2)}, u32[]{:S(2)}) collective-permute-start(bf16[32,3200]{1,0:T(8,128)(2,1)S(1)} %get-tuple-element.19), channel_id=1, source_target_pairs={{0,2},{2,4},{4,6},{6,8},{8,10},{10,12},{12,14},{14,16},{16,18},{18... | collective-permute-start | bytes 614408 | tf_op jit(solution)/shard_map/ppermute | solution.py:347
  4.3 2.7 %collective-permute-start.2 = (bf16[32,3200]{1,0:T(8,128)(2,1)S(1)}, bf16[32,3200]{1,0:T(8,128)(2,1)S(1)}, u32[]{:S(2)}, u32[]{:S(2)}) collective-permute-start(bf16[32,3200]{1,0:T(8,128)(2,1)S(1)} %get-tuple-element.20), channel_id=1, source_target_pairs={{0,4},{2,6},{4,8},{6,10},{8,12},{10,14},{12,16},{14,18},{16,20},{1... | collective-permute-start | bytes 614408 | tf_op jit(solution)/shard_map/ppermute | solution.py:347
  7.0 4.4 %collective-permute-start.3 = (bf16[32,3200]{1,0:T(8,128)(2,1)S(1)}, bf16[32,3200]{1,0:T(8,128)(2,1)S(1)}, u32[]{:S(2)}, u32[]{:S(2)}) collective-permute-start(bf16[32,3200]{1,0:T(8,128)(2,1)S(1)} %get-tuple-element.21), channel_id=1, source_target_pairs={{0,254},{2,0},{4,2},{6,4},{8,6},{10,8},{12,10},{14,12},{16,14},{18... | collective-permute-start | bytes 614408 | tf_op jit(solution)/shard_map/ppermute | solution.py:347
  11.5 0.5 collective-permute-start.4
  12.0 0.0 collective-permute-start
  12.0 5.2 %collective-permute-done.1.ho0_ref = bf16[32,3200]{1,0:T(8,128)(2,1)S(1)} collective-permute-done((bf16[32,3200]{1,0:T(8,128)(2,1)S(1)}, bf16[32,3200]{1,0:T(8,128)(2,1)S(1)}, u32[]{:S(2)}, u32[]{:S(2)}) %collective-permute-start.1) | collective-permute-done | bytes 204832 | tf_op jit(solution)/shard_map/ppermute | solution.py:347
  17.1 0.0 collective-permute-start.5
  17.2 1.1 collective-permute-done.2.ho1_ref
  18.2 0.0 collective-permute-start.6
  18.2 6.0 %collective-permute-done.3.ho2_ref = bf16[32,3200]{1,0:T(8,128)(2,1)S(1)} collective-permute-done((bf16[32,3200]{1,0:T(8,128)(2,1)S(1)}, bf16[32,3200]{1,0:T(8,128)(2,1)S(1)}, u32[]{:S(2)}, u32[]{:S(2)}) %collective-permute-start.3) | collective-permute-done | bytes 204832 | tf_op jit(solution)/shard_map/ppermute | solution.py:347
  24.2 0.0 collective-permute-start.7
  24.2 0.0 collective-permute-done.4.ho3_ref
  24.2 0.5 collective-permute-start.8
  24.7 0.0 collective-permute-done.fx_ref
  24.7 0.0 collective-permute-done.5.hx0_ref
  24.7 0.0 collective-permute-done.6.hx1_ref
  24.7 0.9 collective-permute-done.7.hx2_ref
  25.6 0.3 collective-permute-done.8.hx3_ref
  26.0 0.3 copy-done.14
  26.3 0.3 copy-done.15
  26.6 18.5 %messages.1.mine_ref = bf16[32,6400]{1,0:T(8,128)(2,1)} custom-call(s32[1]{0:T(128)} %bitcast.core_ref, s32[1,256]{1,0:T(1,128)} %bitcast.13, s32[1,256]{1,0:T(1,128)} %bitcast.14, s32[1,256]{1,0:T(1,128)} %bitcast.15, f32[1,256]{1,0:T(1,128)} %bitcast.16, f32[165,512]{1,0:T(8,128)} %bitcast.12, bf16[640,640]{1,0:T(8,128)(2,1)} %mix0_hbm.1, ...), custom_call_target="tpu_custom_call" | custom-call | flops 5000000000 | bytes 6000000 | tf_op jit(solution)/shard_map/messages/pallas_call | solution.py:214
  45.1 0.3 collective-permute-start.9
  45.4 1.7 %collective-permute-done.9.recv_ref = bf16[32,6400]{1,0:T(8,128)(2,1)S(1)} collective-permute-done((bf16[32,6400]{1,0:T(8,128)(2,1)}, bf16[32,6400]{1,0:T(8,128)(2,1)S(1)}, u32[]{:S(2)}, u32[]{:S(2)}) %collective-permute-start.9) | collective-permute-done | bytes 409632 | tf_op jit(solution)/shard_map/ppermute | solution.py:347
  47.2 1.0 copy-done.1
  48.2 0.9 copy-done.3
  49.1 3.3 %head.1 = (bf16[32,32,512]{2,1,0:T(8,128)(2,1)S(1)}, f32[32,1]{1,0:T(8,128)S(1)}, f32[32,3200]{1,0:T(8,128)S(1)}, bf16[32,3200]{1,0:T(8,128)(2,1)S(1)}) custom-call(s32[1]{0:T(128)} %bitcast.core_ref, s32[4]{0:T(128)S(1)} %copy-done.6, s32[1,32]{1,0:T(1,128)S(1)} %bitcast.11, bf16[32,3200]{1,0:T(8,128)(2,1)} %fo_ref.3, bf16[32,3200]{1,0:T(8,128)(2,1)S(1)} %copy-done.3, ...), custom_call_target="tpu_custom_call" | custom-call | flops 300000000 | bytes 6000000 | tf_op jit(solution)/shard_map/head/pallas_call | solution.py:284
  52.4 24.3 %all_to_all.5 = bf16[32,32,512]{2,1,0:T(8,128)(2,1)S(1)} all-to-all(bf16[32,32,512]{2,1,0:T(8,128)(2,1)S(1)} %get-tuple-element.23), channel_id=1, replica_groups=mesh['zh'=4,'zl'=2,'y'=4,'x'=4,'chan'=2] {'zl','y','x'}, dimensions={0} | all-to-all | bytes 2097152 | tf_op jit(solution)/shard_map/all_to_all | solution.py:417
  76.7 0.3 partial_grad.1
  77.0 0.3 collective-permute-start.14
  77.3 5.5 %collective-permute-start.12 = (bf16[200,256]{1,0:T(8,128)(2,1)S(1)}, bf16[200,256]{1,0:T(8,128)(2,1)S(1)}, u32[]{:S(2)}, u32[]{:S(2)}) collective-permute-start(bf16[200,256]{1,0:T(8,128)(2,1)S(1)} %partial_grad.1), channel_id=1, source_target_pairs={{0,128},{64,192},{128,0},{192,64},{1,129},{65,193},{129,1},{193,65... | collective-permute-start | bytes 307208 | tf_op jit(solution)/shard_map/ppermute | solution.py:347
  82.8 1.6 %collective-permute-start.11 = (bf16[200,256]{1,0:T(8,128)(2,1)S(1)}, bf16[200,256]{1,0:T(8,128)(2,1)S(1)}, u32[]{:S(2)}, u32[]{:S(2)}) collective-permute-start(bf16[200,256]{1,0:T(8,128)(2,1)S(1)} %partial_grad.1), channel_id=1, source_target_pairs={{0,192},{64,0},{128,64},{192,128},{1,193},{65,1},{129,65},{193,129... | collective-permute-start | bytes 307208 | tf_op jit(solution)/shard_map/ppermute | solution.py:347
  84.4 1.3 %collective-permute-start.10 = (bf16[200,256]{1,0:T(8,128)(2,1)S(1)}, bf16[200,256]{1,0:T(8,128)(2,1)S(1)}, u32[]{:S(2)}, u32[]{:S(2)}) collective-permute-start(bf16[200,256]{1,0:T(8,128)(2,1)S(1)} %partial_grad.1), channel_id=1, source_target_pairs={{0,64},{64,128},{128,192},{192,0},{1,65},{65,129},{129,193},{193,1... | collective-permute-start | bytes 307208 | tf_op jit(solution)/shard_map/ppermute | solution.py:347
  85.7 0.1 reduce
  85.8 0.1 collective-permute-start.13
  85.9 1.1 collective-permute-done.13
  87.0 2.8 %collective-permute-done.12 = bf16[200,256]{1,0:T(8,128)(2,1)S(1)} collective-permute-done((bf16[200,256]{1,0:T(8,128)(2,1)S(1)}, bf16[200,256]{1,0:T(8,128)(2,1)S(1)}, u32[]{:S(2)}, u32[]{:S(2)}) %collective-permute-start.12) | collective-permute-done | bytes 102432 | tf_op jit(solution)/shard_map/ppermute | solution.py:347
  89.8 1.5 %collective-permute-done.11 = bf16[200,256]{1,0:T(8,128)(2,1)S(1)} collective-permute-done((bf16[200,256]{1,0:T(8,128)(2,1)S(1)}, bf16[200,256]{1,0:T(8,128)(2,1)S(1)}, u32[]{:S(2)}, u32[]{:S(2)}) %collective-permute-start.11) | collective-permute-done | bytes 102432 | tf_op jit(solution)/shard_map/ppermute | solution.py:347
  91.3 1.9 %collective-permute-done.10 = bf16[200,256]{1,0:T(8,128)(2,1)S(1)} collective-permute-done((bf16[200,256]{1,0:T(8,128)(2,1)S(1)}, bf16[200,256]{1,0:T(8,128)(2,1)S(1)}, u32[]{:S(2)}, u32[]{:S(2)}) %collective-permute-start.10) | collective-permute-done | bytes 102432 | tf_op jit(solution)/shard_map/ppermute | solution.py:347
  93.2 0.0 collective-permute-done.14
  93.2 0.1 add_convert_fusion
  93.2 1.5 %collective-permute-start.15 = (bf16[200,256]{1,0:T(8,128)(2,1)S(1)}, bf16[200,256]{1,0:T(8,128)(2,1)S(1)}, u32[]{:S(2)}, u32[]{:S(2)}) collective-permute-start(bf16[200,256]{1,0:T(8,128)(2,1)S(1)} %add_convert_fusion), channel_id=1, source_target_pairs={{0,32},{32,0},{1,33},{33,1},{2,34},{34,2},{3,35},{35,3},{4,36},{36... | collective-permute-start | bytes 307208 | tf_op jit(solution)/shard_map/ppermute | solution.py:347
  94.7 3.4 %collective-permute-done.15 = bf16[200,256]{1,0:T(8,128)(2,1)S(1)} collective-permute-done((bf16[200,256]{1,0:T(8,128)(2,1)S(1)}, bf16[200,256]{1,0:T(8,128)(2,1)S(1)}, u32[]{:S(2)}, u32[]{:S(2)}) %collective-permute-start.15) | collective-permute-done | bytes 102432 | tf_op jit(solution)/shard_map/ppermute | solution.py:347
  98.2 1.0 collective-permute-start.16
  99.1 2.5 %collective-permute-start.17 = (bf16[400,256]{1,0:T(8,128)(2,1)S(1)}, bf16[400,256]{1,0:T(8,128)(2,1)S(1)}, u32[]{:S(2)}, u32[]{:S(2)}) collective-permute-start(bf16[400,256]{1,0:T(8,128)(2,1)S(1)} %pad_maximum_fusion.1), channel_id=1, source_target_pairs={{0,4},{1,17},{2,6},{3,19},{4,0},{5,21},{6,2},{7,23},{8,12},{9,25},... | collective-permute-start | bytes 614408 | tf_op jit(solution)/shard_map/ppermute | solution.py:358
  101.7 1.1 collective-permute-start.18
  102.8 2.4 %collective-permute-done.16 = bf16[400,256]{1,0:T(8,128)(2,1)S(1)} collective-permute-done((bf16[400,256]{1,0:T(8,128)(2,1)S(1)}, bf16[400,256]{1,0:T(8,128)(2,1)S(1)}, u32[]{:S(2)}, u32[]{:S(2)}) %collective-permute-start.16) | collective-permute-done | bytes 204832 | tf_op jit(solution)/shard_map/ppermute | solution.py:358
  105.2 3.0 %collective-permute-start.19 = (bf16[800,256]{1,0:T(8,128)(2,1)S(1)}, bf16[800,256]{1,0:T(8,128)(2,1)S(1)}, u32[]{:S(2)}, u32[]{:S(2)}) collective-permute-start(bf16[800,256]{1,0:T(8,128)(2,1)S(1)} %pad_maximum_fusion.refs_0_), channel_id=1, source_target_pairs={{0,8},{1,3},{2,10},{3,5},{4,12},{5,7},{6,14},{7,1},{8,16},{9,11},{... | collective-permute-start | bytes 1228808 | tf_op jit(solution)/shard_map/ppermute | solution.py:358
  108.3 0.0 collective-permute-done.17
  108.3 0.0 collective-permute-done.18
  108.3 2.9 %collective-permute-start.22 = (bf16[800,256]{1,0:T(8,128)(2,1)S(1)}, bf16[800,256]{1,0:T(8,128)(2,1)S(1)}, u32[]{:S(2)}, u32[]{:S(2)}) collective-permute-start(bf16[800,256]{1,0:T(8,128)(2,1)S(1)} %constant_dynamic-update-slice_fusion.refs_1_), channel_id=1, source_target_pairs={{0,24},{1,7},{2,26},{3,1},{4,28},{5,3},{6,30},{7,5},{8,0},{9,15},{... | collective-permute-start | bytes 1228808 | tf_op jit(solution)/shard_map/ppermute | solution.py:358
  111.2 0.1 pad_add_fusion.place_ref
  111.3 1.8 %collective-permute-start.24 = (bf16[800,256]{1,0:T(8,128)(2,1)S(1)}, bf16[800,256]{1,0:T(8,128)(2,1)S(1)}, u32[]{:S(2)}, u32[]{:S(2)}) collective-permute-start(bf16[800,256]{1,0:T(8,128)(2,1)S(1)} %pad_maximum_fusion.refs_0_), channel_id=1, source_target_pairs={{0,24},{1,7},{2,26},{3,1},{4,28},{5,3},{6,30},{7,5},{8,0},{9,15},{... | collective-permute-start | bytes 1228808 | tf_op jit(solution)/shard_map/ppermute | solution.py:358
  113.1 0.2 collective-permute-start.20
  113.3 3.5 %collective-permute-done.19.refs_2_ = bf16[800,256]{1,0:T(8,128)(2,1)S(1)} collective-permute-done((bf16[800,256]{1,0:T(8,128)(2,1)S(1)}, bf16[800,256]{1,0:T(8,128)(2,1)S(1)}, u32[]{:S(2)}, u32[]{:S(2)}) %collective-permute-start.19) | collective-permute-done | bytes 409632 | tf_op jit(solution)/shard_map/ppermute | solution.py:358
  116.8 0.0 collective-permute-start.21
  116.8 3.6 %collective-permute-start.23 = (bf16[800,256]{1,0:T(8,128)(2,1)S(1)}, bf16[800,256]{1,0:T(8,128)(2,1)S(1)}, u32[]{:S(2)}, u32[]{:S(2)}) collective-permute-start(bf16[800,256]{1,0:T(8,128)(2,1)S(1)} %collective-permute-done.22.refs_7_), channel_id=1, source_target_pairs={{0,24},{1,7},{2,26},{3,1},{4,28},{5,3},{6,30},{7,5},{8,0},{9,15},{... | collective-permute-start | bytes 1228808 | tf_op jit(solution)/shard_map/ppermute | solution.py:358
  120.4 0.8 convert_add_fusion
  121.2 0.5 add.15
  121.7 0.0 collective-permute-done.24.refs_6_
  121.7 0.6 collective-permute-done.20.refs_3_
  122.3 4.4 %collective-permute-done.21.refs_4_ = bf16[800,256]{1,0:T(8,128)(2,1)S(1)} collective-permute-done((bf16[800,256]{1,0:T(8,128)(2,1)S(1)}, bf16[800,256]{1,0:T(8,128)(2,1)S(1)}, u32[]{:S(2)}, u32[]{:S(2)}) %collective-permute-start.21) | collective-permute-done | bytes 409632 | tf_op jit(solution)/shard_map/ppermute | solution.py:358
  126.7 2.4 %assemble.1 = bf16[6400,256]{1,0:T(8,128)(2,1)} custom-call(s32[3]{0:T(128)S(1)} %pad_add_fusion.place_ref, bf16[800,256]{1,0:T(8,128)(2,1)S(1)} %pad_maximum_fusion.refs_0_, bf16[800,256]{1,0:T(8,128)(2,1)S(1)} %constant_dynamic-update-slice_fusion.refs_1_, bf16[800,256]{1,0:T(8,128)(2,1)S(1)} %collective-permute-done.19.refs_2_, ...), custom_call_target="tpu_custom_call" | custom-call | tf_op jit(solution)/shard_map/assemble/pallas_call | solution.py:387
  (34 shorter events, 0.1 us)
Async XLA Ops:
  0.6 0.7 copy-start.5
  2.7 14.4 %collective-permute-start.1 = (bf16[32,3200]{1,0:T(8,128)(2,1)S(1)}, bf16[32,3200]{1,0:T(8,128)(2,1)S(1)}, u32[]{:S(2)}, u32[]{:S(2)}) collective-permute-start(bf16[32,3200]{1,0:T(8,128)(2,1)S(1)} %get-tuple-element.19), channel_id=1, source_target_pairs={{0,2},{2,4},{4,6},{6,8},{8,10},{10,12},{12,14},{14,16},{16,18},{18... | collective-permute-start | bytes 614408 | tf_op jit(solution)/shard_map/ppermute | solution.py:347
  4.3 13.9 %collective-permute-start.2 = (bf16[32,3200]{1,0:T(8,128)(2,1)S(1)}, bf16[32,3200]{1,0:T(8,128)(2,1)S(1)}, u32[]{:S(2)}, u32[]{:S(2)}) collective-permute-start(bf16[32,3200]{1,0:T(8,128)(2,1)S(1)} %get-tuple-element.20), channel_id=1, source_target_pairs={{0,4},{2,6},{4,8},{6,10},{8,12},{10,14},{12,16},{14,18},{16,20},{1... | collective-permute-start | bytes 614408 | tf_op jit(solution)/shard_map/ppermute | solution.py:347
  7.0 17.2 %collective-permute-start.3 = (bf16[32,3200]{1,0:T(8,128)(2,1)S(1)}, bf16[32,3200]{1,0:T(8,128)(2,1)S(1)}, u32[]{:S(2)}, u32[]{:S(2)}) collective-permute-start(bf16[32,3200]{1,0:T(8,128)(2,1)S(1)} %get-tuple-element.21), channel_id=1, source_target_pairs={{0,254},{2,0},{4,2},{6,4},{8,6},{10,8},{12,10},{14,12},{16,14},{18... | collective-permute-start | bytes 614408 | tf_op jit(solution)/shard_map/ppermute | solution.py:347
  11.5 12.7 %collective-permute-start.4 = (bf16[32,3200]{1,0:T(8,128)(2,1)S(1)}, bf16[32,3200]{1,0:T(8,128)(2,1)S(1)}, u32[]{:S(2)}, u32[]{:S(2)}) collective-permute-start(bf16[32,3200]{1,0:T(8,128)(2,1)S(1)} %get-tuple-element.22), channel_id=1, source_target_pairs={{0,252},{2,254},{4,0},{6,2},{8,4},{10,6},{12,8},{14,10},{16,12},{1... | collective-permute-start | bytes 614408 | tf_op jit(solution)/shard_map/ppermute | solution.py:347
  12.0 12.7 %collective-permute-start = (bf16[32,3200]{1,0:T(8,128)(2,1)}, bf16[32,3200]{1,0:T(8,128)(2,1)S(1)}, u32[]{:S(2)}, u32[]{:S(2)}) collective-permute-start(bf16[32,3200]{1,0:T(8,128)(2,1)} %fo_ref.3), channel_id=1, source_target_pairs={{0,1},{1,0},{2,3},{3,2},{4,5},{5,4},{6,7},{7,6},{8,9},{9,8},{10,11... | collective-permute-start | bytes 614408 | tf_op jit(solution)/shard_map/ppermute | solution.py:347
  17.1 8.8 %copy-start.8 = (bf16[32,3200]{1,0:T(8,128)(2,1)}, bf16[32,3200]{1,0:T(8,128)(2,1)S(1)}, u32[]{:S(2)}) copy-start(bf16[32,3200]{1,0:T(8,128)(2,1)S(1)} %collective-permute-done.1.ho0_ref) | copy-start | bytes 614404
  17.1 7.6 %collective-permute-start.5 = (bf16[32,3200]{1,0:T(8,128)(2,1)S(1)}, bf16[32,3200]{1,0:T(8,128)(2,1)S(1)}, u32[]{:S(2)}, u32[]{:S(2)}) collective-permute-start(bf16[32,3200]{1,0:T(8,128)(2,1)S(1)} %collective-permute-done.1.ho0_ref), channel_id=1, source_target_pairs={{0,1},{1,0},{2,3},{3,2},{4,5},{5,4},{6,7},{7,6},{8,9},{9,8},{10,11... | collective-permute-start | bytes 614408 | tf_op jit(solution)/shard_map/ppermute | solution.py:347
  18.2 7.7 %copy-start.9 = (bf16[32,3200]{1,0:T(8,128)(2,1)}, bf16[32,3200]{1,0:T(8,128)(2,1)S(1)}, u32[]{:S(2)}) copy-start(bf16[32,3200]{1,0:T(8,128)(2,1)S(1)} %collective-permute-done.2.ho1_ref) | copy-start | bytes 614404
  18.2 6.5 %collective-permute-start.6 = (bf16[32,3200]{1,0:T(8,128)(2,1)S(1)}, bf16[32,3200]{1,0:T(8,128)(2,1)S(1)}, u32[]{:S(2)}, u32[]{:S(2)}) collective-permute-start(bf16[32,3200]{1,0:T(8,128)(2,1)S(1)} %collective-permute-done.2.ho1_ref), channel_id=1, source_target_pairs={{0,1},{1,0},{2,3},{3,2},{4,5},{5,4},{6,7},{7,6},{8,9},{9,8},{10,11... | collective-permute-start | bytes 614408 | tf_op jit(solution)/shard_map/ppermute | solution.py:347
  24.2 1.8 %copy-start.10 = (bf16[32,3200]{1,0:T(8,128)(2,1)}, bf16[32,3200]{1,0:T(8,128)(2,1)S(1)}, u32[]{:S(2)}) copy-start(bf16[32,3200]{1,0:T(8,128)(2,1)S(1)} %collective-permute-done.3.ho2_ref) | copy-start | bytes 614404
  24.2 1.5 %collective-permute-start.7 = (bf16[32,3200]{1,0:T(8,128)(2,1)S(1)}, bf16[32,3200]{1,0:T(8,128)(2,1)S(1)}, u32[]{:S(2)}, u32[]{:S(2)}) collective-permute-start(bf16[32,3200]{1,0:T(8,128)(2,1)S(1)} %collective-permute-done.3.ho2_ref), channel_id=1, source_target_pairs={{0,1},{1,0},{2,3},{3,2},{4,5},{5,4},{6,7},{7,6},{8,9},{9,8},{10,11... | collective-permute-start | bytes 614408 | tf_op jit(solution)/shard_map/ppermute | solution.py:347
  24.2 1.8 %copy-start.11 = (bf16[32,3200]{1,0:T(8,128)(2,1)}, bf16[32,3200]{1,0:T(8,128)(2,1)S(1)}, u32[]{:S(2)}) copy-start(bf16[32,3200]{1,0:T(8,128)(2,1)S(1)} %collective-permute-done.4.ho3_ref) | copy-start | bytes 614404
  24.2 1.7 %collective-permute-start.8 = (bf16[32,3200]{1,0:T(8,128)(2,1)S(1)}, bf16[32,3200]{1,0:T(8,128)(2,1)S(1)}, u32[]{:S(2)}, u32[]{:S(2)}) collective-permute-start(bf16[32,3200]{1,0:T(8,128)(2,1)S(1)} %collective-permute-done.4.ho3_ref), channel_id=1, source_target_pairs={{0,1},{1,0},{2,3},{3,2},{4,5},{5,4},{6,7},{7,6},{8,9},{9,8},{10,11... | collective-permute-start | bytes 614408 | tf_op jit(solution)/shard_map/ppermute | solution.py:347
  24.7 1.3 copy-start.2
  24.7 1.3 copy-start.12
  24.7 1.2 copy-start.13
  25.6 0.7 copy-start.14
  25.9 0.7 copy-start.15
  26.6 20.5 %copy-start = (bf16[6400,256]{1,0:T(8,128)(2,1)S(1)}, bf16[6400,256]{1,0:T(8,128)(2,1)}, u32[]{:S(2)}) copy-start(bf16[6400,256]{1,0:T(8,128)(2,1)} %weight_ref.1) | copy-start | bytes 9830404
  26.6 20.5 %copy-start.4 = (f32[32,256]{1,0:T(8,128)S(1)}, f32[32,256]{1,0:T(8,128)}, u32[]{:S(2)}) copy-start(f32[32,256]{1,0:T(8,128)} %target_ref.1) | copy-start | bytes 98308
  26.6 20.5 %copy-start.6 = (s32[4]{0:T(128)S(1)}, s32[4]{0:T(128)}, u32[]{:S(2)}) copy-start(s32[4]{0:T(128)} %orbitals_ref.1) | copy-start | bytes 52
  26.6 20.5 %copy-start.7 = (s32[32]{0:T(128)S(1)}, s32[32]{0:T(128)}, u32[]{:S(2)}) copy-start(s32[32]{0:T(128)} %param.24) | copy-start | bytes 388
  45.1 2.0 %collective-permute-start.9 = (bf16[32,6400]{1,0:T(8,128)(2,1)}, bf16[32,6400]{1,0:T(8,128)(2,1)S(1)}, u32[]{:S(2)}, u32[]{:S(2)}) collective-permute-start(bf16[32,6400]{1,0:T(8,128)(2,1)} %messages.1.mine_ref), channel_id=1, source_target_pairs={{0,1},{1,0},{2,3},{3,2},{4,5},{5,4},{6,7},{7,6},{8,9},{9,8},{10,11... | collective-permute-start | bytes 1228808 | tf_op jit(solution)/shard_map/ppermute | solution.py:347
  47.2 1.0 copy-start.1
  48.2 0.9 copy-start.3
  77.0 16.2 %collective-permute-start.14 = (bf16[32,3200]{1,0:T(8,128)(2,1)S(1)}, bf16[32,3200]{1,0:T(8,128)(2,1)S(1)}, u32[]{:S(2)}, u32[]{:S(2)}) collective-permute-start(bf16[32,3200]{1,0:T(8,128)(2,1)S(1)} %get-tuple-element.28), channel_id=1, source_target_pairs={{0,1},{1,0},{2,3},{3,2},{4,5},{5,4},{6,7},{7,6},{8,9},{9,8},{10,11... | collective-permute-start | bytes 614408 | tf_op jit(solution)/shard_map/ppermute | solution.py:347
  77.3 12.5 %collective-permute-start.12 = (bf16[200,256]{1,0:T(8,128)(2,1)S(1)}, bf16[200,256]{1,0:T(8,128)(2,1)S(1)}, u32[]{:S(2)}, u32[]{:S(2)}) collective-permute-start(bf16[200,256]{1,0:T(8,128)(2,1)S(1)} %partial_grad.1), channel_id=1, source_target_pairs={{0,128},{64,192},{128,0},{192,64},{1,129},{65,193},{129,1},{193,65... | collective-permute-start | bytes 307208 | tf_op jit(solution)/shard_map/ppermute | solution.py:347
  82.8 8.5 %collective-permute-start.11 = (bf16[200,256]{1,0:T(8,128)(2,1)S(1)}, bf16[200,256]{1,0:T(8,128)(2,1)S(1)}, u32[]{:S(2)}, u32[]{:S(2)}) collective-permute-start(bf16[200,256]{1,0:T(8,128)(2,1)S(1)} %partial_grad.1), channel_id=1, source_target_pairs={{0,192},{64,0},{128,64},{192,128},{1,193},{65,1},{129,65},{193,129... | collective-permute-start | bytes 307208 | tf_op jit(solution)/shard_map/ppermute | solution.py:347
  84.4 8.8 %collective-permute-start.10 = (bf16[200,256]{1,0:T(8,128)(2,1)S(1)}, bf16[200,256]{1,0:T(8,128)(2,1)S(1)}, u32[]{:S(2)}, u32[]{:S(2)}) collective-permute-start(bf16[200,256]{1,0:T(8,128)(2,1)S(1)} %partial_grad.1), channel_id=1, source_target_pairs={{0,64},{64,128},{128,192},{192,0},{1,65},{65,129},{129,193},{193,1... | collective-permute-start | bytes 307208 | tf_op jit(solution)/shard_map/ppermute | solution.py:347
  85.8 1.2 collective-permute-start.13
  93.2 4.9 %collective-permute-start.15 = (bf16[200,256]{1,0:T(8,128)(2,1)S(1)}, bf16[200,256]{1,0:T(8,128)(2,1)S(1)}, u32[]{:S(2)}, u32[]{:S(2)}) collective-permute-start(bf16[200,256]{1,0:T(8,128)(2,1)S(1)} %add_convert_fusion), channel_id=1, source_target_pairs={{0,32},{32,0},{1,33},{33,1},{2,34},{34,2},{3,35},{35,3},{4,36},{36... | collective-permute-start | bytes 307208 | tf_op jit(solution)/shard_map/ppermute | solution.py:347
  98.2 7.0 %collective-permute-start.16 = (bf16[400,256]{1,0:T(8,128)(2,1)S(1)}, bf16[400,256]{1,0:T(8,128)(2,1)S(1)}, u32[]{:S(2)}, u32[]{:S(2)}) collective-permute-start(bf16[400,256]{1,0:T(8,128)(2,1)S(1)} %pad_maximum_fusion.1), channel_id=1, source_target_pairs={{0,2},{1,9},{2,4},{3,11},{4,6},{5,13},{6,0},{7,15},{8,10},{9,17},{... | collective-permute-start | bytes 614408 | tf_op jit(solution)/shard_map/ppermute | solution.py:358
  99.1 9.1 %collective-permute-start.17 = (bf16[400,256]{1,0:T(8,128)(2,1)S(1)}, bf16[400,256]{1,0:T(8,128)(2,1)S(1)}, u32[]{:S(2)}, u32[]{:S(2)}) collective-permute-start(bf16[400,256]{1,0:T(8,128)(2,1)S(1)} %pad_maximum_fusion.1), channel_id=1, source_target_pairs={{0,4},{1,17},{2,6},{3,19},{4,0},{5,21},{6,2},{7,23},{8,12},{9,25},... | collective-permute-start | bytes 614408 | tf_op jit(solution)/shard_map/ppermute | solution.py:358
  101.7 6.6 %collective-permute-start.18 = (bf16[400,256]{1,0:T(8,128)(2,1)S(1)}, bf16[400,256]{1,0:T(8,128)(2,1)S(1)}, u32[]{:S(2)}, u32[]{:S(2)}) collective-permute-start(bf16[400,256]{1,0:T(8,128)(2,1)S(1)} %pad_maximum_fusion.1), channel_id=1, source_target_pairs={{0,6},{1,25},{2,0},{3,27},{4,2},{5,29},{6,4},{7,31},{8,14},{9,1},{... | collective-permute-start | bytes 614408 | tf_op jit(solution)/shard_map/ppermute | solution.py:358
  105.2 11.6 %collective-permute-start.19 = (bf16[800,256]{1,0:T(8,128)(2,1)S(1)}, bf16[800,256]{1,0:T(8,128)(2,1)S(1)}, u32[]{:S(2)}, u32[]{:S(2)}) collective-permute-start(bf16[800,256]{1,0:T(8,128)(2,1)S(1)} %pad_maximum_fusion.refs_0_), channel_id=1, source_target_pairs={{0,8},{1,3},{2,10},{3,5},{4,12},{5,7},{6,14},{7,1},{8,16},{9,11},{... | collective-permute-start | bytes 1228808 | tf_op jit(solution)/shard_map/ppermute | solution.py:358
  108.3 8.5 %collective-permute-start.22 = (bf16[800,256]{1,0:T(8,128)(2,1)S(1)}, bf16[800,256]{1,0:T(8,128)(2,1)S(1)}, u32[]{:S(2)}, u32[]{:S(2)}) collective-permute-start(bf16[800,256]{1,0:T(8,128)(2,1)S(1)} %constant_dynamic-update-slice_fusion.refs_1_), channel_id=1, source_target_pairs={{0,24},{1,7},{2,26},{3,1},{4,28},{5,3},{6,30},{7,5},{8,0},{9,15},{... | collective-permute-start | bytes 1228808 | tf_op jit(solution)/shard_map/ppermute | solution.py:358
  111.3 10.4 %collective-permute-start.24 = (bf16[800,256]{1,0:T(8,128)(2,1)S(1)}, bf16[800,256]{1,0:T(8,128)(2,1)S(1)}, u32[]{:S(2)}, u32[]{:S(2)}) collective-permute-start(bf16[800,256]{1,0:T(8,128)(2,1)S(1)} %pad_maximum_fusion.refs_0_), channel_id=1, source_target_pairs={{0,24},{1,7},{2,26},{3,1},{4,28},{5,3},{6,30},{7,5},{8,0},{9,15},{... | collective-permute-start | bytes 1228808 | tf_op jit(solution)/shard_map/ppermute | solution.py:358
  113.1 9.2 %collective-permute-start.20 = (bf16[800,256]{1,0:T(8,128)(2,1)S(1)}, bf16[800,256]{1,0:T(8,128)(2,1)S(1)}, u32[]{:S(2)}, u32[]{:S(2)}) collective-permute-start(bf16[800,256]{1,0:T(8,128)(2,1)S(1)} %constant_dynamic-update-slice_fusion.refs_1_), channel_id=1, source_target_pairs={{0,8},{1,3},{2,10},{3,5},{4,12},{5,7},{6,14},{7,1},{8,16},{9,11},{... | collective-permute-start | bytes 1228808 | tf_op jit(solution)/shard_map/ppermute | solution.py:358
  116.8 9.9 %collective-permute-start.21 = (bf16[800,256]{1,0:T(8,128)(2,1)S(1)}, bf16[800,256]{1,0:T(8,128)(2,1)S(1)}, u32[]{:S(2)}, u32[]{:S(2)}) collective-permute-start(bf16[800,256]{1,0:T(8,128)(2,1)S(1)} %collective-permute-done.19.refs_2_), channel_id=1, source_target_pairs={{0,8},{1,3},{2,10},{3,5},{4,12},{5,7},{6,14},{7,1},{8,16},{9,11},{... | collective-permute-start | bytes 1228808 | tf_op jit(solution)/shard_map/ppermute | solution.py:358
  116.8 9.9 %collective-permute-start.23 = (bf16[800,256]{1,0:T(8,128)(2,1)S(1)}, bf16[800,256]{1,0:T(8,128)(2,1)S(1)}, u32[]{:S(2)}, u32[]{:S(2)}) collective-permute-start(bf16[800,256]{1,0:T(8,128)(2,1)S(1)} %collective-permute-done.22.refs_7_), channel_id=1, source_target_pairs={{0,24},{1,7},{2,26},{3,1},{4,28},{5,3},{6,30},{7,5},{8,0},{9,15},{... | collective-permute-start | bytes 1228808 | tf_op jit(solution)/shard_map/ppermute | solution.py:358

commit v4 on v3

--- a/solution.py
+++ b/solution.py
@@ -13,6 +13,8 @@
 OFFSETS = (1, -1, 2, -2)
 HALO_ORDER = (1, 2, -1, -2)
 BRANCH = 0.125
+PREP_MB = 56
+MSG_MB = 54
 GROUP = ("zl", "y", "x")
 ATOMS = ("zh", "zl", "y", "x")
 F32 = jnp.float32
@@ -38,20 +40,11 @@
     return lax.dot_general(a, b, (((ca,), (cb,)), ((), ())), preferred_element_type=F32)
 
 
-def message_kernel(
-    core_ref, esrc_hbm, edst_hbm, erot_hbm, ew_hbm, rot_hbm,
-    mix0_hbm, mix1_hbm, mix2_hbm,
-    fo_ref, ho0_ref, ho1_ref, ho2_ref, ho3_ref,
-    fx_ref, hx0_ref, hx1_ref, hx2_ref, hx3_ref,
-    out_ref,
-    rows, nat, frames, wframes, packed, z0, z1, z2, xb0, xb1, xb2,
-    esrc_ref, edst_ref, erot_ref, ew_ref, rot_ref, mix0_in, mix1_in, mix2_in, mix0_ref, mix1_ref, mix2_ref, sems,
+def prepare_kernel(
+    esrc_hbm, edst_hbm, erot_hbm, ew_hbm, rot_hbm, mix0_hbm, mix1_hbm, mix2_hbm,
+    frames, wframes, onehot_ref, scatter_ref, mix0_ref, mix1_ref, mix2_ref,
+    packed, esrc_ref, edst_ref, erot_ref, ew_ref, rot_ref, mix0_in, mix1_in, mix2_in, sems,
 ):
-    core = core_ref[0]
-    other = 1 - core
-    edges = esrc_ref.shape[1]
-    atoms, half = fo_ref.shape
-
     copies = [
         pltpu.make_async_copy(src, dst, sems.at[i])
         for i, (src, dst) in enumerate(
@@ -61,20 +54,14 @@
             )
         )
     ]
-    moves = []
-    for q, (own, oth) in enumerate(
-        zip((fo_ref, ho0_ref, ho1_ref, ho2_ref, ho3_ref), (fx_ref, hx0_ref, hx1_ref, hx2_ref, hx3_ref))
-    ):
-        at = pl.ds(0 if q == 0 else (1 + OFFSETS.index(HALO_ORDER[q - 1])) * atoms, atoms)
-        moves.append(pltpu.make_async_copy(own, rows.at[core, at, :], sems.at[8 + 2 * q]))
-        moves.append(pltpu.make_async_copy(oth, rows.at[other, at, :], sems.at[9 + 2 * q]))
-    for copy in copies[:5] + moves + copies[5:]:
+    for copy in copies:
         copy.start()
     for copy in copies[:5]:
         copy.wait()
-
-    source_rows = lax.broadcasted_iota(jnp.int32, (5 * atoms, edges), 0)
-    onehot = (esrc_ref[...] == source_rows).astype(BF16)
+    edges = esrc_ref.shape[1]
+
+    onehot_ref[...] = (esrc_ref[...] == lax.broadcasted_iota(jnp.int32, onehot_ref.shape, 0)).astype(BF16)
+    scatter_ref[...] = (edst_ref[...] == lax.broadcasted_iota(jnp.int32, scatter_ref.shape, 0)).astype(BF16)
 
     rot_count = rot_ref.shape[1]
     picks = (erot_ref[...] == lax.broadcasted_iota(jnp.int32, (rot_count, edges), 0)).astype(BF16)
@@ -90,6 +77,74 @@
             frames[blk, slot] = value
             wframes[blk, slot] = value * weight
 
+    for copy in copies[5:]:
+        copy.wait()
+    mix0_ref[...] = mix0_in[...].T
+    for i in range(2):
+        mix1_ref[i] = mix1_in[i].T
+        mix2_ref[i] = mix2_in[i].T
+
+
+def prepare(esrc, edst, erot, ew, rot_table, mixes, atoms):
+    edges = esrc.shape[-1]
+    row = lambda a: a.reshape(1, -1)
+    vmem = pl.BlockSpec(memory_space=pltpu.VMEM)
+    frames = jax.ShapeDtypeStruct((edges // 128, len(SLOTS), 8, 128), F32)
+    return pl.pallas_call(
+        prepare_kernel,
+        out_shape=(
+            frames, frames,
+            jax.ShapeDtypeStruct((5 * atoms, edges), BF16),
+            jax.ShapeDtypeStruct((atoms, edges), BF16),
+        )
+        + tuple(jax.ShapeDtypeStruct(mix.shape, BF16) for mix in mixes),
+        in_specs=[pl.BlockSpec(memory_space=pl.ANY)] * 8,
+        out_specs=(vmem,) * 7,
+        scratch_shapes=[pltpu.VMEM((rot_table.shape[0], edges), F32)]
+        + [pltpu.VMEM((1, edges), jnp.int32)] * 3
+        + [pltpu.VMEM((1, edges), F32), pltpu.VMEM(rot_table.shape, F32)]
+        + [pltpu.VMEM(mix.shape, BF16) for mix in mixes]
+        + [pltpu.SemaphoreType.DMA((8,))],
+        compiler_params=pltpu.CompilerParams(vmem_limit_bytes=PREP_MB * 1024 * 1024),
+        cost_estimate=pl.CostEstimate(flops=100_000_000, bytes_accessed=10_000_000, transcendentals=0),
+        name="prepare",
+    )(row(esrc), row(edst), row(erot), row(ew), rot_table, *mixes)
+
+
+def message_kernel(
+    core_ref, frames_hbm, wframes_hbm, onehot_hbm, scatter_hbm, mix0_hbm, mix1_hbm, mix2_hbm,
+    fo_ref, ho0_ref, ho1_ref, ho2_ref, ho3_ref,
+    fx_ref, hx0_ref, hx1_ref, hx2_ref, hx3_ref,
+    out_ref,
+    rows, nat, z0, z1, z2, xb0, xb1, xb2,
+    frames, wframes, onehot_ref, scatter_ref, mix0_ref, mix1_ref, mix2_ref, sems,
+):
+    core = core_ref[0]
+    other = 1 - core
+    pick, frame, wframe, place, *mixes = [
+        pltpu.make_async_copy(src, dst, sems.at[10 + i])
+        for i, (src, dst) in enumerate(
+            (
+                (onehot_hbm, onehot_ref), (frames_hbm, frames), (wframes_hbm, wframes),
+                (scatter_hbm, scatter_ref), (mix0_hbm, mix0_ref), (mix1_hbm, mix1_ref), (mix2_hbm, mix2_ref),
+            )
+        )
+    ]
+    edges = onehot_ref.shape[1]
+    atoms, half = fo_ref.shape
+
+    moves = []
+    for q, (own, oth) in enumerate(
+        zip((fo_ref, ho0_ref, ho1_ref, ho2_ref, ho3_ref), (fx_ref, hx0_ref, hx1_ref, hx2_ref, hx3_ref))
+    ):
+        at = pl.ds(0 if q == 0 else (1 + OFFSETS.index(HALO_ORDER[q - 1])) * atoms, atoms)
+        moves.append(pltpu.make_async_copy(own, rows.at[core, at, :], sems.at[2 * q]))
+        moves.append(pltpu.make_async_copy(oth, rows.at[other, at, :], sems.at[2 * q + 1]))
+    for move in [pick] + moves + [frame] + mixes + [wframe, place]:
+        move.start()
+    pick.wait()
+    onehot = onehot_ref[...]
+
     step = 640
 
     def gather(i, _):
@@ -101,12 +156,6 @@
             nat[blk, pl.ds(at, step), :] = got[:, blk * 128 : (blk + 1) * 128]
         return 0
 
-    for copy in copies[5:]:
-        copy.wait()
-    mix0_ref[...] = mix0_in[...].T
-    for i in range(2):
-        mix1_ref[i] = mix1_in[i].T
-        mix2_ref[i] = mix2_in[i].T
     for move in moves:
         move.wait()
     lax.fori_loop(0, 2 * half // step, gather, 0)
@@ -134,6 +183,7 @@
                             z2[side, pl.ds(g * 24 + l - 2, 8, stride=3), :] = acc
         return 0
 
+    frame.wait()
     lax.fori_loop(0, groups * (edges // 128), rotate_in, 0)
 
     for nb in range(4):
@@ -148,6 +198,8 @@
         z0[2 * n + 1] = y[:, 128:]
         return 0
 
+    for mix in mixes:
+        mix.wait()
     lax.fori_loop(0, 2, mix_zero, 0)
 
     def mix_pair(mix_ref, xb, z):
@@ -191,9 +243,11 @@
                     nat[blk, pl.ds(g * 400 + p * 25 + l * l + n, 8, stride=50), :] = acc
         return 0
 
+    wframe.wait()
     lax.fori_loop(0, groups * (edges // 128), rotate_out, 0)
-
-    scatter = (edst_ref[...] == lax.broadcasted_iota(jnp.int32, (atoms, edges), 0)).astype(BF16)
+    place.wait()
+
+    scatter = scatter_ref[...]
 
     def aggregate(i, _):
         at = pl.multiple_of(i * step, 128)
@@ -206,22 +260,19 @@
     lax.fori_loop(0, 2 * half // step, aggregate, 0)
 
 
-def messages(core, esrc, edst, erot, ew, rot_table, mixes, own, oth):
-    edges = esrc.shape[-1]
+def messages(core, prepared, own, oth):
+    edges = prepared[2].shape[1]
     atoms, half = own[0].shape
-    row = lambda a: a.reshape(1, -1)
     vmem = pl.BlockSpec(memory_space=pltpu.VMEM)
     return pl.pallas_call(
         message_kernel,
         out_shape=jax.ShapeDtypeStruct((atoms, 2 * half), BF16),
-        in_specs=[pl.BlockSpec(memory_space=pltpu.SMEM)] + [pl.BlockSpec(memory_space=pltpu.HBM)] * 18,
+        in_specs=[pl.BlockSpec(memory_space=pltpu.SMEM)]
+        + [pl.BlockSpec(memory_space=pl.ANY)] * (len(prepared) + 10),
         out_specs=vmem,
         scratch_shapes=[
             pltpu.VMEM((2, 5 * atoms, half), BF16),
             pltpu.VMEM((edges // 128, 2 * half, 128), F32),
-            pltpu.VMEM((edges // 128, len(SLOTS), 8, 128), F32),
-            pltpu.VMEM((edges // 128, len(SLOTS), 8, 128), F32),
-            pltpu.VMEM((rot_table.shape[0], edges), F32),
             pltpu.VMEM((4, 640, 128), F32),
             pltpu.VMEM((8, 512, 128), F32),
             pltpu.VMEM((8, 384, 128), F32),
@@ -229,14 +280,12 @@
             pltpu.VMEM((512, 1024), BF16),
             pltpu.VMEM((384, 1024), BF16),
         ]
-        + [pltpu.VMEM((1, edges), jnp.int32)] * 3
-        + [pltpu.VMEM((1, edges), F32), pltpu.VMEM(rot_table.shape, F32)]
-        + [pltpu.VMEM(mix.shape, BF16) for mix in mixes + mixes]
-        + [pltpu.SemaphoreType.DMA((18,))],
-        compiler_params=pltpu.CompilerParams(vmem_limit_bytes=54 * 1024 * 1024),
+        + [pltpu.VMEM(table.shape, table.dtype) for table in prepared]
+        + [pltpu.SemaphoreType.DMA((17,))],
+        compiler_params=pltpu.CompilerParams(vmem_limit_bytes=MSG_MB * 1024 * 1024),
         cost_estimate=pl.CostEstimate(flops=5_000_000_000, bytes_accessed=6_000_000, transcendentals=0),
         name="messages",
-    )(core, row(esrc), row(edst), row(erot), row(ew), rot_table, *mixes, *own, *oth)
+    )(core, *prepared, *own, *oth)
 
 
 def head_kernel(
@@ -358,20 +407,19 @@
     return lax.ppermute(x, ("y", "x", "chan"), pairs)
 
 
-def assemble_kernel(place_ref, *refs):
-    halves, out_ref, sems = refs[:8], refs[8], refs[9]
+def assemble_kernel(lates, place_ref, *refs):
+    halves, out_ref, sems = refs[: 2 * len(lates)], refs[-2], refs[-1]
     y, x, core = place_ref[0], place_ref[1], place_ref[2]
     rows = out_ref.shape[0] // 16
     copies = []
-    for late in range(4):
+    for i, late in enumerate(lates):
         for early in range(4):
-            ref, at = halves[2 * late + early // 2], early % 2
             dy = late + core * (early - late)
             dx = early + core * (late - early)
             spot = lax.rem(y + 4 - dy, 4) * 4 + lax.rem(x + 4 - dx, 4)
             copies.append(
                 pltpu.make_async_copy(
-                    ref.at[pl.ds(at * rows, rows), :],
+                    halves[2 * i + early // 2].at[pl.ds(early % 2 * rows, rows), :],
                     out_ref.at[pl.ds(pl.multiple_of(spot * rows, 16), rows), :],
                     sems.at[len(copies)],
                 )
@@ -382,18 +430,22 @@
         copy.wait()
 
 
-def assemble(place, blocks):
-    rows, width = 2 * blocks[0].shape[0], blocks[0].shape[1]
+def assemble(place, lates, halves, into=None):
+    rows, width = halves[0].shape
+    hbm = pl.BlockSpec(memory_space=pl.ANY)
+    given = [] if into is None else [into]
     return pl.pallas_call(
-        assemble_kernel,
-        out_shape=jax.ShapeDtypeStruct((4 * rows, width), BF16),
+        functools.partial(assemble_kernel, lates),
+        out_shape=jax.ShapeDtypeStruct((8 * rows, width), BF16),
         in_specs=[pl.BlockSpec(memory_space=pltpu.SMEM)]
-        + [pl.BlockSpec(memory_space=pltpu.VMEM)] * len(blocks),
-        out_specs=pl.BlockSpec(memory_space=pl.ANY),
-        scratch_shapes=[pltpu.SemaphoreType.DMA((16,))],
+        + [pl.BlockSpec(memory_space=pltpu.VMEM)] * len(halves)
+        + [hbm] * len(given),
+        out_specs=hbm,
+        input_output_aliases={1 + len(halves): 0} if given else {},
+        scratch_shapes=[pltpu.SemaphoreType.DMA((4 * len(lates),))],
         compiler_params=pltpu.CompilerParams(vmem_limit_bytes=16 * 1024 * 1024),
         name="assemble",
-    )(place, *blocks)
+    )(place, *halves, *given)
 
 
 def body(
@@ -401,14 +453,16 @@
     mix_zero, mix_one, mix_two, atom_species, species_orbitals, head_weight, target_blocks,
 ):
     core = lax.axis_index("chan").astype(jnp.int32).reshape(1)
-    f_oth = shift(features, "chan", 1)
     leaving = leaving_rows(send_rows, features)
     halo = [shift(leaving[OFFSETS.index(off)], ATOMS, off) for off in HALO_ORDER]
+    prepared = prepare(
+        edge_source, edge_dest, edge_rot, edge_weight, rot_table.T,
+        (mix_zero, mix_one, mix_two), features.shape[0],
+    )
+    features, prepared = lax.optimization_barrier((features, prepared))
+    f_oth = shift(features, "chan", 1)
     halo_oth = [shift(h, "chan", 1) for h in halo]
-    mine = messages(
-        core, edge_source, edge_dest, edge_rot, edge_weight, rot_table.T,
-        (mix_zero, mix_one, mix_two), [features] + halo, [f_oth] + halo_oth,
-    )
+    mine = messages(core, prepared, [features] + halo, [f_oth] + halo_oth)
     recv = shift(mine, "chan", 1)
     parts = lax.axis_size(GROUP)
     load, loss, keep, send = head(
@@ -440,8 +494,9 @@
     high_far = plane_shift(high_ahead, False, -1)
     place = jnp.stack([lax.axis_index(name) for name in ("y", "x", "chan")]).astype(jnp.int32)
     grad_head = assemble(
-        place, [low, high, low_behind, high_behind, low_far, high_far, low_ahead, high_ahead]
+        place, (0, 1, 3), [low, high, low_behind, high_behind, low_ahead, high_ahead]
     )
+    grad_head = assemble(place, (2,), [low_far, high_far], grad_head)
     return (atom_loss, grad_head, grad_features)
 
 

time: 130 us -> 127 us (0.977)
  waiting for transfers between devices: 36.6 us -> 30.4 us
  Pallas kernels: 25.9 us -> 28.1 us
    pallas_call x1 -> x3, Pallas kernels: 2.38 us -> 7.5 us  [the longest x1 3.96 us: prepare(): pl.pallas_call(prepare_kernel, out_shape=(frames, frames, jax.ShapeDtypeS...]
    ppermute x16, waiting for transfers between devices: 25.7 us -> 21.6 us  [shift(): return lax.ppermute(x, axis, [(i, (i + by) % count) for i in range(count)])]
    ppermute x9, waiting for transfers between devices: 10.9 us -> 8.76 us  [plane_shift(): return lax.ppermute(x, ('y', 'x', 'chan'), pairs)]
    pallas_call x1, Pallas kernels: 18.5 us -> 16.9 us  [messages(): pl.pallas_call(message_kernel, out_shape=jax.ShapeDtypeStruct((atoms, 2 *...]
    unnamed x33 -> x37, local copies, waits for them, and re-layouts: 3.29 us -> 4.23 us
  transfers between devices with their start and end apart: 25 -> 25, of which waited for: 15 -> 15; matrix products, arithmetic and copies ran while one was open for 1% -> 1% of each run, Pallas kernels for 0% -> 5%
where the time goes in v4:
time: 127 us; the launch traced here: 126 us
  starting transfers between devices  36.7 us (29%)
  waiting for transfers between devices  30.4 us (24%)
  Pallas kernels  28.1 us (22%)
  blocking collectives  24.3 us (19%)
  local copies, waits for them, and re-layouts  4.25 us (3%)
  other arithmetic  1.6 us (1%)
    all_to_all x1, blocking collectives, body(): got = lax.all_to_all(load, GROUP, split_axis=0, concat_axis=0, tiled=True)  24.3 us
    ppermute x16, waiting for transfers between devices, shift(): return lax.ppermute(x, axis, [(i, (i + by) % count) for i in range(count)])  21.6 us
    ppermute x16, starting transfers between devices, shift(): return lax.ppermute(x, axis, [(i, (i + by) % count) for i in range(count)])  20.5 us
    pallas_call x1, Pallas kernels, messages(): pl.pallas_call(message_kernel, out_shape=jax.ShapeDtypeStruct((atoms, 2 *...  16.9 us
    ppermute x9, starting transfers between devices, plane_shift(): return lax.ppermute(x, ('y', 'x', 'chan'), pairs)  16.2 us
    ppermute x9, waiting for transfers between devices, plane_shift(): return lax.ppermute(x, ('y', 'x', 'chan'), pairs)  8.76 us
    unnamed x37, local copies, waits for them, and re-layouts  4.23 us
    pallas_call x1, Pallas kernels, prepare(): pl.pallas_call(prepare_kernel, out_shape=(frames, frames, jax.ShapeDtypeS...  3.96 us
  transfers between devices with their start and end apart: 25, of which 15 were waited for; matrix products, arithmetic and copies ran while one was open for 1% of the time, Pallas kernels for 5%

profile of v4, /device:TPU:32, one launch (start us, length us, event | category | flops | bytes accessed | tf_op | source)
XLA Modules:
  0.0 126.4 jit_solution(4265231335978135184)
XLA Ops:
  0.6 0.0 copy-start.1
  0.6 0.9 copy-done.1
  1.6 0.7 copy-done.7
  2.2 0.5 leaving.1
  2.7 1.6 %collective-permute-start.1 = (bf16[32,3200]{1,0:T(8,128)(2,1)S(1)}, bf16[32,3200]{1,0:T(8,128)(2,1)S(1)}, u32[]{:S(2)}, u32[]{:S(2)}) collective-permute-start(bf16[32,3200]{1,0:T(8,128)(2,1)S(1)} %get-tuple-element.49), channel_id=1, source_target_pairs={{0,2},{2,4},{4,6},{6,8},{8,10},{10,12},{12,14},{14,16},{16,18},{18... | collective-permute-start | bytes 614408 | tf_op jit(solution)/shard_map/ppermute | solution.py:396
  4.3 2.7 %collective-permute-start.2 = (bf16[32,3200]{1,0:T(8,128)(2,1)S(1)}, bf16[32,3200]{1,0:T(8,128)(2,1)S(1)}, u32[]{:S(2)}, u32[]{:S(2)}) collective-permute-start(bf16[32,3200]{1,0:T(8,128)(2,1)S(1)} %get-tuple-element.50), channel_id=1, source_target_pairs={{0,4},{2,6},{4,8},{6,10},{8,12},{10,14},{12,16},{14,18},{16,20},{1... | collective-permute-start | bytes 614408 | tf_op jit(solution)/shard_map/ppermute | solution.py:396
  7.0 4.4 %collective-permute-start.3 = (bf16[32,3200]{1,0:T(8,128)(2,1)S(1)}, bf16[32,3200]{1,0:T(8,128)(2,1)S(1)}, u32[]{:S(2)}, u32[]{:S(2)}) collective-permute-start(bf16[32,3200]{1,0:T(8,128)(2,1)S(1)} %get-tuple-element.51), channel_id=1, source_target_pairs={{0,254},{2,0},{4,2},{6,4},{8,6},{10,8},{12,10},{14,12},{16,14},{18... | collective-permute-start | bytes 614408 | tf_op jit(solution)/shard_map/ppermute | solution.py:396
  11.5 0.5 collective-permute-start.4
  12.0 4.0 %prepare.1 = (f32[2,115,8,128]{3,2,1,0:T(8,128)}, f32[2,115,8,128]{3,2,1,0:T(8,128)}, bf16[160,256]{1,0:T(8,128)(2,1)}, bf16[32,256]{1,0:T(8,128)(2,1)}, bf16[64...) custom-call(s32[1,256]{1,0:T(1,128)} %bitcast.13, s32[1,256]{1,0:T(1,128)} %bitcast.14, ...), custom_call_target="tpu_custom_call" | custom-call | flops 100000000 | bytes 10000000 | tf_op jit(solution)/shard_map/prepare/pallas_call | solution.py:93
  15.9 0.1 collective-permute-start
  16.0 1.1 collective-permute-done.1.ho0_ref
  17.1 0.0 collective-permute-start.5
  17.2 1.1 collective-permute-done.2.ho1_ref
  18.2 0.0 collective-permute-start.6
  18.2 6.0 %collective-permute-done.3.ho2_ref = bf16[32,3200]{1,0:T(8,128)(2,1)S(1)} collective-permute-done((bf16[32,3200]{1,0:T(8,128)(2,1)S(1)}, bf16[32,3200]{1,0:T(8,128)(2,1)S(1)}, u32[]{:S(2)}, u32[]{:S(2)}) %collective-permute-start.3) | collective-permute-done | bytes 204832 | tf_op jit(solution)/shard_map/ppermute | solution.py:396
  24.2 0.0 collective-permute-start.7
  24.2 0.5 collective-permute-start.8
  24.7 0.0 collective-permute-done.5.hx0_ref
  24.8 0.9 collective-permute-done.7.hx2_ref
  25.7 0.3 collective-permute-done.8.hx3_ref
  26.0 0.3 copy-done.16
  26.3 0.3 copy-done.17
  26.7 0.0 copy-start.9
  26.7 16.9 %messages.1.mine_ref = bf16[32,6400]{1,0:T(8,128)(2,1)} custom-call(s32[1]{0:T(128)} %bitcast.core_ref, f32[2,115,8,128]{3,2,1,0:T(8,128)} %get-tuple-element.42.frames_hbm, f32[2,115,8,128]{3,2,1,0:T(8,128)} %get-tuple-element.43.wframes_hbm, bf16[160,256]{1,0:T(8,128)(2,1)} %get-tuple-element.44.onehot_hbm, bf16[32,256]{1,0:T(8,128)(2,1)} %get-tuple-element.45.scatter_hbm, ...), custom_call_target="tpu_custom_call" | custom-call | flops 5000000000 | bytes 6000000 | tf_op jit(solution)/shard_map/messages/pallas_call | solution.py:267
  43.6 0.3 collective-permute-start.9
  43.9 1.7 %collective-permute-done.9.recv_ref = bf16[32,6400]{1,0:T(8,128)(2,1)S(1)} collective-permute-done((bf16[32,6400]{1,0:T(8,128)(2,1)}, bf16[32,6400]{1,0:T(8,128)(2,1)S(1)}, u32[]{:S(2)}, u32[]{:S(2)}) %collective-permute-start.9) | collective-permute-done | bytes 409632 | tf_op jit(solution)/shard_map/ppermute | solution.py:396
  45.7 1.0 copy-done.3
  46.7 0.9 copy-done.5
  47.6 2.9 %head.1 = (bf16[32,32,512]{2,1,0:T(8,128)(2,1)S(1)}, f32[32,1]{1,0:T(8,128)S(1)}, f32[32,3200]{1,0:T(8,128)S(1)}, bf16[32,3200]{1,0:T(8,128)(2,1)S(1)}) custom-call(s32[1]{0:T(128)} %bitcast.core_ref, s32[4]{0:T(128)S(1)} %copy-done.8, s32[1,32]{1,0:T(1,128)S(1)} %bitcast.11, bf16[32,3200]{1,0:T(8,128)(2,1)S(1)} %copy-done.2, ...), custom_call_target="tpu_custom_call" | custom-call | flops 300000000 | bytes 6000000 | tf_op jit(solution)/shard_map/head/pallas_call | solution.py:333
  50.5 24.3 %all_to_all.5 = bf16[32,32,512]{2,1,0:T(8,128)(2,1)S(1)} all-to-all(bf16[32,32,512]{2,1,0:T(8,128)(2,1)S(1)} %get-tuple-element.53), channel_id=1, replica_groups=mesh['zh'=4,'zl'=2,'y'=4,'x'=4,'chan'=2] {'zl','y','x'}, dimensions={0} | all-to-all | bytes 2097152 | tf_op jit(solution)/shard_map/all_to_all | solution.py:471
  74.8 0.3 partial_grad.1
  75.1 0.3 collective-permute-start.14
  75.4 5.5 %collective-permute-start.12 = (bf16[200,256]{1,0:T(8,128)(2,1)S(1)}, bf16[200,256]{1,0:T(8,128)(2,1)S(1)}, u32[]{:S(2)}, u32[]{:S(2)}) collective-permute-start(bf16[200,256]{1,0:T(8,128)(2,1)S(1)} %partial_grad.1), channel_id=1, source_target_pairs={{0,128},{64,192},{128,0},{192,64},{1,129},{65,193},{129,1},{193,65... | collective-permute-start | bytes 307208 | tf_op jit(solution)/shard_map/ppermute | solution.py:396
  80.9 1.6 %collective-permute-start.11 = (bf16[200,256]{1,0:T(8,128)(2,1)S(1)}, bf16[200,256]{1,0:T(8,128)(2,1)S(1)}, u32[]{:S(2)}, u32[]{:S(2)}) collective-permute-start(bf16[200,256]{1,0:T(8,128)(2,1)S(1)} %partial_grad.1), channel_id=1, source_target_pairs={{0,192},{64,0},{128,64},{192,128},{1,193},{65,1},{129,65},{193,129... | collective-permute-start | bytes 307208 | tf_op jit(solution)/shard_map/ppermute | solution.py:396
  82.4 1.3 %collective-permute-start.10 = (bf16[200,256]{1,0:T(8,128)(2,1)S(1)}, bf16[200,256]{1,0:T(8,128)(2,1)S(1)}, u32[]{:S(2)}, u32[]{:S(2)}) collective-permute-start(bf16[200,256]{1,0:T(8,128)(2,1)S(1)} %partial_grad.1), channel_id=1, source_target_pairs={{0,64},{64,128},{128,192},{192,0},{1,65},{65,129},{129,193},{193,1... | collective-permute-start | bytes 307208 | tf_op jit(solution)/shard_map/ppermute | solution.py:396
  83.8 0.1 reduce
  83.9 0.1 collective-permute-start.13
  84.0 1.1 collective-permute-done.13
  85.1 2.8 %collective-permute-done.12 = bf16[200,256]{1,0:T(8,128)(2,1)S(1)} collective-permute-done((bf16[200,256]{1,0:T(8,128)(2,1)S(1)}, bf16[200,256]{1,0:T(8,128)(2,1)S(1)}, u32[]{:S(2)}, u32[]{:S(2)}) %collective-permute-start.12) | collective-permute-done | bytes 102432 | tf_op jit(solution)/shard_map/ppermute | solution.py:396
  87.9 1.4 %collective-permute-done.11 = bf16[200,256]{1,0:T(8,128)(2,1)S(1)} collective-permute-done((bf16[200,256]{1,0:T(8,128)(2,1)S(1)}, bf16[200,256]{1,0:T(8,128)(2,1)S(1)}, u32[]{:S(2)}, u32[]{:S(2)}) %collective-permute-start.11) | collective-permute-done | bytes 102432 | tf_op jit(solution)/shard_map/ppermute | solution.py:396
  89.4 1.9 %collective-permute-done.10 = bf16[200,256]{1,0:T(8,128)(2,1)S(1)} collective-permute-done((bf16[200,256]{1,0:T(8,128)(2,1)S(1)}, bf16[200,256]{1,0:T(8,128)(2,1)S(1)}, u32[]{:S(2)}, u32[]{:S(2)}) %collective-permute-start.10) | collective-permute-done | bytes 102432 | tf_op jit(solution)/shard_map/ppermute | solution.py:396
  91.2 0.1 add_convert_fusion
  91.3 1.6 %collective-permute-start.15 = (bf16[200,256]{1,0:T(8,128)(2,1)S(1)}, bf16[200,256]{1,0:T(8,128)(2,1)S(1)}, u32[]{:S(2)}, u32[]{:S(2)}) collective-permute-start(bf16[200,256]{1,0:T(8,128)(2,1)S(1)} %add_convert_fusion), channel_id=1, source_target_pairs={{0,32},{32,0},{1,33},{33,1},{2,34},{34,2},{3,35},{35,3},{4,36},{36... | collective-permute-start | bytes 307208 | tf_op jit(solution)/shard_map/ppermute | solution.py:396
  92.8 3.3 %collective-permute-done.15 = bf16[200,256]{1,0:T(8,128)(2,1)S(1)} collective-permute-done((bf16[200,256]{1,0:T(8,128)(2,1)S(1)}, bf16[200,256]{1,0:T(8,128)(2,1)S(1)}, u32[]{:S(2)}, u32[]{:S(2)}) %collective-permute-start.15) | collective-permute-done | bytes 102432 | tf_op jit(solution)/shard_map/ppermute | solution.py:396
  96.2 1.0 collective-permute-start.16
  97.2 2.5 %collective-permute-start.19 = (bf16[400,256]{1,0:T(8,128)(2,1)S(1)}, bf16[400,256]{1,0:T(8,128)(2,1)S(1)}, u32[]{:S(2)}, u32[]{:S(2)}) collective-permute-start(bf16[400,256]{1,0:T(8,128)(2,1)S(1)} %pad_maximum_fusion.1), channel_id=1, source_target_pairs={{0,4},{1,17},{2,6},{3,19},{4,0},{5,21},{6,2},{7,23},{8,12},{9,25},... | collective-permute-start | bytes 614408 | tf_op jit(solution)/shard_map/ppermute | solution.py:407
  99.7 1.2 collective-permute-start.20
  100.9 2.3 %collective-permute-done.16 = bf16[400,256]{1,0:T(8,128)(2,1)S(1)} collective-permute-done((bf16[400,256]{1,0:T(8,128)(2,1)S(1)}, bf16[400,256]{1,0:T(8,128)(2,1)S(1)}, u32[]{:S(2)}, u32[]{:S(2)}) %collective-permute-start.16) | collective-permute-done | bytes 204832 | tf_op jit(solution)/shard_map/ppermute | solution.py:407
  103.3 3.0 %collective-permute-start.17 = (bf16[800,256]{1,0:T(8,128)(2,1)S(1)}, bf16[800,256]{1,0:T(8,128)(2,1)S(1)}, u32[]{:S(2)}, u32[]{:S(2)}) collective-permute-start(bf16[800,256]{1,0:T(8,128)(2,1)S(1)} %pad_maximum_fusion.refs_0_), channel_id=1, source_target_pairs={{0,8},{1,3},{2,10},{3,5},{4,12},{5,7},{6,14},{7,1},{8,16},{9,11},{... | collective-permute-start | bytes 1228808 | tf_op jit(solution)/shard_map/ppermute | solution.py:407
  106.4 2.9 %collective-permute-start.21 = (bf16[800,256]{1,0:T(8,128)(2,1)S(1)}, bf16[800,256]{1,0:T(8,128)(2,1)S(1)}, u32[]{:S(2)}, u32[]{:S(2)}) collective-permute-start(bf16[800,256]{1,0:T(8,128)(2,1)S(1)} %constant_dynamic-update-slice_fusion.refs_1_), channel_id=1, source_target_pairs={{0,24},{1,7},{2,26},{3,1},{4,28},{5,3},{6,30},{7,5},{8,0},{9,15},{... | collective-permute-start | bytes 1228808 | tf_op jit(solution)/shard_map/ppermute | solution.py:407
  109.3 0.1 pad_add_fusion.place_ref
  109.4 1.8 %collective-permute-start.24 = (bf16[800,256]{1,0:T(8,128)(2,1)S(1)}, bf16[800,256]{1,0:T(8,128)(2,1)S(1)}, u32[]{:S(2)}, u32[]{:S(2)}) collective-permute-start(bf16[800,256]{1,0:T(8,128)(2,1)S(1)} %pad_maximum_fusion.refs_0_), channel_id=1, source_target_pairs={{0,24},{1,7},{2,26},{3,1},{4,28},{5,3},{6,30},{7,5},{8,0},{9,15},{... | collective-permute-start | bytes 1228808 | tf_op jit(solution)/shard_map/ppermute | solution.py:407
  111.2 0.2 collective-permute-start.23
  111.4 3.5 %collective-permute-done.17.refs_2_ = bf16[800,256]{1,0:T(8,128)(2,1)S(1)} collective-permute-done((bf16[800,256]{1,0:T(8,128)(2,1)S(1)}, bf16[800,256]{1,0:T(8,128)(2,1)S(1)}, u32[]{:S(2)}, u32[]{:S(2)}) %collective-permute-start.17) | collective-permute-done | bytes 409632 | tf_op jit(solution)/shard_map/ppermute | solution.py:407
  114.9 0.0 collective-permute-start.18
  114.9 0.0 collective-permute-done.21.refs_5_
  114.9 3.5 %collective-permute-start.22 = (bf16[800,256]{1,0:T(8,128)(2,1)S(1)}, bf16[800,256]{1,0:T(8,128)(2,1)S(1)}, u32[]{:S(2)}, u32[]{:S(2)}) collective-permute-start(bf16[800,256]{1,0:T(8,128)(2,1)S(1)} %collective-permute-done.21.refs_5_), channel_id=1, source_target_pairs={{0,24},{1,7},{2,26},{3,1},{4,28},{5,3},{6,30},{7,5},{8,0},{9,15},{... | collective-permute-start | bytes 1228808 | tf_op jit(solution)/shard_map/ppermute | solution.py:407
  118.5 0.8 convert_add_fusion
  119.2 0.5 add.15
  119.8 0.6 collective-permute-done.23.refs_3_
  120.4 2.1 %assemble.2.refs_2_ = bf16[6400,256]{1,0:T(8,128)(2,1)} custom-call(s32[3]{0:T(128)S(1)} %pad_add_fusion.place_ref, bf16[800,256]{1,0:T(8,128)(2,1)S(1)} %pad_maximum_fusion.refs_0_, bf16[800,256]{1,0:T(8,128)(2,1)S(1)} %constant_dynamic-update-slice_fusion.refs_1_, bf16[800,256]{1,0:T(8,128)(2,1)S(1)} %collective-permute-done.17.refs_2_, ...), custom_call_target="tpu_custom_call" | custom-call | tf_op jit(solution)/shard_map/assemble/pallas_call | solution.py:437
  122.5 2.3 %collective-permute-done.18.refs_0_ = bf16[800,256]{1,0:T(8,128)(2,1)S(1)} collective-permute-done((bf16[800,256]{1,0:T(8,128)(2,1)S(1)}, bf16[800,256]{1,0:T(8,128)(2,1)S(1)}, u32[]{:S(2)}, u32[]{:S(2)}) %collective-permute-start.18) | collective-permute-done | bytes 409632 | tf_op jit(solution)/shard_map/ppermute | solution.py:407
  124.8 0.0 collective-permute-done.22.refs_1_
  124.8 1.5 %assemble.3 = bf16[6400,256]{1,0:T(8,128)(2,1)} custom-call(s32[3]{0:T(128)S(1)} %pad_add_fusion.place_ref, bf16[800,256]{1,0:T(8,128)(2,1)S(1)} %collective-permute-done.18.refs_0_, bf16[800,256]{1,0:T(8,128)(2,1)S(1)} %collective-permute-done.22.refs_1_, bf16[6400,256]{1,0:T(8,128)(2,1)} %assemble.2.refs_2_), custom_call_target="tpu_custom_call", output_to_operand_aliasing={{}: (3, {})} | custom-call | tf_op jit(solution)/shard_map/assemble/pallas_call | solution.py:437
  (40 shorter events, 0.2 us)
Async XLA Ops:
  0.6 0.9 copy-start.1
  1.6 0.7 copy-start.7
  2.7 14.4 %collective-permute-start.1 = (bf16[32,3200]{1,0:T(8,128)(2,1)S(1)}, bf16[32,3200]{1,0:T(8,128)(2,1)S(1)}, u32[]{:S(2)}, u32[]{:S(2)}) collective-permute-start(bf16[32,3200]{1,0:T(8,128)(2,1)S(1)} %get-tuple-element.49), channel_id=1, source_target_pairs={{0,2},{2,4},{4,6},{6,8},{8,10},{10,12},{12,14},{14,16},{16,18},{18... | collective-permute-start | bytes 614408 | tf_op jit(solution)/shard_map/ppermute | solution.py:396
  4.3 13.9 %collective-permute-start.2 = (bf16[32,3200]{1,0:T(8,128)(2,1)S(1)}, bf16[32,3200]{1,0:T(8,128)(2,1)S(1)}, u32[]{:S(2)}, u32[]{:S(2)}) collective-permute-start(bf16[32,3200]{1,0:T(8,128)(2,1)S(1)} %get-tuple-element.50), channel_id=1, source_target_pairs={{0,4},{2,6},{4,8},{6,10},{8,12},{10,14},{12,16},{14,18},{16,20},{1... | collective-permute-start | bytes 614408 | tf_op jit(solution)/shard_map/ppermute | solution.py:396
  7.0 17.2 %collective-permute-start.3 = (bf16[32,3200]{1,0:T(8,128)(2,1)S(1)}, bf16[32,3200]{1,0:T(8,128)(2,1)S(1)}, u32[]{:S(2)}, u32[]{:S(2)}) collective-permute-start(bf16[32,3200]{1,0:T(8,128)(2,1)S(1)} %get-tuple-element.51), channel_id=1, source_target_pairs={{0,254},{2,0},{4,2},{6,4},{8,6},{10,8},{12,10},{14,12},{16,14},{18... | collective-permute-start | bytes 614408 | tf_op jit(solution)/shard_map/ppermute | solution.py:396
  11.5 12.7 %collective-permute-start.4 = (bf16[32,3200]{1,0:T(8,128)(2,1)S(1)}, bf16[32,3200]{1,0:T(8,128)(2,1)S(1)}, u32[]{:S(2)}, u32[]{:S(2)}) collective-permute-start(bf16[32,3200]{1,0:T(8,128)(2,1)S(1)} %get-tuple-element.52), channel_id=1, source_target_pairs={{0,252},{2,254},{4,0},{6,2},{8,4},{10,6},{12,8},{14,10},{16,12},{1... | collective-permute-start | bytes 614408 | tf_op jit(solution)/shard_map/ppermute | solution.py:396
  15.9 8.8 %collective-permute-start = (bf16[32,3200]{1,0:T(8,128)(2,1)}, bf16[32,3200]{1,0:T(8,128)(2,1)S(1)}, u32[]{:S(2)}, u32[]{:S(2)}) collective-permute-start(bf16[32,3200]{1,0:T(8,128)(2,1)} %fo_ref.1), channel_id=1, source_target_pairs={{0,1},{1,0},{2,3},{3,2},{4,5},{5,4},{6,7},{7,6},{8,9},{9,8},{10,11... | collective-permute-start | bytes 614408 | tf_op jit(solution)/shard_map/ppermute | solution.py:396
  17.1 8.8 %copy-start.10 = (bf16[32,3200]{1,0:T(8,128)(2,1)}, bf16[32,3200]{1,0:T(8,128)(2,1)S(1)}, u32[]{:S(2)}) copy-start(bf16[32,3200]{1,0:T(8,128)(2,1)S(1)} %collective-permute-done.1.ho0_ref) | copy-start | bytes 614404
  17.1 7.6 %collective-permute-start.5 = (bf16[32,3200]{1,0:T(8,128)(2,1)S(1)}, bf16[32,3200]{1,0:T(8,128)(2,1)S(1)}, u32[]{:S(2)}, u32[]{:S(2)}) collective-permute-start(bf16[32,3200]{1,0:T(8,128)(2,1)S(1)} %collective-permute-done.1.ho0_ref), channel_id=1, source_target_pairs={{0,1},{1,0},{2,3},{3,2},{4,5},{5,4},{6,7},{7,6},{8,9},{9,8},{10,11... | collective-permute-start | bytes 614408 | tf_op jit(solution)/shard_map/ppermute | solution.py:396
  18.2 7.7 %copy-start.11 = (bf16[32,3200]{1,0:T(8,128)(2,1)}, bf16[32,3200]{1,0:T(8,128)(2,1)S(1)}, u32[]{:S(2)}) copy-start(bf16[32,3200]{1,0:T(8,128)(2,1)S(1)} %collective-permute-done.2.ho1_ref) | copy-start | bytes 614404
  18.2 6.5 %collective-permute-start.6 = (bf16[32,3200]{1,0:T(8,128)(2,1)S(1)}, bf16[32,3200]{1,0:T(8,128)(2,1)S(1)}, u32[]{:S(2)}, u32[]{:S(2)}) collective-permute-start(bf16[32,3200]{1,0:T(8,128)(2,1)S(1)} %collective-permute-done.2.ho1_ref), channel_id=1, source_target_pairs={{0,1},{1,0},{2,3},{3,2},{4,5},{5,4},{6,7},{7,6},{8,9},{9,8},{10,11... | collective-permute-start | bytes 614408 | tf_op jit(solution)/shard_map/ppermute | solution.py:396
  24.2 1.8 %copy-start.12 = (bf16[32,3200]{1,0:T(8,128)(2,1)}, bf16[32,3200]{1,0:T(8,128)(2,1)S(1)}, u32[]{:S(2)}) copy-start(bf16[32,3200]{1,0:T(8,128)(2,1)S(1)} %collective-permute-done.3.ho2_ref) | copy-start | bytes 614404
  24.2 1.5 %collective-permute-start.7 = (bf16[32,3200]{1,0:T(8,128)(2,1)S(1)}, bf16[32,3200]{1,0:T(8,128)(2,1)S(1)}, u32[]{:S(2)}, u32[]{:S(2)}) collective-permute-start(bf16[32,3200]{1,0:T(8,128)(2,1)S(1)} %collective-permute-done.3.ho2_ref), channel_id=1, source_target_pairs={{0,1},{1,0},{2,3},{3,2},{4,5},{5,4},{6,7},{7,6},{8,9},{9,8},{10,11... | collective-permute-start | bytes 614408 | tf_op jit(solution)/shard_map/ppermute | solution.py:396
  24.2 1.8 %copy-start.13 = (bf16[32,3200]{1,0:T(8,128)(2,1)}, bf16[32,3200]{1,0:T(8,128)(2,1)S(1)}, u32[]{:S(2)}) copy-start(bf16[32,3200]{1,0:T(8,128)(2,1)S(1)} %collective-permute-done.4.ho3_ref) | copy-start | bytes 614404
  24.2 1.7 %collective-permute-start.8 = (bf16[32,3200]{1,0:T(8,128)(2,1)S(1)}, bf16[32,3200]{1,0:T(8,128)(2,1)S(1)}, u32[]{:S(2)}, u32[]{:S(2)}) collective-permute-start(bf16[32,3200]{1,0:T(8,128)(2,1)S(1)} %collective-permute-done.4.ho3_ref), channel_id=1, source_target_pairs={{0,1},{1,0},{2,3},{3,2},{4,5},{5,4},{6,7},{7,6},{8,9},{9,8},{10,11... | collective-permute-start | bytes 614408 | tf_op jit(solution)/shard_map/ppermute | solution.py:396
  24.7 1.3 copy-start.4
  24.7 1.3 copy-start.14
  24.8 1.2 copy-start.15
  25.7 0.7 copy-start.16
  25.9 0.7 copy-start.17
  26.6 19.0 %copy-start = (bf16[6400,256]{1,0:T(8,128)(2,1)S(1)}, bf16[6400,256]{1,0:T(8,128)(2,1)}, u32[]{:S(2)}) copy-start(bf16[6400,256]{1,0:T(8,128)(2,1)} %weight_ref.1) | copy-start | bytes 9830404
  26.6 19.0 %copy-start.2 = (bf16[32,3200]{1,0:T(8,128)(2,1)S(1)}, bf16[32,3200]{1,0:T(8,128)(2,1)}, u32[]{:S(2)}) copy-start(bf16[32,3200]{1,0:T(8,128)(2,1)} %fo_ref.1) | copy-start | bytes 614404
  26.6 19.0 %copy-start.6 = (f32[32,256]{1,0:T(8,128)S(1)}, f32[32,256]{1,0:T(8,128)}, u32[]{:S(2)}) copy-start(f32[32,256]{1,0:T(8,128)} %target_ref.1) | copy-start | bytes 98308
  26.6 19.0 %copy-start.8 = (s32[4]{0:T(128)S(1)}, s32[4]{0:T(128)}, u32[]{:S(2)}) copy-start(s32[4]{0:T(128)} %orbitals_ref.1) | copy-start | bytes 52
  26.7 19.0 %copy-start.9 = (s32[32]{0:T(128)S(1)}, s32[32]{0:T(128)}, u32[]{:S(2)}) copy-start(s32[32]{0:T(128)} %param.24) | copy-start | bytes 388
  43.6 2.0 %collective-permute-start.9 = (bf16[32,6400]{1,0:T(8,128)(2,1)}, bf16[32,6400]{1,0:T(8,128)(2,1)S(1)}, u32[]{:S(2)}, u32[]{:S(2)}) collective-permute-start(bf16[32,6400]{1,0:T(8,128)(2,1)} %messages.1.mine_ref), channel_id=1, source_target_pairs={{0,1},{1,0},{2,3},{3,2},{4,5},{5,4},{6,7},{7,6},{8,9},{9,8},{10,11... | collective-permute-start | bytes 1228808 | tf_op jit(solution)/shard_map/ppermute | solution.py:396
  45.7 1.0 copy-start.3
  46.7 0.9 copy-start.5
  75.1 16.1 %collective-permute-start.14 = (bf16[32,3200]{1,0:T(8,128)(2,1)S(1)}, bf16[32,3200]{1,0:T(8,128)(2,1)S(1)}, u32[]{:S(2)}, u32[]{:S(2)}) collective-permute-start(bf16[32,3200]{1,0:T(8,128)(2,1)S(1)} %get-tuple-element.58), channel_id=1, source_target_pairs={{0,1},{1,0},{2,3},{3,2},{4,5},{5,4},{6,7},{7,6},{8,9},{9,8},{10,11... | collective-permute-start | bytes 614408 | tf_op jit(solution)/shard_map/ppermute | solution.py:396
  75.4 12.5 %collective-permute-start.12 = (bf16[200,256]{1,0:T(8,128)(2,1)S(1)}, bf16[200,256]{1,0:T(8,128)(2,1)S(1)}, u32[]{:S(2)}, u32[]{:S(2)}) collective-permute-start(bf16[200,256]{1,0:T(8,128)(2,1)S(1)} %partial_grad.1), channel_id=1, source_target_pairs={{0,128},{64,192},{128,0},{192,64},{1,129},{65,193},{129,1},{193,65... | collective-permute-start | bytes 307208 | tf_op jit(solution)/shard_map/ppermute | solution.py:396
  80.9 8.5 %collective-permute-start.11 = (bf16[200,256]{1,0:T(8,128)(2,1)S(1)}, bf16[200,256]{1,0:T(8,128)(2,1)S(1)}, u32[]{:S(2)}, u32[]{:S(2)}) collective-permute-start(bf16[200,256]{1,0:T(8,128)(2,1)S(1)} %partial_grad.1), channel_id=1, source_target_pairs={{0,192},{64,0},{128,64},{192,128},{1,193},{65,1},{129,65},{193,129... | collective-permute-start | bytes 307208 | tf_op jit(solution)/shard_map/ppermute | solution.py:396
  82.4 8.8 %collective-permute-start.10 = (bf16[200,256]{1,0:T(8,128)(2,1)S(1)}, bf16[200,256]{1,0:T(8,128)(2,1)S(1)}, u32[]{:S(2)}, u32[]{:S(2)}) collective-permute-start(bf16[200,256]{1,0:T(8,128)(2,1)S(1)} %partial_grad.1), channel_id=1, source_target_pairs={{0,64},{64,128},{128,192},{192,0},{1,65},{65,129},{129,193},{193,1... | collective-permute-start | bytes 307208 | tf_op jit(solution)/shard_map/ppermute | solution.py:396
  83.9 1.2 collective-permute-start.13
  91.3 4.9 %collective-permute-start.15 = (bf16[200,256]{1,0:T(8,128)(2,1)S(1)}, bf16[200,256]{1,0:T(8,128)(2,1)S(1)}, u32[]{:S(2)}, u32[]{:S(2)}) collective-permute-start(bf16[200,256]{1,0:T(8,128)(2,1)S(1)} %add_convert_fusion), channel_id=1, source_target_pairs={{0,32},{32,0},{1,33},{33,1},{2,34},{34,2},{3,35},{35,3},{4,36},{36... | collective-permute-start | bytes 307208 | tf_op jit(solution)/shard_map/ppermute | solution.py:396
  96.2 7.0 %collective-permute-start.16 = (bf16[400,256]{1,0:T(8,128)(2,1)S(1)}, bf16[400,256]{1,0:T(8,128)(2,1)S(1)}, u32[]{:S(2)}, u32[]{:S(2)}) collective-permute-start(bf16[400,256]{1,0:T(8,128)(2,1)S(1)} %pad_maximum_fusion.1), channel_id=1, source_target_pairs={{0,2},{1,9},{2,4},{3,11},{4,6},{5,13},{6,0},{7,15},{8,10},{9,17},{... | collective-permute-start | bytes 614408 | tf_op jit(solution)/shard_map/ppermute | solution.py:407
  97.2 9.1 %collective-permute-start.19 = (bf16[400,256]{1,0:T(8,128)(2,1)S(1)}, bf16[400,256]{1,0:T(8,128)(2,1)S(1)}, u32[]{:S(2)}, u32[]{:S(2)}) collective-permute-start(bf16[400,256]{1,0:T(8,128)(2,1)S(1)} %pad_maximum_fusion.1), channel_id=1, source_target_pairs={{0,4},{1,17},{2,6},{3,19},{4,0},{5,21},{6,2},{7,23},{8,12},{9,25},... | collective-permute-start | bytes 614408 | tf_op jit(solution)/shard_map/ppermute | solution.py:407
  99.7 6.6 %collective-permute-start.20 = (bf16[400,256]{1,0:T(8,128)(2,1)S(1)}, bf16[400,256]{1,0:T(8,128)(2,1)S(1)}, u32[]{:S(2)}, u32[]{:S(2)}) collective-permute-start(bf16[400,256]{1,0:T(8,128)(2,1)S(1)} %pad_maximum_fusion.1), channel_id=1, source_target_pairs={{0,6},{1,25},{2,0},{3,27},{4,2},{5,29},{6,4},{7,31},{8,14},{9,1},{... | collective-permute-start | bytes 614408 | tf_op jit(solution)/shard_map/ppermute | solution.py:407
  103.3 11.6 %collective-permute-start.17 = (bf16[800,256]{1,0:T(8,128)(2,1)S(1)}, bf16[800,256]{1,0:T(8,128)(2,1)S(1)}, u32[]{:S(2)}, u32[]{:S(2)}) collective-permute-start(bf16[800,256]{1,0:T(8,128)(2,1)S(1)} %pad_maximum_fusion.refs_0_), channel_id=1, source_target_pairs={{0,8},{1,3},{2,10},{3,5},{4,12},{5,7},{6,14},{7,1},{8,16},{9,11},{... | collective-permute-start | bytes 1228808 | tf_op jit(solution)/shard_map/ppermute | solution.py:407
  106.4 8.5 %collective-permute-start.21 = (bf16[800,256]{1,0:T(8,128)(2,1)S(1)}, bf16[800,256]{1,0:T(8,128)(2,1)S(1)}, u32[]{:S(2)}, u32[]{:S(2)}) collective-permute-start(bf16[800,256]{1,0:T(8,128)(2,1)S(1)} %constant_dynamic-update-slice_fusion.refs_1_), channel_id=1, source_target_pairs={{0,24},{1,7},{2,26},{3,1},{4,28},{5,3},{6,30},{7,5},{8,0},{9,15},{... | collective-permute-start | bytes 1228808 | tf_op jit(solution)/shard_map/ppermute | solution.py:407
  109.4 10.4 %collective-permute-start.24 = (bf16[800,256]{1,0:T(8,128)(2,1)S(1)}, bf16[800,256]{1,0:T(8,128)(2,1)S(1)}, u32[]{:S(2)}, u32[]{:S(2)}) collective-permute-start(bf16[800,256]{1,0:T(8,128)(2,1)S(1)} %pad_maximum_fusion.refs_0_), channel_id=1, source_target_pairs={{0,24},{1,7},{2,26},{3,1},{4,28},{5,3},{6,30},{7,5},{8,0},{9,15},{... | collective-permute-start | bytes 1228808 | tf_op jit(solution)/shard_map/ppermute | solution.py:407
  111.2 9.2 %collective-permute-start.23 = (bf16[800,256]{1,0:T(8,128)(2,1)S(1)}, bf16[800,256]{1,0:T(8,128)(2,1)S(1)}, u32[]{:S(2)}, u32[]{:S(2)}) collective-permute-start(bf16[800,256]{1,0:T(8,128)(2,1)S(1)} %constant_dynamic-update-slice_fusion.refs_1_), channel_id=1, source_target_pairs={{0,8},{1,3},{2,10},{3,5},{4,12},{5,7},{6,14},{7,1},{8,16},{9,11},{... | collective-permute-start | bytes 1228808 | tf_op jit(solution)/shard_map/ppermute | solution.py:407
  114.9 9.9 %collective-permute-start.18 = (bf16[800,256]{1,0:T(8,128)(2,1)S(1)}, bf16[800,256]{1,0:T(8,128)(2,1)S(1)}, u32[]{:S(2)}, u32[]{:S(2)}) collective-permute-start(bf16[800,256]{1,0:T(8,128)(2,1)S(1)} %collective-permute-done.17.refs_2_), channel_id=1, source_target_pairs={{0,8},{1,3},{2,10},{3,5},{4,12},{5,7},{6,14},{7,1},{8,16},{9,11},{... | collective-permute-start | bytes 1228808 | tf_op jit(solution)/shard_map/ppermute | solution.py:407
  114.9 9.9 %collective-permute-start.22 = (bf16[800,256]{1,0:T(8,128)(2,1)S(1)}, bf16[800,256]{1,0:T(8,128)(2,1)S(1)}, u32[]{:S(2)}, u32[]{:S(2)}) collective-permute-start(bf16[800,256]{1,0:T(8,128)(2,1)S(1)} %collective-permute-done.21.refs_5_), channel_id=1, source_target_pairs={{0,24},{1,7},{2,26},{3,1},{4,28},{5,3},{6,30},{7,5},{8,0},{9,15},{... | collective-permute-start | bytes 1228808 | tf_op jit(solution)/shard_map/ppermute | solution.py:407

commit v5 on v4

--- a/solution.py
+++ b/solution.py
@@ -158,7 +158,7 @@
 
     for move in moves:
         move.wait()
-    lax.fori_loop(0, 2 * half // step, gather, 0)
+    lax.fori_loop(0, 2 * half // step, gather, 0, unroll=10)
 
     groups = 2 * half // 400
 
@@ -184,7 +184,7 @@
         return 0
 
     frame.wait()
-    lax.fori_loop(0, groups * (edges // 128), rotate_in, 0)
+    lax.fori_loop(0, groups * (edges // 128), rotate_in, 0, unroll=4)
 
     for nb in range(4):
         xb0[:, nb * 128 : (nb + 1) * 128] = z0[nb].astype(BF16)
@@ -200,7 +200,7 @@
 
     for mix in mixes:
         mix.wait()
-    lax.fori_loop(0, 2, mix_zero, 0)
+    lax.fori_loop(0, 2, mix_zero, 0, unroll=True)
 
     def mix_pair(mix_ref, xb, z):
         def part(n, _):
@@ -214,7 +214,7 @@
             z[2 * n + 5] = y[:, 128:]
             return 0
 
-        lax.fori_loop(0, 2, part, 0)
+        lax.fori_loop(0, 2, part, 0, unroll=True)
 
     mix_pair(mix1_ref, xb1, z1)
     mix_pair(mix2_ref, xb2, z2)
@@ -257,7 +257,7 @@
         out_ref[:, pl.ds(at, step)] = dot(scatter, msgs, 1, 1).astype(BF16)
         return 0
 
-    lax.fori_loop(0, 2 * half // step, aggregate, 0)
+    lax.fori_loop(0, 2 * half // step, aggregate, 0, unroll=5)
 
 
 def messages(core, prepared, own, oth):

time: 127 us -> 123 us (0.969)
  Pallas kernels: 28.1 us -> 23.9 us
    pallas_call x1, Pallas kernels: 16.9 us -> 12.7 us  [messages(): pl.pallas_call(message_kernel, out_shape=jax.ShapeDtypeStruct((atoms, 2 *...]
where the time goes in v5:
time: 123 us; the launch traced here: 122 us
  starting transfers between devices  36.7 us (30%)
  waiting for transfers between devices  30.4 us (25%)
  blocking collectives  24.3 us (20%)
  Pallas kernels  23.9 us (19%)
  local copies, waits for them, and re-layouts  4.25 us (3%)
  other arithmetic  1.6 us (1%)
    all_to_all x1, blocking collectives, body(): got = lax.all_to_all(load, GROUP, split_axis=0, concat_axis=0, tiled=True)  24.3 us
    ppermute x16, waiting for transfers between devices, shift(): return lax.ppermute(x, axis, [(i, (i + by) % count) for i in range(count)])  21.6 us
    ppermute x16, starting transfers between devices, shift(): return lax.ppermute(x, axis, [(i, (i + by) % count) for i in range(count)])  20.5 us
    ppermute x9, starting transfers between devices, plane_shift(): return lax.ppermute(x, ('y', 'x', 'chan'), pairs)  16.3 us
    pallas_call x1, Pallas kernels, messages(): pl.pallas_call(message_kernel, out_shape=jax.ShapeDtypeStruct((atoms, 2 *...  12.7 us
    ppermute x9, waiting for transfers between devices, plane_shift(): return lax.ppermute(x, ('y', 'x', 'chan'), pairs)  8.76 us
    unnamed x37, local copies, waits for them, and re-layouts  4.23 us
    pallas_call x1, Pallas kernels, prepare(): pl.pallas_call(prepare_kernel, out_shape=(frames, frames, jax.ShapeDtypeS...  3.96 us
  transfers between devices with their start and end apart: 25, of which 15 were waited for; matrix products, arithmetic and copies ran while one was open for 1% of the time, Pallas kernels for 5%

profile of v5, /device:TPU:32, one launch (start us, length us, event | category | flops | bytes accessed | tf_op | source)
XLA Modules:
  0.0 122.2 jit_solution(3806190561069393592)
XLA Ops:
  0.6 0.0 copy-start.1
  0.6 0.9 copy-done.1
  1.6 0.7 copy-done.7
  2.2 0.5 leaving.1
  2.7 1.6 %collective-permute-start.1 = (bf16[32,3200]{1,0:T(8,128)(2,1)S(1)}, bf16[32,3200]{1,0:T(8,128)(2,1)S(1)}, u32[]{:S(2)}, u32[]{:S(2)}) collective-permute-start(bf16[32,3200]{1,0:T(8,128)(2,1)S(1)} %get-tuple-element.49), channel_id=1, source_target_pairs={{0,2},{2,4},{4,6},{6,8},{8,10},{10,12},{12,14},{14,16},{16,18},{18... | collective-permute-start | bytes 614408 | tf_op jit(solution)/shard_map/ppermute | solution.py:396
  4.3 2.7 %collective-permute-start.2 = (bf16[32,3200]{1,0:T(8,128)(2,1)S(1)}, bf16[32,3200]{1,0:T(8,128)(2,1)S(1)}, u32[]{:S(2)}, u32[]{:S(2)}) collective-permute-start(bf16[32,3200]{1,0:T(8,128)(2,1)S(1)} %get-tuple-element.50), channel_id=1, source_target_pairs={{0,4},{2,6},{4,8},{6,10},{8,12},{10,14},{12,16},{14,18},{16,20},{1... | collective-permute-start | bytes 614408 | tf_op jit(solution)/shard_map/ppermute | solution.py:396
  7.0 4.4 %collective-permute-start.3 = (bf16[32,3200]{1,0:T(8,128)(2,1)S(1)}, bf16[32,3200]{1,0:T(8,128)(2,1)S(1)}, u32[]{:S(2)}, u32[]{:S(2)}) collective-permute-start(bf16[32,3200]{1,0:T(8,128)(2,1)S(1)} %get-tuple-element.51), channel_id=1, source_target_pairs={{0,254},{2,0},{4,2},{6,4},{8,6},{10,8},{12,10},{14,12},{16,14},{18... | collective-permute-start | bytes 614408 | tf_op jit(solution)/shard_map/ppermute | solution.py:396
  11.5 0.5 collective-permute-start.4
  12.0 4.0 %prepare.1 = (f32[2,115,8,128]{3,2,1,0:T(8,128)}, f32[2,115,8,128]{3,2,1,0:T(8,128)}, bf16[160,256]{1,0:T(8,128)(2,1)}, bf16[32,256]{1,0:T(8,128)(2,1)}, bf16[64...) custom-call(s32[1,256]{1,0:T(1,128)} %bitcast.13, s32[1,256]{1,0:T(1,128)} %bitcast.14, ...), custom_call_target="tpu_custom_call" | custom-call | flops 100000000 | bytes 10000000 | tf_op jit(solution)/shard_map/prepare/pallas_call | solution.py:93
  15.9 0.1 collective-permute-start
  16.0 1.1 collective-permute-done.1.ho0_ref
  17.1 0.0 collective-permute-start.5
  17.2 1.1 collective-permute-done.2.ho1_ref
  18.2 6.0 %collective-permute-done.3.ho2_ref = bf16[32,3200]{1,0:T(8,128)(2,1)S(1)} collective-permute-done((bf16[32,3200]{1,0:T(8,128)(2,1)S(1)}, bf16[32,3200]{1,0:T(8,128)(2,1)S(1)}, u32[]{:S(2)}, u32[]{:S(2)}) %collective-permute-start.3) | collective-permute-done | bytes 204832 | tf_op jit(solution)/shard_map/ppermute | solution.py:396
  24.2 0.0 collective-permute-start.7
  24.2 0.5 collective-permute-start.8
  24.7 0.0 collective-permute-done.fx_ref
  24.7 0.0 collective-permute-done.5.hx0_ref
  24.8 0.9 collective-permute-done.7.hx2_ref
  25.7 0.3 collective-permute-done.8.hx3_ref
  26.0 0.3 copy-done.16
  26.3 0.3 copy-done.17
  26.7 0.0 copy-start.9
  26.7 12.7 %messages.1.mine_ref = bf16[32,6400]{1,0:T(8,128)(2,1)} custom-call(s32[1]{0:T(128)} %bitcast.core_ref, f32[2,115,8,128]{3,2,1,0:T(8,128)} %get-tuple-element.42.frames_hbm, f32[2,115,8,128]{3,2,1,0:T(8,128)} %get-tuple-element.43.wframes_hbm, bf16[160,256]{1,0:T(8,128)(2,1)} %get-tuple-element.44.onehot_hbm, bf16[32,256]{1,0:T(8,128)(2,1)} %get-tuple-element.45.scatter_hbm, ...), custom_call_target="tpu_custom_call" | custom-call | flops 5000000000 | bytes 6000000 | tf_op jit(solution)/shard_map/messages/pallas_call | solution.py:267
  39.3 0.5 collective-permute-start.9
  39.8 1.7 %collective-permute-done.9.recv_ref = bf16[32,6400]{1,0:T(8,128)(2,1)S(1)} collective-permute-done((bf16[32,6400]{1,0:T(8,128)(2,1)}, bf16[32,6400]{1,0:T(8,128)(2,1)S(1)}, u32[]{:S(2)}, u32[]{:S(2)}) %collective-permute-start.9) | collective-permute-done | bytes 409632 | tf_op jit(solution)/shard_map/ppermute | solution.py:396
  41.6 1.0 copy-done.3
  42.6 0.9 copy-done.5
  43.5 2.9 %head.1 = (bf16[32,32,512]{2,1,0:T(8,128)(2,1)S(1)}, f32[32,1]{1,0:T(8,128)S(1)}, f32[32,3200]{1,0:T(8,128)S(1)}, bf16[32,3200]{1,0:T(8,128)(2,1)S(1)}) custom-call(s32[1]{0:T(128)} %bitcast.core_ref, s32[4]{0:T(128)S(1)} %copy-done.8, s32[1,32]{1,0:T(1,128)S(1)} %bitcast.11, bf16[32,3200]{1,0:T(8,128)(2,1)S(1)} %copy-done.2, ...), custom_call_target="tpu_custom_call" | custom-call | flops 300000000 | bytes 6000000 | tf_op jit(solution)/shard_map/head/pallas_call | solution.py:333
  46.4 24.3 %all_to_all.5 = bf16[32,32,512]{2,1,0:T(8,128)(2,1)S(1)} all-to-all(bf16[32,32,512]{2,1,0:T(8,128)(2,1)S(1)} %get-tuple-element.53), channel_id=1, replica_groups=mesh['zh'=4,'zl'=2,'y'=4,'x'=4,'chan'=2] {'zl','y','x'}, dimensions={0} | all-to-all | bytes 2097152 | tf_op jit(solution)/shard_map/all_to_all | solution.py:471
  70.7 0.3 partial_grad.1
  71.0 0.1 collective-permute-start.14
  71.1 5.5 %collective-permute-start.12 = (bf16[200,256]{1,0:T(8,128)(2,1)S(1)}, bf16[200,256]{1,0:T(8,128)(2,1)S(1)}, u32[]{:S(2)}, u32[]{:S(2)}) collective-permute-start(bf16[200,256]{1,0:T(8,128)(2,1)S(1)} %partial_grad.1), channel_id=1, source_target_pairs={{0,128},{64,192},{128,0},{192,64},{1,129},{65,193},{129,1},{193,65... | collective-permute-start | bytes 307208 | tf_op jit(solution)/shard_map/ppermute | solution.py:396
  76.6 1.6 %collective-permute-start.11 = (bf16[200,256]{1,0:T(8,128)(2,1)S(1)}, bf16[200,256]{1,0:T(8,128)(2,1)S(1)}, u32[]{:S(2)}, u32[]{:S(2)}) collective-permute-start(bf16[200,256]{1,0:T(8,128)(2,1)S(1)} %partial_grad.1), channel_id=1, source_target_pairs={{0,192},{64,0},{128,64},{192,128},{1,193},{65,1},{129,65},{193,129... | collective-permute-start | bytes 307208 | tf_op jit(solution)/shard_map/ppermute | solution.py:396
  78.2 1.3 %collective-permute-start.10 = (bf16[200,256]{1,0:T(8,128)(2,1)S(1)}, bf16[200,256]{1,0:T(8,128)(2,1)S(1)}, u32[]{:S(2)}, u32[]{:S(2)}) collective-permute-start(bf16[200,256]{1,0:T(8,128)(2,1)S(1)} %partial_grad.1), channel_id=1, source_target_pairs={{0,64},{64,128},{128,192},{192,0},{1,65},{65,129},{129,193},{193,1... | collective-permute-start | bytes 307208 | tf_op jit(solution)/shard_map/ppermute | solution.py:396
  79.5 0.1 reduce
  79.6 0.1 collective-permute-start.13
  79.7 1.1 collective-permute-done.13
  80.8 2.8 %collective-permute-done.12 = bf16[200,256]{1,0:T(8,128)(2,1)S(1)} collective-permute-done((bf16[200,256]{1,0:T(8,128)(2,1)S(1)}, bf16[200,256]{1,0:T(8,128)(2,1)S(1)}, u32[]{:S(2)}, u32[]{:S(2)}) %collective-permute-start.12) | collective-permute-done | bytes 102432 | tf_op jit(solution)/shard_map/ppermute | solution.py:396
  83.7 1.4 %collective-permute-done.11 = bf16[200,256]{1,0:T(8,128)(2,1)S(1)} collective-permute-done((bf16[200,256]{1,0:T(8,128)(2,1)S(1)}, bf16[200,256]{1,0:T(8,128)(2,1)S(1)}, u32[]{:S(2)}, u32[]{:S(2)}) %collective-permute-start.11) | collective-permute-done | bytes 102432 | tf_op jit(solution)/shard_map/ppermute | solution.py:396
  85.1 1.9 %collective-permute-done.10 = bf16[200,256]{1,0:T(8,128)(2,1)S(1)} collective-permute-done((bf16[200,256]{1,0:T(8,128)(2,1)S(1)}, bf16[200,256]{1,0:T(8,128)(2,1)S(1)}, u32[]{:S(2)}, u32[]{:S(2)}) %collective-permute-start.10) | collective-permute-done | bytes 102432 | tf_op jit(solution)/shard_map/ppermute | solution.py:396
  87.0 0.0 collective-permute-done.14
  87.0 0.1 add_convert_fusion
  87.0 1.6 %collective-permute-start.15 = (bf16[200,256]{1,0:T(8,128)(2,1)S(1)}, bf16[200,256]{1,0:T(8,128)(2,1)S(1)}, u32[]{:S(2)}, u32[]{:S(2)}) collective-permute-start(bf16[200,256]{1,0:T(8,128)(2,1)S(1)} %add_convert_fusion), channel_id=1, source_target_pairs={{0,32},{32,0},{1,33},{33,1},{2,34},{34,2},{3,35},{35,3},{4,36},{36... | collective-permute-start | bytes 307208 | tf_op jit(solution)/shard_map/ppermute | solution.py:396
  88.6 3.3 %collective-permute-done.15 = bf16[200,256]{1,0:T(8,128)(2,1)S(1)} collective-permute-done((bf16[200,256]{1,0:T(8,128)(2,1)S(1)}, bf16[200,256]{1,0:T(8,128)(2,1)S(1)}, u32[]{:S(2)}, u32[]{:S(2)}) %collective-permute-start.15) | collective-permute-done | bytes 102432 | tf_op jit(solution)/shard_map/ppermute | solution.py:396
  92.0 1.0 collective-permute-start.16
  93.0 2.5 %collective-permute-start.19 = (bf16[400,256]{1,0:T(8,128)(2,1)S(1)}, bf16[400,256]{1,0:T(8,128)(2,1)S(1)}, u32[]{:S(2)}, u32[]{:S(2)}) collective-permute-start(bf16[400,256]{1,0:T(8,128)(2,1)S(1)} %pad_maximum_fusion.1), channel_id=1, source_target_pairs={{0,4},{1,17},{2,6},{3,19},{4,0},{5,21},{6,2},{7,23},{8,12},{9,25},... | collective-permute-start | bytes 614408 | tf_op jit(solution)/shard_map/ppermute | solution.py:407
  95.5 1.2 collective-permute-start.20
  96.7 2.3 %collective-permute-done.16 = bf16[400,256]{1,0:T(8,128)(2,1)S(1)} collective-permute-done((bf16[400,256]{1,0:T(8,128)(2,1)S(1)}, bf16[400,256]{1,0:T(8,128)(2,1)S(1)}, u32[]{:S(2)}, u32[]{:S(2)}) %collective-permute-start.16) | collective-permute-done | bytes 204832 | tf_op jit(solution)/shard_map/ppermute | solution.py:407
  99.0 3.0 %collective-permute-start.17 = (bf16[800,256]{1,0:T(8,128)(2,1)S(1)}, bf16[800,256]{1,0:T(8,128)(2,1)S(1)}, u32[]{:S(2)}, u32[]{:S(2)}) collective-permute-start(bf16[800,256]{1,0:T(8,128)(2,1)S(1)} %pad_maximum_fusion.refs_0_), channel_id=1, source_target_pairs={{0,8},{1,3},{2,10},{3,5},{4,12},{5,7},{6,14},{7,1},{8,16},{9,11},{... | collective-permute-start | bytes 1228808 | tf_op jit(solution)/shard_map/ppermute | solution.py:407
  102.1 0.0 collective-permute-done.19
  102.1 0.0 collective-permute-done.20
  102.1 2.9 %collective-permute-start.21 = (bf16[800,256]{1,0:T(8,128)(2,1)S(1)}, bf16[800,256]{1,0:T(8,128)(2,1)S(1)}, u32[]{:S(2)}, u32[]{:S(2)}) collective-permute-start(bf16[800,256]{1,0:T(8,128)(2,1)S(1)} %constant_dynamic-update-slice_fusion.refs_1_), channel_id=1, source_target_pairs={{0,24},{1,7},{2,26},{3,1},{4,28},{5,3},{6,30},{7,5},{8,0},{9,15},{... | collective-permute-start | bytes 1228808 | tf_op jit(solution)/shard_map/ppermute | solution.py:407
  105.1 0.1 pad_add_fusion.place_ref
  105.1 1.8 %collective-permute-start.24 = (bf16[800,256]{1,0:T(8,128)(2,1)S(1)}, bf16[800,256]{1,0:T(8,128)(2,1)S(1)}, u32[]{:S(2)}, u32[]{:S(2)}) collective-permute-start(bf16[800,256]{1,0:T(8,128)(2,1)S(1)} %pad_maximum_fusion.refs_0_), channel_id=1, source_target_pairs={{0,24},{1,7},{2,26},{3,1},{4,28},{5,3},{6,30},{7,5},{8,0},{9,15},{... | collective-permute-start | bytes 1228808 | tf_op jit(solution)/shard_map/ppermute | solution.py:407
  107.0 0.2 collective-permute-start.23
  107.2 3.5 %collective-permute-done.17.refs_2_ = bf16[800,256]{1,0:T(8,128)(2,1)S(1)} collective-permute-done((bf16[800,256]{1,0:T(8,128)(2,1)S(1)}, bf16[800,256]{1,0:T(8,128)(2,1)S(1)}, u32[]{:S(2)}, u32[]{:S(2)}) %collective-permute-start.17) | collective-permute-done | bytes 409632 | tf_op jit(solution)/shard_map/ppermute | solution.py:407
  110.7 3.5 %collective-permute-start.22 = (bf16[800,256]{1,0:T(8,128)(2,1)S(1)}, bf16[800,256]{1,0:T(8,128)(2,1)S(1)}, u32[]{:S(2)}, u32[]{:S(2)}) collective-permute-start(bf16[800,256]{1,0:T(8,128)(2,1)S(1)} %collective-permute-done.21.refs_5_), channel_id=1, source_target_pairs={{0,24},{1,7},{2,26},{3,1},{4,28},{5,3},{6,30},{7,5},{8,0},{9,15},{... | collective-permute-start | bytes 1228808 | tf_op jit(solution)/shard_map/ppermute | solution.py:407
  114.2 0.8 convert_add_fusion
  115.0 0.5 add.15
  115.5 0.6 collective-permute-done.23.refs_3_
  116.1 2.1 %assemble.2.refs_2_ = bf16[6400,256]{1,0:T(8,128)(2,1)} custom-call(s32[3]{0:T(128)S(1)} %pad_add_fusion.place_ref, bf16[800,256]{1,0:T(8,128)(2,1)S(1)} %pad_maximum_fusion.refs_0_, bf16[800,256]{1,0:T(8,128)(2,1)S(1)} %constant_dynamic-update-slice_fusion.refs_1_, bf16[800,256]{1,0:T(8,128)(2,1)S(1)} %collective-permute-done.17.refs_2_, ...), custom_call_target="tpu_custom_call" | custom-call | tf_op jit(solution)/shard_map/assemble/pallas_call | solution.py:437
  118.2 2.3 %collective-permute-done.18.refs_0_ = bf16[800,256]{1,0:T(8,128)(2,1)S(1)} collective-permute-done((bf16[800,256]{1,0:T(8,128)(2,1)S(1)}, bf16[800,256]{1,0:T(8,128)(2,1)S(1)}, u32[]{:S(2)}, u32[]{:S(2)}) %collective-permute-start.18) | collective-permute-done | bytes 409632 | tf_op jit(solution)/shard_map/ppermute | solution.py:407
  120.5 1.5 %assemble.3 = bf16[6400,256]{1,0:T(8,128)(2,1)} custom-call(s32[3]{0:T(128)S(1)} %pad_add_fusion.place_ref, bf16[800,256]{1,0:T(8,128)(2,1)S(1)} %collective-permute-done.18.refs_0_, bf16[800,256]{1,0:T(8,128)(2,1)S(1)} %collective-permute-done.22.refs_1_, bf16[6400,256]{1,0:T(8,128)(2,1)} %assemble.2.refs_2_), custom_call_target="tpu_custom_call", output_to_operand_aliasing={{}: (3, {})} | custom-call | tf_op jit(solution)/shard_map/assemble/pallas_call | solution.py:437
  (40 shorter events, 0.2 us)
Async XLA Ops:
  0.6 0.9 copy-start.1
  1.6 0.7 copy-start.7
  2.7 14.4 %collective-permute-start.1 = (bf16[32,3200]{1,0:T(8,128)(2,1)S(1)}, bf16[32,3200]{1,0:T(8,128)(2,1)S(1)}, u32[]{:S(2)}, u32[]{:S(2)}) collective-permute-start(bf16[32,3200]{1,0:T(8,128)(2,1)S(1)} %get-tuple-element.49), channel_id=1, source_target_pairs={{0,2},{2,4},{4,6},{6,8},{8,10},{10,12},{12,14},{14,16},{16,18},{18... | collective-permute-start | bytes 614408 | tf_op jit(solution)/shard_map/ppermute | solution.py:396
  4.3 13.9 %collective-permute-start.2 = (bf16[32,3200]{1,0:T(8,128)(2,1)S(1)}, bf16[32,3200]{1,0:T(8,128)(2,1)S(1)}, u32[]{:S(2)}, u32[]{:S(2)}) collective-permute-start(bf16[32,3200]{1,0:T(8,128)(2,1)S(1)} %get-tuple-element.50), channel_id=1, source_target_pairs={{0,4},{2,6},{4,8},{6,10},{8,12},{10,14},{12,16},{14,18},{16,20},{1... | collective-permute-start | bytes 614408 | tf_op jit(solution)/shard_map/ppermute | solution.py:396
  7.0 17.2 %collective-permute-start.3 = (bf16[32,3200]{1,0:T(8,128)(2,1)S(1)}, bf16[32,3200]{1,0:T(8,128)(2,1)S(1)}, u32[]{:S(2)}, u32[]{:S(2)}) collective-permute-start(bf16[32,3200]{1,0:T(8,128)(2,1)S(1)} %get-tuple-element.51), channel_id=1, source_target_pairs={{0,254},{2,0},{4,2},{6,4},{8,6},{10,8},{12,10},{14,12},{16,14},{18... | collective-permute-start | bytes 614408 | tf_op jit(solution)/shard_map/ppermute | solution.py:396
  11.5 12.7 %collective-permute-start.4 = (bf16[32,3200]{1,0:T(8,128)(2,1)S(1)}, bf16[32,3200]{1,0:T(8,128)(2,1)S(1)}, u32[]{:S(2)}, u32[]{:S(2)}) collective-permute-start(bf16[32,3200]{1,0:T(8,128)(2,1)S(1)} %get-tuple-element.52), channel_id=1, source_target_pairs={{0,252},{2,254},{4,0},{6,2},{8,4},{10,6},{12,8},{14,10},{16,12},{1... | collective-permute-start | bytes 614408 | tf_op jit(solution)/shard_map/ppermute | solution.py:396
  15.9 8.8 %collective-permute-start = (bf16[32,3200]{1,0:T(8,128)(2,1)}, bf16[32,3200]{1,0:T(8,128)(2,1)S(1)}, u32[]{:S(2)}, u32[]{:S(2)}) collective-permute-start(bf16[32,3200]{1,0:T(8,128)(2,1)} %fo_ref.1), channel_id=1, source_target_pairs={{0,1},{1,0},{2,3},{3,2},{4,5},{5,4},{6,7},{7,6},{8,9},{9,8},{10,11... | collective-permute-start | bytes 614408 | tf_op jit(solution)/shard_map/ppermute | solution.py:396
  17.1 8.8 %copy-start.10 = (bf16[32,3200]{1,0:T(8,128)(2,1)}, bf16[32,3200]{1,0:T(8,128)(2,1)S(1)}, u32[]{:S(2)}) copy-start(bf16[32,3200]{1,0:T(8,128)(2,1)S(1)} %collective-permute-done.1.ho0_ref) | copy-start | bytes 614404
  17.1 7.6 %collective-permute-start.5 = (bf16[32,3200]{1,0:T(8,128)(2,1)S(1)}, bf16[32,3200]{1,0:T(8,128)(2,1)S(1)}, u32[]{:S(2)}, u32[]{:S(2)}) collective-permute-start(bf16[32,3200]{1,0:T(8,128)(2,1)S(1)} %collective-permute-done.1.ho0_ref), channel_id=1, source_target_pairs={{0,1},{1,0},{2,3},{3,2},{4,5},{5,4},{6,7},{7,6},{8,9},{9,8},{10,11... | collective-permute-start | bytes 614408 | tf_op jit(solution)/shard_map/ppermute | solution.py:396
  18.2 7.7 %copy-start.11 = (bf16[32,3200]{1,0:T(8,128)(2,1)}, bf16[32,3200]{1,0:T(8,128)(2,1)S(1)}, u32[]{:S(2)}) copy-start(bf16[32,3200]{1,0:T(8,128)(2,1)S(1)} %collective-permute-done.2.ho1_ref) | copy-start | bytes 614404
  18.2 6.5 %collective-permute-start.6 = (bf16[32,3200]{1,0:T(8,128)(2,1)S(1)}, bf16[32,3200]{1,0:T(8,128)(2,1)S(1)}, u32[]{:S(2)}, u32[]{:S(2)}) collective-permute-start(bf16[32,3200]{1,0:T(8,128)(2,1)S(1)} %collective-permute-done.2.ho1_ref), channel_id=1, source_target_pairs={{0,1},{1,0},{2,3},{3,2},{4,5},{5,4},{6,7},{7,6},{8,9},{9,8},{10,11... | collective-permute-start | bytes 614408 | tf_op jit(solution)/shard_map/ppermute | solution.py:396
  24.2 1.8 %copy-start.12 = (bf16[32,3200]{1,0:T(8,128)(2,1)}, bf16[32,3200]{1,0:T(8,128)(2,1)S(1)}, u32[]{:S(2)}) copy-start(bf16[32,3200]{1,0:T(8,128)(2,1)S(1)} %collective-permute-done.3.ho2_ref) | copy-start | bytes 614404
  24.2 1.5 %collective-permute-start.7 = (bf16[32,3200]{1,0:T(8,128)(2,1)S(1)}, bf16[32,3200]{1,0:T(8,128)(2,1)S(1)}, u32[]{:S(2)}, u32[]{:S(2)}) collective-permute-start(bf16[32,3200]{1,0:T(8,128)(2,1)S(1)} %collective-permute-done.3.ho2_ref), channel_id=1, source_target_pairs={{0,1},{1,0},{2,3},{3,2},{4,5},{5,4},{6,7},{7,6},{8,9},{9,8},{10,11... | collective-permute-start | bytes 614408 | tf_op jit(solution)/shard_map/ppermute | solution.py:396
  24.2 1.8 %copy-start.13 = (bf16[32,3200]{1,0:T(8,128)(2,1)}, bf16[32,3200]{1,0:T(8,128)(2,1)S(1)}, u32[]{:S(2)}) copy-start(bf16[32,3200]{1,0:T(8,128)(2,1)S(1)} %collective-permute-done.4.ho3_ref) | copy-start | bytes 614404
  24.2 1.7 %collective-permute-start.8 = (bf16[32,3200]{1,0:T(8,128)(2,1)S(1)}, bf16[32,3200]{1,0:T(8,128)(2,1)S(1)}, u32[]{:S(2)}, u32[]{:S(2)}) collective-permute-start(bf16[32,3200]{1,0:T(8,128)(2,1)S(1)} %collective-permute-done.4.ho3_ref), channel_id=1, source_target_pairs={{0,1},{1,0},{2,3},{3,2},{4,5},{5,4},{6,7},{7,6},{8,9},{9,8},{10,11... | collective-permute-start | bytes 614408 | tf_op jit(solution)/shard_map/ppermute | solution.py:396
  24.7 1.3 %copy-start.4 = (bf16[32,3200]{1,0:T(8,128)(2,1)}, bf16[32,3200]{1,0:T(8,128)(2,1)S(1)}, u32[]{:S(2)}) copy-start(bf16[32,3200]{1,0:T(8,128)(2,1)S(1)} %collective-permute-done.fx_ref) | copy-start | bytes 614404
  24.7 1.3 %copy-start.14 = (bf16[32,3200]{1,0:T(8,128)(2,1)}, bf16[32,3200]{1,0:T(8,128)(2,1)S(1)}, u32[]{:S(2)}) copy-start(bf16[32,3200]{1,0:T(8,128)(2,1)S(1)} %collective-permute-done.5.hx0_ref) | copy-start | bytes 614404
  24.8 1.2 %copy-start.15 = (bf16[32,3200]{1,0:T(8,128)(2,1)}, bf16[32,3200]{1,0:T(8,128)(2,1)S(1)}, u32[]{:S(2)}) copy-start(bf16[32,3200]{1,0:T(8,128)(2,1)S(1)} %collective-permute-done.6.hx1_ref) | copy-start | bytes 614404
  25.7 0.7 copy-start.16
  25.9 0.7 copy-start.17
  26.6 14.9 %copy-start = (bf16[6400,256]{1,0:T(8,128)(2,1)S(1)}, bf16[6400,256]{1,0:T(8,128)(2,1)}, u32[]{:S(2)}) copy-start(bf16[6400,256]{1,0:T(8,128)(2,1)} %weight_ref.1) | copy-start | bytes 9830404
  26.6 14.9 %copy-start.2 = (bf16[32,3200]{1,0:T(8,128)(2,1)S(1)}, bf16[32,3200]{1,0:T(8,128)(2,1)}, u32[]{:S(2)}) copy-start(bf16[32,3200]{1,0:T(8,128)(2,1)} %fo_ref.1) | copy-start | bytes 614404
  26.6 14.9 %copy-start.6 = (f32[32,256]{1,0:T(8,128)S(1)}, f32[32,256]{1,0:T(8,128)}, u32[]{:S(2)}) copy-start(f32[32,256]{1,0:T(8,128)} %target_ref.1) | copy-start | bytes 98308
  26.6 14.9 %copy-start.8 = (s32[4]{0:T(128)S(1)}, s32[4]{0:T(128)}, u32[]{:S(2)}) copy-start(s32[4]{0:T(128)} %orbitals_ref.1) | copy-start | bytes 52
  26.7 14.9 %copy-start.9 = (s32[32]{0:T(128)S(1)}, s32[32]{0:T(128)}, u32[]{:S(2)}) copy-start(s32[32]{0:T(128)} %param.24) | copy-start | bytes 388
  39.3 2.2 %collective-permute-start.9 = (bf16[32,6400]{1,0:T(8,128)(2,1)}, bf16[32,6400]{1,0:T(8,128)(2,1)S(1)}, u32[]{:S(2)}, u32[]{:S(2)}) collective-permute-start(bf16[32,6400]{1,0:T(8,128)(2,1)} %messages.1.mine_ref), channel_id=1, source_target_pairs={{0,1},{1,0},{2,3},{3,2},{4,5},{5,4},{6,7},{7,6},{8,9},{9,8},{10,11... | collective-permute-start | bytes 1228808 | tf_op jit(solution)/shard_map/ppermute | solution.py:396
  41.6 1.0 copy-start.3
  42.6 0.9 copy-start.5
  71.0 15.9 %collective-permute-start.14 = (bf16[32,3200]{1,0:T(8,128)(2,1)S(1)}, bf16[32,3200]{1,0:T(8,128)(2,1)S(1)}, u32[]{:S(2)}, u32[]{:S(2)}) collective-permute-start(bf16[32,3200]{1,0:T(8,128)(2,1)S(1)} %get-tuple-element.58), channel_id=1, source_target_pairs={{0,1},{1,0},{2,3},{3,2},{4,5},{5,4},{6,7},{7,6},{8,9},{9,8},{10,11... | collective-permute-start | bytes 614408 | tf_op jit(solution)/shard_map/ppermute | solution.py:396
  71.1 12.5 %collective-permute-start.12 = (bf16[200,256]{1,0:T(8,128)(2,1)S(1)}, bf16[200,256]{1,0:T(8,128)(2,1)S(1)}, u32[]{:S(2)}, u32[]{:S(2)}) collective-permute-start(bf16[200,256]{1,0:T(8,128)(2,1)S(1)} %partial_grad.1), channel_id=1, source_target_pairs={{0,128},{64,192},{128,0},{192,64},{1,129},{65,193},{129,1},{193,65... | collective-permute-start | bytes 307208 | tf_op jit(solution)/shard_map/ppermute | solution.py:396
  76.6 8.5 %collective-permute-start.11 = (bf16[200,256]{1,0:T(8,128)(2,1)S(1)}, bf16[200,256]{1,0:T(8,128)(2,1)S(1)}, u32[]{:S(2)}, u32[]{:S(2)}) collective-permute-start(bf16[200,256]{1,0:T(8,128)(2,1)S(1)} %partial_grad.1), channel_id=1, source_target_pairs={{0,192},{64,0},{128,64},{192,128},{1,193},{65,1},{129,65},{193,129... | collective-permute-start | bytes 307208 | tf_op jit(solution)/shard_map/ppermute | solution.py:396
  78.2 8.8 %collective-permute-start.10 = (bf16[200,256]{1,0:T(8,128)(2,1)S(1)}, bf16[200,256]{1,0:T(8,128)(2,1)S(1)}, u32[]{:S(2)}, u32[]{:S(2)}) collective-permute-start(bf16[200,256]{1,0:T(8,128)(2,1)S(1)} %partial_grad.1), channel_id=1, source_target_pairs={{0,64},{64,128},{128,192},{192,0},{1,65},{65,129},{129,193},{193,1... | collective-permute-start | bytes 307208 | tf_op jit(solution)/shard_map/ppermute | solution.py:396
  79.6 1.2 collective-permute-start.13
  87.0 4.9 %collective-permute-start.15 = (bf16[200,256]{1,0:T(8,128)(2,1)S(1)}, bf16[200,256]{1,0:T(8,128)(2,1)S(1)}, u32[]{:S(2)}, u32[]{:S(2)}) collective-permute-start(bf16[200,256]{1,0:T(8,128)(2,1)S(1)} %add_convert_fusion), channel_id=1, source_target_pairs={{0,32},{32,0},{1,33},{33,1},{2,34},{34,2},{3,35},{35,3},{4,36},{36... | collective-permute-start | bytes 307208 | tf_op jit(solution)/shard_map/ppermute | solution.py:396
  92.0 7.0 %collective-permute-start.16 = (bf16[400,256]{1,0:T(8,128)(2,1)S(1)}, bf16[400,256]{1,0:T(8,128)(2,1)S(1)}, u32[]{:S(2)}, u32[]{:S(2)}) collective-permute-start(bf16[400,256]{1,0:T(8,128)(2,1)S(1)} %pad_maximum_fusion.1), channel_id=1, source_target_pairs={{0,2},{1,9},{2,4},{3,11},{4,6},{5,13},{6,0},{7,15},{8,10},{9,17},{... | collective-permute-start | bytes 614408 | tf_op jit(solution)/shard_map/ppermute | solution.py:407
  93.0 9.1 %collective-permute-start.19 = (bf16[400,256]{1,0:T(8,128)(2,1)S(1)}, bf16[400,256]{1,0:T(8,128)(2,1)S(1)}, u32[]{:S(2)}, u32[]{:S(2)}) collective-permute-start(bf16[400,256]{1,0:T(8,128)(2,1)S(1)} %pad_maximum_fusion.1), channel_id=1, source_target_pairs={{0,4},{1,17},{2,6},{3,19},{4,0},{5,21},{6,2},{7,23},{8,12},{9,25},... | collective-permute-start | bytes 614408 | tf_op jit(solution)/shard_map/ppermute | solution.py:407
  95.5 6.6 %collective-permute-start.20 = (bf16[400,256]{1,0:T(8,128)(2,1)S(1)}, bf16[400,256]{1,0:T(8,128)(2,1)S(1)}, u32[]{:S(2)}, u32[]{:S(2)}) collective-permute-start(bf16[400,256]{1,0:T(8,128)(2,1)S(1)} %pad_maximum_fusion.1), channel_id=1, source_target_pairs={{0,6},{1,25},{2,0},{3,27},{4,2},{5,29},{6,4},{7,31},{8,14},{9,1},{... | collective-permute-start | bytes 614408 | tf_op jit(solution)/shard_map/ppermute | solution.py:407
  99.0 11.6 %collective-permute-start.17 = (bf16[800,256]{1,0:T(8,128)(2,1)S(1)}, bf16[800,256]{1,0:T(8,128)(2,1)S(1)}, u32[]{:S(2)}, u32[]{:S(2)}) collective-permute-start(bf16[800,256]{1,0:T(8,128)(2,1)S(1)} %pad_maximum_fusion.refs_0_), channel_id=1, source_target_pairs={{0,8},{1,3},{2,10},{3,5},{4,12},{5,7},{6,14},{7,1},{8,16},{9,11},{... | collective-permute-start | bytes 1228808 | tf_op jit(solution)/shard_map/ppermute | solution.py:407
  102.1 8.5 %collective-permute-start.21 = (bf16[800,256]{1,0:T(8,128)(2,1)S(1)}, bf16[800,256]{1,0:T(8,128)(2,1)S(1)}, u32[]{:S(2)}, u32[]{:S(2)}) collective-permute-start(bf16[800,256]{1,0:T(8,128)(2,1)S(1)} %constant_dynamic-update-slice_fusion.refs_1_), channel_id=1, source_target_pairs={{0,24},{1,7},{2,26},{3,1},{4,28},{5,3},{6,30},{7,5},{8,0},{9,15},{... | collective-permute-start | bytes 1228808 | tf_op jit(solution)/shard_map/ppermute | solution.py:407
  105.1 10.4 %collective-permute-start.24 = (bf16[800,256]{1,0:T(8,128)(2,1)S(1)}, bf16[800,256]{1,0:T(8,128)(2,1)S(1)}, u32[]{:S(2)}, u32[]{:S(2)}) collective-permute-start(bf16[800,256]{1,0:T(8,128)(2,1)S(1)} %pad_maximum_fusion.refs_0_), channel_id=1, source_target_pairs={{0,24},{1,7},{2,26},{3,1},{4,28},{5,3},{6,30},{7,5},{8,0},{9,15},{... | collective-permute-start | bytes 1228808 | tf_op jit(solution)/shard_map/ppermute | solution.py:407
  107.0 9.2 %collective-permute-start.23 = (bf16[800,256]{1,0:T(8,128)(2,1)S(1)}, bf16[800,256]{1,0:T(8,128)(2,1)S(1)}, u32[]{:S(2)}, u32[]{:S(2)}) collective-permute-start(bf16[800,256]{1,0:T(8,128)(2,1)S(1)} %constant_dynamic-update-slice_fusion.refs_1_), channel_id=1, source_target_pairs={{0,8},{1,3},{2,10},{3,5},{4,12},{5,7},{6,14},{7,1},{8,16},{9,11},{... | collective-permute-start | bytes 1228808 | tf_op jit(solution)/shard_map/ppermute | solution.py:407
  110.7 9.9 %collective-permute-start.18 = (bf16[800,256]{1,0:T(8,128)(2,1)S(1)}, bf16[800,256]{1,0:T(8,128)(2,1)S(1)}, u32[]{:S(2)}, u32[]{:S(2)}) collective-permute-start(bf16[800,256]{1,0:T(8,128)(2,1)S(1)} %collective-permute-done.17.refs_2_), channel_id=1, source_target_pairs={{0,8},{1,3},{2,10},{3,5},{4,12},{5,7},{6,14},{7,1},{8,16},{9,11},{... | collective-permute-start | bytes 1228808 | tf_op jit(solution)/shard_map/ppermute | solution.py:407
  110.7 9.9 %collective-permute-start.22 = (bf16[800,256]{1,0:T(8,128)(2,1)S(1)}, bf16[800,256]{1,0:T(8,128)(2,1)S(1)}, u32[]{:S(2)}, u32[]{:S(2)}) collective-permute-start(bf16[800,256]{1,0:T(8,128)(2,1)S(1)} %collective-permute-done.21.refs_5_), channel_id=1, source_target_pairs={{0,24},{1,7},{2,26},{3,1},{4,28},{5,3},{6,30},{7,5},{8,0},{9,15},{... | collective-permute-start | bytes 1228808 | tf_op jit(solution)/shard_map/ppermute | solution.py:407

commit v6 on v5

--- a/solution.py
+++ b/solution.py
@@ -14,7 +14,7 @@
 HALO_ORDER = (1, 2, -1, -2)
 BRANCH = 0.125
 PREP_MB = 56
-MSG_MB = 54
+MSG_MB = 52
 GROUP = ("zl", "y", "x")
 ATOMS = ("zh", "zl", "y", "x")
 F32 = jnp.float32
@@ -42,7 +42,7 @@
 
 def prepare_kernel(
     esrc_hbm, edst_hbm, erot_hbm, ew_hbm, rot_hbm, mix0_hbm, mix1_hbm, mix2_hbm,
-    frames, wframes, onehot_ref, scatter_ref, mix0_ref, mix1_ref, mix2_ref,
+    frames, wframes, mix0_ref, mix1_ref, mix2_ref,
     packed, esrc_ref, edst_ref, erot_ref, ew_ref, rot_ref, mix0_in, mix1_in, mix2_in, sems,
 ):
     copies = [
@@ -60,8 +60,12 @@
         copy.wait()
     edges = esrc_ref.shape[1]
 
-    onehot_ref[...] = (esrc_ref[...] == lax.broadcasted_iota(jnp.int32, onehot_ref.shape, 0)).astype(BF16)
-    scatter_ref[...] = (edst_ref[...] == lax.broadcasted_iota(jnp.int32, scatter_ref.shape, 0)).astype(BF16)
+    depth, width = mix0_in.shape
+    atoms = (mix0_ref.shape[0] - depth) // 6
+    mix0_ref[depth:, edges:] = jnp.zeros((6 * atoms, width - edges), BF16)
+    for ids, start, count in ((esrc_ref, depth, 5 * atoms), (edst_ref, depth + 5 * atoms, atoms)):
+        places = lax.broadcasted_iota(jnp.int32, (count, edges), 0)
+        mix0_ref[start : start + count, :edges] = (ids[...] == places).astype(BF16)
 
     rot_count = rot_ref.shape[1]
     picks = (erot_ref[...] == lax.broadcasted_iota(jnp.int32, (rot_count, edges), 0)).astype(BF16)
@@ -79,7 +83,7 @@
 
     for copy in copies[5:]:
         copy.wait()
-    mix0_ref[...] = mix0_in[...].T
+    mix0_ref[:depth, :] = mix0_in[...].T
     for i in range(2):
         mix1_ref[i] = mix1_in[i].T
         mix2_ref[i] = mix2_in[i].T
@@ -92,14 +96,10 @@
     frames = jax.ShapeDtypeStruct((edges // 128, len(SLOTS), 8, 128), F32)
     return pl.pallas_call(
         prepare_kernel,
-        out_shape=(
-            frames, frames,
-            jax.ShapeDtypeStruct((5 * atoms, edges), BF16),
-            jax.ShapeDtypeStruct((atoms, edges), BF16),
-        )
-        + tuple(jax.ShapeDtypeStruct(mix.shape, BF16) for mix in mixes),
+        out_shape=(frames, frames, jax.ShapeDtypeStruct((mixes[0].shape[0] + 6 * atoms, mixes[0].shape[1]), BF16))
+        + tuple(jax.ShapeDtypeStruct(mix.shape, BF16) for mix in mixes[1:]),
         in_specs=[pl.BlockSpec(memory_space=pl.ANY)] * 8,
-        out_specs=(vmem,) * 7,
+        out_specs=(vmem,) * 5,
         scratch_shapes=[pltpu.VMEM((rot_table.shape[0], edges), F32)]
         + [pltpu.VMEM((1, edges), jnp.int32)] * 3
         + [pltpu.VMEM((1, edges), F32), pltpu.VMEM(rot_table.shape, F32)]
@@ -112,25 +112,28 @@
 
 
 def message_kernel(
-    core_ref, frames_hbm, wframes_hbm, onehot_hbm, scatter_hbm, mix0_hbm, mix1_hbm, mix2_hbm,
+    core_ref, frames_hbm, wframes_hbm, mix0_hbm, mix1_hbm, mix2_hbm,
     fo_ref, ho0_ref, ho1_ref, ho2_ref, ho3_ref,
     fx_ref, hx0_ref, hx1_ref, hx2_ref, hx3_ref,
     out_ref,
     rows, nat, z0, z1, z2, xb0, xb1, xb2,
-    frames, wframes, onehot_ref, scatter_ref, mix0_ref, mix1_ref, mix2_ref, sems,
+    frames, wframes, mix0_ref, mix1_ref, mix2_ref, onehot_ref, scatter_ref, sems,
 ):
     core = core_ref[0]
     other = 1 - core
+    depth, edges = mix0_ref.shape[0], onehot_ref.shape[1]
+    pick_rows, place_rows = onehot_ref.shape[0], scatter_ref.shape[0]
     pick, frame, wframe, place, *mixes = [
         pltpu.make_async_copy(src, dst, sems.at[10 + i])
         for i, (src, dst) in enumerate(
             (
-                (onehot_hbm, onehot_ref), (frames_hbm, frames), (wframes_hbm, wframes),
-                (scatter_hbm, scatter_ref), (mix0_hbm, mix0_ref), (mix1_hbm, mix1_ref), (mix2_hbm, mix2_ref),
+                (mix0_hbm.at[pl.ds(depth, pick_rows), pl.ds(0, edges)], onehot_ref),
+                (frames_hbm, frames), (wframes_hbm, wframes),
+                (mix0_hbm.at[pl.ds(depth + pick_rows, place_rows), pl.ds(0, edges)], scatter_ref),
+                (mix0_hbm.at[pl.ds(0, depth), :], mix0_ref), (mix1_hbm, mix1_ref), (mix2_hbm, mix2_ref),
             )
         )
     ]
-    edges = onehot_ref.shape[1]
     atoms, half = fo_ref.shape
 
     moves = []
@@ -261,8 +264,10 @@
 
 
 def messages(core, prepared, own, oth):
-    edges = prepared[2].shape[1]
+    frames, wframes, mix0, mix1, mix2 = prepared
     atoms, half = own[0].shape
+    edges = 128 * frames.shape[0]
+    depth = mix0.shape[0] - 6 * atoms
     vmem = pl.BlockSpec(memory_space=pltpu.VMEM)
     return pl.pallas_call(
         message_kernel,
@@ -280,7 +285,9 @@
             pltpu.VMEM((512, 1024), BF16),
             pltpu.VMEM((384, 1024), BF16),
         ]
-        + [pltpu.VMEM(table.shape, table.dtype) for table in prepared]
+        + [pltpu.VMEM(frames.shape, F32)] * 2
+        + [pltpu.VMEM((depth, depth), BF16), pltpu.VMEM(mix1.shape, BF16), pltpu.VMEM(mix2.shape, BF16)]
+        + [pltpu.VMEM((5 * atoms, edges), BF16), pltpu.VMEM((atoms, edges), BF16)]
         + [pltpu.SemaphoreType.DMA((17,))],
         compiler_params=pltpu.CompilerParams(vmem_limit_bytes=MSG_MB * 1024 * 1024),
         cost_estimate=pl.CostEstimate(flops=5_000_000_000, bytes_accessed=6_000_000, transcendentals=0),

time: 123 us -> 124 us (level)
  Pallas kernels: 23.9 us -> 25.4 us
    pallas_call x1, Pallas kernels: 12.7 us -> 14.2 us  [messages(): pl.pallas_call(message_kernel, out_shape=jax.ShapeDtypeStruct((atoms, 2 *...]
    unnamed x37 -> x19, local copies, waits for them, and re-layouts: 4.23 us -> 4.23 us
where the time goes in v6:
time: 124 us
  starting transfers between devices  36.7 us (30%)
  waiting for transfers between devices  30.4 us (25%)
  Pallas kernels  25.4 us (20%)
  blocking collectives  24.3 us (20%)
  local copies, waits for them, and re-layouts  4.24 us (3%)
  other arithmetic  1.61 us (1%)
    all_to_all x1, blocking collectives, body(): got = lax.all_to_all(load, GROUP, split_axis=0, concat_axis=0, tiled=True)  24.3 us
    ppermute x16, waiting for transfers between devices, shift(): return lax.ppermute(x, axis, [(i, (i + by) % count) for i in range(count)])  21.7 us
    ppermute x16, starting transfers between devices, shift(): return lax.ppermute(x, axis, [(i, (i + by) % count) for i in range(count)])  20.5 us
    ppermute x9, starting transfers between devices, plane_shift(): return lax.ppermute(x, ('y', 'x', 'chan'), pairs)  16.3 us
    pallas_call x1, Pallas kernels, messages(): pl.pallas_call(message_kernel, out_shape=jax.ShapeDtypeStruct((atoms, 2 *...  14.2 us
    ppermute x9, waiting for transfers between devices, plane_shift(): return lax.ppermute(x, ('y', 'x', 'chan'), pairs)  8.78 us
    unnamed x19, local copies, waits for them, and re-layouts  4.23 us
    pallas_call x1, Pallas kernels, prepare(): pl.pallas_call(prepare_kernel, out_shape=(frames, frames, jax.ShapeDtypeS...  4 us
  transfers between devices with their start and end apart: 25, of which 15 were waited for; matrix products, arithmetic and copies ran while one was open for 1% of the time, Pallas kernels for 5%

profile of v6, /device:TPU:32, one launch (start us, length us, event | category | flops | bytes accessed | tf_op | source)
XLA Modules:
  0.0 123.7 jit_solution(14856480628888640361)
XLA Ops:
  0.6 0.0 copy-start.1
  0.6 0.9 copy-done.1
  1.6 0.7 copy-done.5
  2.2 0.5 leaving.1
  2.7 1.6 %collective-permute-start.1 = (bf16[32,3200]{1,0:T(8,128)(2,1)S(1)}, bf16[32,3200]{1,0:T(8,128)(2,1)S(1)}, u32[]{:S(2)}, u32[]{:S(2)}) collective-permute-start(bf16[32,3200]{1,0:T(8,128)(2,1)S(1)} %get-tuple-element.41), channel_id=1, source_target_pairs={{0,2},{2,4},{4,6},{6,8},{8,10},{10,12},{12,14},{14,16},{16,18},{18... | collective-permute-start | bytes 614408 | tf_op jit(solution)/shard_map/ppermute | solution.py:403
  4.3 2.7 %collective-permute-start.2 = (bf16[32,3200]{1,0:T(8,128)(2,1)S(1)}, bf16[32,3200]{1,0:T(8,128)(2,1)S(1)}, u32[]{:S(2)}, u32[]{:S(2)}) collective-permute-start(bf16[32,3200]{1,0:T(8,128)(2,1)S(1)} %get-tuple-element.42), channel_id=1, source_target_pairs={{0,4},{2,6},{4,8},{6,10},{8,12},{10,14},{12,16},{14,18},{16,20},{1... | collective-permute-start | bytes 614408 | tf_op jit(solution)/shard_map/ppermute | solution.py:403
  7.0 4.4 %collective-permute-start.3 = (bf16[32,3200]{1,0:T(8,128)(2,1)S(1)}, bf16[32,3200]{1,0:T(8,128)(2,1)S(1)}, u32[]{:S(2)}, u32[]{:S(2)}) collective-permute-start(bf16[32,3200]{1,0:T(8,128)(2,1)S(1)} %get-tuple-element.43), channel_id=1, source_target_pairs={{0,254},{2,0},{4,2},{6,4},{8,6},{10,8},{12,10},{14,12},{16,14},{18... | collective-permute-start | bytes 614408 | tf_op jit(solution)/shard_map/ppermute | solution.py:403
  11.5 0.5 collective-permute-start.4
  12.0 4.0 %prepare.1 = (f32[2,115,8,128]{3,2,1,0:T(8,128)}, f32[2,115,8,128]{3,2,1,0:T(8,128)}, bf16[832,640]{1,0:T(8,128)(2,1)}, bf16[2,512,512]{2,1,0:T(8,128)(2,1)}, bf16[2,384,384]{2,1,0:T(8,128)(2,1)}) custom-call(s32[1,256]{1,0:T(1,128)} %bitcast.13, s32[1,256]{1,0:T(1,128)} %bitcast.14, s32[1,256]{1,0:T(1,128)} %bitcast.15, f32[1,256]{1,0:T(1,128)} %bitcast.16, ...), custom_call_target="tpu_custom_call" | custom-call | flops 100000000 | bytes 10000000 | tf_op jit(solution)/shard_map/prepare/pallas_call | solution.py:97
  16.0 0.1 collective-permute-start
  16.1 1.1 collective-permute-done.1.ho0_ref
  17.1 0.0 collective-permute-start.5
  17.1 1.1 collective-permute-done.2.ho1_ref
  18.2 0.0 collective-permute-start.6
  18.2 6.0 %collective-permute-done.3.ho2_ref = bf16[32,3200]{1,0:T(8,128)(2,1)S(1)} collective-permute-done((bf16[32,3200]{1,0:T(8,128)(2,1)S(1)}, bf16[32,3200]{1,0:T(8,128)(2,1)S(1)}, u32[]{:S(2)}, u32[]{:S(2)}) %collective-permute-start.3) | collective-permute-done | bytes 204832 | tf_op jit(solution)/shard_map/ppermute | solution.py:403
  24.2 0.0 collective-permute-start.7
  24.2 0.0 collective-permute-done.4.ho3_ref
  24.2 0.5 collective-permute-start.8
  24.7 0.0 collective-permute-done.fx_ref
  24.7 0.9 collective-permute-done.7.hx2_ref
  25.7 0.3 collective-permute-done.8.hx3_ref
  25.9 0.7 copy-done.8
  26.6 0.9 copy-done.2
  27.6 14.2 %messages.1.mine_ref = bf16[32,6400]{1,0:T(8,128)(2,1)} custom-call(s32[1]{0:T(128)} %bitcast.core_ref, f32[2,115,8,128]{3,2,1,0:T(8,128)} %get-tuple-element.36.frames_hbm, f32[2,115,8,128]{3,2,1,0:T(8,128)} %get-tuple-element.37.wframes_hbm, bf16[832,640]{1,0:T(8,128)(2,1)} %get-tuple-element.38.mix0_hbm, bf16[2,512,512]{2,1,0:T(8,128)(2,1)} %get-tuple-element.39.mix1_hbm, ...), custom_call_target="tpu_custom_call" | custom-call | flops 5000000000 | bytes 6000000 | tf_op jit(solution)/shard_map/messages/pallas_call | solution.py:272
  41.7 0.5 collective-permute-start.9
  42.2 1.7 %collective-permute-done.9.recv_ref = bf16[32,6400]{1,0:T(8,128)(2,1)S(1)} collective-permute-done((bf16[32,6400]{1,0:T(8,128)(2,1)}, bf16[32,6400]{1,0:T(8,128)(2,1)S(1)}, u32[]{:S(2)}, u32[]{:S(2)}) %collective-permute-start.9) | collective-permute-done | bytes 409632 | tf_op jit(solution)/shard_map/ppermute | solution.py:403
  44.0 1.0 copy-done.3
  45.0 2.9 %head.1 = (bf16[32,32,512]{2,1,0:T(8,128)(2,1)S(1)}, f32[32,1]{1,0:T(8,128)S(1)}, f32[32,3200]{1,0:T(8,128)S(1)}, bf16[32,3200]{1,0:T(8,128)(2,1)S(1)}) custom-call(s32[1]{0:T(128)} %bitcast.core_ref, s32[4]{0:T(128)S(1)} %copy-done.6, s32[1,32]{1,0:T(1,128)S(1)} %bitcast.11, bf16[32,3200]{1,0:T(8,128)(2,1)S(1)} %copy-done.2, ...), custom_call_target="tpu_custom_call" | custom-call | flops 300000000 | bytes 6000000 | tf_op jit(solution)/shard_map/head/pallas_call | solution.py:340
  47.9 24.3 %all_to_all.5 = bf16[32,32,512]{2,1,0:T(8,128)(2,1)S(1)} all-to-all(bf16[32,32,512]{2,1,0:T(8,128)(2,1)S(1)} %get-tuple-element.45), channel_id=1, replica_groups=mesh['zh'=4,'zl'=2,'y'=4,'x'=4,'chan'=2] {'zl','y','x'}, dimensions={0} | all-to-all | bytes 2097152 | tf_op jit(solution)/shard_map/all_to_all | solution.py:478
  72.2 0.3 partial_grad.1
  72.5 0.1 collective-permute-start.14
  72.6 5.5 %collective-permute-start.12 = (bf16[200,256]{1,0:T(8,128)(2,1)S(1)}, bf16[200,256]{1,0:T(8,128)(2,1)S(1)}, u32[]{:S(2)}, u32[]{:S(2)}) collective-permute-start(bf16[200,256]{1,0:T(8,128)(2,1)S(1)} %partial_grad.1), channel_id=1, source_target_pairs={{0,128},{64,192},{128,0},{192,64},{1,129},{65,193},{129,1},{193,65... | collective-permute-start | bytes 307208 | tf_op jit(solution)/shard_map/ppermute | solution.py:403
  78.1 1.6 %collective-permute-start.11 = (bf16[200,256]{1,0:T(8,128)(2,1)S(1)}, bf16[200,256]{1,0:T(8,128)(2,1)S(1)}, u32[]{:S(2)}, u32[]{:S(2)}) collective-permute-start(bf16[200,256]{1,0:T(8,128)(2,1)S(1)} %partial_grad.1), channel_id=1, source_target_pairs={{0,192},{64,0},{128,64},{192,128},{1,193},{65,1},{129,65},{193,129... | collective-permute-start | bytes 307208 | tf_op jit(solution)/shard_map/ppermute | solution.py:403
  79.7 1.3 %collective-permute-start.10 = (bf16[200,256]{1,0:T(8,128)(2,1)S(1)}, bf16[200,256]{1,0:T(8,128)(2,1)S(1)}, u32[]{:S(2)}, u32[]{:S(2)}) collective-permute-start(bf16[200,256]{1,0:T(8,128)(2,1)S(1)} %partial_grad.1), channel_id=1, source_target_pairs={{0,64},{64,128},{128,192},{192,0},{1,65},{65,129},{129,193},{193,1... | collective-permute-start | bytes 307208 | tf_op jit(solution)/shard_map/ppermute | solution.py:403
  81.0 0.1 reduce
  81.1 0.1 collective-permute-start.13
  81.2 1.1 collective-permute-done.13
  82.3 2.8 %collective-permute-done.12 = bf16[200,256]{1,0:T(8,128)(2,1)S(1)} collective-permute-done((bf16[200,256]{1,0:T(8,128)(2,1)S(1)}, bf16[200,256]{1,0:T(8,128)(2,1)S(1)}, u32[]{:S(2)}, u32[]{:S(2)}) %collective-permute-start.12) | collective-permute-done | bytes 102432 | tf_op jit(solution)/shard_map/ppermute | solution.py:403
  85.1 1.5 %collective-permute-done.11 = bf16[200,256]{1,0:T(8,128)(2,1)S(1)} collective-permute-done((bf16[200,256]{1,0:T(8,128)(2,1)S(1)}, bf16[200,256]{1,0:T(8,128)(2,1)S(1)}, u32[]{:S(2)}, u32[]{:S(2)}) %collective-permute-start.11) | collective-permute-done | bytes 102432 | tf_op jit(solution)/shard_map/ppermute | solution.py:403
  86.6 1.9 %collective-permute-done.10 = bf16[200,256]{1,0:T(8,128)(2,1)S(1)} collective-permute-done((bf16[200,256]{1,0:T(8,128)(2,1)S(1)}, bf16[200,256]{1,0:T(8,128)(2,1)S(1)}, u32[]{:S(2)}, u32[]{:S(2)}) %collective-permute-start.10) | collective-permute-done | bytes 102432 | tf_op jit(solution)/shard_map/ppermute | solution.py:403
  88.5 0.0 collective-permute-done.14
  88.5 0.1 add_convert_fusion
  88.5 1.6 %collective-permute-start.15 = (bf16[200,256]{1,0:T(8,128)(2,1)S(1)}, bf16[200,256]{1,0:T(8,128)(2,1)S(1)}, u32[]{:S(2)}, u32[]{:S(2)}) collective-permute-start(bf16[200,256]{1,0:T(8,128)(2,1)S(1)} %add_convert_fusion), channel_id=1, source_target_pairs={{0,32},{32,0},{1,33},{33,1},{2,34},{34,2},{3,35},{35,3},{4,36},{36... | collective-permute-start | bytes 307208 | tf_op jit(solution)/shard_map/ppermute | solution.py:403
  90.1 3.3 %collective-permute-done.15 = bf16[200,256]{1,0:T(8,128)(2,1)S(1)} collective-permute-done((bf16[200,256]{1,0:T(8,128)(2,1)S(1)}, bf16[200,256]{1,0:T(8,128)(2,1)S(1)}, u32[]{:S(2)}, u32[]{:S(2)}) %collective-permute-start.15) | collective-permute-done | bytes 102432 | tf_op jit(solution)/shard_map/ppermute | solution.py:403
  93.5 1.0 collective-permute-start.16
  94.5 2.5 %collective-permute-start.19 = (bf16[400,256]{1,0:T(8,128)(2,1)S(1)}, bf16[400,256]{1,0:T(8,128)(2,1)S(1)}, u32[]{:S(2)}, u32[]{:S(2)}) collective-permute-start(bf16[400,256]{1,0:T(8,128)(2,1)S(1)} %pad_maximum_fusion.1), channel_id=1, source_target_pairs={{0,4},{1,17},{2,6},{3,19},{4,0},{5,21},{6,2},{7,23},{8,12},{9,25},... | collective-permute-start | bytes 614408 | tf_op jit(solution)/shard_map/ppermute | solution.py:414
  97.0 1.2 collective-permute-start.20
  98.2 2.3 %collective-permute-done.16 = bf16[400,256]{1,0:T(8,128)(2,1)S(1)} collective-permute-done((bf16[400,256]{1,0:T(8,128)(2,1)S(1)}, bf16[400,256]{1,0:T(8,128)(2,1)S(1)}, u32[]{:S(2)}, u32[]{:S(2)}) %collective-permute-start.16) | collective-permute-done | bytes 204832 | tf_op jit(solution)/shard_map/ppermute | solution.py:414
  100.5 3.1 %collective-permute-start.17 = (bf16[800,256]{1,0:T(8,128)(2,1)S(1)}, bf16[800,256]{1,0:T(8,128)(2,1)S(1)}, u32[]{:S(2)}, u32[]{:S(2)}) collective-permute-start(bf16[800,256]{1,0:T(8,128)(2,1)S(1)} %pad_maximum_fusion.refs_0_), channel_id=1, source_target_pairs={{0,8},{1,3},{2,10},{3,5},{4,12},{5,7},{6,14},{7,1},{8,16},{9,11},{... | collective-permute-start | bytes 1228808 | tf_op jit(solution)/shard_map/ppermute | solution.py:414
  103.6 2.9 %collective-permute-start.21 = (bf16[800,256]{1,0:T(8,128)(2,1)S(1)}, bf16[800,256]{1,0:T(8,128)(2,1)S(1)}, u32[]{:S(2)}, u32[]{:S(2)}) collective-permute-start(bf16[800,256]{1,0:T(8,128)(2,1)S(1)} %constant_dynamic-update-slice_fusion.refs_1_), channel_id=1, source_target_pairs={{0,24},{1,7},{2,26},{3,1},{4,28},{5,3},{6,30},{7,5},{8,0},{9,15},{... | collective-permute-start | bytes 1228808 | tf_op jit(solution)/shard_map/ppermute | solution.py:414
  106.5 0.1 pad_add_fusion.place_ref
  106.6 1.9 %collective-permute-start.24 = (bf16[800,256]{1,0:T(8,128)(2,1)S(1)}, bf16[800,256]{1,0:T(8,128)(2,1)S(1)}, u32[]{:S(2)}, u32[]{:S(2)}) collective-permute-start(bf16[800,256]{1,0:T(8,128)(2,1)S(1)} %pad_maximum_fusion.refs_0_), channel_id=1, source_target_pairs={{0,24},{1,7},{2,26},{3,1},{4,28},{5,3},{6,30},{7,5},{8,0},{9,15},{... | collective-permute-start | bytes 1228808 | tf_op jit(solution)/shard_map/ppermute | solution.py:414
  108.5 0.2 collective-permute-start.23
  108.7 3.5 %collective-permute-done.17.refs_2_ = bf16[800,256]{1,0:T(8,128)(2,1)S(1)} collective-permute-done((bf16[800,256]{1,0:T(8,128)(2,1)S(1)}, bf16[800,256]{1,0:T(8,128)(2,1)S(1)}, u32[]{:S(2)}, u32[]{:S(2)}) %collective-permute-start.17) | collective-permute-done | bytes 409632 | tf_op jit(solution)/shard_map/ppermute | solution.py:414
  112.2 0.0 collective-permute-start.18
  112.2 3.5 %collective-permute-start.22 = (bf16[800,256]{1,0:T(8,128)(2,1)S(1)}, bf16[800,256]{1,0:T(8,128)(2,1)S(1)}, u32[]{:S(2)}, u32[]{:S(2)}) collective-permute-start(bf16[800,256]{1,0:T(8,128)(2,1)S(1)} %collective-permute-done.21.refs_5_), channel_id=1, source_target_pairs={{0,24},{1,7},{2,26},{3,1},{4,28},{5,3},{6,30},{7,5},{8,0},{9,15},{... | collective-permute-start | bytes 1228808 | tf_op jit(solution)/shard_map/ppermute | solution.py:414
  115.7 0.8 convert_add_fusion
  116.5 0.5 add.15
  117.0 0.0 collective-permute-done.24.refs_4_
  117.0 0.6 collective-permute-done.23.refs_3_
  117.6 2.1 %assemble.2.refs_2_ = bf16[6400,256]{1,0:T(8,128)(2,1)} custom-call(s32[3]{0:T(128)S(1)} %pad_add_fusion.place_ref, bf16[800,256]{1,0:T(8,128)(2,1)S(1)} %pad_maximum_fusion.refs_0_, bf16[800,256]{1,0:T(8,128)(2,1)S(1)} %constant_dynamic-update-slice_fusion.refs_1_, bf16[800,256]{1,0:T(8,128)(2,1)S(1)} %collective-permute-done.17.refs_2_, ...), custom_call_target="tpu_custom_call" | custom-call | tf_op jit(solution)/shard_map/assemble/pallas_call | solution.py:444
  119.7 2.3 %collective-permute-done.18.refs_0_ = bf16[800,256]{1,0:T(8,128)(2,1)S(1)} collective-permute-done((bf16[800,256]{1,0:T(8,128)(2,1)S(1)}, bf16[800,256]{1,0:T(8,128)(2,1)S(1)}, u32[]{:S(2)}, u32[]{:S(2)}) %collective-permute-start.18) | collective-permute-done | bytes 409632 | tf_op jit(solution)/shard_map/ppermute | solution.py:414
  122.0 0.0 collective-permute-done.22.refs_1_
  122.0 1.5 %assemble.3 = bf16[6400,256]{1,0:T(8,128)(2,1)} custom-call(s32[3]{0:T(128)S(1)} %pad_add_fusion.place_ref, bf16[800,256]{1,0:T(8,128)(2,1)S(1)} %collective-permute-done.18.refs_0_, bf16[800,256]{1,0:T(8,128)(2,1)S(1)} %collective-permute-done.22.refs_1_, bf16[6400,256]{1,0:T(8,128)(2,1)} %assemble.2.refs_2_), custom_call_target="tpu_custom_call", output_to_operand_aliasing={{}: (3, {})} | custom-call | tf_op jit(solution)/shard_map/assemble/pallas_call | solution.py:444
  (22 shorter events, 0.1 us)
Async XLA Ops:
  0.6 0.9 copy-start.1
  1.6 0.7 copy-start.5
  2.7 14.4 %collective-permute-start.1 = (bf16[32,3200]{1,0:T(8,128)(2,1)S(1)}, bf16[32,3200]{1,0:T(8,128)(2,1)S(1)}, u32[]{:S(2)}, u32[]{:S(2)}) collective-permute-start(bf16[32,3200]{1,0:T(8,128)(2,1)S(1)} %get-tuple-element.41), channel_id=1, source_target_pairs={{0,2},{2,4},{4,6},{6,8},{8,10},{10,12},{12,14},{14,16},{16,18},{18... | collective-permute-start | bytes 614408 | tf_op jit(solution)/shard_map/ppermute | solution.py:403
  4.3 13.9 %collective-permute-start.2 = (bf16[32,3200]{1,0:T(8,128)(2,1)S(1)}, bf16[32,3200]{1,0:T(8,128)(2,1)S(1)}, u32[]{:S(2)}, u32[]{:S(2)}) collective-permute-start(bf16[32,3200]{1,0:T(8,128)(2,1)S(1)} %get-tuple-element.42), channel_id=1, source_target_pairs={{0,4},{2,6},{4,8},{6,10},{8,12},{10,14},{12,16},{14,18},{16,20},{1... | collective-permute-start | bytes 614408 | tf_op jit(solution)/shard_map/ppermute | solution.py:403
  7.0 17.2 %collective-permute-start.3 = (bf16[32,3200]{1,0:T(8,128)(2,1)S(1)}, bf16[32,3200]{1,0:T(8,128)(2,1)S(1)}, u32[]{:S(2)}, u32[]{:S(2)}) collective-permute-start(bf16[32,3200]{1,0:T(8,128)(2,1)S(1)} %get-tuple-element.43), channel_id=1, source_target_pairs={{0,254},{2,0},{4,2},{6,4},{8,6},{10,8},{12,10},{14,12},{16,14},{18... | collective-permute-start | bytes 614408 | tf_op jit(solution)/shard_map/ppermute | solution.py:403
  11.5 12.7 %collective-permute-start.4 = (bf16[32,3200]{1,0:T(8,128)(2,1)S(1)}, bf16[32,3200]{1,0:T(8,128)(2,1)S(1)}, u32[]{:S(2)}, u32[]{:S(2)}) collective-permute-start(bf16[32,3200]{1,0:T(8,128)(2,1)S(1)} %get-tuple-element.44), channel_id=1, source_target_pairs={{0,252},{2,254},{4,0},{6,2},{8,4},{10,6},{12,8},{14,10},{16,12},{1... | collective-permute-start | bytes 614408 | tf_op jit(solution)/shard_map/ppermute | solution.py:403
  16.0 8.7 %collective-permute-start = (bf16[32,3200]{1,0:T(8,128)(2,1)}, bf16[32,3200]{1,0:T(8,128)(2,1)S(1)}, u32[]{:S(2)}, u32[]{:S(2)}) collective-permute-start(bf16[32,3200]{1,0:T(8,128)(2,1)} %fo_ref.1), channel_id=1, source_target_pairs={{0,1},{1,0},{2,3},{3,2},{4,5},{5,4},{6,7},{7,6},{8,9},{9,8},{10,11... | collective-permute-start | bytes 614408 | tf_op jit(solution)/shard_map/ppermute | solution.py:403
  17.1 7.6 %collective-permute-start.5 = (bf16[32,3200]{1,0:T(8,128)(2,1)S(1)}, bf16[32,3200]{1,0:T(8,128)(2,1)S(1)}, u32[]{:S(2)}, u32[]{:S(2)}) collective-permute-start(bf16[32,3200]{1,0:T(8,128)(2,1)S(1)} %collective-permute-done.1.ho0_ref), channel_id=1, source_target_pairs={{0,1},{1,0},{2,3},{3,2},{4,5},{5,4},{6,7},{7,6},{8,9},{9,8},{10,11... | collective-permute-start | bytes 614408 | tf_op jit(solution)/shard_map/ppermute | solution.py:403
  18.2 6.5 %collective-permute-start.6 = (bf16[32,3200]{1,0:T(8,128)(2,1)S(1)}, bf16[32,3200]{1,0:T(8,128)(2,1)S(1)}, u32[]{:S(2)}, u32[]{:S(2)}) collective-permute-start(bf16[32,3200]{1,0:T(8,128)(2,1)S(1)} %collective-permute-done.2.ho1_ref), channel_id=1, source_target_pairs={{0,1},{1,0},{2,3},{3,2},{4,5},{5,4},{6,7},{7,6},{8,9},{9,8},{10,11... | collective-permute-start | bytes 614408 | tf_op jit(solution)/shard_map/ppermute | solution.py:403
  24.2 1.5 %collective-permute-start.7 = (bf16[32,3200]{1,0:T(8,128)(2,1)S(1)}, bf16[32,3200]{1,0:T(8,128)(2,1)S(1)}, u32[]{:S(2)}, u32[]{:S(2)}) collective-permute-start(bf16[32,3200]{1,0:T(8,128)(2,1)S(1)} %collective-permute-done.3.ho2_ref), channel_id=1, source_target_pairs={{0,1},{1,0},{2,3},{3,2},{4,5},{5,4},{6,7},{7,6},{8,9},{9,8},{10,11... | collective-permute-start | bytes 614408 | tf_op jit(solution)/shard_map/ppermute | solution.py:403
  24.2 1.7 %collective-permute-start.8 = (bf16[32,3200]{1,0:T(8,128)(2,1)S(1)}, bf16[32,3200]{1,0:T(8,128)(2,1)S(1)}, u32[]{:S(2)}, u32[]{:S(2)}) collective-permute-start(bf16[32,3200]{1,0:T(8,128)(2,1)S(1)} %collective-permute-done.4.ho3_ref), channel_id=1, source_target_pairs={{0,1},{1,0},{2,3},{3,2},{4,5},{5,4},{6,7},{7,6},{8,9},{9,8},{10,11... | collective-permute-start | bytes 614408 | tf_op jit(solution)/shard_map/ppermute | solution.py:403
  25.9 0.7 copy-start.8
  26.6 0.9 copy-start.2
  27.5 16.4 %copy-start = (bf16[6400,256]{1,0:T(8,128)(2,1)S(1)}, bf16[6400,256]{1,0:T(8,128)(2,1)}, u32[]{:S(2)}) copy-start(bf16[6400,256]{1,0:T(8,128)(2,1)} %weight_ref.1) | copy-start | bytes 9830404
  27.5 16.4 %copy-start.4 = (f32[32,256]{1,0:T(8,128)S(1)}, f32[32,256]{1,0:T(8,128)}, u32[]{:S(2)}) copy-start(f32[32,256]{1,0:T(8,128)} %target_ref.1) | copy-start | bytes 98308
  27.6 16.4 %copy-start.6 = (s32[4]{0:T(128)S(1)}, s32[4]{0:T(128)}, u32[]{:S(2)}) copy-start(s32[4]{0:T(128)} %orbitals_ref.1) | copy-start | bytes 52
  27.6 16.4 %copy-start.7 = (s32[32]{0:T(128)S(1)}, s32[32]{0:T(128)}, u32[]{:S(2)}) copy-start(s32[32]{0:T(128)} %param.24) | copy-start | bytes 388
  41.7 2.2 %collective-permute-start.9 = (bf16[32,6400]{1,0:T(8,128)(2,1)}, bf16[32,6400]{1,0:T(8,128)(2,1)S(1)}, u32[]{:S(2)}, u32[]{:S(2)}) collective-permute-start(bf16[32,6400]{1,0:T(8,128)(2,1)} %messages.1.mine_ref), channel_id=1, source_target_pairs={{0,1},{1,0},{2,3},{3,2},{4,5},{5,4},{6,7},{7,6},{8,9},{9,8},{10,11... | collective-permute-start | bytes 1228808 | tf_op jit(solution)/shard_map/ppermute | solution.py:403
  44.0 1.0 copy-start.3
  72.5 15.9 %collective-permute-start.14 = (bf16[32,3200]{1,0:T(8,128)(2,1)S(1)}, bf16[32,3200]{1,0:T(8,128)(2,1)S(1)}, u32[]{:S(2)}, u32[]{:S(2)}) collective-permute-start(bf16[32,3200]{1,0:T(8,128)(2,1)S(1)} %get-tuple-element.50), channel_id=1, source_target_pairs={{0,1},{1,0},{2,3},{3,2},{4,5},{5,4},{6,7},{7,6},{8,9},{9,8},{10,11... | collective-permute-start | bytes 614408 | tf_op jit(solution)/shard_map/ppermute | solution.py:403
  72.6 12.5 %collective-permute-start.12 = (bf16[200,256]{1,0:T(8,128)(2,1)S(1)}, bf16[200,256]{1,0:T(8,128)(2,1)S(1)}, u32[]{:S(2)}, u32[]{:S(2)}) collective-permute-start(bf16[200,256]{1,0:T(8,128)(2,1)S(1)} %partial_grad.1), channel_id=1, source_target_pairs={{0,128},{64,192},{128,0},{192,64},{1,129},{65,193},{129,1},{193,65... | collective-permute-start | bytes 307208 | tf_op jit(solution)/shard_map/ppermute | solution.py:403
  78.1 8.5 %collective-permute-start.11 = (bf16[200,256]{1,0:T(8,128)(2,1)S(1)}, bf16[200,256]{1,0:T(8,128)(2,1)S(1)}, u32[]{:S(2)}, u32[]{:S(2)}) collective-permute-start(bf16[200,256]{1,0:T(8,128)(2,1)S(1)} %partial_grad.1), channel_id=1, source_target_pairs={{0,192},{64,0},{128,64},{192,128},{1,193},{65,1},{129,65},{193,129... | collective-permute-start | bytes 307208 | tf_op jit(solution)/shard_map/ppermute | solution.py:403
  79.7 8.8 %collective-permute-start.10 = (bf16[200,256]{1,0:T(8,128)(2,1)S(1)}, bf16[200,256]{1,0:T(8,128)(2,1)S(1)}, u32[]{:S(2)}, u32[]{:S(2)}) collective-permute-start(bf16[200,256]{1,0:T(8,128)(2,1)S(1)} %partial_grad.1), channel_id=1, source_target_pairs={{0,64},{64,128},{128,192},{192,0},{1,65},{65,129},{129,193},{193,1... | collective-permute-start | bytes 307208 | tf_op jit(solution)/shard_map/ppermute | solution.py:403
  81.1 1.2 collective-permute-start.13
  88.5 4.9 %collective-permute-start.15 = (bf16[200,256]{1,0:T(8,128)(2,1)S(1)}, bf16[200,256]{1,0:T(8,128)(2,1)S(1)}, u32[]{:S(2)}, u32[]{:S(2)}) collective-permute-start(bf16[200,256]{1,0:T(8,128)(2,1)S(1)} %add_convert_fusion), channel_id=1, source_target_pairs={{0,32},{32,0},{1,33},{33,1},{2,34},{34,2},{3,35},{35,3},{4,36},{36... | collective-permute-start | bytes 307208 | tf_op jit(solution)/shard_map/ppermute | solution.py:403
  93.5 7.0 %collective-permute-start.16 = (bf16[400,256]{1,0:T(8,128)(2,1)S(1)}, bf16[400,256]{1,0:T(8,128)(2,1)S(1)}, u32[]{:S(2)}, u32[]{:S(2)}) collective-permute-start(bf16[400,256]{1,0:T(8,128)(2,1)S(1)} %pad_maximum_fusion.1), channel_id=1, source_target_pairs={{0,2},{1,9},{2,4},{3,11},{4,6},{5,13},{6,0},{7,15},{8,10},{9,17},{... | collective-permute-start | bytes 614408 | tf_op jit(solution)/shard_map/ppermute | solution.py:414
  94.5 9.1 %collective-permute-start.19 = (bf16[400,256]{1,0:T(8,128)(2,1)S(1)}, bf16[400,256]{1,0:T(8,128)(2,1)S(1)}, u32[]{:S(2)}, u32[]{:S(2)}) collective-permute-start(bf16[400,256]{1,0:T(8,128)(2,1)S(1)} %pad_maximum_fusion.1), channel_id=1, source_target_pairs={{0,4},{1,17},{2,6},{3,19},{4,0},{5,21},{6,2},{7,23},{8,12},{9,25},... | collective-permute-start | bytes 614408 | tf_op jit(solution)/shard_map/ppermute | solution.py:414
  97.0 6.6 %collective-permute-start.20 = (bf16[400,256]{1,0:T(8,128)(2,1)S(1)}, bf16[400,256]{1,0:T(8,128)(2,1)S(1)}, u32[]{:S(2)}, u32[]{:S(2)}) collective-permute-start(bf16[400,256]{1,0:T(8,128)(2,1)S(1)} %pad_maximum_fusion.1), channel_id=1, source_target_pairs={{0,6},{1,25},{2,0},{3,27},{4,2},{5,29},{6,4},{7,31},{8,14},{9,1},{... | collective-permute-start | bytes 614408 | tf_op jit(solution)/shard_map/ppermute | solution.py:414
  100.5 11.6 %collective-permute-start.17 = (bf16[800,256]{1,0:T(8,128)(2,1)S(1)}, bf16[800,256]{1,0:T(8,128)(2,1)S(1)}, u32[]{:S(2)}, u32[]{:S(2)}) collective-permute-start(bf16[800,256]{1,0:T(8,128)(2,1)S(1)} %pad_maximum_fusion.refs_0_), channel_id=1, source_target_pairs={{0,8},{1,3},{2,10},{3,5},{4,12},{5,7},{6,14},{7,1},{8,16},{9,11},{... | collective-permute-start | bytes 1228808 | tf_op jit(solution)/shard_map/ppermute | solution.py:414
  103.6 8.5 %collective-permute-start.21 = (bf16[800,256]{1,0:T(8,128)(2,1)S(1)}, bf16[800,256]{1,0:T(8,128)(2,1)S(1)}, u32[]{:S(2)}, u32[]{:S(2)}) collective-permute-start(bf16[800,256]{1,0:T(8,128)(2,1)S(1)} %constant_dynamic-update-slice_fusion.refs_1_), channel_id=1, source_target_pairs={{0,24},{1,7},{2,26},{3,1},{4,28},{5,3},{6,30},{7,5},{8,0},{9,15},{... | collective-permute-start | bytes 1228808 | tf_op jit(solution)/shard_map/ppermute | solution.py:414
  106.6 10.4 %collective-permute-start.24 = (bf16[800,256]{1,0:T(8,128)(2,1)S(1)}, bf16[800,256]{1,0:T(8,128)(2,1)S(1)}, u32[]{:S(2)}, u32[]{:S(2)}) collective-permute-start(bf16[800,256]{1,0:T(8,128)(2,1)S(1)} %pad_maximum_fusion.refs_0_), channel_id=1, source_target_pairs={{0,24},{1,7},{2,26},{3,1},{4,28},{5,3},{6,30},{7,5},{8,0},{9,15},{... | collective-permute-start | bytes 1228808 | tf_op jit(solution)/shard_map/ppermute | solution.py:414
  108.5 9.2 %collective-permute-start.23 = (bf16[800,256]{1,0:T(8,128)(2,1)S(1)}, bf16[800,256]{1,0:T(8,128)(2,1)S(1)}, u32[]{:S(2)}, u32[]{:S(2)}) collective-permute-start(bf16[800,256]{1,0:T(8,128)(2,1)S(1)} %constant_dynamic-update-slice_fusion.refs_1_), channel_id=1, source_target_pairs={{0,8},{1,3},{2,10},{3,5},{4,12},{5,7},{6,14},{7,1},{8,16},{9,11},{... | collective-permute-start | bytes 1228808 | tf_op jit(solution)/shard_map/ppermute | solution.py:414
  112.2 9.9 %collective-permute-start.18 = (bf16[800,256]{1,0:T(8,128)(2,1)S(1)}, bf16[800,256]{1,0:T(8,128)(2,1)S(1)}, u32[]{:S(2)}, u32[]{:S(2)}) collective-permute-start(bf16[800,256]{1,0:T(8,128)(2,1)S(1)} %collective-permute-done.17.refs_2_), channel_id=1, source_target_pairs={{0,8},{1,3},{2,10},{3,5},{4,12},{5,7},{6,14},{7,1},{8,16},{9,11},{... | collective-permute-start | bytes 1228808 | tf_op jit(solution)/shard_map/ppermute | solution.py:414
  112.2 9.9 %collective-permute-start.22 = (bf16[800,256]{1,0:T(8,128)(2,1)S(1)}, bf16[800,256]{1,0:T(8,128)(2,1)S(1)}, u32[]{:S(2)}, u32[]{:S(2)}) collective-permute-start(bf16[800,256]{1,0:T(8,128)(2,1)S(1)} %collective-permute-done.21.refs_5_), channel_id=1, source_target_pairs={{0,24},{1,7},{2,26},{3,1},{4,28},{5,3},{6,30},{7,5},{8,0},{9,15},{... | collective-permute-start | bytes 1228808 | tf_op jit(solution)/shard_map/ppermute | solution.py:414

commit v7 on v5

--- a/solution.py
+++ b/solution.py
@@ -11,7 +11,6 @@
 LMAX = 4
 MMAX = 2
 OFFSETS = (1, -1, 2, -2)
-HALO_ORDER = (1, 2, -1, -2)
 BRANCH = 0.125
 PREP_MB = 56
 MSG_MB = 54
@@ -137,7 +136,8 @@
     for q, (own, oth) in enumerate(
         zip((fo_ref, ho0_ref, ho1_ref, ho2_ref, ho3_ref), (fx_ref, hx0_ref, hx1_ref, hx2_ref, hx3_ref))
     ):
-        at = pl.ds(0 if q == 0 else (1 + OFFSETS.index(HALO_ORDER[q - 1])) * atoms, atoms)
+        slot = 0 if q == 0 else 1 + core_ref[q]
+        at = pl.ds(pl.multiple_of(slot * atoms, 32), atoms)
         moves.append(pltpu.make_async_copy(own, rows.at[core, at, :], sems.at[2 * q]))
         moves.append(pltpu.make_async_copy(oth, rows.at[other, at, :], sems.at[2 * q + 1]))
     for move in [pick] + moves + [frame] + mixes + [wframe, place]:
@@ -350,27 +350,27 @@
     )(core, orbitals, species.reshape(1, -1), f_own, f_oth, mine, recv, weight, target)
 
 
-def leaving_kernel(sends_ref, feats_ref, *outs):
+def leaving_kernel(order_ref, sends_ref, feats_ref, *outs):
     atoms = feats_ref.shape[0]
     places = lax.broadcasted_iota(jnp.int32, (atoms, atoms), 0)
     picks = jnp.concatenate(
-        [(sends_ref[q : q + 1, :] == places).astype(F32) for q in range(len(outs))], axis=1
+        [(sends_ref[pl.ds(order_ref[q], 1), :] == places).astype(F32) for q in range(len(outs))], axis=1
     ).astype(BF16)
     rows = dot(picks, feats_ref[...], 0, 0).astype(BF16)
     for q, out in enumerate(outs):
         out[...] = rows[q * atoms : (q + 1) * atoms, :]
 
 
-def leaving_rows(send_rows, features):
+def leaving_rows(order, send_rows, features):
     vmem = pl.BlockSpec(memory_space=pltpu.VMEM)
     return pl.pallas_call(
         leaving_kernel,
         out_shape=(jax.ShapeDtypeStruct(features.shape, BF16),) * len(OFFSETS),
-        in_specs=[vmem, vmem],
+        in_specs=[pl.BlockSpec(memory_space=pltpu.SMEM), vmem, vmem],
         out_specs=(vmem,) * len(OFFSETS),
         compiler_params=pltpu.CompilerParams(vmem_limit_bytes=24 * 1024 * 1024),
         name="leaving",
-    )(send_rows, features)
+    )(order, send_rows, features)
 
 
 def partial_kernel(got_ref, out_ref):
@@ -453,8 +453,19 @@
     mix_zero, mix_one, mix_two, atom_species, species_orbitals, head_weight, target_blocks,
 ):
     core = lax.axis_index("chan").astype(jnp.int32).reshape(1)
-    leaving = leaving_rows(send_rows, features)
-    halo = [shift(leaving[OFFSETS.index(off)], ATOMS, off) for off in HALO_ORDER]
+    count = lax.axis_size(ATOMS)
+    me = lax.axis_index(ATOMS)
+    swaps = []
+    for later in (False, True):
+        for step in (1, 2):
+            to = [i + step if (i // step % 2 == 0) != later else i - step for i in range(count)]
+            forward = (me // step % 2 == 0) != later
+            ahead, back = OFFSETS.index(step), OFFSETS.index(-step)
+            swaps.append(([(i, t % count) for i, t in enumerate(to)], jnp.where(forward, ahead, back), ahead + back))
+    sent = jnp.stack([q for _, q, _ in swaps]).astype(jnp.int32)
+    got_from = jnp.stack([both - q for _, q, both in swaps]).astype(jnp.int32)
+    leaving = leaving_rows(sent, send_rows, features)
+    halo = [lax.ppermute(rows, ATOMS, pairs) for rows, (pairs, _, _) in zip(leaving, swaps)]
     prepared = prepare(
         edge_source, edge_dest, edge_rot, edge_weight, rot_table.T,
         (mix_zero, mix_one, mix_two), features.shape[0],
@@ -462,7 +473,7 @@
     features, prepared = lax.optimization_barrier((features, prepared))
     f_oth = shift(features, "chan", 1)
     halo_oth = [shift(h, "chan", 1) for h in halo]
-    mine = messages(core, prepared, [features] + halo, [f_oth] + halo_oth)
+    mine = messages(jnp.concatenate([core, got_from]), prepared, [features] + halo, [f_oth] + halo_oth)
     recv = shift(mine, "chan", 1)
     parts = lax.axis_size(GROUP)
     load, loss, keep, send = head(

time: 123 us -> 123 us (level)
  waiting for transfers between devices: 30.4 us -> 28.5 us
    ppermute x16 -> x12, waiting for transfers between devices: 21.6 us -> 12.2 us  [shift(): return lax.ppermute(x, axis, [(i, (i + by) % count) for i in range(count)])]
    ppermute x0 -> x4, starting transfers between devices: none -> 8.59 us  [body(): lax.ppermute(rows, ATOMS, pairs)]
    ppermute x16 -> x12, starting transfers between devices: 20.5 us -> 12.4 us  [shift(): return lax.ppermute(x, axis, [(i, (i + by) % count) for i in range(count)])]
    ppermute x0 -> x4, waiting for transfers between devices: none -> 7.44 us  [body(): lax.ppermute(rows, ATOMS, pairs)]
  transfers between devices with their start and end apart: 25 -> 25, of which waited for: 15 -> 15; matrix products, arithmetic and copies ran while one was open for 1% -> 2% of each run, Pallas kernels for 5% -> 5%
where the time goes in v7:
time: 123 us; the launch traced here: 122 us
  starting transfers between devices  36.5 us (30%)
  waiting for transfers between devices  28.5 us (23%)
  Pallas kernels  24.9 us (20%)
  blocking collectives  24 us (20%)
  local copies, waits for them, and re-layouts  5.01 us (4%)
  other arithmetic  1.69 us (1%)
    all_to_all x1, blocking collectives, body(): got = lax.all_to_all(load, GROUP, split_axis=0, concat_axis=0, tiled=True)  24 us
    ppermute x9, starting transfers between devices, plane_shift(): return lax.ppermute(x, ('y', 'x', 'chan'), pairs)  15.5 us
    pallas_call x1, Pallas kernels, messages(): pl.pallas_call(message_kernel, out_shape=jax.ShapeDtypeStruct((atoms, 2 *...  13.2 us
    ppermute x12, starting transfers between devices, shift(): return lax.ppermute(x, axis, [(i, (i + by) % count) for i in range(count)])  12.4 us
    ppermute x12, waiting for transfers between devices, shift(): return lax.ppermute(x, axis, [(i, (i + by) % count) for i in range(count)])  12.2 us
    ppermute x9, waiting for transfers between devices, plane_shift(): return lax.ppermute(x, ('y', 'x', 'chan'), pairs)  8.94 us
    ppermute x4, starting transfers between devices, body(): lax.ppermute(rows, ATOMS, pairs)  8.59 us
    ppermute x4, waiting for transfers between devices, body(): lax.ppermute(rows, ATOMS, pairs)  7.44 us
  transfers between devices with their start and end apart: 25, of which 15 were waited for; matrix products, arithmetic and copies ran while one was open for 2% of the time, Pallas kernels for 5%

profile of v7, /device:TPU:32, one launch (start us, length us, event | category | flops | bytes accessed | tf_op | source)
XLA Modules:
  0.0 121.9 jit_solution(15098247506546022345)
XLA Ops:
  0.7 0.1 pad_add_fusion.order_ref
  0.8 0.9 copy-done.1
  1.7 0.7 copy-done.7
  2.4 1.0 leaving.1
  3.4 1.6 %collective-permute-start.1 = (bf16[32,3200]{1,0:T(8,128)(2,1)S(1)}, bf16[32,3200]{1,0:T(8,128)(2,1)S(1)}, u32[]{:S(2)}, u32[]{:S(2)}) collective-permute-start(bf16[32,3200]{1,0:T(8,128)(2,1)S(1)} %get-tuple-element.49), channel_id=1, source_target_pairs={{0,2},{2,0},{4,6},{6,4},{8,10},{10,8},{12,14},{14,12},{16,18},{18,... | collective-permute-start | bytes 614408 | tf_op jit(solution)/shard_map/ppermute | solution.py:468
  5.0 2.7 %collective-permute-start.2 = (bf16[32,3200]{1,0:T(8,128)(2,1)S(1)}, bf16[32,3200]{1,0:T(8,128)(2,1)S(1)}, u32[]{:S(2)}, u32[]{:S(2)}) collective-permute-start(bf16[32,3200]{1,0:T(8,128)(2,1)S(1)} %get-tuple-element.50), channel_id=1, source_target_pairs={{0,4},{2,6},{4,0},{6,2},{8,12},{10,14},{12,8},{14,10},{16,20},{18,... | collective-permute-start | bytes 614408 | tf_op jit(solution)/shard_map/ppermute | solution.py:468
  7.7 2.5 %collective-permute-start.3 = (bf16[32,3200]{1,0:T(8,128)(2,1)S(1)}, bf16[32,3200]{1,0:T(8,128)(2,1)S(1)}, u32[]{:S(2)}, u32[]{:S(2)}) collective-permute-start(bf16[32,3200]{1,0:T(8,128)(2,1)S(1)} %get-tuple-element.51), channel_id=1, source_target_pairs={{0,254},{2,4},{4,2},{6,8},{8,6},{10,12},{12,10},{14,16},{16,14},{1... | collective-permute-start | bytes 614408 | tf_op jit(solution)/shard_map/ppermute | solution.py:468
  10.2 1.8 %collective-permute-start.4 = (bf16[32,3200]{1,0:T(8,128)(2,1)S(1)}, bf16[32,3200]{1,0:T(8,128)(2,1)S(1)}, u32[]{:S(2)}, u32[]{:S(2)}) collective-permute-start(bf16[32,3200]{1,0:T(8,128)(2,1)S(1)} %get-tuple-element.52), channel_id=1, source_target_pairs={{0,252},{2,254},{4,8},{6,10},{8,4},{10,6},{12,16},{14,18},{16,12},... | collective-permute-start | bytes 614408 | tf_op jit(solution)/shard_map/ppermute | solution.py:468
  12.0 4.0 %prepare.1 = (f32[2,115,8,128]{3,2,1,0:T(8,128)}, f32[2,115,8,128]{3,2,1,0:T(8,128)}, bf16[160,256]{1,0:T(8,128)(2,1)}, bf16[32,256]{1,0:T(8,128)(2,1)}, bf16[64...) custom-call(s32[1,256]{1,0:T(1,128)} %bitcast.21, s32[1,256]{1,0:T(1,128)} %bitcast.22, ...), custom_call_target="tpu_custom_call" | custom-call | flops 100000000 | bytes 10000000 | tf_op jit(solution)/shard_map/prepare/pallas_call | solution.py:92
  16.0 0.1 collective-permute-start
  16.1 0.5 collective-permute-start.5
  16.6 1.6 %collective-permute-done.2.ho1_ref = bf16[32,3200]{1,0:T(8,128)(2,1)S(1)} collective-permute-done((bf16[32,3200]{1,0:T(8,128)(2,1)S(1)}, bf16[32,3200]{1,0:T(8,128)(2,1)S(1)}, u32[]{:S(2)}, u32[]{:S(2)}) %collective-permute-start.2) | collective-permute-done | bytes 204832 | tf_op jit(solution)/shard_map/ppermute | solution.py:468
  18.1 0.0 collective-permute-start.6
  18.1 4.3 %collective-permute-done.3.ho2_ref = bf16[32,3200]{1,0:T(8,128)(2,1)S(1)} collective-permute-done((bf16[32,3200]{1,0:T(8,128)(2,1)S(1)}, bf16[32,3200]{1,0:T(8,128)(2,1)S(1)}, u32[]{:S(2)}, u32[]{:S(2)}) %collective-permute-start.3) | collective-permute-done | bytes 204832 | tf_op jit(solution)/shard_map/ppermute | solution.py:468
  22.5 1.5 %collective-permute-done.4.ho3_ref = bf16[32,3200]{1,0:T(8,128)(2,1)S(1)} collective-permute-done((bf16[32,3200]{1,0:T(8,128)(2,1)S(1)}, bf16[32,3200]{1,0:T(8,128)(2,1)S(1)}, u32[]{:S(2)}, u32[]{:S(2)}) %collective-permute-start.4) | collective-permute-done | bytes 204832 | tf_op jit(solution)/shard_map/ppermute | solution.py:468
  24.0 0.0 collective-permute-start.8
  24.0 0.6 concatenate.13.core_ref
  24.7 0.0 copy-start.9
  24.7 0.0 collective-permute-done.fx_ref
  24.7 0.0 collective-permute-done.5.hx0_ref
  24.7 0.0 collective-permute-done.7.hx2_ref
  24.7 0.7 collective-permute-done.8.hx3_ref
  25.5 0.1 copy-done.16
  25.6 0.7 copy-done.17
  26.3 13.2 %messages.1.mine_ref = bf16[32,6400]{1,0:T(8,128)(2,1)} custom-call(s32[5]{0:T(128)} %concatenate.13.core_ref, f32[2,115,8,128]{3,2,1,0:T(8,128)} %get-tuple-element.42.frames_hbm, f32[2,115,8,128]{3,2,1,0:T(8,128)} %get-tuple-element.43.wframes_hbm, bf16[160,256]{1,0:T(8,128)(2,1)} %get-tuple-element.44.onehot_hbm, ...), custom_call_target="tpu_custom_call" | custom-call | flops 5000000000 | bytes 6000000 | tf_op jit(solution)/shard_map/messages/pallas_call | solution.py:267
  39.5 0.8 collective-permute-start.9
  40.3 1.6 %collective-permute-done.9.recv_ref = bf16[32,6400]{1,0:T(8,128)(2,1)S(1)} collective-permute-done((bf16[32,6400]{1,0:T(8,128)(2,1)}, bf16[32,6400]{1,0:T(8,128)(2,1)S(1)}, u32[]{:S(2)}, u32[]{:S(2)}) %collective-permute-start.9) | collective-permute-done | bytes 409632 | tf_op jit(solution)/shard_map/ppermute | solution.py:396
  41.9 1.0 copy-done.3
  42.9 0.9 copy-done.5
  43.8 2.9 %head.1 = (bf16[32,32,512]{2,1,0:T(8,128)(2,1)S(1)}, f32[32,1]{1,0:T(8,128)S(1)}, f32[32,3200]{1,0:T(8,128)S(1)}, bf16[32,3200]{1,0:T(8,128)(2,1)S(1)}) custom-call(s32[1]{0:T(128)} %bitcast.core_ref, s32[4]{0:T(128)S(1)} %copy-done.8, s32[1,32]{1,0:T(1,128)S(1)} %bitcast.19, bf16[32,3200]{1,0:T(8,128)(2,1)S(1)} %copy-done.2, ...), custom_call_target="tpu_custom_call" | custom-call | flops 300000000 | bytes 6000000 | tf_op jit(solution)/shard_map/head/pallas_call | solution.py:333
  46.7 24.0 %all_to_all.5 = bf16[32,32,512]{2,1,0:T(8,128)(2,1)S(1)} all-to-all(bf16[32,32,512]{2,1,0:T(8,128)(2,1)S(1)} %get-tuple-element.53), channel_id=1, replica_groups=mesh['zh'=4,'zl'=2,'y'=4,'x'=4,'chan'=2] {'zl','y','x'}, dimensions={0} | all-to-all | bytes 2097152 | tf_op jit(solution)/shard_map/all_to_all | solution.py:482
  70.8 0.3 partial_grad.1
  71.1 0.1 collective-permute-start.14
  71.2 6.1 %collective-permute-start.12 = (bf16[200,256]{1,0:T(8,128)(2,1)S(1)}, bf16[200,256]{1,0:T(8,128)(2,1)S(1)}, u32[]{:S(2)}, u32[]{:S(2)}) collective-permute-start(bf16[200,256]{1,0:T(8,128)(2,1)S(1)} %partial_grad.1), channel_id=1, source_target_pairs={{0,128},{64,192},{128,0},{192,64},{1,129},{65,193},{129,1},{193,65... | collective-permute-start | bytes 307208 | tf_op jit(solution)/shard_map/ppermute | solution.py:396
  77.3 0.6 collective-permute-start.11
  77.9 2.4 %collective-permute-start.10 = (bf16[200,256]{1,0:T(8,128)(2,1)S(1)}, bf16[200,256]{1,0:T(8,128)(2,1)S(1)}, u32[]{:S(2)}, u32[]{:S(2)}) collective-permute-start(bf16[200,256]{1,0:T(8,128)(2,1)S(1)} %partial_grad.1), channel_id=1, source_target_pairs={{0,64},{64,128},{128,192},{192,0},{1,65},{65,129},{129,193},{193,1... | collective-permute-start | bytes 307208 | tf_op jit(solution)/shard_map/ppermute | solution.py:396
  80.2 0.1 reduce
  80.4 0.1 collective-permute-start.13
  80.5 1.1 collective-permute-done.13
  81.6 3.7 %collective-permute-done.12 = bf16[200,256]{1,0:T(8,128)(2,1)S(1)} collective-permute-done((bf16[200,256]{1,0:T(8,128)(2,1)S(1)}, bf16[200,256]{1,0:T(8,128)(2,1)S(1)}, u32[]{:S(2)}, u32[]{:S(2)}) %collective-permute-start.12) | collective-permute-done | bytes 102432 | tf_op jit(solution)/shard_map/ppermute | solution.py:396
  85.2 1.0 collective-permute-done.11
  86.2 1.1 collective-permute-done.10
  87.3 0.1 add_convert_fusion
  87.3 1.9 %collective-permute-start.15 = (bf16[200,256]{1,0:T(8,128)(2,1)S(1)}, bf16[200,256]{1,0:T(8,128)(2,1)S(1)}, u32[]{:S(2)}, u32[]{:S(2)}) collective-permute-start(bf16[200,256]{1,0:T(8,128)(2,1)S(1)} %add_convert_fusion), channel_id=1, source_target_pairs={{0,32},{32,0},{1,33},{33,1},{2,34},{34,2},{3,35},{35,3},{4,36},{36... | collective-permute-start | bytes 307208 | tf_op jit(solution)/shard_map/ppermute | solution.py:396
  89.2 3.0 %collective-permute-done.15 = bf16[200,256]{1,0:T(8,128)(2,1)S(1)} collective-permute-done((bf16[200,256]{1,0:T(8,128)(2,1)S(1)}, bf16[200,256]{1,0:T(8,128)(2,1)S(1)}, u32[]{:S(2)}, u32[]{:S(2)}) %collective-permute-start.15) | collective-permute-done | bytes 102432 | tf_op jit(solution)/shard_map/ppermute | solution.py:396
  92.3 1.0 collective-permute-start.16
  93.3 2.4 %collective-permute-start.19 = (bf16[400,256]{1,0:T(8,128)(2,1)S(1)}, bf16[400,256]{1,0:T(8,128)(2,1)S(1)}, u32[]{:S(2)}, u32[]{:S(2)}) collective-permute-start(bf16[400,256]{1,0:T(8,128)(2,1)S(1)} %pad_maximum_fusion.1), channel_id=1, source_target_pairs={{0,4},{1,17},{2,6},{3,19},{4,0},{5,21},{6,2},{7,23},{8,12},{9,25},... | collective-permute-start | bytes 614408 | tf_op jit(solution)/shard_map/ppermute | solution.py:407
  95.7 1.4 %collective-permute-start.20 = (bf16[400,256]{1,0:T(8,128)(2,1)S(1)}, bf16[400,256]{1,0:T(8,128)(2,1)S(1)}, u32[]{:S(2)}, u32[]{:S(2)}) collective-permute-start(bf16[400,256]{1,0:T(8,128)(2,1)S(1)} %pad_maximum_fusion.1), channel_id=1, source_target_pairs={{0,6},{1,25},{2,0},{3,27},{4,2},{5,29},{6,4},{7,31},{8,14},{9,1},{... | collective-permute-start | bytes 614408 | tf_op jit(solution)/shard_map/ppermute | solution.py:407
  97.1 2.2 %collective-permute-done.16 = bf16[400,256]{1,0:T(8,128)(2,1)S(1)} collective-permute-done((bf16[400,256]{1,0:T(8,128)(2,1)S(1)}, bf16[400,256]{1,0:T(8,128)(2,1)S(1)}, u32[]{:S(2)}, u32[]{:S(2)}) %collective-permute-start.16) | collective-permute-done | bytes 204832 | tf_op jit(solution)/shard_map/ppermute | solution.py:407
  99.3 2.8 %collective-permute-start.17 = (bf16[800,256]{1,0:T(8,128)(2,1)S(1)}, bf16[800,256]{1,0:T(8,128)(2,1)S(1)}, u32[]{:S(2)}, u32[]{:S(2)}) collective-permute-start(bf16[800,256]{1,0:T(8,128)(2,1)S(1)} %pad_maximum_fusion.refs_0_), channel_id=1, source_target_pairs={{0,8},{1,3},{2,10},{3,5},{4,12},{5,7},{6,14},{7,1},{8,16},{9,11},{... | collective-permute-start | bytes 1228808 | tf_op jit(solution)/shard_map/ppermute | solution.py:407
  102.2 0.2 collective-permute-done.20
  102.4 2.3 %collective-permute-start.21 = (bf16[800,256]{1,0:T(8,128)(2,1)S(1)}, bf16[800,256]{1,0:T(8,128)(2,1)S(1)}, u32[]{:S(2)}, u32[]{:S(2)}) collective-permute-start(bf16[800,256]{1,0:T(8,128)(2,1)S(1)} %constant_dynamic-update-slice_fusion.refs_1_), channel_id=1, source_target_pairs={{0,24},{1,7},{2,26},{3,1},{4,28},{5,3},{6,30},{7,5},{8,0},{9,15},{... | collective-permute-start | bytes 1228808 | tf_op jit(solution)/shard_map/ppermute | solution.py:407
  104.7 0.1 pad_add_fusion.1.place_ref
  104.8 1.9 %collective-permute-start.24 = (bf16[800,256]{1,0:T(8,128)(2,1)S(1)}, bf16[800,256]{1,0:T(8,128)(2,1)S(1)}, u32[]{:S(2)}, u32[]{:S(2)}) collective-permute-start(bf16[800,256]{1,0:T(8,128)(2,1)S(1)} %pad_maximum_fusion.refs_0_), channel_id=1, source_target_pairs={{0,24},{1,7},{2,26},{3,1},{4,28},{5,3},{6,30},{7,5},{8,0},{9,15},{... | collective-permute-start | bytes 1228808 | tf_op jit(solution)/shard_map/ppermute | solution.py:407
  106.7 0.1 collective-permute-start.23
  106.8 3.6 %collective-permute-done.17.refs_2_ = bf16[800,256]{1,0:T(8,128)(2,1)S(1)} collective-permute-done((bf16[800,256]{1,0:T(8,128)(2,1)S(1)}, bf16[800,256]{1,0:T(8,128)(2,1)S(1)}, u32[]{:S(2)}, u32[]{:S(2)}) %collective-permute-start.17) | collective-permute-done | bytes 409632 | tf_op jit(solution)/shard_map/ppermute | solution.py:407
  110.4 0.0 collective-permute-done.21.refs_5_
  110.4 3.5 %collective-permute-start.22 = (bf16[800,256]{1,0:T(8,128)(2,1)S(1)}, bf16[800,256]{1,0:T(8,128)(2,1)S(1)}, u32[]{:S(2)}, u32[]{:S(2)}) collective-permute-start(bf16[800,256]{1,0:T(8,128)(2,1)S(1)} %collective-permute-done.21.refs_5_), channel_id=1, source_target_pairs={{0,24},{1,7},{2,26},{3,1},{4,28},{5,3},{6,30},{7,5},{8,0},{9,15},{... | collective-permute-start | bytes 1228808 | tf_op jit(solution)/shard_map/ppermute | solution.py:407
  113.9 0.8 convert_add_fusion
  114.7 0.5 add.40
  115.2 0.7 collective-permute-done.23.refs_3_
  115.9 2.1 %assemble.2.refs_2_ = bf16[6400,256]{1,0:T(8,128)(2,1)} custom-call(s32[3]{0:T(128)S(1)} %pad_add_fusion.1.place_ref, bf16[800,256]{1,0:T(8,128)(2,1)S(1)} %pad_maximum_fusion.refs_0_, bf16[800,256]{1,0:T(8,128)(2,1)S(1)} %constant_dynamic-update-slice_fusion.refs_1_, bf16[800,256]{1,0:T(8,128)(2,1)S(1)} %collective-permute-done.17.refs_2_, ...), custom_call_target="tpu_custom_call" | custom-call | tf_op jit(solution)/shard_map/assemble/pallas_call | solution.py:437
  117.9 2.3 %collective-permute-done.18.refs_0_ = bf16[800,256]{1,0:T(8,128)(2,1)S(1)} collective-permute-done((bf16[800,256]{1,0:T(8,128)(2,1)S(1)}, bf16[800,256]{1,0:T(8,128)(2,1)S(1)}, u32[]{:S(2)}, u32[]{:S(2)}) %collective-permute-start.18) | collective-permute-done | bytes 409632 | tf_op jit(solution)/shard_map/ppermute | solution.py:407
  120.2 1.5 %assemble.3 = bf16[6400,256]{1,0:T(8,128)(2,1)} custom-call(s32[3]{0:T(128)S(1)} %pad_add_fusion.1.place_ref, bf16[800,256]{1,0:T(8,128)(2,1)S(1)} %collective-permute-done.18.refs_0_, bf16[800,256]{1,0:T(8,128)(2,1)S(1)} %collective-permute-done.22.refs_1_, bf16[6400,256]{1,0:T(8,128)(2,1)} %assemble.2.refs_2_), custom_call_target="tpu_custom_call", output_to_operand_aliasing={{}: (3, {})} | custom-call | tf_op jit(solution)/shard_map/assemble/pallas_call | solution.py:437
  (42 shorter events, 0.2 us)
Async XLA Ops:
  0.8 0.9 copy-start.1
  1.7 0.7 copy-start.7
  3.4 12.7 %collective-permute-start.1 = (bf16[32,3200]{1,0:T(8,128)(2,1)S(1)}, bf16[32,3200]{1,0:T(8,128)(2,1)S(1)}, u32[]{:S(2)}, u32[]{:S(2)}) collective-permute-start(bf16[32,3200]{1,0:T(8,128)(2,1)S(1)} %get-tuple-element.49), channel_id=1, source_target_pairs={{0,2},{2,0},{4,6},{6,4},{8,10},{10,8},{12,14},{14,12},{16,18},{18,... | collective-permute-start | bytes 614408 | tf_op jit(solution)/shard_map/ppermute | solution.py:468
  5.0 13.2 %collective-permute-start.2 = (bf16[32,3200]{1,0:T(8,128)(2,1)S(1)}, bf16[32,3200]{1,0:T(8,128)(2,1)S(1)}, u32[]{:S(2)}, u32[]{:S(2)}) collective-permute-start(bf16[32,3200]{1,0:T(8,128)(2,1)S(1)} %get-tuple-element.50), channel_id=1, source_target_pairs={{0,4},{2,6},{4,0},{6,2},{8,12},{10,14},{12,8},{14,10},{16,20},{18,... | collective-permute-start | bytes 614408 | tf_op jit(solution)/shard_map/ppermute | solution.py:468
  7.7 14.8 %collective-permute-start.3 = (bf16[32,3200]{1,0:T(8,128)(2,1)S(1)}, bf16[32,3200]{1,0:T(8,128)(2,1)S(1)}, u32[]{:S(2)}, u32[]{:S(2)}) collective-permute-start(bf16[32,3200]{1,0:T(8,128)(2,1)S(1)} %get-tuple-element.51), channel_id=1, source_target_pairs={{0,254},{2,4},{4,2},{6,8},{8,6},{10,12},{12,10},{14,16},{16,14},{1... | collective-permute-start | bytes 614408 | tf_op jit(solution)/shard_map/ppermute | solution.py:468
  10.2 13.8 %collective-permute-start.4 = (bf16[32,3200]{1,0:T(8,128)(2,1)S(1)}, bf16[32,3200]{1,0:T(8,128)(2,1)S(1)}, u32[]{:S(2)}, u32[]{:S(2)}) collective-permute-start(bf16[32,3200]{1,0:T(8,128)(2,1)S(1)} %get-tuple-element.52), channel_id=1, source_target_pairs={{0,252},{2,254},{4,8},{6,10},{8,4},{10,6},{12,16},{14,18},{16,12},... | collective-permute-start | bytes 614408 | tf_op jit(solution)/shard_map/ppermute | solution.py:468
  16.0 8.7 %collective-permute-start = (bf16[32,3200]{1,0:T(8,128)(2,1)}, bf16[32,3200]{1,0:T(8,128)(2,1)S(1)}, u32[]{:S(2)}, u32[]{:S(2)}) collective-permute-start(bf16[32,3200]{1,0:T(8,128)(2,1)} %fo_ref.1), channel_id=1, source_target_pairs={{0,1},{1,0},{2,3},{3,2},{4,5},{5,4},{6,7},{7,6},{8,9},{9,8},{10,11... | collective-permute-start | bytes 614408 | tf_op jit(solution)/shard_map/ppermute | solution.py:396
  16.1 9.4 %copy-start.10 = (bf16[32,3200]{1,0:T(8,128)(2,1)}, bf16[32,3200]{1,0:T(8,128)(2,1)S(1)}, u32[]{:S(2)}) copy-start(bf16[32,3200]{1,0:T(8,128)(2,1)S(1)} %collective-permute-done.1.ho0_ref) | copy-start | bytes 614404
  16.1 8.6 %collective-permute-start.5 = (bf16[32,3200]{1,0:T(8,128)(2,1)S(1)}, bf16[32,3200]{1,0:T(8,128)(2,1)S(1)}, u32[]{:S(2)}, u32[]{:S(2)}) collective-permute-start(bf16[32,3200]{1,0:T(8,128)(2,1)S(1)} %collective-permute-done.1.ho0_ref), channel_id=1, source_target_pairs={{0,1},{1,0},{2,3},{3,2},{4,5},{5,4},{6,7},{7,6},{8,9},{9,8},{10,11... | collective-permute-start | bytes 614408 | tf_op jit(solution)/shard_map/ppermute | solution.py:396
  18.1 7.3 %copy-start.11 = (bf16[32,3200]{1,0:T(8,128)(2,1)}, bf16[32,3200]{1,0:T(8,128)(2,1)S(1)}, u32[]{:S(2)}) copy-start(bf16[32,3200]{1,0:T(8,128)(2,1)S(1)} %collective-permute-done.2.ho1_ref) | copy-start | bytes 614404
  18.1 6.6 %collective-permute-start.6 = (bf16[32,3200]{1,0:T(8,128)(2,1)S(1)}, bf16[32,3200]{1,0:T(8,128)(2,1)S(1)}, u32[]{:S(2)}, u32[]{:S(2)}) collective-permute-start(bf16[32,3200]{1,0:T(8,128)(2,1)S(1)} %collective-permute-done.2.ho1_ref), channel_id=1, source_target_pairs={{0,1},{1,0},{2,3},{3,2},{4,5},{5,4},{6,7},{7,6},{8,9},{9,8},{10,11... | collective-permute-start | bytes 614408 | tf_op jit(solution)/shard_map/ppermute | solution.py:396
  22.5 3.0 %copy-start.12 = (bf16[32,3200]{1,0:T(8,128)(2,1)}, bf16[32,3200]{1,0:T(8,128)(2,1)S(1)}, u32[]{:S(2)}) copy-start(bf16[32,3200]{1,0:T(8,128)(2,1)S(1)} %collective-permute-done.3.ho2_ref) | copy-start | bytes 614404
  22.5 2.2 %collective-permute-start.7 = (bf16[32,3200]{1,0:T(8,128)(2,1)S(1)}, bf16[32,3200]{1,0:T(8,128)(2,1)S(1)}, u32[]{:S(2)}, u32[]{:S(2)}) collective-permute-start(bf16[32,3200]{1,0:T(8,128)(2,1)S(1)} %collective-permute-done.3.ho2_ref), channel_id=1, source_target_pairs={{0,1},{1,0},{2,3},{3,2},{4,5},{5,4},{6,7},{7,6},{8,9},{9,8},{10,11... | collective-permute-start | bytes 614408 | tf_op jit(solution)/shard_map/ppermute | solution.py:396
  24.0 1.5 %copy-start.13 = (bf16[32,3200]{1,0:T(8,128)(2,1)}, bf16[32,3200]{1,0:T(8,128)(2,1)S(1)}, u32[]{:S(2)}) copy-start(bf16[32,3200]{1,0:T(8,128)(2,1)S(1)} %collective-permute-done.4.ho3_ref) | copy-start | bytes 614404
  24.0 1.5 %collective-permute-start.8 = (bf16[32,3200]{1,0:T(8,128)(2,1)S(1)}, bf16[32,3200]{1,0:T(8,128)(2,1)S(1)}, u32[]{:S(2)}, u32[]{:S(2)}) collective-permute-start(bf16[32,3200]{1,0:T(8,128)(2,1)S(1)} %collective-permute-done.4.ho3_ref), channel_id=1, source_target_pairs={{0,1},{1,0},{2,3},{3,2},{4,5},{5,4},{6,7},{7,6},{8,9},{9,8},{10,11... | collective-permute-start | bytes 614408 | tf_op jit(solution)/shard_map/ppermute | solution.py:396
  24.6 17.2 %copy-start = (bf16[6400,256]{1,0:T(8,128)(2,1)S(1)}, bf16[6400,256]{1,0:T(8,128)(2,1)}, u32[]{:S(2)}) copy-start(bf16[6400,256]{1,0:T(8,128)(2,1)} %weight_ref.1) | copy-start | bytes 9830404
  24.6 17.2 %copy-start.2 = (bf16[32,3200]{1,0:T(8,128)(2,1)S(1)}, bf16[32,3200]{1,0:T(8,128)(2,1)}, u32[]{:S(2)}) copy-start(bf16[32,3200]{1,0:T(8,128)(2,1)} %fo_ref.1) | copy-start | bytes 614404
  24.6 17.2 %copy-start.6 = (f32[32,256]{1,0:T(8,128)S(1)}, f32[32,256]{1,0:T(8,128)}, u32[]{:S(2)}) copy-start(f32[32,256]{1,0:T(8,128)} %target_ref.1) | copy-start | bytes 98308
  24.6 17.2 %copy-start.8 = (s32[4]{0:T(128)S(1)}, s32[4]{0:T(128)}, u32[]{:S(2)}) copy-start(s32[4]{0:T(128)} %orbitals_ref.1) | copy-start | bytes 52
  24.7 17.2 %copy-start.9 = (s32[32]{0:T(128)S(1)}, s32[32]{0:T(128)}, u32[]{:S(2)}) copy-start(s32[32]{0:T(128)} %param.24) | copy-start | bytes 388
  24.7 0.8 copy-start.4
  24.7 0.8 copy-start.14
  24.7 0.8 copy-start.15
  24.7 0.9 copy-start.16
  25.6 0.7 copy-start.17
  39.5 2.4 %collective-permute-start.9 = (bf16[32,6400]{1,0:T(8,128)(2,1)}, bf16[32,6400]{1,0:T(8,128)(2,1)S(1)}, u32[]{:S(2)}, u32[]{:S(2)}) collective-permute-start(bf16[32,6400]{1,0:T(8,128)(2,1)} %messages.1.mine_ref), channel_id=1, source_target_pairs={{0,1},{1,0},{2,3},{3,2},{4,5},{5,4},{6,7},{7,6},{8,9},{9,8},{10,11... | collective-permute-start | bytes 1228808 | tf_op jit(solution)/shard_map/ppermute | solution.py:396
  41.9 1.0 copy-start.3
  42.9 0.9 copy-start.5
  71.1 16.2 %collective-permute-start.14 = (bf16[32,3200]{1,0:T(8,128)(2,1)S(1)}, bf16[32,3200]{1,0:T(8,128)(2,1)S(1)}, u32[]{:S(2)}, u32[]{:S(2)}) collective-permute-start(bf16[32,3200]{1,0:T(8,128)(2,1)S(1)} %get-tuple-element.58), channel_id=1, source_target_pairs={{0,1},{1,0},{2,3},{3,2},{4,5},{5,4},{6,7},{7,6},{8,9},{9,8},{10,11... | collective-permute-start | bytes 614408 | tf_op jit(solution)/shard_map/ppermute | solution.py:396
  71.2 14.0 %collective-permute-start.12 = (bf16[200,256]{1,0:T(8,128)(2,1)S(1)}, bf16[200,256]{1,0:T(8,128)(2,1)S(1)}, u32[]{:S(2)}, u32[]{:S(2)}) collective-permute-start(bf16[200,256]{1,0:T(8,128)(2,1)S(1)} %partial_grad.1), channel_id=1, source_target_pairs={{0,128},{64,192},{128,0},{192,64},{1,129},{65,193},{129,1},{193,65... | collective-permute-start | bytes 307208 | tf_op jit(solution)/shard_map/ppermute | solution.py:396
  77.3 8.9 %collective-permute-start.11 = (bf16[200,256]{1,0:T(8,128)(2,1)S(1)}, bf16[200,256]{1,0:T(8,128)(2,1)S(1)}, u32[]{:S(2)}, u32[]{:S(2)}) collective-permute-start(bf16[200,256]{1,0:T(8,128)(2,1)S(1)} %partial_grad.1), channel_id=1, source_target_pairs={{0,192},{64,0},{128,64},{192,128},{1,193},{65,1},{129,65},{193,129... | collective-permute-start | bytes 307208 | tf_op jit(solution)/shard_map/ppermute | solution.py:396
  77.9 9.4 %collective-permute-start.10 = (bf16[200,256]{1,0:T(8,128)(2,1)S(1)}, bf16[200,256]{1,0:T(8,128)(2,1)S(1)}, u32[]{:S(2)}, u32[]{:S(2)}) collective-permute-start(bf16[200,256]{1,0:T(8,128)(2,1)S(1)} %partial_grad.1), channel_id=1, source_target_pairs={{0,64},{64,128},{128,192},{192,0},{1,65},{65,129},{129,193},{193,1... | collective-permute-start | bytes 307208 | tf_op jit(solution)/shard_map/ppermute | solution.py:396
  80.4 1.2 collective-permute-start.13
  87.3 4.9 %collective-permute-start.15 = (bf16[200,256]{1,0:T(8,128)(2,1)S(1)}, bf16[200,256]{1,0:T(8,128)(2,1)S(1)}, u32[]{:S(2)}, u32[]{:S(2)}) collective-permute-start(bf16[200,256]{1,0:T(8,128)(2,1)S(1)} %add_convert_fusion), channel_id=1, source_target_pairs={{0,32},{32,0},{1,33},{33,1},{2,34},{34,2},{3,35},{35,3},{4,36},{36... | collective-permute-start | bytes 307208 | tf_op jit(solution)/shard_map/ppermute | solution.py:396
  92.3 7.0 %collective-permute-start.16 = (bf16[400,256]{1,0:T(8,128)(2,1)S(1)}, bf16[400,256]{1,0:T(8,128)(2,1)S(1)}, u32[]{:S(2)}, u32[]{:S(2)}) collective-permute-start(bf16[400,256]{1,0:T(8,128)(2,1)S(1)} %pad_maximum_fusion.1), channel_id=1, source_target_pairs={{0,2},{1,9},{2,4},{3,11},{4,6},{5,13},{6,0},{7,15},{8,10},{9,17},{... | collective-permute-start | bytes 614408 | tf_op jit(solution)/shard_map/ppermute | solution.py:407
  93.3 8.9 %collective-permute-start.19 = (bf16[400,256]{1,0:T(8,128)(2,1)S(1)}, bf16[400,256]{1,0:T(8,128)(2,1)S(1)}, u32[]{:S(2)}, u32[]{:S(2)}) collective-permute-start(bf16[400,256]{1,0:T(8,128)(2,1)S(1)} %pad_maximum_fusion.1), channel_id=1, source_target_pairs={{0,4},{1,17},{2,6},{3,19},{4,0},{5,21},{6,2},{7,23},{8,12},{9,25},... | collective-permute-start | bytes 614408 | tf_op jit(solution)/shard_map/ppermute | solution.py:407
  95.7 6.7 %collective-permute-start.20 = (bf16[400,256]{1,0:T(8,128)(2,1)S(1)}, bf16[400,256]{1,0:T(8,128)(2,1)S(1)}, u32[]{:S(2)}, u32[]{:S(2)}) collective-permute-start(bf16[400,256]{1,0:T(8,128)(2,1)S(1)} %pad_maximum_fusion.1), channel_id=1, source_target_pairs={{0,6},{1,25},{2,0},{3,27},{4,2},{5,29},{6,4},{7,31},{8,14},{9,1},{... | collective-permute-start | bytes 614408 | tf_op jit(solution)/shard_map/ppermute | solution.py:407
  99.3 11.0 %collective-permute-start.17 = (bf16[800,256]{1,0:T(8,128)(2,1)S(1)}, bf16[800,256]{1,0:T(8,128)(2,1)S(1)}, u32[]{:S(2)}, u32[]{:S(2)}) collective-permute-start(bf16[800,256]{1,0:T(8,128)(2,1)S(1)} %pad_maximum_fusion.refs_0_), channel_id=1, source_target_pairs={{0,8},{1,3},{2,10},{3,5},{4,12},{5,7},{6,14},{7,1},{8,16},{9,11},{... | collective-permute-start | bytes 1228808 | tf_op jit(solution)/shard_map/ppermute | solution.py:407
  102.4 8.0 %collective-permute-start.21 = (bf16[800,256]{1,0:T(8,128)(2,1)S(1)}, bf16[800,256]{1,0:T(8,128)(2,1)S(1)}, u32[]{:S(2)}, u32[]{:S(2)}) collective-permute-start(bf16[800,256]{1,0:T(8,128)(2,1)S(1)} %constant_dynamic-update-slice_fusion.refs_1_), channel_id=1, source_target_pairs={{0,24},{1,7},{2,26},{3,1},{4,28},{5,3},{6,30},{7,5},{8,0},{9,15},{... | collective-permute-start | bytes 1228808 | tf_op jit(solution)/shard_map/ppermute | solution.py:407
  104.8 10.4 %collective-permute-start.24 = (bf16[800,256]{1,0:T(8,128)(2,1)S(1)}, bf16[800,256]{1,0:T(8,128)(2,1)S(1)}, u32[]{:S(2)}, u32[]{:S(2)}) collective-permute-start(bf16[800,256]{1,0:T(8,128)(2,1)S(1)} %pad_maximum_fusion.refs_0_), channel_id=1, source_target_pairs={{0,24},{1,7},{2,26},{3,1},{4,28},{5,3},{6,30},{7,5},{8,0},{9,15},{... | collective-permute-start | bytes 1228808 | tf_op jit(solution)/shard_map/ppermute | solution.py:407
  106.7 9.2 %collective-permute-start.23 = (bf16[800,256]{1,0:T(8,128)(2,1)S(1)}, bf16[800,256]{1,0:T(8,128)(2,1)S(1)}, u32[]{:S(2)}, u32[]{:S(2)}) collective-permute-start(bf16[800,256]{1,0:T(8,128)(2,1)S(1)} %constant_dynamic-update-slice_fusion.refs_1_), channel_id=1, source_target_pairs={{0,8},{1,3},{2,10},{3,5},{4,12},{5,7},{6,14},{7,1},{8,16},{9,11},{... | collective-permute-start | bytes 1228808 | tf_op jit(solution)/shard_map/ppermute | solution.py:407
  110.4 9.9 %collective-permute-start.18 = (bf16[800,256]{1,0:T(8,128)(2,1)S(1)}, bf16[800,256]{1,0:T(8,128)(2,1)S(1)}, u32[]{:S(2)}, u32[]{:S(2)}) collective-permute-start(bf16[800,256]{1,0:T(8,128)(2,1)S(1)} %collective-permute-done.17.refs_2_), channel_id=1, source_target_pairs={{0,8},{1,3},{2,10},{3,5},{4,12},{5,7},{6,14},{7,1},{8,16},{9,11},{... | collective-permute-start | bytes 1228808 | tf_op jit(solution)/shard_map/ppermute | solution.py:407
  110.4 9.8 %collective-permute-start.22 = (bf16[800,256]{1,0:T(8,128)(2,1)S(1)}, bf16[800,256]{1,0:T(8,128)(2,1)S(1)}, u32[]{:S(2)}, u32[]{:S(2)}) collective-permute-start(bf16[800,256]{1,0:T(8,128)(2,1)S(1)} %collective-permute-done.21.refs_5_), channel_id=1, source_target_pairs={{0,24},{1,7},{2,26},{3,1},{4,28},{5,3},{6,30},{7,5},{8,0},{9,15},{... | collective-permute-start | bytes 1228808 | tf_op jit(solution)/shard_map/ppermute | solution.py:407

commit v8 on v5

--- a/solution.py
+++ b/solution.py
@@ -472,11 +472,11 @@
     share = 2 * features.shape[1] // parts
     part = partial_grad(got.reshape(-1, got.shape[2]), share)
     part, loss, send = lax.optimization_barrier((part, loss, send))
-    sums = [shift(part, "zh", by) for by in (1, -1, 2)]
+    sums = [shift(part, "zh", by) for by in (2, 1, -1)]
     loss_oth, feat_oth = shift(loss[:, 0], "chan", 1), shift(send, "chan", 1)
     sums, loss_oth, feat_oth = lax.optimization_barrier((sums, loss_oth, feat_oth))
-    near = sums[0].astype(F32) + sums[1].astype(F32)
-    total = (part.astype(F32) + sums[2].astype(F32) + near).astype(BF16)
+    near = sums[1].astype(F32) + sums[2].astype(F32)
+    total = (part.astype(F32) + sums[0].astype(F32) + near).astype(BF16)
     atom_loss = loss[:, 0] + loss_oth
     grad_features = keep + feat_oth.astype(F32)
     twin = shift(total, "zl", 1)

time: 123 us -> 123 us (level); the launches traced: 122 us -> 120 us
  starting transfers between devices: 36.7 us -> 33.9 us
    ppermute x16, starting transfers between devices: 20.5 us -> 19 us  [shift(): return lax.ppermute(x, axis, [(i, (i + by) % count) for i in range(count)])]
    ppermute x9, starting transfers between devices: 16.3 us -> 14.9 us  [plane_shift(): return lax.ppermute(x, ('y', 'x', 'chan'), pairs)]
where the time goes in v8:
time: 123 us; the launch traced here: 120 us
  starting transfers between devices  33.9 us (28%)
  waiting for transfers between devices  31.4 us (26%)
  blocking collectives  24.3 us (20%)
  Pallas kernels  23.9 us (19%)
  local copies, waits for them, and re-layouts  4.25 us (3%)
  other arithmetic  1.61 us (1%)
    all_to_all x1, blocking collectives, body(): got = lax.all_to_all(load, GROUP, split_axis=0, concat_axis=0, tiled=True)  24.3 us
    ppermute x16, waiting for transfers between devices, shift(): return lax.ppermute(x, axis, [(i, (i + by) % count) for i in range(count)])  22.8 us
    ppermute x16, starting transfers between devices, shift(): return lax.ppermute(x, axis, [(i, (i + by) % count) for i in range(count)])  19 us
    ppermute x9, starting transfers between devices, plane_shift(): return lax.ppermute(x, ('y', 'x', 'chan'), pairs)  14.9 us
    pallas_call x1, Pallas kernels, messages(): pl.pallas_call(message_kernel, out_shape=jax.ShapeDtypeStruct((atoms, 2 *...  12.7 us
    ppermute x9, waiting for transfers between devices, plane_shift(): return lax.ppermute(x, ('y', 'x', 'chan'), pairs)  8.61 us
    unnamed x37, local copies, waits for them, and re-layouts  4.23 us
    pallas_call x1, Pallas kernels, prepare(): pl.pallas_call(prepare_kernel, out_shape=(frames, frames, jax.ShapeDtypeS...  3.96 us
  transfers between devices with their start and end apart: 25, of which 15 were waited for; matrix products, arithmetic and copies ran while one was open for 1% of the time, Pallas kernels for 5%

profile of v8, /device:TPU:32, one launch (start us, length us, event | category | flops | bytes accessed | tf_op | source)
XLA Modules:
  0.0 120.3 jit_solution(15479831305887197666)
XLA Ops:
  0.6 0.0 copy-start.1
  0.6 0.9 copy-done.1
  1.6 0.7 copy-done.7
  2.2 0.5 leaving.1
  2.7 1.6 %collective-permute-start.1 = (bf16[32,3200]{1,0:T(8,128)(2,1)S(1)}, bf16[32,3200]{1,0:T(8,128)(2,1)S(1)}, u32[]{:S(2)}, u32[]{:S(2)}) collective-permute-start(bf16[32,3200]{1,0:T(8,128)(2,1)S(1)} %get-tuple-element.49), channel_id=1, source_target_pairs={{0,2},{2,4},{4,6},{6,8},{8,10},{10,12},{12,14},{14,16},{16,18},{18... | collective-permute-start | bytes 614408 | tf_op jit(solution)/shard_map/ppermute | solution.py:396
  4.3 2.7 %collective-permute-start.2 = (bf16[32,3200]{1,0:T(8,128)(2,1)S(1)}, bf16[32,3200]{1,0:T(8,128)(2,1)S(1)}, u32[]{:S(2)}, u32[]{:S(2)}) collective-permute-start(bf16[32,3200]{1,0:T(8,128)(2,1)S(1)} %get-tuple-element.50), channel_id=1, source_target_pairs={{0,4},{2,6},{4,8},{6,10},{8,12},{10,14},{12,16},{14,18},{16,20},{1... | collective-permute-start | bytes 614408 | tf_op jit(solution)/shard_map/ppermute | solution.py:396
  7.0 4.4 %collective-permute-start.3 = (bf16[32,3200]{1,0:T(8,128)(2,1)S(1)}, bf16[32,3200]{1,0:T(8,128)(2,1)S(1)}, u32[]{:S(2)}, u32[]{:S(2)}) collective-permute-start(bf16[32,3200]{1,0:T(8,128)(2,1)S(1)} %get-tuple-element.51), channel_id=1, source_target_pairs={{0,254},{2,0},{4,2},{6,4},{8,6},{10,8},{12,10},{14,12},{16,14},{18... | collective-permute-start | bytes 614408 | tf_op jit(solution)/shard_map/ppermute | solution.py:396
  11.5 0.5 collective-permute-start.4
  12.0 4.0 %prepare.1 = (f32[2,115,8,128]{3,2,1,0:T(8,128)}, f32[2,115,8,128]{3,2,1,0:T(8,128)}, bf16[160,256]{1,0:T(8,128)(2,1)}, bf16[32,256]{1,0:T(8,128)(2,1)}, bf16[64...) custom-call(s32[1,256]{1,0:T(1,128)} %bitcast.13, s32[1,256]{1,0:T(1,128)} %bitcast.14, ...), custom_call_target="tpu_custom_call" | custom-call | flops 100000000 | bytes 10000000 | tf_op jit(solution)/shard_map/prepare/pallas_call | solution.py:93
  15.9 0.1 collective-permute-start
  16.0 1.1 collective-permute-done.1.ho0_ref
  17.1 0.0 collective-permute-start.5
  17.2 1.1 collective-permute-done.2.ho1_ref
  18.2 0.0 collective-permute-start.6
  18.2 6.0 %collective-permute-done.3.ho2_ref = bf16[32,3200]{1,0:T(8,128)(2,1)S(1)} collective-permute-done((bf16[32,3200]{1,0:T(8,128)(2,1)S(1)}, bf16[32,3200]{1,0:T(8,128)(2,1)S(1)}, u32[]{:S(2)}, u32[]{:S(2)}) %collective-permute-start.3) | collective-permute-done | bytes 204832 | tf_op jit(solution)/shard_map/ppermute | solution.py:396
  24.2 0.0 collective-permute-done.4.ho3_ref
  24.2 0.5 collective-permute-start.8
  24.7 0.0 collective-permute-done.6.hx1_ref
  24.8 0.9 collective-permute-done.7.hx2_ref
  25.7 0.3 collective-permute-done.8.hx3_ref
  26.0 0.3 copy-done.16
  26.3 0.3 copy-done.17
  26.7 0.0 copy-start.9
  26.7 12.7 %messages.1.mine_ref = bf16[32,6400]{1,0:T(8,128)(2,1)} custom-call(s32[1]{0:T(128)} %bitcast.core_ref, f32[2,115,8,128]{3,2,1,0:T(8,128)} %get-tuple-element.42.frames_hbm, f32[2,115,8,128]{3,2,1,0:T(8,128)} %get-tuple-element.43.wframes_hbm, bf16[160,256]{1,0:T(8,128)(2,1)} %get-tuple-element.44.onehot_hbm, bf16[32,256]{1,0:T(8,128)(2,1)} %get-tuple-element.45.scatter_hbm, ...), custom_call_target="tpu_custom_call" | custom-call | flops 5000000000 | bytes 6000000 | tf_op jit(solution)/shard_map/messages/pallas_call | solution.py:267
  39.3 0.5 collective-permute-start.9
  39.8 1.7 %collective-permute-done.9.recv_ref = bf16[32,6400]{1,0:T(8,128)(2,1)S(1)} collective-permute-done((bf16[32,6400]{1,0:T(8,128)(2,1)}, bf16[32,6400]{1,0:T(8,128)(2,1)S(1)}, u32[]{:S(2)}, u32[]{:S(2)}) %collective-permute-start.9) | collective-permute-done | bytes 409632 | tf_op jit(solution)/shard_map/ppermute | solution.py:396
  41.6 1.0 copy-done.3
  42.6 0.9 copy-done.5
  43.5 2.9 %head.1 = (bf16[32,32,512]{2,1,0:T(8,128)(2,1)S(1)}, f32[32,1]{1,0:T(8,128)S(1)}, f32[32,3200]{1,0:T(8,128)S(1)}, bf16[32,3200]{1,0:T(8,128)(2,1)S(1)}) custom-call(s32[1]{0:T(128)} %bitcast.core_ref, s32[4]{0:T(128)S(1)} %copy-done.8, s32[1,32]{1,0:T(1,128)S(1)} %bitcast.11, bf16[32,3200]{1,0:T(8,128)(2,1)S(1)} %copy-done.2, ...), custom_call_target="tpu_custom_call" | custom-call | flops 300000000 | bytes 6000000 | tf_op jit(solution)/shard_map/head/pallas_call | solution.py:333
  46.4 24.3 %all_to_all.5 = bf16[32,32,512]{2,1,0:T(8,128)(2,1)S(1)} all-to-all(bf16[32,32,512]{2,1,0:T(8,128)(2,1)S(1)} %get-tuple-element.53), channel_id=1, replica_groups=mesh['zh'=4,'zl'=2,'y'=4,'x'=4,'chan'=2] {'zl','y','x'}, dimensions={0} | all-to-all | bytes 2097152 | tf_op jit(solution)/shard_map/all_to_all | solution.py:471
  70.7 0.3 partial_grad.1
  71.0 0.1 collective-permute-start.14
  71.1 4.1 %collective-permute-start.12 = (bf16[200,256]{1,0:T(8,128)(2,1)S(1)}, bf16[200,256]{1,0:T(8,128)(2,1)S(1)}, u32[]{:S(2)}, u32[]{:S(2)}) collective-permute-start(bf16[200,256]{1,0:T(8,128)(2,1)S(1)} %partial_grad.1), channel_id=1, source_target_pairs={{0,192},{64,0},{128,64},{192,128},{1,193},{65,1},{129,65},{193,129... | collective-permute-start | bytes 307208 | tf_op jit(solution)/shard_map/ppermute | solution.py:396
  75.2 0.0 collective-permute-start.11
  75.2 4.3 %collective-permute-start.10 = (bf16[200,256]{1,0:T(8,128)(2,1)S(1)}, bf16[200,256]{1,0:T(8,128)(2,1)S(1)}, u32[]{:S(2)}, u32[]{:S(2)}) collective-permute-start(bf16[200,256]{1,0:T(8,128)(2,1)S(1)} %partial_grad.1), channel_id=1, source_target_pairs={{0,128},{64,192},{128,0},{192,64},{1,129},{65,193},{129,1},{193,65... | collective-permute-start | bytes 307208 | tf_op jit(solution)/shard_map/ppermute | solution.py:396
  79.5 0.1 reduce
  79.6 0.1 collective-permute-start.13
  79.7 1.1 collective-permute-done.13
  80.8 0.0 collective-permute-done.12
  80.8 5.8 %collective-permute-done.11 = bf16[200,256]{1,0:T(8,128)(2,1)S(1)} collective-permute-done((bf16[200,256]{1,0:T(8,128)(2,1)S(1)}, bf16[200,256]{1,0:T(8,128)(2,1)S(1)}, u32[]{:S(2)}, u32[]{:S(2)}) %collective-permute-start.11) | collective-permute-done | bytes 102432 | tf_op jit(solution)/shard_map/ppermute | solution.py:396
  86.6 0.0 collective-permute-done.14
  86.6 0.1 add_convert_fusion
  86.7 0.1 collective-permute-start.15
  86.8 4.8 %collective-permute-done.15 = bf16[200,256]{1,0:T(8,128)(2,1)S(1)} collective-permute-done((bf16[200,256]{1,0:T(8,128)(2,1)S(1)}, bf16[200,256]{1,0:T(8,128)(2,1)S(1)}, u32[]{:S(2)}, u32[]{:S(2)}) %collective-permute-start.15) | collective-permute-done | bytes 102432 | tf_op jit(solution)/shard_map/ppermute | solution.py:396
  91.7 0.4 collective-permute-start.16
  92.1 3.1 %collective-permute-start.19 = (bf16[400,256]{1,0:T(8,128)(2,1)S(1)}, bf16[400,256]{1,0:T(8,128)(2,1)S(1)}, u32[]{:S(2)}, u32[]{:S(2)}) collective-permute-start(bf16[400,256]{1,0:T(8,128)(2,1)S(1)} %pad_maximum_fusion.1), channel_id=1, source_target_pairs={{0,4},{1,17},{2,6},{3,19},{4,0},{5,21},{6,2},{7,23},{8,12},{9,25},... | collective-permute-start | bytes 614408 | tf_op jit(solution)/shard_map/ppermute | solution.py:407
  95.2 0.9 collective-permute-start.20
  96.1 2.6 %collective-permute-done.16 = bf16[400,256]{1,0:T(8,128)(2,1)S(1)} collective-permute-done((bf16[400,256]{1,0:T(8,128)(2,1)S(1)}, bf16[400,256]{1,0:T(8,128)(2,1)S(1)}, u32[]{:S(2)}, u32[]{:S(2)}) %collective-permute-start.16) | collective-permute-done | bytes 204832 | tf_op jit(solution)/shard_map/ppermute | solution.py:407
  98.7 3.1 %collective-permute-start.17 = (bf16[800,256]{1,0:T(8,128)(2,1)S(1)}, bf16[800,256]{1,0:T(8,128)(2,1)S(1)}, u32[]{:S(2)}, u32[]{:S(2)}) collective-permute-start(bf16[800,256]{1,0:T(8,128)(2,1)S(1)} %pad_maximum_fusion.refs_0_), channel_id=1, source_target_pairs={{0,8},{1,3},{2,10},{3,5},{4,12},{5,7},{6,14},{7,1},{8,16},{9,11},{... | collective-permute-start | bytes 1228808 | tf_op jit(solution)/shard_map/ppermute | solution.py:407
  101.9 1.3 %collective-permute-start.21 = (bf16[800,256]{1,0:T(8,128)(2,1)S(1)}, bf16[800,256]{1,0:T(8,128)(2,1)S(1)}, u32[]{:S(2)}, u32[]{:S(2)}) collective-permute-start(bf16[800,256]{1,0:T(8,128)(2,1)S(1)} %constant_dynamic-update-slice_fusion.refs_1_), channel_id=1, source_target_pairs={{0,24},{1,7},{2,26},{3,1},{4,28},{5,3},{6,30},{7,5},{8,0},{9,15},{... | collective-permute-start | bytes 1228808 | tf_op jit(solution)/shard_map/ppermute | solution.py:407
  103.2 0.1 pad_add_fusion.place_ref
  103.3 1.3 %collective-permute-start.24 = (bf16[800,256]{1,0:T(8,128)(2,1)S(1)}, bf16[800,256]{1,0:T(8,128)(2,1)S(1)}, u32[]{:S(2)}, u32[]{:S(2)}) collective-permute-start(bf16[800,256]{1,0:T(8,128)(2,1)S(1)} %pad_maximum_fusion.refs_0_), channel_id=1, source_target_pairs={{0,24},{1,7},{2,26},{3,1},{4,28},{5,3},{6,30},{7,5},{8,0},{9,15},{... | collective-permute-start | bytes 1228808 | tf_op jit(solution)/shard_map/ppermute | solution.py:407
  104.6 0.7 collective-permute-start.23
  105.3 3.0 %collective-permute-done.17.refs_2_ = bf16[800,256]{1,0:T(8,128)(2,1)S(1)} collective-permute-done((bf16[800,256]{1,0:T(8,128)(2,1)S(1)}, bf16[800,256]{1,0:T(8,128)(2,1)S(1)}, u32[]{:S(2)}, u32[]{:S(2)}) %collective-permute-start.17) | collective-permute-done | bytes 409632 | tf_op jit(solution)/shard_map/ppermute | solution.py:407
  108.3 1.5 %collective-permute-start.18 = (bf16[800,256]{1,0:T(8,128)(2,1)S(1)}, bf16[800,256]{1,0:T(8,128)(2,1)S(1)}, u32[]{:S(2)}, u32[]{:S(2)}) collective-permute-start(bf16[800,256]{1,0:T(8,128)(2,1)S(1)} %collective-permute-done.17.refs_2_), channel_id=1, source_target_pairs={{0,8},{1,3},{2,10},{3,5},{4,12},{5,7},{6,14},{7,1},{8,16},{9,11},{... | collective-permute-start | bytes 1228808 | tf_op jit(solution)/shard_map/ppermute | solution.py:407
  109.8 0.1 collective-permute-done.21.refs_5_
  109.9 2.5 %collective-permute-start.22 = (bf16[800,256]{1,0:T(8,128)(2,1)S(1)}, bf16[800,256]{1,0:T(8,128)(2,1)S(1)}, u32[]{:S(2)}, u32[]{:S(2)}) collective-permute-start(bf16[800,256]{1,0:T(8,128)(2,1)S(1)} %collective-permute-done.21.refs_5_), channel_id=1, source_target_pairs={{0,24},{1,7},{2,26},{3,1},{4,28},{5,3},{6,30},{7,5},{8,0},{9,15},{... | collective-permute-start | bytes 1228808 | tf_op jit(solution)/shard_map/ppermute | solution.py:407
  112.4 0.8 convert_add_fusion
  113.2 0.5 add.15
  113.7 0.6 collective-permute-done.24.refs_4_
  114.3 2.1 %assemble.2.refs_2_ = bf16[6400,256]{1,0:T(8,128)(2,1)} custom-call(s32[3]{0:T(128)S(1)} %pad_add_fusion.place_ref, bf16[800,256]{1,0:T(8,128)(2,1)S(1)} %pad_maximum_fusion.refs_0_, bf16[800,256]{1,0:T(8,128)(2,1)S(1)} %constant_dynamic-update-slice_fusion.refs_1_, bf16[800,256]{1,0:T(8,128)(2,1)S(1)} %collective-permute-done.17.refs_2_, ...), custom_call_target="tpu_custom_call" | custom-call | tf_op jit(solution)/shard_map/assemble/pallas_call | solution.py:437
  116.4 1.8 %collective-permute-done.18.refs_0_ = bf16[800,256]{1,0:T(8,128)(2,1)S(1)} collective-permute-done((bf16[800,256]{1,0:T(8,128)(2,1)S(1)}, bf16[800,256]{1,0:T(8,128)(2,1)S(1)}, u32[]{:S(2)}, u32[]{:S(2)}) %collective-permute-start.18) | collective-permute-done | bytes 409632 | tf_op jit(solution)/shard_map/ppermute | solution.py:407
  118.2 0.5 collective-permute-done.22.refs_1_
  118.7 1.5 %assemble.3 = bf16[6400,256]{1,0:T(8,128)(2,1)} custom-call(s32[3]{0:T(128)S(1)} %pad_add_fusion.place_ref, bf16[800,256]{1,0:T(8,128)(2,1)S(1)} %collective-permute-done.18.refs_0_, bf16[800,256]{1,0:T(8,128)(2,1)S(1)} %collective-permute-done.22.refs_1_, bf16[6400,256]{1,0:T(8,128)(2,1)} %assemble.2.refs_2_), custom_call_target="tpu_custom_call", output_to_operand_aliasing={{}: (3, {})} | custom-call | tf_op jit(solution)/shard_map/assemble/pallas_call | solution.py:437
  (40 shorter events, 0.2 us)
Async XLA Ops:
  0.6 0.9 copy-start.1
  1.6 0.7 copy-start.7
  2.7 14.4 %collective-permute-start.1 = (bf16[32,3200]{1,0:T(8,128)(2,1)S(1)}, bf16[32,3200]{1,0:T(8,128)(2,1)S(1)}, u32[]{:S(2)}, u32[]{:S(2)}) collective-permute-start(bf16[32,3200]{1,0:T(8,128)(2,1)S(1)} %get-tuple-element.49), channel_id=1, source_target_pairs={{0,2},{2,4},{4,6},{6,8},{8,10},{10,12},{12,14},{14,16},{16,18},{18... | collective-permute-start | bytes 614408 | tf_op jit(solution)/shard_map/ppermute | solution.py:396
  4.3 13.9 %collective-permute-start.2 = (bf16[32,3200]{1,0:T(8,128)(2,1)S(1)}, bf16[32,3200]{1,0:T(8,128)(2,1)S(1)}, u32[]{:S(2)}, u32[]{:S(2)}) collective-permute-start(bf16[32,3200]{1,0:T(8,128)(2,1)S(1)} %get-tuple-element.50), channel_id=1, source_target_pairs={{0,4},{2,6},{4,8},{6,10},{8,12},{10,14},{12,16},{14,18},{16,20},{1... | collective-permute-start | bytes 614408 | tf_op jit(solution)/shard_map/ppermute | solution.py:396
  7.0 17.2 %collective-permute-start.3 = (bf16[32,3200]{1,0:T(8,128)(2,1)S(1)}, bf16[32,3200]{1,0:T(8,128)(2,1)S(1)}, u32[]{:S(2)}, u32[]{:S(2)}) collective-permute-start(bf16[32,3200]{1,0:T(8,128)(2,1)S(1)} %get-tuple-element.51), channel_id=1, source_target_pairs={{0,254},{2,0},{4,2},{6,4},{8,6},{10,8},{12,10},{14,12},{16,14},{18... | collective-permute-start | bytes 614408 | tf_op jit(solution)/shard_map/ppermute | solution.py:396
  11.5 12.7 %collective-permute-start.4 = (bf16[32,3200]{1,0:T(8,128)(2,1)S(1)}, bf16[32,3200]{1,0:T(8,128)(2,1)S(1)}, u32[]{:S(2)}, u32[]{:S(2)}) collective-permute-start(bf16[32,3200]{1,0:T(8,128)(2,1)S(1)} %get-tuple-element.52), channel_id=1, source_target_pairs={{0,252},{2,254},{4,0},{6,2},{8,4},{10,6},{12,8},{14,10},{16,12},{1... | collective-permute-start | bytes 614408 | tf_op jit(solution)/shard_map/ppermute | solution.py:396
  15.9 8.8 %collective-permute-start = (bf16[32,3200]{1,0:T(8,128)(2,1)}, bf16[32,3200]{1,0:T(8,128)(2,1)S(1)}, u32[]{:S(2)}, u32[]{:S(2)}) collective-permute-start(bf16[32,3200]{1,0:T(8,128)(2,1)} %fo_ref.1), channel_id=1, source_target_pairs={{0,1},{1,0},{2,3},{3,2},{4,5},{5,4},{6,7},{7,6},{8,9},{9,8},{10,11... | collective-permute-start | bytes 614408 | tf_op jit(solution)/shard_map/ppermute | solution.py:396
  17.1 8.8 %copy-start.10 = (bf16[32,3200]{1,0:T(8,128)(2,1)}, bf16[32,3200]{1,0:T(8,128)(2,1)S(1)}, u32[]{:S(2)}) copy-start(bf16[32,3200]{1,0:T(8,128)(2,1)S(1)} %collective-permute-done.1.ho0_ref) | copy-start | bytes 614404
  17.1 7.6 %collective-permute-start.5 = (bf16[32,3200]{1,0:T(8,128)(2,1)S(1)}, bf16[32,3200]{1,0:T(8,128)(2,1)S(1)}, u32[]{:S(2)}, u32[]{:S(2)}) collective-permute-start(bf16[32,3200]{1,0:T(8,128)(2,1)S(1)} %collective-permute-done.1.ho0_ref), channel_id=1, source_target_pairs={{0,1},{1,0},{2,3},{3,2},{4,5},{5,4},{6,7},{7,6},{8,9},{9,8},{10,11... | collective-permute-start | bytes 614408 | tf_op jit(solution)/shard_map/ppermute | solution.py:396
  18.2 7.7 %copy-start.11 = (bf16[32,3200]{1,0:T(8,128)(2,1)}, bf16[32,3200]{1,0:T(8,128)(2,1)S(1)}, u32[]{:S(2)}) copy-start(bf16[32,3200]{1,0:T(8,128)(2,1)S(1)} %collective-permute-done.2.ho1_ref) | copy-start | bytes 614404
  18.2 6.5 %collective-permute-start.6 = (bf16[32,3200]{1,0:T(8,128)(2,1)S(1)}, bf16[32,3200]{1,0:T(8,128)(2,1)S(1)}, u32[]{:S(2)}, u32[]{:S(2)}) collective-permute-start(bf16[32,3200]{1,0:T(8,128)(2,1)S(1)} %collective-permute-done.2.ho1_ref), channel_id=1, source_target_pairs={{0,1},{1,0},{2,3},{3,2},{4,5},{5,4},{6,7},{7,6},{8,9},{9,8},{10,11... | collective-permute-start | bytes 614408 | tf_op jit(solution)/shard_map/ppermute | solution.py:396
  24.2 1.8 %copy-start.12 = (bf16[32,3200]{1,0:T(8,128)(2,1)}, bf16[32,3200]{1,0:T(8,128)(2,1)S(1)}, u32[]{:S(2)}) copy-start(bf16[32,3200]{1,0:T(8,128)(2,1)S(1)} %collective-permute-done.3.ho2_ref) | copy-start | bytes 614404
  24.2 1.5 %collective-permute-start.7 = (bf16[32,3200]{1,0:T(8,128)(2,1)S(1)}, bf16[32,3200]{1,0:T(8,128)(2,1)S(1)}, u32[]{:S(2)}, u32[]{:S(2)}) collective-permute-start(bf16[32,3200]{1,0:T(8,128)(2,1)S(1)} %collective-permute-done.3.ho2_ref), channel_id=1, source_target_pairs={{0,1},{1,0},{2,3},{3,2},{4,5},{5,4},{6,7},{7,6},{8,9},{9,8},{10,11... | collective-permute-start | bytes 614408 | tf_op jit(solution)/shard_map/ppermute | solution.py:396
  24.2 1.8 %copy-start.13 = (bf16[32,3200]{1,0:T(8,128)(2,1)}, bf16[32,3200]{1,0:T(8,128)(2,1)S(1)}, u32[]{:S(2)}) copy-start(bf16[32,3200]{1,0:T(8,128)(2,1)S(1)} %collective-permute-done.4.ho3_ref) | copy-start | bytes 614404
  24.2 1.7 %collective-permute-start.8 = (bf16[32,3200]{1,0:T(8,128)(2,1)S(1)}, bf16[32,3200]{1,0:T(8,128)(2,1)S(1)}, u32[]{:S(2)}, u32[]{:S(2)}) collective-permute-start(bf16[32,3200]{1,0:T(8,128)(2,1)S(1)} %collective-permute-done.4.ho3_ref), channel_id=1, source_target_pairs={{0,1},{1,0},{2,3},{3,2},{4,5},{5,4},{6,7},{7,6},{8,9},{9,8},{10,11... | collective-permute-start | bytes 614408 | tf_op jit(solution)/shard_map/ppermute | solution.py:396
  24.7 1.3 %copy-start.4 = (bf16[32,3200]{1,0:T(8,128)(2,1)}, bf16[32,3200]{1,0:T(8,128)(2,1)S(1)}, u32[]{:S(2)}) copy-start(bf16[32,3200]{1,0:T(8,128)(2,1)S(1)} %collective-permute-done.fx_ref) | copy-start | bytes 614404
  24.7 1.3 %copy-start.14 = (bf16[32,3200]{1,0:T(8,128)(2,1)}, bf16[32,3200]{1,0:T(8,128)(2,1)S(1)}, u32[]{:S(2)}) copy-start(bf16[32,3200]{1,0:T(8,128)(2,1)S(1)} %collective-permute-done.5.hx0_ref) | copy-start | bytes 614404
  24.8 1.2 %copy-start.15 = (bf16[32,3200]{1,0:T(8,128)(2,1)}, bf16[32,3200]{1,0:T(8,128)(2,1)S(1)}, u32[]{:S(2)}) copy-start(bf16[32,3200]{1,0:T(8,128)(2,1)S(1)} %collective-permute-done.6.hx1_ref) | copy-start | bytes 614404
  25.7 0.7 copy-start.16
  25.9 0.7 copy-start.17
  26.6 14.9 %copy-start = (bf16[6400,256]{1,0:T(8,128)(2,1)S(1)}, bf16[6400,256]{1,0:T(8,128)(2,1)}, u32[]{:S(2)}) copy-start(bf16[6400,256]{1,0:T(8,128)(2,1)} %weight_ref.1) | copy-start | bytes 9830404
  26.6 14.9 %copy-start.2 = (bf16[32,3200]{1,0:T(8,128)(2,1)S(1)}, bf16[32,3200]{1,0:T(8,128)(2,1)}, u32[]{:S(2)}) copy-start(bf16[32,3200]{1,0:T(8,128)(2,1)} %fo_ref.1) | copy-start | bytes 614404
  26.6 14.9 %copy-start.6 = (f32[32,256]{1,0:T(8,128)S(1)}, f32[32,256]{1,0:T(8,128)}, u32[]{:S(2)}) copy-start(f32[32,256]{1,0:T(8,128)} %target_ref.1) | copy-start | bytes 98308
  26.6 14.9 %copy-start.8 = (s32[4]{0:T(128)S(1)}, s32[4]{0:T(128)}, u32[]{:S(2)}) copy-start(s32[4]{0:T(128)} %orbitals_ref.1) | copy-start | bytes 52
  26.7 14.9 %copy-start.9 = (s32[32]{0:T(128)S(1)}, s32[32]{0:T(128)}, u32[]{:S(2)}) copy-start(s32[32]{0:T(128)} %param.24) | copy-start | bytes 388
  39.3 2.2 %collective-permute-start.9 = (bf16[32,6400]{1,0:T(8,128)(2,1)}, bf16[32,6400]{1,0:T(8,128)(2,1)S(1)}, u32[]{:S(2)}, u32[]{:S(2)}) collective-permute-start(bf16[32,6400]{1,0:T(8,128)(2,1)} %messages.1.mine_ref), channel_id=1, source_target_pairs={{0,1},{1,0},{2,3},{3,2},{4,5},{5,4},{6,7},{7,6},{8,9},{9,8},{10,11... | collective-permute-start | bytes 1228808 | tf_op jit(solution)/shard_map/ppermute | solution.py:396
  41.6 1.0 copy-start.3
  42.6 0.9 copy-start.5
  71.0 15.6 %collective-permute-start.14 = (bf16[32,3200]{1,0:T(8,128)(2,1)S(1)}, bf16[32,3200]{1,0:T(8,128)(2,1)S(1)}, u32[]{:S(2)}, u32[]{:S(2)}) collective-permute-start(bf16[32,3200]{1,0:T(8,128)(2,1)S(1)} %get-tuple-element.58), channel_id=1, source_target_pairs={{0,1},{1,0},{2,3},{3,2},{4,5},{5,4},{6,7},{7,6},{8,9},{9,8},{10,11... | collective-permute-start | bytes 614408 | tf_op jit(solution)/shard_map/ppermute | solution.py:396
  71.1 9.7 %collective-permute-start.12 = (bf16[200,256]{1,0:T(8,128)(2,1)S(1)}, bf16[200,256]{1,0:T(8,128)(2,1)S(1)}, u32[]{:S(2)}, u32[]{:S(2)}) collective-permute-start(bf16[200,256]{1,0:T(8,128)(2,1)S(1)} %partial_grad.1), channel_id=1, source_target_pairs={{0,192},{64,0},{128,64},{192,128},{1,193},{65,1},{129,65},{193,129... | collective-permute-start | bytes 307208 | tf_op jit(solution)/shard_map/ppermute | solution.py:396
  75.2 11.4 %collective-permute-start.11 = (bf16[200,256]{1,0:T(8,128)(2,1)S(1)}, bf16[200,256]{1,0:T(8,128)(2,1)S(1)}, u32[]{:S(2)}, u32[]{:S(2)}) collective-permute-start(bf16[200,256]{1,0:T(8,128)(2,1)S(1)} %partial_grad.1), channel_id=1, source_target_pairs={{0,64},{64,128},{128,192},{192,0},{1,65},{65,129},{129,193},{193,1... | collective-permute-start | bytes 307208 | tf_op jit(solution)/shard_map/ppermute | solution.py:396
  75.2 11.4 %collective-permute-start.10 = (bf16[200,256]{1,0:T(8,128)(2,1)S(1)}, bf16[200,256]{1,0:T(8,128)(2,1)S(1)}, u32[]{:S(2)}, u32[]{:S(2)}) collective-permute-start(bf16[200,256]{1,0:T(8,128)(2,1)S(1)} %partial_grad.1), channel_id=1, source_target_pairs={{0,128},{64,192},{128,0},{192,64},{1,129},{65,193},{129,1},{193,65... | collective-permute-start | bytes 307208 | tf_op jit(solution)/shard_map/ppermute | solution.py:396
  79.6 1.2 %collective-permute-start.13 = (f32[32]{0:T(128)S(1)}, f32[32]{0:T(128)S(1)}, u32[]{:S(2)}, u32[]{:S(2)}) collective-permute-start(f32[32]{0:T(128)S(1)} %reduce), channel_id=1, source_target_pairs={{0,1},{1,0},{2,3},{3,2},{4,5},{5,4},{6,7},{7,6},{8,9},{9,8},{10,11... | collective-permute-start | bytes 392 | tf_op jit(solution)/shard_map/ppermute | solution.py:396
  86.7 4.9 %collective-permute-start.15 = (bf16[200,256]{1,0:T(8,128)(2,1)S(1)}, bf16[200,256]{1,0:T(8,128)(2,1)S(1)}, u32[]{:S(2)}, u32[]{:S(2)}) collective-permute-start(bf16[200,256]{1,0:T(8,128)(2,1)S(1)} %add_convert_fusion), channel_id=1, source_target_pairs={{0,32},{32,0},{1,33},{33,1},{2,34},{34,2},{3,35},{35,3},{4,36},{36... | collective-permute-start | bytes 307208 | tf_op jit(solution)/shard_map/ppermute | solution.py:396
  91.7 7.0 %collective-permute-start.16 = (bf16[400,256]{1,0:T(8,128)(2,1)S(1)}, bf16[400,256]{1,0:T(8,128)(2,1)S(1)}, u32[]{:S(2)}, u32[]{:S(2)}) collective-permute-start(bf16[400,256]{1,0:T(8,128)(2,1)S(1)} %pad_maximum_fusion.1), channel_id=1, source_target_pairs={{0,2},{1,9},{2,4},{3,11},{4,6},{5,13},{6,0},{7,15},{8,10},{9,17},{... | collective-permute-start | bytes 614408 | tf_op jit(solution)/shard_map/ppermute | solution.py:407
  92.1 9.7 %collective-permute-start.19 = (bf16[400,256]{1,0:T(8,128)(2,1)S(1)}, bf16[400,256]{1,0:T(8,128)(2,1)S(1)}, u32[]{:S(2)}, u32[]{:S(2)}) collective-permute-start(bf16[400,256]{1,0:T(8,128)(2,1)S(1)} %pad_maximum_fusion.1), channel_id=1, source_target_pairs={{0,4},{1,17},{2,6},{3,19},{4,0},{5,21},{6,2},{7,23},{8,12},{9,25},... | collective-permute-start | bytes 614408 | tf_op jit(solution)/shard_map/ppermute | solution.py:407
  95.2 6.7 %collective-permute-start.20 = (bf16[400,256]{1,0:T(8,128)(2,1)S(1)}, bf16[400,256]{1,0:T(8,128)(2,1)S(1)}, u32[]{:S(2)}, u32[]{:S(2)}) collective-permute-start(bf16[400,256]{1,0:T(8,128)(2,1)S(1)} %pad_maximum_fusion.1), channel_id=1, source_target_pairs={{0,6},{1,25},{2,0},{3,27},{4,2},{5,29},{6,4},{7,31},{8,14},{9,1},{... | collective-permute-start | bytes 614408 | tf_op jit(solution)/shard_map/ppermute | solution.py:407
  98.7 9.6 %collective-permute-start.17 = (bf16[800,256]{1,0:T(8,128)(2,1)S(1)}, bf16[800,256]{1,0:T(8,128)(2,1)S(1)}, u32[]{:S(2)}, u32[]{:S(2)}) collective-permute-start(bf16[800,256]{1,0:T(8,128)(2,1)S(1)} %pad_maximum_fusion.refs_0_), channel_id=1, source_target_pairs={{0,8},{1,3},{2,10},{3,5},{4,12},{5,7},{6,14},{7,1},{8,16},{9,11},{... | collective-permute-start | bytes 1228808 | tf_op jit(solution)/shard_map/ppermute | solution.py:407
  101.9 8.0 %collective-permute-start.21 = (bf16[800,256]{1,0:T(8,128)(2,1)S(1)}, bf16[800,256]{1,0:T(8,128)(2,1)S(1)}, u32[]{:S(2)}, u32[]{:S(2)}) collective-permute-start(bf16[800,256]{1,0:T(8,128)(2,1)S(1)} %constant_dynamic-update-slice_fusion.refs_1_), channel_id=1, source_target_pairs={{0,24},{1,7},{2,26},{3,1},{4,28},{5,3},{6,30},{7,5},{8,0},{9,15},{... | collective-permute-start | bytes 1228808 | tf_op jit(solution)/shard_map/ppermute | solution.py:407
  103.3 11.0 %collective-permute-start.24 = (bf16[800,256]{1,0:T(8,128)(2,1)S(1)}, bf16[800,256]{1,0:T(8,128)(2,1)S(1)}, u32[]{:S(2)}, u32[]{:S(2)}) collective-permute-start(bf16[800,256]{1,0:T(8,128)(2,1)S(1)} %pad_maximum_fusion.refs_0_), channel_id=1, source_target_pairs={{0,24},{1,7},{2,26},{3,1},{4,28},{5,3},{6,30},{7,5},{8,0},{9,15},{... | collective-permute-start | bytes 1228808 | tf_op jit(solution)/shard_map/ppermute | solution.py:407
  104.6 9.7 %collective-permute-start.23 = (bf16[800,256]{1,0:T(8,128)(2,1)S(1)}, bf16[800,256]{1,0:T(8,128)(2,1)S(1)}, u32[]{:S(2)}, u32[]{:S(2)}) collective-permute-start(bf16[800,256]{1,0:T(8,128)(2,1)S(1)} %constant_dynamic-update-slice_fusion.refs_1_), channel_id=1, source_target_pairs={{0,8},{1,3},{2,10},{3,5},{4,12},{5,7},{6,14},{7,1},{8,16},{9,11},{... | collective-permute-start | bytes 1228808 | tf_op jit(solution)/shard_map/ppermute | solution.py:407
  108.3 9.9 %collective-permute-start.18 = (bf16[800,256]{1,0:T(8,128)(2,1)S(1)}, bf16[800,256]{1,0:T(8,128)(2,1)S(1)}, u32[]{:S(2)}, u32[]{:S(2)}) collective-permute-start(bf16[800,256]{1,0:T(8,128)(2,1)S(1)} %collective-permute-done.17.refs_2_), channel_id=1, source_target_pairs={{0,8},{1,3},{2,10},{3,5},{4,12},{5,7},{6,14},{7,1},{8,16},{9,11},{... | collective-permute-start | bytes 1228808 | tf_op jit(solution)/shard_map/ppermute | solution.py:407
  109.9 8.8 %collective-permute-start.22 = (bf16[800,256]{1,0:T(8,128)(2,1)S(1)}, bf16[800,256]{1,0:T(8,128)(2,1)S(1)}, u32[]{:S(2)}, u32[]{:S(2)}) collective-permute-start(bf16[800,256]{1,0:T(8,128)(2,1)S(1)} %collective-permute-done.21.refs_5_), channel_id=1, source_target_pairs={{0,24},{1,7},{2,26},{3,1},{4,28},{5,3},{6,30},{7,5},{8,0},{9,15},{... | collective-permute-start | bytes 1228808 | tf_op jit(solution)/shard_map/ppermute | solution.py:407
